TPU v7x, 256 devices: a whole 4x4x8 slice. The times are simulated.
256 devices in a mesh: slab: 128 (over y_hi, z, x, core), feat: 2 (over y_lo).
Axes of the slice: x: 4, y: 4 (y_hi: 2, y_lo: 2; y = y_hi * 2 + y_lo), z: 8, core: 2. Of those that a mesh axis runs over, the one named last changes fastest.
Arguments:
- node_feats: bfloat16 [128, 524288], P('feat', 'slab'), may hold values from -6 to 6
- neighbours: int32 [16, 524288], P(None, 'slab'), may hold values from 0 to 12287, as said below
- degrees: int32 [524288], P('slab'), may hold values from 1 to 16
- hub_rows: int32 [4096], P('slab'), may hold values from 0 to 4095, as said below
- weight: bfloat16 [128, 128], replicated, may hold values from -0.5 to 0.5
- bias_terms: float32 [128], replicated, may hold values from -3 to 3
Outputs:
- new_feats: bfloat16 [128, 524288], P('feat', 'slab')
Inputs may be any that keep to these rules, and one draw needn't show every extreme that they name: `neighbours`: slots index frame columns; positions 0..2047 are the lower halo (never used by slab 0), 6144..8191 the upper halo (never used by the last slab), from 8192 on the hub panel. `hub_rows`: distinct within each slab.
All inputs are finite; a program needn't handle non-finite values.
Results may differ from a plain program's by a relative error of at most 0.0034.
Values may be sent and summed in bfloat16 or wider, within the bound.
No kernel may reach another device: no remote copies, remote signals or barrier semaphores. Data moves between devices by JAX's collectives and lax.ppermute only.
A program may use at most 64 MiB of HBM per device.

v0:
```python
import jax
import jax.numpy as jnp
from jax import lax
from jax.sharding import PartitionSpec as P


def with_halo(block, sides, width):
    for axis, dim in sides:
        count = lax.axis_size(axis)
        forward = [(i, i + 1) for i in range(count - 1)]
        backward = [(target, source) for source, target in forward]
        low = lax.ppermute(
            lax.slice_in_dim(block, block.shape[dim] - width, None, axis=dim), axis, forward
        )
        high = lax.ppermute(lax.slice_in_dim(block, 0, width, axis=dim), axis, backward)
        block = jnp.concatenate([low, block, high], axis=dim)
    return block


def aggregate(frame_rows, zero_index, slot_ids, degree_counts, own_cols):
    slot_count, block_cols = slot_ids.shape
    chan_count = frame_rows.shape[1]
    slot_mask = jnp.arange(slot_count, dtype=jnp.int32)[:, None] < degree_counts[None, :]
    safe_ids = jnp.where(slot_mask, slot_ids, zero_index)
    picked = jnp.take(frame_rows, safe_ids.reshape(slot_count * block_cols), axis=0)
    picked = picked.reshape(slot_count, block_cols, chan_count).astype(jnp.float32)
    totals = jnp.sum(picked, axis=0) + own_cols.T.astype(jnp.float32)
    means = totals / (degree_counts + 1).astype(jnp.float32)[:, None]
    return means.T.astype(jnp.bfloat16)


def local(node_feats, neighbours, degrees, hub_rows, weight, bias_terms):
    chan_count, node_count = node_feats.shape
    slot_count = neighbours.shape[0]
    halo_width = node_count // 2
    padded = with_halo(node_feats, (("slab", 1),), halo_width)
    hub_local = jnp.take(node_feats, hub_rows, axis=1)
    hub_panel = lax.all_gather(hub_local, "slab", axis=1, tiled=True)
    frame = jnp.concatenate([padded, hub_panel], axis=1)
    frame_rows = jnp.concatenate([frame.T, jnp.zeros((1, chan_count), frame.dtype)], axis=0)
    zero_index = frame_rows.shape[0] - 1
    block_cols = min(node_count, 2048)
    block_count = node_count // block_cols
    slot_blocks = neighbours.reshape(slot_count, block_count, block_cols).transpose(1, 0, 2)
    degree_blocks = degrees.reshape(block_count, block_cols)
    own_blocks = node_feats.reshape(chan_count, block_count, block_cols).transpose(1, 0, 2)

    def one_block(inputs):
        return aggregate(frame_rows, zero_index, inputs[0], inputs[1], inputs[2])

    mean_blocks = lax.map(one_block, (slot_blocks, degree_blocks, own_blocks))
    mean_cols = mean_blocks.transpose(1, 0, 2).reshape(chan_count, node_count)
    channel_first = lax.axis_index("feat") * chan_count
    bias_part = lax.dynamic_slice_in_dim(bias_terms, channel_first, chan_count, 0)
    contract = (((0,), (0,)), ((), ()))
    weight_rows = lax.dynamic_slice_in_dim(weight, channel_first, chan_count, 0)
    product_terms = lax.dot_general(
        weight_rows, mean_cols, contract, preferred_element_type=jnp.float32
    )
    summed = lax.psum_scatter(product_terms, "feat", scatter_dimension=0, tiled=True)
    return jax.nn.relu(summed + bias_part[:, None]).astype(jnp.bfloat16)


def solution(mesh):
    in_specs = (P("feat", "slab"), P(None, "slab"), P("slab"), P("slab"), P(), P())
    out_specs = P("feat", "slab")
    return jax.shard_map(local, mesh=mesh, in_specs=in_specs, out_specs=out_specs, check_vma=False)
```

profile of v0, /device:TPU:16, one launch (start us, length us, event | category | flops | bytes accessed | tf_op | source)
XLA Modules:
  0.0 524.9 jit_solution(11113238992640638752)
XLA Ops:
  6.5 0.0 copy-start
  6.5 0.0 reduce-scatter.2.cloned.1.call-start
  6.5 1.5 copy.18
  8.1 0.1 fusion.7
  8.2 1.9 collective-permute-start
  10.1 9.4 %collective-permute-start.1 = (bf16[64,2048]{0,1:T(8,128)(2,1)S(1)}, bf16[64,2048]{0,1:T(8,128)(2,1)S(1)}, u32[]{:S(2)}, u32[]{:S(2)}) collective-permute-start(bf16[64,2048]{0,1:T(8,128)(2,1)S(1)} %get-tuple-element.65), channel_id=1, source_target_pairs={{2,0},{4,2},{6,4},{8,6},{10,8},{12,10},{14,12},{16,14},{18,16},{20... | collective-permute-start | bytes 786440 | tf_op jit(solution)/shard_map/ppermute | solution.py:15
  19.5 0.7 compare_select_fusion.2
  20.1 0.7 compare_and_fusion.1
  20.8 0.6 gather_fusion.1
  21.4 0.1 select_bitcast_fusion
  21.5 2.2 reshape.86
  23.7 1.9 reshape.85
  25.5 0.7 reshape.84
  26.3 179.7 %all_gather.3 = bf16[64,4096]{0,1:T(8,128)(2,1)S(1)} all-gather(bf16[64,32]{0,1:T(8,128)(2,1)S(1)} %select_bitcast_fusion), channel_id=1, replica_groups=mesh['slab'=128,'feat'=2] {'slab'}, dimensions={1}, use_global_device_ids=true | all-gather | bytes 528384 | tf_op jit(solution)/shard_map/all_gather | solution.py:38
  206.0 0.0 collective-permute-done
  206.0 0.0 collective-permute-done.1
  206.0 15.5 %maximum_bitcast_fusion = bf16[12288,64]{1,0:T(8,128)(2,1)S(1)} fusion(bf16[64,4096]{0,1:T(8,128)(2,1)S(1)} %all_gather.3, bf16[64,2048]{0,1:T(8,128)(2,1)S(1)} %collective-permute-done.1, bf16[64,4096]{0,1:T(8,128)(2,1)S(1)} %copy.18, bf16[64,2048]{0,1:T(8,128)(2,1)S(1)} %collective-permute-done), kind=kLoop, calls=%fused_computation.19 | loop fusion | flops 6291456 | bytes 3145728 | tf_op jit(solution)/shard_map/transpose | solution.py:40
  221.6 0.7 concatenate.7
  222.3 0.0 copy-start.2
  222.3 259.3 %while.10 = (s32[]{:T(128)}, bf16[2,64,2048]{1,2,0:T(8,128)(2,1)}, s32[2,2048]{1,0:T(2,128)S(1)}, s32[2,16,2048]{2,0,1:T(2,128)}, bf16[12289,64]{1,0:T(8,128)(2,1)S(1)}, /*index=5*/bf16[2,64,2048]{2,0,1:T(2,128)(2,1)}, s32[]{:T(128)}) while((s32[]{:T(128)}, bf16[2,64,2048]{1,2,0:T(8,128)(2,1)}, s32[2,2048]{1,0:T(2,128)S(1)}, ...), condition=%wide.region_2.3_spmd, body=%wide.region_0.0_spmd.sunk | while | flops 7114754 | bytes 19645044 | solution.py:51
  222.3 1.1 constant_dynamic-slice_fusion.8
  223.4 0.1 compare_and_fusion.3
  223.5 0.1 copy.41
  223.6 0.3 compare_select_fusion.4
  223.9 114.2 %gather_fusion = bf16[32768,64]{1,0:T(8,128)(2,1)} fusion(bf16[12289,64]{1,0:T(8,128)(2,1)S(1)} %get-tuple-element.125, s32[32768]{0:T(1024)S(1)} %broadcast_clamp_fusion.2), kind=kCustom, calls=%fused_computation.clone.1 | custom fusion | bytes 8519680 | tf_op jit(solution)/shard_map/while/body/eval_jaxpr/jit(_take)/gather | solution.py:25
  338.1 0.0 copy-start.1
  338.1 8.0 %convert_reduce_fusion.2 = f32[2048,64]{1,0:T(8,128)} fusion(bf16[16,2048,64]{2,1,0:T(8,128)(2,1)} %bitcast.56, pred[16,2048]{1,0:T(8,128)(4,1)S(1)} %get-tuple-element.106), kind=kLoop, calls=%fused_computation.2.clone.1 | loop fusion | flops 6160384 | bytes 4751360 | tf_op jit(solution)/shard_map/while/body/eval_jaxpr/reduce_sum | solution.py:27
  346.0 0.0 copy-done.1
  346.0 1.3 constant_dynamic-slice_fusion.7
  347.4 2.0 copy.40
  349.4 2.5 bitcast_dynamic-update-slice_fusion.2
  351.9 1.1 constant_dynamic-slice_fusion.8
  353.0 0.1 compare_and_fusion.3
  353.1 0.1 copy.41
  353.3 0.3 compare_select_fusion.4
  353.6 114.2 %gather_fusion = bf16[32768,64]{1,0:T(8,128)(2,1)} fusion(bf16[12289,64]{1,0:T(8,128)(2,1)S(1)} %get-tuple-element.125, s32[32768]{0:T(1024)S(1)} %broadcast_clamp_fusion.2), kind=kCustom, calls=%fused_computation.clone.1 | custom fusion | bytes 8519680 | tf_op jit(solution)/shard_map/while/body/eval_jaxpr/jit(_take)/gather | solution.py:25
  467.7 0.0 copy-start.1
  467.7 8.0 %convert_reduce_fusion.2 = f32[2048,64]{1,0:T(8,128)} fusion(bf16[16,2048,64]{2,1,0:T(8,128)(2,1)} %bitcast.56, pred[16,2048]{1,0:T(8,128)(4,1)S(1)} %get-tuple-element.106), kind=kLoop, calls=%fused_computation.2.clone.1 | loop fusion | flops 6160384 | bytes 4751360 | tf_op jit(solution)/shard_map/while/body/eval_jaxpr/reduce_sum | solution.py:27
  475.7 0.0 copy-done.1
  475.7 1.3 constant_dynamic-slice_fusion.7
  477.0 2.0 copy.40
  479.1 2.5 bitcast_dynamic-update-slice_fusion.2
  481.6 0.0 copy-done
  481.6 3.0 fusion.4
  484.6 0.0 reduce-scatter.2.cloned.1.call-update
  484.6 0.0 copy-done.2
  484.6 0.1 dynamic_slice.19
  484.7 31.2 %reduce-scatter.2.cloned.1.call-done = f32[64,4096]{1,0:T(8,128)} async-done(((f32[128,4096]{1,0:T(8,128)}), f32[64,4096]{1,0:T(8,128)}) %reduce-scatter.2.cloned.1.call-update) | async-done | bytes 1048592 | tf_op jit(solution)/shard_map/reduce_scatter | solution.py:60
  515.9 2.2 maximum_convert_fusion
  (8 shorter events, 0.1 us)
Async XLA Ops:
  6.5 475.0 %copy-start = (bf16[128,128]{1,0:T(8,128)(2,1)S(1)}, bf16[128,128]{1,0:T(8,128)(2,1)}, u32[]{:S(2)}) copy-start(bf16[128,128]{1,0:T(8,128)(2,1)} %param.12) | copy-start | bytes 98308
  6.5 509.3 %reduce-scatter.2.cloned.1.call-start = ((), (), s32[]{:S(2)}) async-start(), calls=%async_computation.1 | async-start | bytes 3145728 | tf_op jit(solution)/shard_map/reduce_scatter | solution.py:60
  8.2 197.9 %collective-permute-start = (bf16[64,2048]{0,1:T(8,128)(2,1)S(1)}, bf16[64,2048]{0,1:T(8,128)(2,1)S(1)}, u32[]{:S(2)}, u32[]{:S(2)}) collective-permute-start(bf16[64,2048]{0,1:T(8,128)(2,1)S(1)} %get-tuple-element.64), channel_id=1, source_target_pairs={{0,2},{2,4},{4,6},{6,8},{8,10},{10,12},{12,14},{14,16},{16,18},{18... | collective-permute-start | bytes 786440 | tf_op jit(solution)/shard_map/ppermute | solution.py:12
  10.1 195.9 %collective-permute-start.1 = (bf16[64,2048]{0,1:T(8,128)(2,1)S(1)}, bf16[64,2048]{0,1:T(8,128)(2,1)S(1)}, u32[]{:S(2)}, u32[]{:S(2)}) collective-permute-start(bf16[64,2048]{0,1:T(8,128)(2,1)S(1)} %get-tuple-element.65), channel_id=1, source_target_pairs={{2,0},{4,2},{6,4},{8,6},{10,8},{12,10},{14,12},{16,14},{18,16},{20... | collective-permute-start | bytes 786440 | tf_op jit(solution)/shard_map/ppermute | solution.py:15
  222.3 262.4 %copy-start.2 = (f32[128]{0:T(128)S(1)}, f32[128]{0:T(128)}, u32[]{:S(2)}) copy-start(f32[128]{0:T(128)} %param.13) | copy-start | bytes 1540
  338.1 8.0 %copy-start.1 = (bf16[2,64,2048]{2,0,1:T(2,128)(2,1)S(1)}, bf16[2,64,2048]{2,0,1:T(2,128)(2,1)}, u32[]{:S(2)}) copy-start(bf16[2,64,2048]{2,0,1:T(2,128)(2,1)} %get-tuple-element.126) | copy-start | bytes 1572868 | tf_op jit(solution)/shard_map/while
  467.7 8.0 %copy-start.1 = (bf16[2,64,2048]{2,0,1:T(2,128)(2,1)S(1)}, bf16[2,64,2048]{2,0,1:T(2,128)(2,1)}, u32[]{:S(2)}) copy-start(bf16[2,64,2048]{2,0,1:T(2,128)(2,1)} %get-tuple-element.126) | copy-start | bytes 1572868 | tf_op jit(solution)/shard_map/while
Sparse Core Ops, SparseCore 0:
  484.8 31.0 reduce-scatter.1
where the time goes:
time: 527 us; the launch traced here: 525 us
  local copies, waits for them, and re-layouts  245 us (46%)
  blocking collectives  180 us (34%)
  other arithmetic  40.8 us (8%)
  waiting for transfers between devices  31.2 us (6%)
  between operations  13.5 us (3%)
  starting transfers between devices  11.3 us (2%)
    gather x2, local copies, waits for them, and re-layouts, aggregate(): jnp.take(frame_rows, safe_ids.reshape(slot_count * block_cols), axis=0)  228 us
    all_gather x1, blocking collectives, local(): hub_panel = lax.all_gather(hub_local, 'slab', axis=1, tiled=True)  180 us
    reduce_scatter x1, waiting for transfers between devices, local(): lax.psum_scatter(product_terms, 'feat', scatter_dimension=0, tiled=True)  31.2 us
    reduce_sum x2, other arithmetic, aggregate(): totals = jnp.sum(picked, axis=0) + own_cols.T.astype(jnp.float32)  15.9 us
    transpose x1, other arithmetic, local(): frame_rows = jnp.concatenate([frame.T, jnp.zeros((1, chan_count), frame.d...  15.5 us
  transfers between devices with their start and end apart: 3, of which 1 were waited for; matrix products, arithmetic and copies ran while one was open for 1% of the time, Pallas kernels for 0%

commit v1 on v0

v1 whole, which is shorter than its diff:
```python
import functools

import jax
import jax.numpy as jnp
from jax import lax
from jax.experimental import pallas as pl
from jax.experimental.pallas import tpu as pltpu
from jax.sharding import PartitionSpec as P

VMEM = pltpu.VMEM
SMEM = pltpu.SMEM
LANES = 128
CHUNK = 1024
GROUP = 16
STAGES = (32, 8, 16, 64, 4, 2, 1)


def hub_pick_kernel(rows_ref, x_ref, out_ref):
    hubs, nodes = rows_ref.shape[1], x_ref.shape[1]
    diagonal = lax.broadcasted_iota(jnp.int32, (hubs, hubs), 0) == lax.broadcasted_iota(
        jnp.int32, (hubs, hubs), 1
    )
    rows = jnp.sum(jnp.where(diagonal, rows_ref[...], 0), axis=1, keepdims=True)
    onehot = (lax.broadcasted_iota(jnp.int32, (hubs, nodes), 1) == rows).astype(jnp.bfloat16)
    picked = lax.dot_general(
        onehot, x_ref[...], (((1,), (1,)), ((), ())), preferred_element_type=jnp.float32
    ).astype(jnp.bfloat16)
    out_ref[...] = jnp.concatenate([picked[: hubs // 2], picked[hubs // 2 :]], axis=1)


def frame_kernel(low_ref, x_ref, high_ref, after_ref, frame_ref):
    nodes = x_ref.shape[1]
    half = low_ref.shape[1]
    step = 256
    unit = (
        lax.broadcasted_iota(jnp.int32, (step, step), 0)
        == lax.broadcasted_iota(jnp.int32, (step, step), 1)
    ).astype(jnp.bfloat16)

    def fill(ref, first, count):
        for at in range(0, count, step):
            cols = ref[:, at : at + step]
            frame_ref[first + at : first + at + step, :] = lax.dot_general(
                unit,
                jnp.concatenate([cols, cols], axis=0),
                (((1,), (1,)), ((), ())),
                preferred_element_type=jnp.float32,
            )

    fill(low_ref, 0, half)
    fill(x_ref, half, nodes)
    fill(high_ref, half + nodes, half)
    frame_ref[2 * half + nodes :, :] = jnp.zeros((8, LANES), jnp.float32)


def hub_frame_kernel(near_ref, far_ref, frame_ref):
    blocks = near_ref.shape[0] // 16
    me = lax.axis_index("slab")
    lane = lax.broadcasted_iota(jnp.int32, (16, LANES), 1)
    for p in range(2 * blocks):
        ref, i = (near_ref, p) if p < blocks else (far_ref, p - blocks)
        differs = sum(bit for k, bit in enumerate(STAGES) if p >> k & 1)
        pair = ref[16 * i : 16 * i + 16, :].astype(jnp.float32)
        turned = pltpu.roll(pair, LANES // 2, 1)
        at = pl.multiple_of((me ^ differs) * 32, 32)
        frame_ref[pl.ds(at, 16), :] = jnp.where(lane < LANES // 2, pair, turned)
        frame_ref[pl.ds(at + 16, 16), :] = jnp.where(lane < LANES // 2, turned, pair)
    frame_ref[64 * blocks :, :] = jnp.zeros((8, LANES), jnp.float32)


def comparators(count):
    pairs, p = [], 1
    while p < count:
        k = p
        while k >= 1:
            for j in range(k % p, count - k, 2 * k):
                for i in range(min(k, count - j - k)):
                    if (i + j) // (2 * p) == (i + j + k) // (2 * p):
                        pairs.append((i + j, i + j + k))
            k //= 2
        p *= 2
    return pairs


def sort_network(values):
    for a, b in comparators(len(values)):
        values[a], values[b] = jnp.minimum(values[a], values[b]), jnp.maximum(values[a], values[b])
    return values


def sorted_tiles(keys):
    shape = keys.shape
    sub = lax.broadcasted_iota(jnp.int32, shape, 1)
    lane = lax.broadcasted_iota(jnp.int32, shape, 2)
    at = sub * LANES + lane
    size = 2
    while size <= CHUNK:
        distance = size // 2
        while distance >= 1:
            axis, by, extent = (2, distance, LANES) if distance < LANES else (1, distance // LANES, 8)
            lower = (at & distance) == 0
            partner = jnp.where(
                lower, pltpu.roll(keys, extent - by, axis), pltpu.roll(keys, by, axis)
            )
            ascending = (at & size) == 0
            keys = jnp.where(
                lower == ascending, jnp.minimum(keys, partner), jnp.maximum(keys, partner)
            )
            distance //= 2
        size *= 2
    return keys


def plan_kernel(first, after, nbr_ref, deg_ref, after_ref, ids_ref, order_ref, class_ref):
    slots = nbr_ref.shape[0]
    chunks = deg_ref.shape[0] // 8
    at = lax.broadcasted_iota(jnp.int32, (8, LANES), 0) * LANES + lax.broadcasted_iota(
        jnp.int32, (8, LANES), 1
    )
    keys = []
    for c in range(chunks):
        rows = slice(8 * c, 8 * c + 8)
        degree = deg_ref[rows, :]
        ids = []
        count = jnp.zeros((8, LANES), jnp.int32)
        for j in range(slots):
            nbr = nbr_ref[j, rows, :]
            inside = (degree > j) & ((nbr < after) if first == 0 else (nbr >= first))
            ids.append(jnp.where(inside, nbr, after) - first)
            count = count + inside.astype(jnp.int32)
        for j, sorted_ids in enumerate(sort_network(ids)):
            ids_ref[c, j] = sorted_ids
        keys.append(count * CHUNK + at)
    keys = sorted_tiles(jnp.stack(keys))
    order_ref[...] = keys & (CHUNK - 1)
    class_ref[...] = keys >> 10


def scale_kernel(deg_ref, after_ref, scale_ref):
    half = CHUNK // LANES // 2
    inverse = 1.0 / (deg_ref[...] + 1).astype(jnp.float32)
    for c in range(scale_ref.shape[0]):
        for t in range(half):
            a = inverse[8 * c + t : 8 * c + t + 1, :]
            b = inverse[8 * c + half + t : 8 * c + half + t + 1, :]
            both = jnp.concatenate(
                [jnp.broadcast_to(row, (LANES // 2, LANES)) for row in (a, b)], axis=0
            )
            scale_ref[c, LANES * t : LANES * (t + 1), :] = both.T


def halo_kernel(x_ref, after_ref, low_ref, high_ref):
    half = low_ref.shape[1]
    low_ref[...] = x_ref[:, half:]
    high_ref[...] = x_ref[:, :half]


def add_tree(parts):
    while len(parts) > 1:
        tail = [parts[-1]] if len(parts) % 2 else []
        parts = [parts[i] + parts[i + 1] for i in range(0, len(parts) - 1, 2)] + tail
    return parts[0]


def load_plan(slots, chunk, ids_ref, order_ref, class_ref, slot_ids, order, classes, sem):
    rows = pl.ds(chunk * CHUNK, CHUNK)
    first = [
        pltpu.make_async_copy(order_ref.at[rows], order, sem.at[slots]),
        pltpu.make_async_copy(class_ref.at[rows], classes.at[pl.ds(0, CHUNK)], sem.at[slots + 1]),
    ]
    by_slot = [
        pltpu.make_async_copy(
            ids_ref.at[pl.ds((chunk * slots + j) * CHUNK, CHUNK)],
            slot_ids.at[pl.ds(j * CHUNK, CHUNK)],
            sem.at[j],
        )
        for j in range(slots)
    ]
    for copy in first + by_slot:
        copy.start()
    return first, by_slot


def sum_slots(slots, by_slot, slot_ids, order, classes, frame_ref, total_ref):
    last = GROUP - 1
    classes[CHUNK + last] = slots + 1
    of_slot = [slot_ids.at[pl.ds(j * CHUNK, CHUNK)] for j in range(slots)]

    def body(count, carry):
        g, _ = carry
        base = g * GROUP
        for k in range(GROUP):
            node = order[base + k]
            total_ref[pl.ds(node, 1), :] = add_tree(
                [frame_ref[pl.ds(of_slot[j][node], 1), :] for j in range(count)]
            )
        return g + 1, classes[base + GROUP + last]

    def skip(carry):
        g, _ = carry
        return g + 1, classes[g * GROUP + GROUP + last]

    carry = (jnp.int32(0), classes[last])
    carry = lax.while_loop(lambda carry: carry[1] == 0, skip, carry)
    for count in range(1, slots + 1):
        by_slot[count - 1].wait()
        carry = lax.while_loop(
            lambda carry, count=count: carry[1] == count, functools.partial(body, count), carry
        )


def near_kernel(slots, chunk, own, ids_ref, order_ref, class_ref, frame_ref, after_ref, total_ref, *plan):
    first, by_slot = load_plan(slots, chunk, ids_ref, order_ref, class_ref, *plan)
    total_ref[...] = jnp.zeros_like(total_ref)
    for copy in first:
        copy.wait()
    sum_slots(slots, by_slot, *plan[:3], frame_ref, total_ref)
    total_ref[...] = total_ref[...] + frame_ref[pl.ds(own + chunk * CHUNK, CHUNK), :]


def far_kernel(slots, chunk, ids_ref, order_ref, class_ref, frame_ref, near_ref, scale_ref, after_ref, out_ref, total_ref, *plan):
    first, by_slot = load_plan(slots, chunk, ids_ref, order_ref, class_ref, *plan)
    total_ref[...] = jnp.zeros_like(total_ref)
    for copy in first:
        copy.wait()
    sum_slots(slots, by_slot, *plan[:3], frame_ref, total_ref)
    pairs = out_ref.shape[0]
    step = 64
    lane = lax.broadcasted_iota(jnp.int32, (step, LANES), 1)
    for at in range(0, pairs, step):
        a, b = slice(at, at + step), slice(pairs + at, pairs + at + step)
        total = jnp.where(
            lane < LANES // 2, total_ref[a, :] + near_ref[a, :], total_ref[b, :] + near_ref[b, :]
        )
        out_ref[a, :] = (total * scale_ref[chunk, a, :]).astype(jnp.bfloat16)


def join_kernel(near_ref, far_ref, after_ref, out_ref):
    rows = near_ref.shape[0]
    out_ref[:rows] = near_ref[...]
    out_ref[rows:] = far_ref[...]


def layer_kernel(chunks, weight_ref, bias_ref, *refs):
    mine, theirs, out_ref = refs[:chunks], refs[chunks : 2 * chunks], refs[2 * chunks]
    pairs = mine[0].shape[0]
    chans = out_ref.shape[0]
    first = lax.axis_index("feat") == 0
    by_out = weight_ref[...].astype(jnp.float32).T
    by_out = jnp.where(first, by_out[:chans], by_out[chans:]).astype(jnp.bfloat16)
    own = jnp.where(first, by_out[:, :chans], by_out[:, chans:])
    far = jnp.where(first, by_out[:, chans:], by_out[:, :chans])
    none = jnp.zeros_like(own)
    weights = [
        jnp.concatenate([own, none, far, none], axis=1),
        jnp.concatenate([none, own, none, far], axis=1),
    ]
    row = lax.broadcasted_iota(jnp.int32, (chans, 2 * chans), 0) + jnp.where(first, 0, chans)
    lane = lax.broadcasted_iota(jnp.int32, (chans, 2 * chans), 1)
    bias = jnp.sum(jnp.where(row == lane, bias_ref[...], 0.0), axis=1, keepdims=True)
    for c in range(chunks):
        rows = jnp.concatenate([mine[c][...], theirs[c][...]], axis=1)
        for h in range(2):
            product = lax.dot_general(
                weights[h], rows, (((1,), (1,)), ((), ())), preferred_element_type=jnp.float32
            )
            out_ref[:, pl.ds((2 * c + h) * pairs, pairs)] = jnp.maximum(product + bias, 0.0).astype(
                jnp.bfloat16
            )


def pallas(kernel, out_shape, in_specs, scratch=(), us=1.0):
    return pl.pallas_call(
        kernel,
        out_shape=out_shape,
        in_specs=in_specs,
        out_specs=jax.tree.map(lambda _: IN_VMEM, out_shape),
        scratch_shapes=list(scratch),
        compiler_params=pltpu.CompilerParams(vmem_limit_bytes=6 * 2**20),
        cost_estimate=pl.CostEstimate(flops=0, bytes_accessed=int(us * 3_000_000), transcendentals=0),
    )


IN_VMEM = pl.BlockSpec(memory_space=VMEM)
ANYWHERE = pl.BlockSpec(memory_space=pl.ANY)


def local(node_feats, neighbours, degrees, hub_rows, weight, bias_terms):
    chans, nodes = node_feats.shape
    slots = neighbours.shape[0]
    hubs = hub_rows.shape[0]
    slabs = lax.axis_size("slab")
    half = nodes // 2
    chunks = nodes // CHUNK
    pairs = CHUNK // 2

    block = pallas(
        hub_pick_kernel, jax.ShapeDtypeStruct((hubs // 2, 2 * chans), jnp.bfloat16), [IN_VMEM] * 2
    )(hub_rows[None, :], node_feats)

    def stage(block, bit):
        return lax.ppermute(block, "slab", [(i, i ^ bit) for i in range(slabs)])

    table = jax.ShapeDtypeStruct((chunks, slots, 8, LANES), jnp.int32)
    tiles = jax.ShapeDtypeStruct((chunks, 8, LANES), jnp.int32)
    frame_rows, hub_count = 2 * half + nodes, slabs * hubs
    nbr_tiles = neighbours.reshape(slots, nodes // LANES, LANES)
    deg_tiles = degrees.reshape(nodes // LANES, LANES)

    def plan(first, after, behind):
        return pallas(
            functools.partial(plan_kernel, first, after),
            (table, tiles, tiles),
            [IN_VMEM, IN_VMEM, ANYWHERE],
            us=3.0,
        )(nbr_tiles, deg_tiles, behind)

    near_plan = plan(0, frame_rows, block)

    plan_scratch = [
        SMEM((slots * CHUNK,), jnp.int32),
        SMEM((CHUNK,), jnp.int32),
        SMEM((CHUNK + GROUP,), jnp.int32),
        pltpu.SemaphoreType.DMA((slots + 2,)),
    ]
    totals = jax.ShapeDtypeStruct((CHUNK, LANES), jnp.float32)
    beside = [near_plan[1]]
    near = []
    for k, bit in enumerate(STAGES):
        arrived = stage(block, bit)
        if k == len(STAGES) - 1:
            break
        if k == 1:
            halo = jax.ShapeDtypeStruct((chans, half), jnp.bfloat16)
            low, high = pallas(halo_kernel, (halo, halo), [IN_VMEM, ANYWHERE], us=0.3)(node_feats, block)
            low = lax.ppermute(low, "slab", [(i, i + 1) for i in range(slabs - 1)])
            high = lax.ppermute(high, "slab", [(i + 1, i) for i in range(slabs - 1)])
            far_plan = plan(frame_rows, frame_rows + hub_count, block)
            scale = pallas(
                scale_kernel,
                jax.ShapeDtypeStruct((chunks, pairs, LANES), jnp.float32),
                [IN_VMEM, ANYWHERE],
            )(deg_tiles, far_plan[1])
            frame = pallas(
                frame_kernel,
                jax.ShapeDtypeStruct((frame_rows + 8, LANES), jnp.float32),
                [IN_VMEM] * 3 + [ANYWHERE],
                us=2.0,
            )(low, node_feats, high, scale)
            beside.append(frame)
        if k >= 2:
            near.append(
                pallas(
                    functools.partial(near_kernel, slots, k - 2, half),
                    totals,
                    [ANYWHERE] * 3 + [IN_VMEM, ANYWHERE],
                    plan_scratch,
                    us=6.0,
                )(*(a.reshape(-1) for a in near_plan), frame, block)
            )
            beside.append(near[-1])
        rows = block.shape[0]
        block = pallas(
            join_kernel,
            jax.ShapeDtypeStruct((2 * rows, 2 * chans), jnp.bfloat16),
            [IN_VMEM, IN_VMEM, ANYWHERE],
            us=0.5,
        )(block, arrived, beside[k])

    hub_frame = pallas(
        hub_frame_kernel, jax.ShapeDtypeStruct((hub_count + 8, LANES), jnp.float32), [IN_VMEM, IN_VMEM]
    )(block, arrived)

    swap = [(0, 1), (1, 0)]
    mine, theirs = [], []
    for c in range(chunks):
        after = theirs[c - 2] if c >= 2 else hub_rows
        rows = pallas(
            functools.partial(far_kernel, slots, c),
            jax.ShapeDtypeStruct((pairs, 2 * chans), jnp.bfloat16),
            [ANYWHERE] * 3 + [IN_VMEM] * 3 + [ANYWHERE],
            [VMEM((CHUNK, LANES), jnp.float32)] + plan_scratch,
            us=3.0,
        )(*(a.reshape(-1) for a in far_plan), hub_frame, near[c], scale, after)
        mine.append(rows)
        theirs.append(lax.ppermute(rows, "feat", swap))

    return pallas(
        functools.partial(layer_kernel, chunks),
        jax.ShapeDtypeStruct((chans, nodes), jnp.bfloat16),
        [IN_VMEM] * (2 + 2 * chunks),
    )(weight, bias_terms[None, :], *mine, *theirs)


def solution(mesh):
    in_specs = (P("feat", "slab"), P(None, "slab"), P("slab"), P("slab"), P(), P())
    return jax.shard_map(local, mesh=mesh, in_specs=in_specs, out_specs=P("feat", "slab"), check_vma=False)
```

time: 527 us -> 93.1 us (0.18)
  the two profiles are of different devices: /device:TPU:16 before, /device:TPU:6 now
where the time goes in v1:
time: 93.1 us; the launch traced here: 92.6 us
  Pallas kernels  52.1 us (56%)
  starting transfers between devices  28.3 us (30%)
  local copies, waits for them, and re-layouts  6.22 us (7%)
  waiting for transfers between devices  5.71 us (6%)
    pallas_call x4, Pallas kernels, local(): pallas(functools.partial(near_kernel, slots, k - 2, half), totals, [ANYWH...  29 us
    ppermute x7, starting transfers between devices, stage(): return lax.ppermute(block, 'slab', [(i, i ^ bit) for i in range(slabs)])  18.3 us
    pallas_call x4, Pallas kernels, local(): pallas(functools.partial(far_kernel, slots, c), jax.ShapeDtypeStruct((pai...  11.5 us
    pallas_call x2, Pallas kernels, plan(): pallas(functools.partial(plan_kernel, first, after), (table, tiles, tiles...  7.58 us
    unnamed x19, local copies, waits for them, and re-layouts  6.22 us
    ppermute x4, starting transfers between devices, local(): theirs.append(lax.ppermute(rows, 'feat', swap))  4.4 us
    ppermute x4, waiting for transfers between devices, local(): theirs.append(lax.ppermute(rows, 'feat', swap))  4.17 us
    ppermute x1, starting transfers between devices, local(): high = lax.ppermute(high, 'slab', [(i + 1, i) for i in range(slabs - 1)])  3.64 us
  transfers between devices with their start and end apart: 13, of which 3 were waited for; matrix products, arithmetic and copies ran while one was open for 1% of the time, Pallas kernels for 51%

profile of v1, /device:TPU:6, one launch (start us, length us, event | category | flops | bytes accessed | tf_op | source)
XLA Modules:
  0.0 92.6 jit_solution(7929531562188997122)
XLA Ops:
  0.0 0.0 copy-start
  0.0 1.0 %copy-done = bf16[64,4096]{1,0:T(8,128)(2,1)S(1)} copy-done((bf16[64,4096]{1,0:T(8,128)(2,1)S(1)}, bf16[64,4096]{1,0:T(8,128)(2,1)}, u32[]{:S(2)}) %copy-start) | copy-done | bytes 524312
  1.0 0.0 copy-start.6
  1.0 0.7 copy-done.6
  1.7 0.4 shard_map.64.after_ref.near_ref
  2.1 7.2 %collective-permute-start = (bf16[16,128]{1,0:T(8,128)(2,1)S(1)}, bf16[16,128]{1,0:T(8,128)(2,1)S(1)}, u32[]{:S(2)}, u32[]{:S(2)}) collective-permute-start(bf16[16,128]{1,0:T(8,128)(2,1)S(1)} %shard_map.64.after_ref.near_ref), channel_id=1, source_target_pairs={{0,64},{2,66},{4,68},{6,70},{8,72},{10,74},{12,76},{14,78},{16,80}... | collective-permute-start | bytes 12296 | tf_op jit(solution)/shard_map/ppermute | solution.py:302
  9.3 1.0 %copy.7 = s32[2,8,32,128]{3,2,1,0:T(8,128)S(1)} copy(s32[2,8,32,128]{3,1,2,0:T(8,128)} %bitcast.42) | data formatting | bytes 524288
  10.3 0.0 copy-start.3
  10.4 0.7 copy-done.3
  11.1 3.8 %shard_map.65 = (s32[4,16,8,128]{3,2,1,0:T(8,128)S(1)}, s32[4,8,128]{2,1,0:T(8,128)S(1)}, s32[4,8,128]{2,1,0:T(8,128)S(1)}) custom-call(s32[16,32,128]{2,1,0:T(8,128)S(1)} %bitcast.19, s32[32,128]{1,0:T(8,128)S(1)} %bitcast.37, bf16[16,128]{1,0:T(8,128)(2,1)S(1)} %shard_map.64.after_ref.near_ref), custom_call_target="tpu_custom_call" | custom-call | bytes 9000000 | tf_op jit(solution)/shard_map/pallas_call | solution.py:311
  14.9 0.0 collective-permute-done.far_ref
  14.9 0.0 copy-start.1
  14.9 1.0 %copy-done.1 = bf16[64,4096]{1,0:T(8,128)(2,1)S(1)} copy-done((bf16[64,4096]{1,0:T(8,128)(2,1)S(1)}, bf16[64,4096]{1,0:T(8,128)(2,1)}, u32[]{:S(2)}) %copy-start.1) | copy-done | bytes 524312
  16.0 1.9 %collective-permute-start.2 = (bf16[64,2048]{1,0:T(8,128)(2,1)S(1)}, bf16[64,2048]{1,0:T(8,128)(2,1)S(1)}, u32[]{:S(2)}, u32[]{:S(2)}) collective-permute-start(bf16[64,2048]{1,0:T(8,128)(2,1)S(1)} %get-tuple-element.17), channel_id=1, source_target_pairs={{0,2},{2,4},{4,6},{6,8},{8,10},{10,12},{12,14},{14,16},{16,18},{18... | collective-permute-start | bytes 786440 | tf_op jit(solution)/shard_map/ppermute | solution.py:336
  17.9 3.6 %collective-permute-start.3 = (bf16[64,2048]{1,0:T(8,128)(2,1)S(1)}, bf16[64,2048]{1,0:T(8,128)(2,1)S(1)}, u32[]{:S(2)}, u32[]{:S(2)}) collective-permute-start(bf16[64,2048]{1,0:T(8,128)(2,1)S(1)} %get-tuple-element.18), channel_id=1, source_target_pairs={{2,0},{4,2},{6,4},{8,6},{10,8},{12,10},{14,12},{16,14},{18,16},{20... | collective-permute-start | bytes 786440 | tf_op jit(solution)/shard_map/ppermute | solution.py:337
  21.5 1.1 %collective-permute-start.1 = (bf16[32,128]{1,0:T(8,128)(2,1)S(1)}, bf16[32,128]{1,0:T(8,128)(2,1)S(1)}, u32[]{:S(2)}, u32[]{:S(2)}) collective-permute-start(bf16[32,128]{1,0:T(8,128)(2,1)S(1)} %shard_map.66.after_ref.near_ref), channel_id=1, source_target_pairs={{0,16},{2,18},{4,20},{6,22},{8,24},{10,26},{12,28},{14,30},{16,0},... | collective-permute-start | bytes 24584 | tf_op jit(solution)/shard_map/ppermute | solution.py:302
  22.7 0.0 copy-start.4
  22.7 0.7 copy-done.4
  23.4 3.8 %shard_map.67 = (s32[4,16,8,128]{3,2,1,0:T(8,128)S(1)}, s32[4,8,128]{2,1,0:T(8,128)S(1)}, s32[4,8,128]{2,1,0:T(8,128)S(1)}) custom-call(s32[16,32,128]{2,1,0:T(8,128)S(1)} %bitcast.20, s32[32,128]{1,0:T(8,128)S(1)} %bitcast.38, bf16[32,128]{1,0:T(8,128)(2,1)S(1)} %shard_map.66.after_ref.near_ref), custom_call_target="tpu_custom_call" | custom-call | bytes 9000000 | tf_op jit(solution)/shard_map/pallas_call | solution.py:311
  27.2 0.3 shard_map.69.after_ref.scale_ref
  27.5 0.0 collective-permute-done.2.low_ref
  27.5 0.0 collective-permute-done.3.high_ref
  27.5 0.0 copy-start.2
  27.6 1.0 %copy-done.2 = bf16[64,4096]{1,0:T(8,128)(2,1)S(1)} copy-done((bf16[64,4096]{1,0:T(8,128)(2,1)S(1)}, bf16[64,4096]{1,0:T(8,128)(2,1)}, u32[]{:S(2)}) %copy-start.2) | copy-done | bytes 524312
  28.6 1.2 %shard_map.70.after_ref.frame_ref = f32[8200,128]{1,0:T(8,128)S(1)} custom-call(bf16[64,2048]{1,0:T(8,128)(2,1)S(1)} %collective-permute-done.2.low_ref, bf16[64,4096]{1,0:T(8,128)(2,1)S(1)} %copy-done.2, bf16[64,2048]{1,0:T(8,128)(2,1)S(1)} %collective-permute-done.3.high_ref, f32[4,512,128]{2,1,0:T(8,128)S(1)} %shard_map.69.after_ref.scale_ref), custom_call_target="tpu_custom_call" | custom-call | bytes 6000000 | tf_op jit(solution)/shard_map/pallas_call | solution.py:344
  29.8 0.0 collective-permute-done.1.far_ref
  29.9 1.6 %collective-permute-start.4 = (bf16[64,128]{1,0:T(8,128)(2,1)S(1)}, bf16[64,128]{1,0:T(8,128)(2,1)S(1)}, u32[]{:S(2)}, u32[]{:S(2)}) collective-permute-start(bf16[64,128]{1,0:T(8,128)(2,1)S(1)} %shard_map.71.after_ref.near_ref), channel_id=1, source_target_pairs={{0,32},{2,34},{4,36},{6,38},{8,40},{10,42},{12,44},{14,46},{16,48}... | collective-permute-start | bytes 49160 | tf_op jit(solution)/shard_map/ppermute | solution.py:302
  31.4 7.2 %shard_map.72.after_ref.near_ref = f32[1024,128]{1,0:T(8,128)S(1)} custom-call(s32[65536]{0:T(1024)S(1)} %bitcast.15, s32[4096]{0:T(1024)S(1)} %bitcast.25, s32[4096]{0:T(1024)S(1)} %bitcast.33, f32[8200,128]{1,0:T(8,128)S(1)} %shard_map.70.after_ref.frame_ref, bf16[64,128]{1,0:T(8,128)(2,1)S(1)} %shard_map.71.after_ref.near_ref), custom_call_target="tpu_custom_call" | custom-call | bytes 18000000 | tf_op jit(solution)/shard_map/pallas_call | solution.py:353
  38.6 0.0 collective-permute-done.4.far_ref
  38.6 3.2 %collective-permute-start.5 = (bf16[128,128]{1,0:T(8,128)(2,1)S(1)}, bf16[128,128]{1,0:T(8,128)(2,1)S(1)}, u32[]{:S(2)}, u32[]{:S(2)}) collective-permute-start(bf16[128,128]{1,0:T(8,128)(2,1)S(1)} %shard_map.73.after_ref.near_ref), channel_id=1, source_target_pairs={{0,128},{2,130},{4,132},{6,134},{8,136},{10,138},{12,140},{14,142}... | collective-permute-start | bytes 98312 | tf_op jit(solution)/shard_map/ppermute | solution.py:302
  41.8 7.1 %shard_map.74.after_ref.near_ref = f32[1024,128]{1,0:T(8,128)S(1)} custom-call(s32[65536]{0:T(1024)S(1)} %bitcast.16, s32[4096]{0:T(1024)S(1)} %bitcast.26, s32[4096]{0:T(1024)S(1)} %bitcast.34, f32[8200,128]{1,0:T(8,128)S(1)} %shard_map.70.after_ref.frame_ref, bf16[128,128]{1,0:T(8,128)(2,1)S(1)} %shard_map.73.after_ref.near_ref), custom_call_target="tpu_custom_call" | custom-call | bytes 18000000 | tf_op jit(solution)/shard_map/pallas_call | solution.py:353
  48.9 0.0 collective-permute-done.5.far_ref
  48.9 1.7 %collective-permute-start.6 = (bf16[256,128]{1,0:T(8,128)(2,1)S(1)}, bf16[256,128]{1,0:T(8,128)(2,1)S(1)}, u32[]{:S(2)}, u32[]{:S(2)}) collective-permute-start(bf16[256,128]{1,0:T(8,128)(2,1)S(1)} %shard_map.75.after_ref.near_ref), channel_id=1, source_target_pairs={{0,8},{2,10},{4,12},{6,14},{8,0},{10,2},{12,4},{14,6},{16,24},{18,... | collective-permute-start | bytes 196616 | tf_op jit(solution)/shard_map/ppermute | solution.py:302
  50.6 7.5 %shard_map.76.after_ref.near_ref = f32[1024,128]{1,0:T(8,128)S(1)} custom-call(s32[65536]{0:T(1024)S(1)} %bitcast.17, s32[4096]{0:T(1024)S(1)} %bitcast.27, s32[4096]{0:T(1024)S(1)} %bitcast.35, f32[8200,128]{1,0:T(8,128)S(1)} %shard_map.70.after_ref.frame_ref, bf16[256,128]{1,0:T(8,128)(2,1)S(1)} %shard_map.75.after_ref.near_ref), custom_call_target="tpu_custom_call" | custom-call | bytes 18000000 | tf_op jit(solution)/shard_map/pallas_call | solution.py:353
  58.1 0.0 collective-permute-done.6.far_ref
  58.1 0.0 copy-start.7
  58.1 3.5 %collective-permute-start.7 = (bf16[512,128]{1,0:T(8,128)(2,1)S(1)}, bf16[512,128]{1,0:T(8,128)(2,1)S(1)}, u32[]{:S(2)}, u32[]{:S(2)}) collective-permute-start(bf16[512,128]{1,0:T(8,128)(2,1)S(1)} %shard_map.77.after_ref.near_ref), channel_id=1, source_target_pairs={{0,4},{2,6},{4,0},{6,2},{8,12},{10,14},{12,8},{14,10},{16,20},{18,... | collective-permute-start | bytes 393224 | tf_op jit(solution)/shard_map/ppermute | solution.py:302
  61.6 7.3 %shard_map.78.after_ref.near_ref = f32[1024,128]{1,0:T(8,128)S(1)} custom-call(s32[65536]{0:T(1024)S(1)} %bitcast.18, s32[4096]{0:T(1024)S(1)} %bitcast.28, s32[4096]{0:T(1024)S(1)} %bitcast.36, f32[8200,128]{1,0:T(8,128)S(1)} %shard_map.70.after_ref.frame_ref, bf16[512,128]{1,0:T(8,128)(2,1)S(1)} %shard_map.77.after_ref.near_ref), custom_call_target="tpu_custom_call" | custom-call | bytes 18000000 | tf_op jit(solution)/shard_map/pallas_call | solution.py:353
  68.9 0.0 collective-permute-done.7.far_ref
  68.9 0.1 collective-permute-start.8
  69.0 1.5 %collective-permute-done.8.far_ref = bf16[1024,128]{1,0:T(8,128)(2,1)S(1)} collective-permute-done((bf16[1024,128]{1,0:T(8,128)(2,1)S(1)}, bf16[1024,128]{1,0:T(8,128)(2,1)S(1)}, u32[]{:S(2)}, u32[]{:S(2)}) %collective-permute-start.8) | collective-permute-done | bytes 262176 | tf_op jit(solution)/shard_map/ppermute | solution.py:302
  70.5 0.3 shard_map.80.frame_ref
  70.8 0.0 copy-done.7
  70.8 2.9 %shard_map.81.refs_0_ = bf16[512,128]{1,0:T(8,128)(2,1)S(1)} custom-call(s32[65536]{0:T(1024)S(1)} %bitcast.11, s32[4096]{0:T(1024)S(1)} %bitcast.21, s32[4096]{0:T(1024)S(1)} %bitcast.29, f32[4104,128]{1,0:T(8,128)S(1)} %shard_map.80.frame_ref, f32[1024,128]{1,0:T(8,128)S(1)} %shard_map.72.after_ref.near_ref, ...), custom_call_target="tpu_custom_call" | custom-call | bytes 9000000 | tf_op jit(solution)/shard_map/pallas_call | solution.py:378
  73.7 0.8 collective-permute-start.9
  74.4 2.9 %shard_map.82.refs_1_ = bf16[512,128]{1,0:T(8,128)(2,1)S(1)} custom-call(s32[65536]{0:T(1024)S(1)} %bitcast.12, s32[4096]{0:T(1024)S(1)} %bitcast.22, s32[4096]{0:T(1024)S(1)} %bitcast.30, f32[4104,128]{1,0:T(8,128)S(1)} %shard_map.80.frame_ref, f32[1024,128]{1,0:T(8,128)S(1)} %shard_map.74.after_ref.near_ref, ...), custom_call_target="tpu_custom_call" | custom-call | bytes 9000000 | tf_op jit(solution)/shard_map/pallas_call | solution.py:378
  77.3 0.0 copy-start.5
  77.3 0.0 copy-start.8
  77.3 1.4 %collective-permute-start.10 = (bf16[512,128]{1,0:T(8,128)(2,1)S(1)}, bf16[512,128]{1,0:T(8,128)(2,1)S(1)}, u32[]{:S(2)}, u32[]{:S(2)}) collective-permute-start(bf16[512,128]{1,0:T(8,128)(2,1)S(1)} %shard_map.82.refs_1_), channel_id=1, source_target_pairs={{0,1},{1,0},{2,3},{3,2},{4,5},{5,4},{6,7},{7,6},{8,9},{9,8},{10,11... | collective-permute-start | bytes 393224 | tf_op jit(solution)/shard_map/ppermute | solution.py:386
  78.8 0.5 collective-permute-done.9.after_ref.refs_4_
  79.3 2.9 %shard_map.83.refs_2_ = bf16[512,128]{1,0:T(8,128)(2,1)S(1)} custom-call(s32[65536]{0:T(1024)S(1)} %bitcast.13, s32[4096]{0:T(1024)S(1)} %bitcast.23, s32[4096]{0:T(1024)S(1)} %bitcast.31, f32[4104,128]{1,0:T(8,128)S(1)} %shard_map.80.frame_ref, f32[1024,128]{1,0:T(8,128)S(1)} %shard_map.76.after_ref.near_ref, ...), custom_call_target="tpu_custom_call" | custom-call | bytes 9000000 | tf_op jit(solution)/shard_map/pallas_call | solution.py:378
  82.2 0.8 collective-permute-start.11
  83.0 0.0 collective-permute-done.10.after_ref.refs_5_
  83.0 2.9 %shard_map.84.refs_3_ = bf16[512,128]{1,0:T(8,128)(2,1)S(1)} custom-call(s32[65536]{0:T(1024)S(1)} %bitcast.14, s32[4096]{0:T(1024)S(1)} %bitcast.24, s32[4096]{0:T(1024)S(1)} %bitcast.32, f32[4104,128]{1,0:T(8,128)S(1)} %shard_map.80.frame_ref, f32[1024,128]{1,0:T(8,128)S(1)} %shard_map.78.after_ref.near_ref, ...), custom_call_target="tpu_custom_call" | custom-call | bytes 9000000 | tf_op jit(solution)/shard_map/pallas_call | solution.py:378
  85.8 1.4 %collective-permute-start.12 = (bf16[512,128]{1,0:T(8,128)(2,1)S(1)}, bf16[512,128]{1,0:T(8,128)(2,1)S(1)}, u32[]{:S(2)}, u32[]{:S(2)}) collective-permute-start(bf16[512,128]{1,0:T(8,128)(2,1)S(1)} %shard_map.84.refs_3_), channel_id=1, source_target_pairs={{0,1},{1,0},{2,3},{3,2},{4,5},{5,4},{6,7},{7,6},{8,9},{9,8},{10,11... | collective-permute-start | bytes 393224 | tf_op jit(solution)/shard_map/ppermute | solution.py:386
  87.3 0.0 collective-permute-done.11.refs_6_
  87.3 3.6 %collective-permute-done.12.refs_7_ = bf16[512,128]{1,0:T(8,128)(2,1)S(1)} collective-permute-done((bf16[512,128]{1,0:T(8,128)(2,1)S(1)}, bf16[512,128]{1,0:T(8,128)(2,1)S(1)}, u32[]{:S(2)}, u32[]{:S(2)}) %collective-permute-start.12) | collective-permute-done | bytes 131104 | tf_op jit(solution)/shard_map/ppermute | solution.py:386
  90.9 0.0 copy-done.5
  90.9 0.0 copy-done.8
  90.9 1.7 %shard_map.85 = bf16[64,4096]{1,0:T(8,128)(2,1)} custom-call(bf16[128,128]{1,0:T(8,128)(2,1)S(1)} %copy-done.5, f32[1,128]{1,0:T(1,128)S(1)} %bitcast.41, bf16[512,128]{1,0:T(8,128)(2,1)S(1)} %shard_map.81.refs_0_, bf16[512,128]{1,0:T(8,128)(2,1)S(1)} %shard_map.82.refs_1_, bf16[512,128]{1,0:T(8,128)(2,1)S(1)} %shard_map.83.refs_2_, ...), custom_call_target="tpu_custom_call" | custom-call | bytes 3000000 | tf_op jit(solution)/shard_map/pallas_call | solution.py:388
  (7 shorter events, 0.1 us)
Async XLA Ops:
  0.0 1.0 %copy-start = (bf16[64,4096]{1,0:T(8,128)(2,1)S(1)}, bf16[64,4096]{1,0:T(8,128)(2,1)}, u32[]{:S(2)}) copy-start(bf16[64,4096]{1,0:T(8,128)(2,1)} %x_ref.5) | copy-start | bytes 1572868
  1.0 0.7 copy-start.6
  2.1 12.7 %collective-permute-start = (bf16[16,128]{1,0:T(8,128)(2,1)S(1)}, bf16[16,128]{1,0:T(8,128)(2,1)S(1)}, u32[]{:S(2)}, u32[]{:S(2)}) collective-permute-start(bf16[16,128]{1,0:T(8,128)(2,1)S(1)} %shard_map.64.after_ref.near_ref), channel_id=1, source_target_pairs={{0,64},{2,66},{4,68},{6,70},{8,72},{10,74},{12,76},{14,78},{16,80}... | collective-permute-start | bytes 12296 | tf_op jit(solution)/shard_map/ppermute | solution.py:302
  10.3 0.7 copy-start.3
  14.9 1.0 %copy-start.1 = (bf16[64,4096]{1,0:T(8,128)(2,1)S(1)}, bf16[64,4096]{1,0:T(8,128)(2,1)}, u32[]{:S(2)}) copy-start(bf16[64,4096]{1,0:T(8,128)(2,1)} %x_ref.5) | copy-start | bytes 1572868
  16.0 11.6 %collective-permute-start.2 = (bf16[64,2048]{1,0:T(8,128)(2,1)S(1)}, bf16[64,2048]{1,0:T(8,128)(2,1)S(1)}, u32[]{:S(2)}, u32[]{:S(2)}) collective-permute-start(bf16[64,2048]{1,0:T(8,128)(2,1)S(1)} %get-tuple-element.17), channel_id=1, source_target_pairs={{0,2},{2,4},{4,6},{6,8},{8,10},{10,12},{12,14},{14,16},{16,18},{18... | collective-permute-start | bytes 786440 | tf_op jit(solution)/shard_map/ppermute | solution.py:336
  17.9 9.6 %collective-permute-start.3 = (bf16[64,2048]{1,0:T(8,128)(2,1)S(1)}, bf16[64,2048]{1,0:T(8,128)(2,1)S(1)}, u32[]{:S(2)}, u32[]{:S(2)}) collective-permute-start(bf16[64,2048]{1,0:T(8,128)(2,1)S(1)} %get-tuple-element.18), channel_id=1, source_target_pairs={{2,0},{4,2},{6,4},{8,6},{10,8},{12,10},{14,12},{16,14},{18,16},{20... | collective-permute-start | bytes 786440 | tf_op jit(solution)/shard_map/ppermute | solution.py:337
  21.5 8.3 %collective-permute-start.1 = (bf16[32,128]{1,0:T(8,128)(2,1)S(1)}, bf16[32,128]{1,0:T(8,128)(2,1)S(1)}, u32[]{:S(2)}, u32[]{:S(2)}) collective-permute-start(bf16[32,128]{1,0:T(8,128)(2,1)S(1)} %shard_map.66.after_ref.near_ref), channel_id=1, source_target_pairs={{0,16},{2,18},{4,20},{6,22},{8,24},{10,26},{12,28},{14,30},{16,0},... | collective-permute-start | bytes 24584 | tf_op jit(solution)/shard_map/ppermute | solution.py:302
  22.7 0.7 copy-start.4
  27.5 1.0 %copy-start.2 = (bf16[64,4096]{1,0:T(8,128)(2,1)S(1)}, bf16[64,4096]{1,0:T(8,128)(2,1)}, u32[]{:S(2)}) copy-start(bf16[64,4096]{1,0:T(8,128)(2,1)} %x_ref.5) | copy-start | bytes 1572868
  29.9 8.7 %collective-permute-start.4 = (bf16[64,128]{1,0:T(8,128)(2,1)S(1)}, bf16[64,128]{1,0:T(8,128)(2,1)S(1)}, u32[]{:S(2)}, u32[]{:S(2)}) collective-permute-start(bf16[64,128]{1,0:T(8,128)(2,1)S(1)} %shard_map.71.after_ref.near_ref), channel_id=1, source_target_pairs={{0,32},{2,34},{4,36},{6,38},{8,40},{10,42},{12,44},{14,46},{16,48}... | collective-permute-start | bytes 49160 | tf_op jit(solution)/shard_map/ppermute | solution.py:302
  38.6 10.3 %collective-permute-start.5 = (bf16[128,128]{1,0:T(8,128)(2,1)S(1)}, bf16[128,128]{1,0:T(8,128)(2,1)S(1)}, u32[]{:S(2)}, u32[]{:S(2)}) collective-permute-start(bf16[128,128]{1,0:T(8,128)(2,1)S(1)} %shard_map.73.after_ref.near_ref), channel_id=1, source_target_pairs={{0,128},{2,130},{4,132},{6,134},{8,136},{10,138},{12,140},{14,142}... | collective-permute-start | bytes 98312 | tf_op jit(solution)/shard_map/ppermute | solution.py:302
  48.9 9.2 %collective-permute-start.6 = (bf16[256,128]{1,0:T(8,128)(2,1)S(1)}, bf16[256,128]{1,0:T(8,128)(2,1)S(1)}, u32[]{:S(2)}, u32[]{:S(2)}) collective-permute-start(bf16[256,128]{1,0:T(8,128)(2,1)S(1)} %shard_map.75.after_ref.near_ref), channel_id=1, source_target_pairs={{0,8},{2,10},{4,12},{6,14},{8,0},{10,2},{12,4},{14,6},{16,24},{18,... | collective-permute-start | bytes 196616 | tf_op jit(solution)/shard_map/ppermute | solution.py:302
  58.1 12.7 %copy-start.7 = (s32[32]{0:T(128)S(1)}, s32[32]{0:T(128)}, u32[]{:S(2)}) copy-start(s32[32]{0:T(128)} %after_ref.3) | copy-start | bytes 388
  58.1 10.8 %collective-permute-start.7 = (bf16[512,128]{1,0:T(8,128)(2,1)S(1)}, bf16[512,128]{1,0:T(8,128)(2,1)S(1)}, u32[]{:S(2)}, u32[]{:S(2)}) collective-permute-start(bf16[512,128]{1,0:T(8,128)(2,1)S(1)} %shard_map.77.after_ref.near_ref), channel_id=1, source_target_pairs={{0,4},{2,6},{4,0},{6,2},{8,12},{10,14},{12,8},{14,10},{16,20},{18,... | collective-permute-start | bytes 393224 | tf_op jit(solution)/shard_map/ppermute | solution.py:302
  68.9 1.6 %collective-permute-start.8 = (bf16[1024,128]{1,0:T(8,128)(2,1)S(1)}, bf16[1024,128]{1,0:T(8,128)(2,1)S(1)}, u32[]{:S(2)}, u32[]{:S(2)}) collective-permute-start(bf16[1024,128]{1,0:T(8,128)(2,1)S(1)} %shard_map.79.near_ref), channel_id=1, source_target_pairs={{0,2},{2,0},{4,6},{6,4},{8,10},{10,8},{12,14},{14,12},{16,18},{18,... | collective-permute-start | bytes 786440 | tf_op jit(solution)/shard_map/ppermute | solution.py:302
  73.7 5.6 %collective-permute-start.9 = (bf16[512,128]{1,0:T(8,128)(2,1)S(1)}, bf16[512,128]{1,0:T(8,128)(2,1)S(1)}, u32[]{:S(2)}, u32[]{:S(2)}) collective-permute-start(bf16[512,128]{1,0:T(8,128)(2,1)S(1)} %shard_map.81.refs_0_), channel_id=1, source_target_pairs={{0,1},{1,0},{2,3},{3,2},{4,5},{5,4},{6,7},{7,6},{8,9},{9,8},{10,11... | collective-permute-start | bytes 393224 | tf_op jit(solution)/shard_map/ppermute | solution.py:386
  77.3 13.6 %copy-start.5 = (bf16[128,128]{1,0:T(8,128)(2,1)S(1)}, bf16[128,128]{1,0:T(8,128)(2,1)}, u32[]{:S(2)}) copy-start(bf16[128,128]{1,0:T(8,128)(2,1)} %weight_ref.1) | copy-start | bytes 98308
  77.3 13.6 %copy-start.8 = (f32[128]{0:T(128)S(1)}, f32[128]{0:T(128)}, u32[]{:S(2)}) copy-start(f32[128]{0:T(128)} %param.11) | copy-start | bytes 1540
  77.3 5.6 %collective-permute-start.10 = (bf16[512,128]{1,0:T(8,128)(2,1)S(1)}, bf16[512,128]{1,0:T(8,128)(2,1)S(1)}, u32[]{:S(2)}, u32[]{:S(2)}) collective-permute-start(bf16[512,128]{1,0:T(8,128)(2,1)S(1)} %shard_map.82.refs_1_), channel_id=1, source_target_pairs={{0,1},{1,0},{2,3},{3,2},{4,5},{5,4},{6,7},{7,6},{8,9},{9,8},{10,11... | collective-permute-start | bytes 393224 | tf_op jit(solution)/shard_map/ppermute | solution.py:386
  82.2 5.1 %collective-permute-start.11 = (bf16[512,128]{1,0:T(8,128)(2,1)S(1)}, bf16[512,128]{1,0:T(8,128)(2,1)S(1)}, u32[]{:S(2)}, u32[]{:S(2)}) collective-permute-start(bf16[512,128]{1,0:T(8,128)(2,1)S(1)} %shard_map.83.refs_2_), channel_id=1, source_target_pairs={{0,1},{1,0},{2,3},{3,2},{4,5},{5,4},{6,7},{7,6},{8,9},{9,8},{10,11... | collective-permute-start | bytes 393224 | tf_op jit(solution)/shard_map/ppermute | solution.py:386
  85.8 5.1 %collective-permute-start.12 = (bf16[512,128]{1,0:T(8,128)(2,1)S(1)}, bf16[512,128]{1,0:T(8,128)(2,1)S(1)}, u32[]{:S(2)}, u32[]{:S(2)}) collective-permute-start(bf16[512,128]{1,0:T(8,128)(2,1)S(1)} %shard_map.84.refs_3_), channel_id=1, source_target_pairs={{0,1},{1,0},{2,3},{3,2},{4,5},{5,4},{6,7},{7,6},{8,9},{9,8},{10,11... | collective-permute-start | bytes 393224 | tf_op jit(solution)/shard_map/ppermute | solution.py:386

commit v2 on v0

v2 whole, which is shorter than its diff:
```python
import functools

import jax
import jax.numpy as jnp
from jax import lax
from jax.experimental import pallas as pl
from jax.experimental.pallas import tpu as pltpu
from jax.sharding import PartitionSpec as P

VMEM = pltpu.VMEM
SMEM = pltpu.SMEM
LANES = 128
CHUNK = 1024
GROUP = 16
STAGES = ((32,), (8, 16, 24), (64,), (2, 4, 6), (1,))


def hub_pick_kernel(rows_ref, x_hbm, out_ref, x_ref, sem):
    hubs, nodes = rows_ref.shape[1], x_ref.shape[1]
    parts = sem.shape[0]
    copies = [
        pltpu.make_async_copy(x_hbm.at[:, part], x_ref.at[:, part], sem.at[i])
        for i in range(parts)
        for part in [pl.ds(i * (nodes // parts), nodes // parts)]
    ]
    for copy in copies:
        copy.start()
    diagonal = lax.broadcasted_iota(jnp.int32, (hubs, hubs), 0) == lax.broadcasted_iota(
        jnp.int32, (hubs, hubs), 1
    )
    rows = jnp.sum(jnp.where(diagonal, rows_ref[...], 0), axis=1, keepdims=True)
    onehot = (lax.broadcasted_iota(jnp.int32, (hubs, nodes), 1) == rows).astype(jnp.bfloat16)
    for copy in copies:
        copy.wait()
    picked = lax.dot_general(
        onehot, x_ref[...], (((1,), (1,)), ((), ())), preferred_element_type=jnp.float32
    ).astype(jnp.bfloat16)
    out_ref[...] = jnp.concatenate([picked[: hubs // 2], picked[hubs // 2 :]], axis=1)


def join_kernel(*refs):
    blocks, out_ref = refs[:-2], refs[-1]
    rows = blocks[0].shape[0]
    for i, ref in enumerate(blocks):
        out_ref[i * rows : (i + 1) * rows] = ref[...]


def join_feat_kernel(mine_ref, other_ref, after_ref, out_ref):
    first = lax.axis_index("feat") == 0
    lane = lax.broadcasted_iota(jnp.int32, (16, LANES), 1)
    for i in range(mine_ref.shape[0] // 16):
        mine = mine_ref[16 * i : 16 * i + 16, :].astype(jnp.float32)
        other = other_ref[16 * i : 16 * i + 16, :].astype(jnp.float32)
        low = jnp.where(first, mine, other)
        high = jnp.where(first, other, mine)
        row = jnp.where(lane < LANES // 2, low, pltpu.roll(high, LANES // 2, 1))
        out_ref[32 * i : 32 * i + 16, :] = row.astype(jnp.bfloat16)
        row = jnp.where(lane < LANES // 2, pltpu.roll(low, LANES // 2, 1), high)
        out_ref[32 * i + 16 : 32 * i + 32, :] = row.astype(jnp.bfloat16)


def halves_kernel(x_ref, other_ref, after_ref, outer_ref, inner_ref):
    feat = lax.axis_index("feat")
    odd = lax.axis_index("slab") & 1
    chans, half = x_ref.shape[0], outer_ref.shape[1]
    for ref, channels in ((x_ref, feat), (other_ref, 1 - feat)):
        rows = pl.ds(pl.multiple_of(channels * chans, chans), chans)
        outer_ref[rows, :] = ref[:, pl.ds(pl.multiple_of(odd * half, half), half)]
        inner_ref[rows, :] = ref[:, pl.ds(pl.multiple_of((1 - odd) * half, half), half)]


def frame_kernel(outer_halo_ref, outer_ref, inner_ref, inner_halo_ref, after_ref, frame_ref):
    odd = lax.axis_index("slab") & 1
    half = outer_ref.shape[1]
    step = 256
    unit = (
        lax.broadcasted_iota(jnp.int32, (step, step), 0)
        == lax.broadcasted_iota(jnp.int32, (step, step), 1)
    ).astype(jnp.bfloat16)
    for place, ref in enumerate((outer_halo_ref, outer_ref, inner_ref, inner_halo_ref)):
        first = (place + odd * (3 - 2 * place)) * half
        for at in range(0, half, step):
            frame_ref[pl.ds(pl.multiple_of(first + at, step), step), :] = lax.dot_general(
                unit,
                ref[:, at : at + step],
                (((1,), (1,)), ((), ())),
                preferred_element_type=jnp.float32,
            )
    rows = frame_ref.shape[0]
    frame_ref[rows - 8 :, :] = jnp.zeros((8, LANES), jnp.float32)


def origins():
    differs = [0]
    for bits in STAGES:
        differs = [d ^ bit for bit in (0,) + bits for d in differs]
    return differs


def hub_frame_kernel(first, hubs, frame_in, near_ref, far_ref, after_ref, frame_ref):
    blocks = near_ref.shape[0] // hubs
    me = lax.axis_index("slab")
    for p, differs in enumerate(origins()):
        ref, i = (near_ref, p) if p < blocks else (far_ref, p - blocks)
        at = pl.multiple_of(first + (me ^ differs) * hubs, hubs)
        frame_ref[pl.ds(at, hubs), :] = ref[hubs * i : hubs * (i + 1), :].astype(jnp.float32)


def comparators(count):
    pairs, p = [], 1
    while p < count:
        k = p
        while k >= 1:
            for j in range(k % p, count - k, 2 * k):
                for i in range(min(k, count - j - k)):
                    if (i + j) // (2 * p) == (i + j + k) // (2 * p):
                        pairs.append((i + j, i + j + k))
            k //= 2
        p *= 2
    return pairs


def sort_network(values):
    for a, b in comparators(len(values)):
        values[a], values[b] = jnp.minimum(values[a], values[b]), jnp.maximum(values[a], values[b])
    return values


def sorted_tiles(keys, halved):
    shape = keys.shape
    apart = lax.broadcasted_iota(jnp.int32, shape, 0) == halved
    sub = lax.broadcasted_iota(jnp.int32, shape, 1)
    lane = lax.broadcasted_iota(jnp.int32, shape, 2)
    at = sub * LANES + lane
    size = 2
    while size <= CHUNK:
        distance = size // 2
        while distance >= 1:
            axis, by, extent = (2, distance, LANES) if distance < LANES else (1, distance // LANES, 8)
            lower = (at & distance) == 0
            partner = jnp.where(
                lower, pltpu.roll(keys, extent - by, axis), pltpu.roll(keys, by, axis)
            )
            ascending = (at & size) == 0
            if 2 * size == CHUNK:
                ascending = ascending | apart
            merged = jnp.where(
                lower == ascending, jnp.minimum(keys, partner), jnp.maximum(keys, partner)
            )
            keys = jnp.where(apart, keys, merged) if size == CHUNK else merged
            distance //= 2
        size *= 2
    return keys


def plan_kernel(frame_rows, all_rows, nbr_ref, deg_ref, after_ref, near_ids, near_order, near_class, far_ids, far_order, far_class, full_ids, full_order, full_class):
    slots = nbr_ref.shape[0]
    first = lax.axis_index("feat") * 16
    at = lax.broadcasted_iota(jnp.int32, (8, LANES), 0) * LANES + lax.broadcasted_iota(
        jnp.int32, (8, LANES), 1
    )
    rows = pl.ds(pl.multiple_of(first, 8), 8)
    degree = deg_ref[rows, :]
    near, far = [], []
    near_count = jnp.zeros((8, LANES), jnp.int32)
    for j in range(slots):
        nbr = nbr_ref[j, rows, :]
        used = degree > j
        is_near = used & (nbr < frame_rows)
        near.append(jnp.where(is_near, nbr, all_rows))
        far.append(jnp.where(used & (nbr >= frame_rows), nbr, all_rows))
        near_count = near_count + is_near.astype(jnp.int32)
    for j, ids in enumerate(sort_network(near)):
        near_ids[j] = ids
    for j, ids in enumerate(sort_network(far)):
        far_ids[j] = ids
    rows = pl.ds(pl.multiple_of(first + 8, 8), 8)
    full_degree = deg_ref[rows, :]
    for j in range(slots):
        full_ids[j] = jnp.where(full_degree > j, nbr_ref[j, rows, :], all_rows)
    counts = (near_count, degree - near_count, full_degree)
    keys = sorted_tiles(jnp.stack([count * CHUNK + at for count in counts]), 2)
    for i, order in enumerate((near_order, far_order)):
        order[...] = keys[i] & (CHUNK - 1)
    full_order[...] = keys[2] & (CHUNK // 2 - 1)
    for i, classes in enumerate((near_class, far_class, full_class)):
        classes[...] = keys[i] >> 10


def constants_kernel(deg_ref, weight_ref, bias_ref, after_ref, scale_ref, weight_out, bias_out):
    tiles = scale_ref.shape[0] // LANES
    first = pl.multiple_of(lax.axis_index("feat") * tiles, tiles)
    inverse = 1.0 / (deg_ref[pl.ds(first, tiles), :] + 1).astype(jnp.float32)
    for t in range(tiles):
        scale_ref[LANES * t : LANES * (t + 1), :] = jnp.broadcast_to(
            inverse[t : t + 1, :], (LANES, LANES)
        ).T
    weight_out[...] = weight_ref[...].astype(jnp.float32).T.astype(jnp.bfloat16)
    bias_out[...] = jnp.broadcast_to(bias_ref[...], (LANES, LANES)).T


def add_tree(parts):
    while len(parts) > 1:
        tail = [parts[-1]] if len(parts) % 2 else []
        parts = [parts[i] + parts[i + 1] for i in range(0, len(parts) - 1, 2)] + tail
    return parts[0]


def load_plan(slots, start, ids_ref, order_ref, class_ref, slot_ids, order, classes, sem):
    size = order.shape[0]
    rows = pl.ds(start, size)
    first = [
        pltpu.make_async_copy(order_ref.at[rows], order, sem.at[slots]),
        pltpu.make_async_copy(class_ref.at[rows], classes.at[pl.ds(0, size)], sem.at[slots + 1]),
    ]
    by_slot = [
        pltpu.make_async_copy(
            ids_ref.at[pl.ds(j * CHUNK + start, size)], slot_ids.at[pl.ds(j * size, size)], sem.at[j]
        )
        for j in range(slots)
    ]
    for copy in first + by_slot:
        copy.start()
    return first, by_slot


def sum_slots(slots, start, part, parts, plan_refs, frame_ref, total_ref, slot_ids, order, classes, sem):
    size = order.shape[0]
    first, by_slot = load_plan(slots, start, *plan_refs, slot_ids, order, classes, sem)
    total_ref[...] = jnp.zeros_like(total_ref)
    for copy in first:
        copy.wait()
    last = GROUP - 1
    classes[size + part * GROUP + last] = slots + 1
    of_slot = [slot_ids.at[pl.ds(j * size, size)] for j in range(slots)]

    def body(count, carry):
        base, _ = carry
        for k in range(GROUP):
            node = order[base + k]
            total_ref[pl.ds(node, 1), :] = add_tree(
                [frame_ref[pl.ds(of_slot[j][node], 1), :] for j in range(count)]
            )
        return base + parts * GROUP, classes[base + parts * GROUP + last]

    def skip(carry):
        base, _ = carry
        return base + parts * GROUP, classes[base + parts * GROUP + last]

    carry = (jnp.int32(part * GROUP), classes[part * GROUP + last])
    carry = lax.while_loop(lambda carry: carry[1] == 0, skip, carry)
    for count in range(1, slots + 1):
        by_slot[count - 1].wait()
        carry = lax.while_loop(
            lambda carry, count=count: carry[1] == count, functools.partial(body, count), carry
        )


def near_kernel(slots, part, parts, ids_ref, order_ref, class_ref, frame_ref, after_ref, total_ref, *plan):
    sum_slots(slots, 0, part, parts, (ids_ref, order_ref, class_ref), frame_ref, total_ref, *plan)


def layer_kernel(slots, first, start, parts, own, ids_ref, order_ref, class_ref, frame_ref, scale_ref, weight_ref, bias_ref, after_ref, *refs):
    near, (keep_ref, send_ref, total_ref), plan = refs[:parts], refs[parts : parts + 3], refs[parts + 3 :]
    sum_slots(slots, start, 0, 1, (ids_ref, order_ref, class_ref), frame_ref, total_ref, *plan)
    chans, size = keep_ref.shape
    feat = lax.axis_index("feat")
    step = 256
    for at in range(0, size, step):
        rows = slice(at, at + step)
        own_at = pl.multiple_of(own + feat * own + first + at, step)
        total = total_ref[rows, :] + frame_ref[pl.ds(own_at, step), :]
        for ref in near:
            total = total + ref[rows, :]
        product = lax.dot_general(
            weight_ref[...],
            (total * scale_ref[first + at : first + at + step, :]).astype(jnp.bfloat16),
            (((1,), (1,)), ((), ())),
            preferred_element_type=jnp.float32,
        )
        bias = jnp.concatenate([bias_ref[...]] * (step // LANES), axis=1)
        result = jnp.maximum(product + bias, 0.0)
        low, high = result[:chans], result[chans:]
        keep_ref[:, rows] = jnp.where(feat == 0, low, high).astype(jnp.bfloat16)
        if send_ref.shape[0] == chans:
            result = jnp.where(feat == 0, high, low)
        send_ref[:, rows] = result.astype(jnp.bfloat16)


def output_kernel(*refs):
    out_ref = refs[-1]
    count = len(refs) // 2
    feat = lax.axis_index("feat")
    chans = out_ref.shape[0]
    for refs, part in ((refs[:count], feat), (refs[count:-1], 1 - feat)):
        at = part * (out_ref.shape[1] // 2)
        for ref in refs:
            size = ref.shape[1]
            rows = pl.ds(pl.multiple_of(feat * chans, chans), chans) if ref.shape[0] > chans else slice(None)
            out_ref[:, pl.ds(pl.multiple_of(at, size), size)] = ref[rows, :]
            at = at + size


def pallas(kernel, out_shape, in_specs, scratch=(), us=1.0, aliases=None):
    return pl.pallas_call(
        kernel,
        out_shape=out_shape,
        in_specs=in_specs,
        out_specs=jax.tree.map(lambda _: IN_VMEM, out_shape),
        scratch_shapes=list(scratch),
        input_output_aliases=aliases or {},
        compiler_params=pltpu.CompilerParams(vmem_limit_bytes=6 * 2**20),
        cost_estimate=pl.CostEstimate(flops=0, bytes_accessed=int(us * 3_000_000), transcendentals=0),
    )


IN_VMEM = pl.BlockSpec(memory_space=VMEM)
ANYWHERE = pl.BlockSpec(memory_space=pl.ANY)


def local(node_feats, neighbours, degrees, hub_rows, weight, bias_terms):
    chans, nodes = node_feats.shape
    slots = neighbours.shape[0]
    hubs = hub_rows.shape[0]
    slabs = lax.axis_size("slab")
    half = nodes // 2
    chunks = half // CHUNK
    frame_rows, hub_count = 2 * half + nodes, slabs * hubs
    swap = [(0, 1), (1, 0)]

    def bf16(*shape):
        return jax.ShapeDtypeStruct(shape, jnp.bfloat16)

    def f32(*shape):
        return jax.ShapeDtypeStruct(shape, jnp.float32)

    def i32(*shape):
        return jax.ShapeDtypeStruct(shape, jnp.int32)

    block = pallas(
        hub_pick_kernel,
        bf16(hubs // 2, 2 * chans),
        [IN_VMEM, ANYWHERE],
        [VMEM((chans, nodes), jnp.bfloat16), pltpu.SemaphoreType.DMA((4,))],
    )(hub_rows[None, :], node_feats)
    arrived = None

    def stage(block, bits):
        return [lax.ppermute(block, "slab", [(i, i ^ bit) for i in range(slabs)]) for bit in bits]

    def join(block, arrived, after):
        rows = block.shape[0] * (1 + len(arrived))
        specs = [IN_VMEM] * (1 + len(arrived)) + [ANYWHERE]
        return pallas(join_kernel, bf16(rows, 2 * chans), specs, us=0.5)(block, *arrived, after)

    arrived = stage(block, STAGES[0])
    deg_tiles = degrees.reshape(nodes // LANES, LANES)
    scale, by_out, bias = pallas(
        constants_kernel,
        (f32(half, LANES), bf16(2 * chans, 2 * chans), f32(LANES, LANES)),
        [IN_VMEM] * 3 + [ANYWHERE],
        us=1.0,
    )(deg_tiles, weight, bias_terms[None, :], block)
    other = lax.ppermute(node_feats, "feat", swap)

    block = join(block, arrived, scale)
    arrived = stage(block, STAGES[1])
    block = join(block, arrived, scale)
    arrived = lax.ppermute(block, "feat", swap)
    outer, inner = pallas(
        halves_kernel, (bf16(2 * chans, half),) * 2, [IN_VMEM, IN_VMEM, ANYWHERE], us=0.5
    )(node_feats, other, block)
    block = pallas(
        join_feat_kernel, bf16(2 * block.shape[0], 2 * chans), [IN_VMEM, IN_VMEM, ANYWHERE], us=0.5
    )(block, arrived, outer)
    arrived = stage(block, STAGES[2])
    inner_halo = lax.ppermute(inner, "slab", [(i, i ^ 1) for i in range(slabs)])
    outer_halo = lax.ppermute(
        outer, "slab", [(i, j) for i in range(slabs) for j in [i + 2 * (i & 1) - 1] if 0 <= j < slabs]
    )
    table, tile = i32(slots, 8, LANES), i32(8, LANES)
    plan = pallas(
        functools.partial(plan_kernel, frame_rows, frame_rows + hub_count),
        (table, tile, tile) * 3,
        [IN_VMEM, IN_VMEM, ANYWHERE],
        us=4.0,
    )(neighbours.reshape(slots, nodes // LANES, LANES), deg_tiles, block)
    plan = [a.reshape(-1) for a in plan]
    near_plan, far_plan, full_plan = plan[:3], plan[3:6], plan[6:]
    frame = pallas(
        frame_kernel,
        f32(frame_rows + hub_count + 8, LANES),
        [IN_VMEM] * 4 + [ANYWHERE],
        us=2.0,
    )(outer_halo, outer, inner, inner_halo, near_plan[1])

    def plan_scratch(size):
        return [
            SMEM((slots * size,), jnp.int32),
            SMEM((size,), jnp.int32),
            SMEM((size + 2 * GROUP,), jnp.int32),
            pltpu.SemaphoreType.DMA((slots + 2,)),
        ]

    def near_sum(part, after):
        return pallas(
            functools.partial(near_kernel, slots, part, 2),
            f32(CHUNK, LANES),
            [ANYWHERE] * 3 + [IN_VMEM, ANYWHERE],
            plan_scratch(CHUNK),
            us=4.0,
        )(*near_plan, frame, after)

    near = [near_sum(0, block)]
    block = join(block, arrived, near[0])
    arrived = stage(block, STAGES[3])
    near.append(near_sum(1, block))
    block = join(block, arrived, near[1])
    arrived = stage(block, STAGES[4])
    frame = pallas(
        functools.partial(hub_frame_kernel, frame_rows, hubs),
        f32(*frame.shape),
        [IN_VMEM] * 3 + [ANYWHERE],
        us=0.5,
        aliases={0: 0},
    )(frame, block, arrived[0], near[1])

    def layer(plan, first, start, size, sent_chans, near, after, us):
        return pallas(
            functools.partial(layer_kernel, slots, first, start, len(near), half),
            (bf16(chans, size), bf16(sent_chans, size)),
            [ANYWHERE] * 3 + [IN_VMEM] * 4 + [ANYWHERE] + [IN_VMEM] * len(near),
            [VMEM((size, LANES), jnp.float32)] + plan_scratch(size),
            us=us,
        )(*plan, frame, scale, by_out, bias, after, *near)

    keep, received = [hub_rows], []
    for plan, first, start, size, sent_chans, near, us in (
        (far_plan, 0, 0, CHUNK, 2 * chans, near, 3.0),
        (full_plan, CHUNK, 0, CHUNK // 2, 2 * chans, [], 4.0),
        (full_plan, CHUNK + CHUNK // 2, CHUNK // 2, CHUNK // 2, chans, [], 4.0),
    ):
        kept, sent = layer(plan, first, start, size, sent_chans, near, keep[-1], us)
        keep.append(kept)
        received.append(lax.ppermute(sent, "feat", swap))
    pieces = keep[1:] + received
    return pallas(output_kernel, bf16(chans, nodes), [IN_VMEM] * len(pieces), us=0.5)(*pieces)


def solution(mesh):
    in_specs = (P("feat", "slab"), P(None, "slab"), P("slab"), P("slab"), P(), P())
    return jax.shard_map(local, mesh=mesh, in_specs=in_specs, out_specs=P("feat", "slab"), check_vma=False)
```

time: 527 us -> 77.3 us (0.15)
  the two profiles are of different devices: /device:TPU:16 before, /device:TPU:1 now
where the time goes in v2:
time: 77.3 us; the launch traced here: 77 us
  starting transfers between devices  33.8 us (44%)
  Pallas kernels  27.7 us (36%)
  waiting for transfers between devices  8.77 us (11%)
  local copies, waits for them, and re-layouts  6.62 us (9%)
    ppermute x9, starting transfers between devices, stage(): lax.ppermute(block, 'slab', [(i, i ^ bit) for i in range(slabs)])  23.4 us
    pallas_call x3, Pallas kernels, layer(): pallas(functools.partial(layer_kernel, slots, first, start, len(near), ha...  12.3 us
    pallas_call x2, Pallas kernels, near_sum(): pallas(functools.partial(near_kernel, slots, part, 2), f32(CHUNK, LANES),...  8.4 us
    unnamed x17, local copies, waits for them, and re-layouts  6.62 us
    pallas_call x1, Pallas kernels, local(): pallas(functools.partial(plan_kernel, frame_rows, frame_rows + hub_count)...  3.58 us
    ppermute x1, starting transfers between devices, local(): inner_halo = lax.ppermute(inner, 'slab', [(i, i ^ 1) for i in range(slabs)])  3.16 us
    ppermute x3, waiting for transfers between devices, local(): received.append(lax.ppermute(sent, 'feat', swap))  3.1 us
    ppermute x9, waiting for transfers between devices, stage(): lax.ppermute(block, 'slab', [(i, i ^ bit) for i in range(slabs)])  3.05 us
  transfers between devices with their start and end apart: 16, of which 5 were waited for; matrix products, arithmetic and copies ran while one was open for 1% of the time, Pallas kernels for 30%

profile of v2, /device:TPU:1, one launch (start us, length us, event | category | flops | bytes accessed | tf_op | source)
XLA Modules:
  0.0 77.0 jit_solution(11932181965920173381)
XLA Ops:
  0.0 2.1 %collective-permute-start.5 = (bf16[64,4096]{1,0:T(8,128)(2,1)}, bf16[64,4096]{1,0:T(8,128)(2,1)S(1)}, u32[]{:S(2)}, u32[]{:S(2)}) collective-permute-start(bf16[64,4096]{1,0:T(8,128)(2,1)} %x_ref.1), channel_id=1, source_target_pairs={{0,1},{1,0},{2,3},{3,2},{4,5},{5,4},{6,7},{7,6},{8,9},{9,8},{10,11... | collective-permute-start | bytes 1572872 | tf_op jit(solution)/shard_map/ppermute | solution.py:364
  2.1 0.0 copy-start
  2.1 1.1 %copy-done = bf16[64,4096]{1,0:T(8,128)(2,1)S(1)} copy-done((bf16[64,4096]{1,0:T(8,128)(2,1)S(1)}, bf16[64,4096]{1,0:T(8,128)(2,1)}, u32[]{:S(2)}) %copy-start) | copy-done | bytes 524312
  3.2 0.0 copy-start.5
  3.2 0.7 copy-done.5
  3.9 0.6 shard_map.64.after_ref.refs_0_
  4.5 7.0 %collective-permute-start = (bf16[16,128]{1,0:T(8,128)(2,1)S(1)}, bf16[16,128]{1,0:T(8,128)(2,1)S(1)}, u32[]{:S(2)}, u32[]{:S(2)}) collective-permute-start(bf16[16,128]{1,0:T(8,128)(2,1)S(1)} %shard_map.64.after_ref.refs_0_), channel_id=1, source_target_pairs={{0,64},{2,66},{4,68},{6,70},{8,72},{10,74},{12,76},{14,78},{16,80}... | collective-permute-start | bytes 12296 | tf_op jit(solution)/shard_map/ppermute | solution.py:349
  11.5 0.0 copy-start.2
  11.5 0.7 copy-done.2
  12.2 0.0 copy-start.4
  12.2 0.8 copy-done.4
  12.9 0.0 copy-start.7
  12.9 0.7 copy-done.7
  13.6 0.4 shard_map.65
  14.0 0.0 collective-permute-done.refs_1_
  14.0 1.7 %collective-permute-start.3 = (bf16[32,128]{1,0:T(8,128)(2,1)S(1)}, bf16[32,128]{1,0:T(8,128)(2,1)S(1)}, u32[]{:S(2)}, u32[]{:S(2)}) collective-permute-start(bf16[32,128]{1,0:T(8,128)(2,1)S(1)} %shard_map.66.refs_0_), channel_id=1, source_target_pairs={{0,48},{2,50},{4,52},{6,54},{8,56},{10,58},{12,60},{14,62},{16,32}... | collective-permute-start | bytes 24584 | tf_op jit(solution)/shard_map/ppermute | solution.py:349
  15.7 0.3 collective-permute-start.2
  16.0 1.6 %collective-permute-start.1 = (bf16[32,128]{1,0:T(8,128)(2,1)S(1)}, bf16[32,128]{1,0:T(8,128)(2,1)S(1)}, u32[]{:S(2)}, u32[]{:S(2)}) collective-permute-start(bf16[32,128]{1,0:T(8,128)(2,1)S(1)} %shard_map.66.refs_0_), channel_id=1, source_target_pairs={{0,16},{2,18},{4,20},{6,22},{8,24},{10,26},{12,28},{14,30},{16,0},... | collective-permute-start | bytes 24584 | tf_op jit(solution)/shard_map/ppermute | solution.py:349
  17.6 0.8 collective-permute-done.3.refs_3_
  18.4 0.7 collective-permute-done.2.refs_2_
  19.1 0.0 collective-permute-done.1.refs_1_
  19.1 0.0 collective-permute-done.5.other_ref
  19.1 0.0 copy-start.1
  19.2 1.0 %copy-done.1 = bf16[64,4096]{1,0:T(8,128)(2,1)S(1)} copy-done((bf16[64,4096]{1,0:T(8,128)(2,1)S(1)}, bf16[64,4096]{1,0:T(8,128)(2,1)}, u32[]{:S(2)}) %copy-start.1) | copy-done | bytes 524312
  20.2 0.1 shard_map.68
  20.3 3.2 %collective-permute-start.7 = (bf16[128,2048]{1,0:T(8,128)(2,1)S(1)}, bf16[128,2048]{1,0:T(8,128)(2,1)S(1)}, u32[]{:S(2)}, u32[]{:S(2)}) collective-permute-start(bf16[128,2048]{1,0:T(8,128)(2,1)S(1)} %get-tuple-element.30.inner_ref), channel_id=1, source_target_pairs={{0,2},{2,0},{4,6},{6,4},{8,10},{10,8},{12,14},{14,12},{16,18},{18,... | collective-permute-start | bytes 1572872 | tf_op jit(solution)/shard_map/ppermute | solution.py:377
  23.4 3.0 %collective-permute-start.6 = (bf16[128,2048]{1,0:T(8,128)(2,1)S(1)}, bf16[128,2048]{1,0:T(8,128)(2,1)S(1)}, u32[]{:S(2)}, u32[]{:S(2)}) collective-permute-start(bf16[128,2048]{1,0:T(8,128)(2,1)S(1)} %get-tuple-element.26.after_ref.outer_ref), channel_id=1, source_target_pairs={{2,4},{4,2},{6,8},{8,6},{10,12},{12,10},{14,16},{16,14},{18,20},{2... | collective-permute-start | bytes 1572872 | tf_op jit(solution)/shard_map/ppermute | solution.py:378
  26.4 0.3 collective-permute-start.4
  26.7 2.6 %collective-permute-done.4.other_ref = bf16[128,128]{1,0:T(8,128)(2,1)S(1)} collective-permute-done((bf16[128,128]{1,0:T(8,128)(2,1)S(1)}, bf16[128,128]{1,0:T(8,128)(2,1)S(1)}, u32[]{:S(2)}, u32[]{:S(2)}) %collective-permute-start.4) | collective-permute-done | bytes 32800 | tf_op jit(solution)/shard_map/ppermute | solution.py:369
  29.3 0.1 shard_map.69.after_ref.refs_0_
  29.4 2.7 %collective-permute-start.8 = (bf16[256,128]{1,0:T(8,128)(2,1)S(1)}, bf16[256,128]{1,0:T(8,128)(2,1)S(1)}, u32[]{:S(2)}, u32[]{:S(2)}) collective-permute-start(bf16[256,128]{1,0:T(8,128)(2,1)S(1)} %shard_map.69.after_ref.refs_0_), channel_id=1, source_target_pairs={{0,128},{2,130},{4,132},{6,134},{8,136},{10,138},{12,140},{14,142}... | collective-permute-start | bytes 196616 | tf_op jit(solution)/shard_map/ppermute | solution.py:349
  32.1 1.0 %copy.8 = s32[2,8,32,128]{3,2,1,0:T(8,128)S(1)} copy(s32[2,8,32,128]{3,1,2,0:T(8,128)} %bitcast.35) | data formatting | bytes 524288
  33.1 0.0 copy-start.3
  33.1 0.7 copy-done.3
  33.8 3.6 %shard_map.70 = (s32[16,8,128]{2,1,0:T(8,128)S(1)}, s32[8,128]{1,0:T(8,128)S(1)}, s32[8,128]{1,0:T(8,128)S(1)}, s32[16,8,128]{2,1,0:T(8,128)S(1)}, s32[8,128]{1,...) custom-call(s32[16,32,128]{2,1,0:T(8,128)S(1)} %bitcast.14, ...), custom_call_target="tpu_custom_call" | custom-call | bytes 12000000 | tf_op jit(solution)/shard_map/pallas_call | solution.py:382
  37.4 0.0 collective-permute-done.7.inner_halo_ref
  37.4 0.0 collective-permute-done.6.outer_halo_ref
  37.4 1.2 %shard_map.71.frame_ref.frame_in = f32[12296,128]{1,0:T(8,128)S(1)} custom-call(bf16[128,2048]{1,0:T(8,128)(2,1)S(1)} %collective-permute-done.6.outer_halo_ref, bf16[128,2048]{1,0:T(8,128)(2,1)S(1)} %get-tuple-element.26.after_ref.outer_ref, bf16[128,2048]{1,0:T(8,128)(2,1)S(1)} %get-tuple-element.30.inner_ref, ...), custom_call_target="tpu_custom_call" | custom-call | bytes 6000000 | tf_op jit(solution)/shard_map/pallas_call | solution.py:390
  38.7 4.1 %shard_map.72.refs_2_.refs_0_ = f32[1024,128]{1,0:T(8,128)S(1)} custom-call(s32[16384]{0:T(1024)S(1)} %bitcast.17, s32[1024]{0:T(1024)S(1)} %bitcast.23, s32[1024]{0:T(1024)S(1)} %bitcast.29, f32[12296,128]{1,0:T(8,128)S(1)} %shard_map.71.frame_ref.frame_in, bf16[256,128]{1,0:T(8,128)(2,1)S(1)} %shard_map.69.after_ref.refs_0_), custom_call_target="tpu_custom_call" | custom-call | bytes 12000000 | tf_op jit(solution)/shard_map/pallas_call | solution.py:406
  42.8 0.0 collective-permute-done.8.refs_1_
  42.8 2.4 %collective-permute-start.11 = (bf16[512,128]{1,0:T(8,128)(2,1)S(1)}, bf16[512,128]{1,0:T(8,128)(2,1)S(1)}, u32[]{:S(2)}, u32[]{:S(2)}) collective-permute-start(bf16[512,128]{1,0:T(8,128)(2,1)S(1)} %shard_map.73.after_ref.refs_0_), channel_id=1, source_target_pairs={{0,12},{2,14},{4,8},{6,10},{8,4},{10,6},{12,0},{14,2},{16,28},{18,... | collective-permute-start | bytes 393224 | tf_op jit(solution)/shard_map/ppermute | solution.py:349
  45.2 1.2 %collective-permute-start.10 = (bf16[512,128]{1,0:T(8,128)(2,1)S(1)}, bf16[512,128]{1,0:T(8,128)(2,1)S(1)}, u32[]{:S(2)}, u32[]{:S(2)}) collective-permute-start(bf16[512,128]{1,0:T(8,128)(2,1)S(1)} %shard_map.73.after_ref.refs_0_), channel_id=1, source_target_pairs={{0,8},{2,10},{4,12},{6,14},{8,0},{10,2},{12,4},{14,6},{16,24},{18,... | collective-permute-start | bytes 393224 | tf_op jit(solution)/shard_map/ppermute | solution.py:349
  46.4 0.0 collective-permute-start.9
  46.4 4.3 %shard_map.74.refs_4_.after_ref.refs_1_ = f32[1024,128]{1,0:T(8,128)S(1)} custom-call(s32[16384]{0:T(1024)S(1)} %bitcast.18, s32[1024]{0:T(1024)S(1)} %bitcast.24, s32[1024]{0:T(1024)S(1)} %bitcast.30, f32[12296,128]{1,0:T(8,128)S(1)} %shard_map.71.frame_ref.frame_in, bf16[512,128]{1,0:T(8,128)(2,1)S(1)} %shard_map.73.after_ref.refs_0_), custom_call_target="tpu_custom_call" | custom-call | bytes 12000000 | tf_op jit(solution)/shard_map/pallas_call | solution.py:406
  50.8 0.0 collective-permute-done.11.refs_3_
  50.8 0.0 collective-permute-done.10.refs_2_
  50.8 0.0 collective-permute-done.9.refs_1_
  50.8 0.0 copy-start.6
  50.8 6.5 %collective-permute-start.12 = (bf16[2048,128]{1,0:T(8,128)(2,1)S(1)}, bf16[2048,128]{1,0:T(8,128)(2,1)S(1)}, u32[]{:S(2)}, u32[]{:S(2)}) collective-permute-start(bf16[2048,128]{1,0:T(8,128)(2,1)S(1)} %shard_map.75.near_ref), channel_id=1, source_target_pairs={{0,2},{2,0},{4,6},{6,4},{8,10},{10,8},{12,14},{14,12},{16,18},{18,... | collective-permute-start | bytes 1572872 | tf_op jit(solution)/shard_map/ppermute | solution.py:349
  57.3 1.5 %collective-permute-done.12.far_ref = bf16[2048,128]{1,0:T(8,128)(2,1)S(1)} collective-permute-done((bf16[2048,128]{1,0:T(8,128)(2,1)S(1)}, bf16[2048,128]{1,0:T(8,128)(2,1)S(1)}, u32[]{:S(2)}, u32[]{:S(2)}) %collective-permute-start.12) | collective-permute-done | bytes 524320 | tf_op jit(solution)/shard_map/ppermute | solution.py:349
  58.8 0.1 shard_map.76.frame_ref
  59.0 0.0 copy-done.6
  59.0 3.1 %shard_map.77 = (bf16[64,1024]{1,0:T(8,128)(2,1)S(1)}, bf16[128,1024]{1,0:T(8,128)(2,1)S(1)}) custom-call(s32[16384]{0:T(1024)S(1)} %bitcast.19, s32[1024]{0:T(1024)S(1)} %bitcast.31, s32[1024]{0:T(1024)S(1)} %bitcast.32, f32[12296,128]{1,0:T(8,128)S(1)} %shard_map.76.frame_ref, f32[2048,128]{1,0:T(8,128)S(1)} %get-tuple-element.25.refs_2_.refs_4_.scale_ref, ...), custom_call_target="tpu_custom_call" | custom-call | bytes 9000000 | tf_op jit(solution)/shard_map/pallas_call | solution.py:429
  62.1 0.3 collective-permute-start.13
  62.4 4.5 %shard_map.78 = (bf16[64,512]{1,0:T(8,128)(2,1)S(1)}, bf16[128,512]{1,0:T(8,128)(2,1)S(1)}) custom-call(s32[16384]{0:T(1024)S(1)} %bitcast.15, s32[1024]{0:T(1024)S(1)} %bitcast.25, s32[1024]{0:T(1024)S(1)} %bitcast.27, f32[12296,128]{1,0:T(8,128)S(1)} %shard_map.76.frame_ref, f32[2048,128]{1,0:T(8,128)S(1)} %get-tuple-element.25.refs_2_.refs_4_.scale_ref, ...), custom_call_target="tpu_custom_call" | custom-call | bytes 12000000 | tf_op jit(solution)/shard_map/pallas_call | solution.py:429
  66.9 1.4 %collective-permute-start.14 = (bf16[128,512]{1,0:T(8,128)(2,1)S(1)}, bf16[128,512]{1,0:T(8,128)(2,1)S(1)}, u32[]{:S(2)}, u32[]{:S(2)}) collective-permute-start(bf16[128,512]{1,0:T(8,128)(2,1)S(1)} %get-tuple-element.43), channel_id=1, source_target_pairs={{0,1},{1,0},{2,3},{3,2},{4,5},{5,4},{6,7},{7,6},{8,9},{9,8},{10,11... | collective-permute-start | bytes 393224 | tf_op jit(solution)/shard_map/ppermute | solution.py:445
  68.4 4.6 %shard_map.79 = (bf16[64,512]{1,0:T(8,128)(2,1)S(1)}, bf16[64,512]{1,0:T(8,128)(2,1)S(1)}) custom-call(s32[16384]{0:T(1024)S(1)} %bitcast.16, s32[1024]{0:T(1024)S(1)} %bitcast.26, s32[1024]{0:T(1024)S(1)} %bitcast.28, f32[12296,128]{1,0:T(8,128)S(1)} %shard_map.76.frame_ref, f32[2048,128]{1,0:T(8,128)S(1)} %get-tuple-element.25.refs_2_.refs_4_.scale_ref, ...), custom_call_target="tpu_custom_call" | custom-call | bytes 12000000 | tf_op jit(solution)/shard_map/pallas_call | solution.py:429
  73.0 0.1 collective-permute-start.15
  73.1 3.1 %collective-permute-done.15.refs_5_ = bf16[64,512]{1,0:T(8,128)(2,1)S(1)} collective-permute-done((bf16[64,512]{1,0:T(8,128)(2,1)S(1)}, bf16[64,512]{1,0:T(8,128)(2,1)S(1)}, u32[]{:S(2)}, u32[]{:S(2)}) %collective-permute-start.15) | collective-permute-done | bytes 65568 | tf_op jit(solution)/shard_map/ppermute | solution.py:445
  76.2 0.0 collective-permute-done.14.refs_4_
  76.2 0.0 collective-permute-done.13.refs_3_
  76.2 0.8 %shard_map.80 = bf16[64,4096]{1,0:T(8,128)(2,1)} custom-call(bf16[64,1024]{1,0:T(8,128)(2,1)S(1)} %get-tuple-element.36.after_ref.refs_0_, bf16[64,512]{1,0:T(8,128)(2,1)S(1)} %get-tuple-element.40.after_ref.refs_1_, bf16[64,512]{1,0:T(8,128)(2,1)S(1)} %get-tuple-element.41.refs_2_, bf16[128,1024]{1,0:T(8,128)(2,1)S(1)} %collective-permute-done.13.refs_3_, ...), custom_call_target="tpu_custom_call" | custom-call | bytes 1500000 | tf_op jit(solution)/shard_map/pallas_call | solution.py:447
  (4 shorter events, 0.1 us)
Async XLA Ops:
  0.0 19.1 %collective-permute-start.5 = (bf16[64,4096]{1,0:T(8,128)(2,1)}, bf16[64,4096]{1,0:T(8,128)(2,1)S(1)}, u32[]{:S(2)}, u32[]{:S(2)}) collective-permute-start(bf16[64,4096]{1,0:T(8,128)(2,1)} %x_ref.1), channel_id=1, source_target_pairs={{0,1},{1,0},{2,3},{3,2},{4,5},{5,4},{6,7},{7,6},{8,9},{9,8},{10,11... | collective-permute-start | bytes 1572872 | tf_op jit(solution)/shard_map/ppermute | solution.py:364
  2.1 1.1 %copy-start = (bf16[64,4096]{1,0:T(8,128)(2,1)S(1)}, bf16[64,4096]{1,0:T(8,128)(2,1)}, u32[]{:S(2)}) copy-start(bf16[64,4096]{1,0:T(8,128)(2,1)} %x_ref.1) | copy-start | bytes 1572868
  3.2 0.7 copy-start.5
  4.5 9.5 %collective-permute-start = (bf16[16,128]{1,0:T(8,128)(2,1)S(1)}, bf16[16,128]{1,0:T(8,128)(2,1)S(1)}, u32[]{:S(2)}, u32[]{:S(2)}) collective-permute-start(bf16[16,128]{1,0:T(8,128)(2,1)S(1)} %shard_map.64.after_ref.refs_0_), channel_id=1, source_target_pairs={{0,64},{2,66},{4,68},{6,70},{8,72},{10,74},{12,76},{14,78},{16,80}... | collective-permute-start | bytes 12296 | tf_op jit(solution)/shard_map/ppermute | solution.py:349
  11.5 0.7 copy-start.2
  12.2 0.8 copy-start.4
  12.9 0.7 copy-start.7
  14.0 4.4 %collective-permute-start.3 = (bf16[32,128]{1,0:T(8,128)(2,1)S(1)}, bf16[32,128]{1,0:T(8,128)(2,1)S(1)}, u32[]{:S(2)}, u32[]{:S(2)}) collective-permute-start(bf16[32,128]{1,0:T(8,128)(2,1)S(1)} %shard_map.66.refs_0_), channel_id=1, source_target_pairs={{0,48},{2,50},{4,52},{6,54},{8,56},{10,58},{12,60},{14,62},{16,32}... | collective-permute-start | bytes 24584 | tf_op jit(solution)/shard_map/ppermute | solution.py:349
  15.7 3.4 %collective-permute-start.2 = (bf16[32,128]{1,0:T(8,128)(2,1)S(1)}, bf16[32,128]{1,0:T(8,128)(2,1)S(1)}, u32[]{:S(2)}, u32[]{:S(2)}) collective-permute-start(bf16[32,128]{1,0:T(8,128)(2,1)S(1)} %shard_map.66.refs_0_), channel_id=1, source_target_pairs={{0,32},{2,34},{4,36},{6,38},{8,40},{10,42},{12,44},{14,46},{16,48}... | collective-permute-start | bytes 24584 | tf_op jit(solution)/shard_map/ppermute | solution.py:349
  16.0 3.1 %collective-permute-start.1 = (bf16[32,128]{1,0:T(8,128)(2,1)S(1)}, bf16[32,128]{1,0:T(8,128)(2,1)S(1)}, u32[]{:S(2)}, u32[]{:S(2)}) collective-permute-start(bf16[32,128]{1,0:T(8,128)(2,1)S(1)} %shard_map.66.refs_0_), channel_id=1, source_target_pairs={{0,16},{2,18},{4,20},{6,22},{8,24},{10,26},{12,28},{14,30},{16,0},... | collective-permute-start | bytes 24584 | tf_op jit(solution)/shard_map/ppermute | solution.py:349
  19.1 1.0 %copy-start.1 = (bf16[64,4096]{1,0:T(8,128)(2,1)S(1)}, bf16[64,4096]{1,0:T(8,128)(2,1)}, u32[]{:S(2)}) copy-start(bf16[64,4096]{1,0:T(8,128)(2,1)} %x_ref.1) | copy-start | bytes 1572868
  20.3 17.2 %collective-permute-start.7 = (bf16[128,2048]{1,0:T(8,128)(2,1)S(1)}, bf16[128,2048]{1,0:T(8,128)(2,1)S(1)}, u32[]{:S(2)}, u32[]{:S(2)}) collective-permute-start(bf16[128,2048]{1,0:T(8,128)(2,1)S(1)} %get-tuple-element.30.inner_ref), channel_id=1, source_target_pairs={{0,2},{2,0},{4,6},{6,4},{8,10},{10,8},{12,14},{14,12},{16,18},{18,... | collective-permute-start | bytes 1572872 | tf_op jit(solution)/shard_map/ppermute | solution.py:377
  23.4 14.0 %collective-permute-start.6 = (bf16[128,2048]{1,0:T(8,128)(2,1)S(1)}, bf16[128,2048]{1,0:T(8,128)(2,1)S(1)}, u32[]{:S(2)}, u32[]{:S(2)}) collective-permute-start(bf16[128,2048]{1,0:T(8,128)(2,1)S(1)} %get-tuple-element.26.after_ref.outer_ref), channel_id=1, source_target_pairs={{2,4},{4,2},{6,8},{8,6},{10,12},{12,10},{14,16},{16,14},{18,20},{2... | collective-permute-start | bytes 1572872 | tf_op jit(solution)/shard_map/ppermute | solution.py:378
  26.4 2.9 %collective-permute-start.4 = (bf16[128,128]{1,0:T(8,128)(2,1)S(1)}, bf16[128,128]{1,0:T(8,128)(2,1)S(1)}, u32[]{:S(2)}, u32[]{:S(2)}) collective-permute-start(bf16[128,128]{1,0:T(8,128)(2,1)S(1)} %shard_map.67.after_ref.mine_ref), channel_id=1, source_target_pairs={{0,1},{1,0},{2,3},{3,2},{4,5},{5,4},{6,7},{7,6},{8,9},{9,8},{10,11... | collective-permute-start | bytes 98312 | tf_op jit(solution)/shard_map/ppermute | solution.py:369
  29.4 13.4 %collective-permute-start.8 = (bf16[256,128]{1,0:T(8,128)(2,1)S(1)}, bf16[256,128]{1,0:T(8,128)(2,1)S(1)}, u32[]{:S(2)}, u32[]{:S(2)}) collective-permute-start(bf16[256,128]{1,0:T(8,128)(2,1)S(1)} %shard_map.69.after_ref.refs_0_), channel_id=1, source_target_pairs={{0,128},{2,130},{4,132},{6,134},{8,136},{10,138},{12,140},{14,142}... | collective-permute-start | bytes 196616 | tf_op jit(solution)/shard_map/ppermute | solution.py:349
  33.1 0.7 copy-start.3
  42.8 7.9 %collective-permute-start.11 = (bf16[512,128]{1,0:T(8,128)(2,1)S(1)}, bf16[512,128]{1,0:T(8,128)(2,1)S(1)}, u32[]{:S(2)}, u32[]{:S(2)}) collective-permute-start(bf16[512,128]{1,0:T(8,128)(2,1)S(1)} %shard_map.73.after_ref.refs_0_), channel_id=1, source_target_pairs={{0,12},{2,14},{4,8},{6,10},{8,4},{10,6},{12,0},{14,2},{16,28},{18,... | collective-permute-start | bytes 393224 | tf_op jit(solution)/shard_map/ppermute | solution.py:349
  45.2 5.6 %collective-permute-start.10 = (bf16[512,128]{1,0:T(8,128)(2,1)S(1)}, bf16[512,128]{1,0:T(8,128)(2,1)S(1)}, u32[]{:S(2)}, u32[]{:S(2)}) collective-permute-start(bf16[512,128]{1,0:T(8,128)(2,1)S(1)} %shard_map.73.after_ref.refs_0_), channel_id=1, source_target_pairs={{0,8},{2,10},{4,12},{6,14},{8,0},{10,2},{12,4},{14,6},{16,24},{18,... | collective-permute-start | bytes 393224 | tf_op jit(solution)/shard_map/ppermute | solution.py:349
  46.4 4.3 %collective-permute-start.9 = (bf16[512,128]{1,0:T(8,128)(2,1)S(1)}, bf16[512,128]{1,0:T(8,128)(2,1)S(1)}, u32[]{:S(2)}, u32[]{:S(2)}) collective-permute-start(bf16[512,128]{1,0:T(8,128)(2,1)S(1)} %shard_map.73.after_ref.refs_0_), channel_id=1, source_target_pairs={{0,4},{2,6},{4,0},{6,2},{8,12},{10,14},{12,8},{14,10},{16,20},{18,... | collective-permute-start | bytes 393224 | tf_op jit(solution)/shard_map/ppermute | solution.py:349
  50.8 8.2 %copy-start.6 = (s32[32]{0:T(128)S(1)}, s32[32]{0:T(128)}, u32[]{:S(2)}) copy-start(s32[32]{0:T(128)} %after_ref.1) | copy-start | bytes 388
  50.8 8.0 %collective-permute-start.12 = (bf16[2048,128]{1,0:T(8,128)(2,1)S(1)}, bf16[2048,128]{1,0:T(8,128)(2,1)S(1)}, u32[]{:S(2)}, u32[]{:S(2)}) collective-permute-start(bf16[2048,128]{1,0:T(8,128)(2,1)S(1)} %shard_map.75.near_ref), channel_id=1, source_target_pairs={{0,2},{2,0},{4,6},{6,4},{8,10},{10,8},{12,14},{14,12},{16,18},{18,... | collective-permute-start | bytes 1572872 | tf_op jit(solution)/shard_map/ppermute | solution.py:349
  62.1 14.0 %collective-permute-start.13 = (bf16[128,1024]{1,0:T(8,128)(2,1)S(1)}, bf16[128,1024]{1,0:T(8,128)(2,1)S(1)}, u32[]{:S(2)}, u32[]{:S(2)}) collective-permute-start(bf16[128,1024]{1,0:T(8,128)(2,1)S(1)} %get-tuple-element.42), channel_id=1, source_target_pairs={{0,1},{1,0},{2,3},{3,2},{4,5},{5,4},{6,7},{7,6},{8,9},{9,8},{10,11... | collective-permute-start | bytes 786440 | tf_op jit(solution)/shard_map/ppermute | solution.py:445
  66.9 9.3 %collective-permute-start.14 = (bf16[128,512]{1,0:T(8,128)(2,1)S(1)}, bf16[128,512]{1,0:T(8,128)(2,1)S(1)}, u32[]{:S(2)}, u32[]{:S(2)}) collective-permute-start(bf16[128,512]{1,0:T(8,128)(2,1)S(1)} %get-tuple-element.43), channel_id=1, source_target_pairs={{0,1},{1,0},{2,3},{3,2},{4,5},{5,4},{6,7},{7,6},{8,9},{9,8},{10,11... | collective-permute-start | bytes 393224 | tf_op jit(solution)/shard_map/ppermute | solution.py:445
  73.0 3.2 %collective-permute-start.15 = (bf16[64,512]{1,0:T(8,128)(2,1)S(1)}, bf16[64,512]{1,0:T(8,128)(2,1)S(1)}, u32[]{:S(2)}, u32[]{:S(2)}) collective-permute-start(bf16[64,512]{1,0:T(8,128)(2,1)S(1)} %get-tuple-element.44), channel_id=1, source_target_pairs={{0,1},{1,0},{2,3},{3,2},{4,5},{5,4},{6,7},{7,6},{8,9},{9,8},{10,11... | collective-permute-start | bytes 196616 | tf_op jit(solution)/shard_map/ppermute | solution.py:445

commit v3 on v2

--- a/solution.py
+++ b/solution.py
@@ -45,7 +45,7 @@
         out_ref[i * rows : (i + 1) * rows] = ref[...]
 
 
-def join_feat_kernel(mine_ref, other_ref, after_ref, out_ref):
+def join_feat_kernel(mine_ref, other_ref, out_ref):
     first = lax.axis_index("feat") == 0
     lane = lax.broadcasted_iota(jnp.int32, (16, LANES), 1)
     for i in range(mine_ref.shape[0] // 16):
@@ -59,14 +59,22 @@
         out_ref[32 * i + 16 : 32 * i + 32, :] = row.astype(jnp.bfloat16)
 
 
-def halves_kernel(x_ref, other_ref, after_ref, outer_ref, inner_ref):
+def halves_kernel(x_ref, other_ref, after_ref, outer_ref, inner_ref, sem):
     feat = lax.axis_index("feat")
     odd = lax.axis_index("slab") & 1
     chans, half = x_ref.shape[0], outer_ref.shape[1]
+    copies = []
     for ref, channels in ((x_ref, feat), (other_ref, 1 - feat)):
         rows = pl.ds(pl.multiple_of(channels * chans, chans), chans)
-        outer_ref[rows, :] = ref[:, pl.ds(pl.multiple_of(odd * half, half), half)]
-        inner_ref[rows, :] = ref[:, pl.ds(pl.multiple_of((1 - odd) * half, half), half)]
+        for out_ref, part in ((outer_ref, odd), (inner_ref, 1 - odd)):
+            cols = pl.ds(pl.multiple_of(part * half, half), half)
+            copies.append(
+                pltpu.make_async_copy(ref.at[:, cols], out_ref.at[rows, :], sem.at[len(copies)])
+            )
+    for copy in copies:
+        copy.start()
+    for copy in copies:
+        copy.wait()
 
 
 def frame_kernel(outer_halo_ref, outer_ref, inner_ref, inner_halo_ref, after_ref, frame_ref):
@@ -316,6 +324,7 @@
 
 IN_VMEM = pl.BlockSpec(memory_space=VMEM)
 ANYWHERE = pl.BlockSpec(memory_space=pl.ANY)
+IN_HBM = pl.BlockSpec(memory_space=pltpu.HBM)
 
 
 def local(node_feats, neighbours, degrees, hub_rows, weight, bias_terms):
@@ -340,7 +349,7 @@
     block = pallas(
         hub_pick_kernel,
         bf16(hubs // 2, 2 * chans),
-        [IN_VMEM, ANYWHERE],
+        [IN_VMEM, IN_HBM],
         [VMEM((chans, nodes), jnp.bfloat16), pltpu.SemaphoreType.DMA((4,))],
     )(hub_rows[None, :], node_feats)
     arrived = None
@@ -355,29 +364,6 @@
 
     arrived = stage(block, STAGES[0])
     deg_tiles = degrees.reshape(nodes // LANES, LANES)
-    scale, by_out, bias = pallas(
-        constants_kernel,
-        (f32(half, LANES), bf16(2 * chans, 2 * chans), f32(LANES, LANES)),
-        [IN_VMEM] * 3 + [ANYWHERE],
-        us=1.0,
-    )(deg_tiles, weight, bias_terms[None, :], block)
-    other = lax.ppermute(node_feats, "feat", swap)
-
-    block = join(block, arrived, scale)
-    arrived = stage(block, STAGES[1])
-    block = join(block, arrived, scale)
-    arrived = lax.ppermute(block, "feat", swap)
-    outer, inner = pallas(
-        halves_kernel, (bf16(2 * chans, half),) * 2, [IN_VMEM, IN_VMEM, ANYWHERE], us=0.5
-    )(node_feats, other, block)
-    block = pallas(
-        join_feat_kernel, bf16(2 * block.shape[0], 2 * chans), [IN_VMEM, IN_VMEM, ANYWHERE], us=0.5
-    )(block, arrived, outer)
-    arrived = stage(block, STAGES[2])
-    inner_halo = lax.ppermute(inner, "slab", [(i, i ^ 1) for i in range(slabs)])
-    outer_halo = lax.ppermute(
-        outer, "slab", [(i, j) for i in range(slabs) for j in [i + 2 * (i & 1) - 1] if 0 <= j < slabs]
-    )
     table, tile = i32(slots, 8, LANES), i32(8, LANES)
     plan = pallas(
         functools.partial(plan_kernel, frame_rows, frame_rows + hub_count),
@@ -387,12 +373,42 @@
     )(neighbours.reshape(slots, nodes // LANES, LANES), deg_tiles, block)
     plan = [a.reshape(-1) for a in plan]
     near_plan, far_plan, full_plan = plan[:3], plan[3:6], plan[6:]
+    other = lax.ppermute(node_feats, "feat", swap)
+
+    block = join(block, arrived, near_plan[1])
+    arrived = stage(block, STAGES[1])
+    scale, by_out, bias = pallas(
+        constants_kernel,
+        (f32(half, LANES), bf16(2 * chans, 2 * chans), f32(LANES, LANES)),
+        [IN_VMEM] * 3 + [ANYWHERE],
+        us=1.0,
+    )(deg_tiles, weight, bias_terms[None, :], block)
+
+    block = join(block, arrived, scale)
+    arrived = lax.ppermute(block, "feat", swap)
+    block = pallas(
+        join_feat_kernel, bf16(2 * block.shape[0], 2 * chans), [IN_VMEM] * 2, us=0.5
+    )(block, arrived)
+    arrived = stage(block, STAGES[2])
+    outer, inner = pallas(
+        halves_kernel,
+        (bf16(2 * chans, half),) * 2,
+        [IN_HBM, ANYWHERE, ANYWHERE],
+        [pltpu.SemaphoreType.DMA((4,))],
+        us=0.5,
+    )(node_feats, other, block)
+    inner_halo = lax.ppermute(inner, "slab", [(i, i ^ 1) for i in range(slabs)])
+    outer_halo = lax.ppermute(
+        outer, "slab", [(i, j) for i in range(slabs) for j in [i + 2 * (i & 1) - 1] if 0 <= j < slabs]
+    )
+    block = join(block, arrived, outer)
+    arrived = stage(block, STAGES[3])
     frame = pallas(
         frame_kernel,
         f32(frame_rows + hub_count + 8, LANES),
         [IN_VMEM] * 4 + [ANYWHERE],
         us=2.0,
-    )(outer_halo, outer, inner, inner_halo, near_plan[1])
+    )(outer_halo, outer, inner, inner_halo, block)
 
     def plan_scratch(size):
         return [
@@ -413,10 +429,8 @@
 
     near = [near_sum(0, block)]
     block = join(block, arrived, near[0])
-    arrived = stage(block, STAGES[3])
+    arrived = stage(block, STAGES[4])
     near.append(near_sum(1, block))
-    block = join(block, arrived, near[1])
-    arrived = stage(block, STAGES[4])
     frame = pallas(
         functools.partial(hub_frame_kernel, frame_rows, hubs),
         f32(*frame.shape),

time: 77.3 us -> 78.9 us (1.021)
  the two profiles are of different devices: /device:TPU:1 before, /device:TPU:16 now
where the time goes in v3:
time: 78.9 us; the launch traced here: 78.1 us
  starting transfers between devices  27.3 us (35%)
  Pallas kernels  27.3 us (35%)
  waiting for transfers between devices  16.9 us (21%)
  local copies, waits for them, and re-layouts  6.38 us (8%)
    ppermute x9, starting transfers between devices, stage(): lax.ppermute(block, 'slab', [(i, i ^ bit) for i in range(slabs)])  16.1 us
    pallas_call x3, Pallas kernels, layer(): pallas(functools.partial(layer_kernel, slots, first, start, len(near), ha...  12.1 us
    ppermute x9, waiting for transfers between devices, stage(): lax.ppermute(block, 'slab', [(i, i ^ bit) for i in range(slabs)])  11.2 us
    pallas_call x2, Pallas kernels, near_sum(): pallas(functools.partial(near_kernel, slots, part, 2), f32(CHUNK, LANES),...  8.15 us
    unnamed x15, local copies, waits for them, and re-layouts  6.38 us
    ppermute x1, starting transfers between devices, local(): lax.ppermute(outer, 'slab', [(i, j) for i in range(slabs) for j in [i + 2...  4.99 us
    ppermute x3, starting transfers between devices, local(): received.append(lax.ppermute(sent, 'feat', swap))  4.11 us
    pallas_call x1, Pallas kernels, local(): pallas(functools.partial(plan_kernel, frame_rows, frame_rows + hub_count)...  3.58 us
  transfers between devices with their start and end apart: 16, of which 4 were waited for; matrix products, arithmetic and copies ran while one was open for 1% of the time, Pallas kernels for 29%

profile of v3, /device:TPU:16, one launch (start us, length us, event | category | flops | bytes accessed | tf_op | source)
XLA Modules:
  0.0 78.1 jit_solution(14648727740525417412)
XLA Ops:
  0.0 1.3 %collective-permute-start = (bf16[64,4096]{1,0:T(8,128)(2,1)}, bf16[64,4096]{1,0:T(8,128)(2,1)S(1)}, u32[]{:S(2)}, u32[]{:S(2)}) collective-permute-start(bf16[64,4096]{1,0:T(8,128)(2,1)} %x_ref.1), channel_id=1, source_target_pairs={{0,1},{1,0},{2,3},{3,2},{4,5},{5,4},{6,7},{7,6},{8,9},{9,8},{10,11... | collective-permute-start | bytes 1572872 | tf_op jit(solution)/shard_map/ppermute | solution.py:376
  1.3 0.0 copy-start
  1.3 1.1 %copy-done = bf16[64,4096]{1,0:T(8,128)(2,1)S(1)} copy-done((bf16[64,4096]{1,0:T(8,128)(2,1)S(1)}, bf16[64,4096]{1,0:T(8,128)(2,1)}, u32[]{:S(2)}) %copy-start) | copy-done | bytes 524312
  2.4 0.0 copy-start.4
  2.4 0.7 copy-done.4
  3.0 0.6 shard_map.64.after_ref.refs_0_
  3.6 7.3 %collective-permute-start.1 = (bf16[16,128]{1,0:T(8,128)(2,1)S(1)}, bf16[16,128]{1,0:T(8,128)(2,1)S(1)}, u32[]{:S(2)}, u32[]{:S(2)}) collective-permute-start(bf16[16,128]{1,0:T(8,128)(2,1)S(1)} %shard_map.64.after_ref.refs_0_), channel_id=1, source_target_pairs={{0,64},{2,66},{4,68},{6,70},{8,72},{10,74},{12,76},{14,78},{16,80}... | collective-permute-start | bytes 12296 | tf_op jit(solution)/shard_map/ppermute | solution.py:358
  10.9 1.0 %copy.8 = s32[2,8,32,128]{3,2,1,0:T(8,128)S(1)} copy(s32[2,8,32,128]{3,1,2,0:T(8,128)} %bitcast.35) | data formatting | bytes 524288
  11.9 0.0 copy-start.2
  11.9 0.7 copy-done.2
  12.6 3.6 %shard_map.65 = (s32[16,8,128]{2,1,0:T(8,128)S(1)}, s32[8,128]{1,0:T(8,128)S(1)}, s32[8,128]{1,0:T(8,128)S(1)}, s32[16,8,128]{2,1,0:T(8,128)S(1)}, s32[8,128]{1,...) custom-call(s32[16,32,128]{2,1,0:T(8,128)S(1)} %bitcast.14, ...), custom_call_target="tpu_custom_call" | custom-call | bytes 12000000 | tf_op jit(solution)/shard_map/pallas_call | solution.py:368
  16.2 0.0 collective-permute-done.1.refs_1_
  16.2 2.0 %collective-permute-start.4 = (bf16[32,128]{1,0:T(8,128)(2,1)S(1)}, bf16[32,128]{1,0:T(8,128)(2,1)S(1)}, u32[]{:S(2)}, u32[]{:S(2)}) collective-permute-start(bf16[32,128]{1,0:T(8,128)(2,1)S(1)} %shard_map.66.after_ref.refs_0_), channel_id=1, source_target_pairs={{0,48},{2,50},{4,52},{6,54},{8,56},{10,58},{12,60},{14,62},{16,32}... | collective-permute-start | bytes 24584 | tf_op jit(solution)/shard_map/ppermute | solution.py:358
  18.3 0.6 collective-permute-start.3
  18.8 1.9 %collective-permute-start.2 = (bf16[32,128]{1,0:T(8,128)(2,1)S(1)}, bf16[32,128]{1,0:T(8,128)(2,1)S(1)}, u32[]{:S(2)}, u32[]{:S(2)}) collective-permute-start(bf16[32,128]{1,0:T(8,128)(2,1)S(1)} %shard_map.66.after_ref.refs_0_), channel_id=1, source_target_pairs={{0,16},{2,18},{4,20},{6,22},{8,24},{10,26},{12,28},{14,30},{16,0},... | collective-permute-start | bytes 24584 | tf_op jit(solution)/shard_map/ppermute | solution.py:358
  20.7 0.0 copy-start.3
  20.7 0.8 copy-done.3
  21.5 0.0 copy-start.6
  21.5 0.7 copy-done.6
  22.1 0.4 shard_map.67
  22.5 0.0 collective-permute-done.4.refs_3_
  22.5 0.3 collective-permute-done.3.refs_2_
  22.8 0.0 collective-permute-done.2.refs_1_
  22.8 0.8 collective-permute-start.5
  23.6 3.2 %collective-permute-done.5.other_ref = bf16[128,128]{1,0:T(8,128)(2,1)S(1)} collective-permute-done((bf16[128,128]{1,0:T(8,128)(2,1)S(1)}, bf16[128,128]{1,0:T(8,128)(2,1)S(1)}, u32[]{:S(2)}, u32[]{:S(2)}) %collective-permute-start.5) | collective-permute-done | bytes 32800 | tf_op jit(solution)/shard_map/ppermute | solution.py:388
  26.7 0.1 shard_map.69.after_ref.refs_0_
  26.8 0.0 collective-permute-done.other_ref
  26.9 0.0 copy-start.1
  26.9 1.0 %copy-done.1 = bf16[64,4096]{1,0:T(8,128)(2,1)S(1)} copy-done((bf16[64,4096]{1,0:T(8,128)(2,1)S(1)}, bf16[64,4096]{1,0:T(8,128)(2,1)}, u32[]{:S(2)}) %copy-start.1) | copy-done | bytes 524312
  27.9 0.1 shard_map.70
  28.0 0.1 collective-permute-start.7
  28.1 5.0 %collective-permute-start.6 = (bf16[128,2048]{1,0:T(8,128)(2,1)S(1)}, bf16[128,2048]{1,0:T(8,128)(2,1)S(1)}, u32[]{:S(2)}, u32[]{:S(2)}) collective-permute-start(bf16[128,2048]{1,0:T(8,128)(2,1)S(1)} %get-tuple-element.30.refs_2_.outer_ref), channel_id=1, source_target_pairs={{2,4},{4,2},{6,8},{8,6},{10,12},{12,10},{14,16},{16,14},{18,20},{2... | collective-permute-start | bytes 1572872 | tf_op jit(solution)/shard_map/ppermute | solution.py:401
  33.1 0.1 collective-permute-start.8
  33.2 10.9 %collective-permute-done.8.refs_1_ = bf16[256,128]{1,0:T(8,128)(2,1)S(1)} collective-permute-done((bf16[256,128]{1,0:T(8,128)(2,1)S(1)}, bf16[256,128]{1,0:T(8,128)(2,1)S(1)}, u32[]{:S(2)}, u32[]{:S(2)}) %collective-permute-start.8) | collective-permute-done | bytes 65568 | tf_op jit(solution)/shard_map/ppermute | solution.py:358
  44.1 0.1 collective-permute-start.11
  44.2 0.1 collective-permute-start.10
  44.3 4.0 %collective-permute-start.9 = (bf16[512,128]{1,0:T(8,128)(2,1)S(1)}, bf16[512,128]{1,0:T(8,128)(2,1)S(1)}, u32[]{:S(2)}, u32[]{:S(2)}) collective-permute-start(bf16[512,128]{1,0:T(8,128)(2,1)S(1)} %shard_map.71.after_ref.refs_0_), channel_id=1, source_target_pairs={{0,4},{2,6},{4,0},{6,2},{8,12},{10,14},{12,8},{14,10},{16,20},{18,... | collective-permute-start | bytes 393224 | tf_op jit(solution)/shard_map/ppermute | solution.py:358
  48.3 0.0 collective-permute-done.7.inner_halo_ref
  48.3 0.0 collective-permute-done.6.outer_halo_ref
  48.3 1.2 %shard_map.72.frame_ref.frame_in = f32[12296,128]{1,0:T(8,128)S(1)} custom-call(bf16[128,2048]{1,0:T(8,128)(2,1)S(1)} %collective-permute-done.6.outer_halo_ref, bf16[128,2048]{1,0:T(8,128)(2,1)S(1)} %get-tuple-element.30.refs_2_.outer_ref, bf16[128,2048]{1,0:T(8,128)(2,1)S(1)} %get-tuple-element.31.inner_ref, ...), custom_call_target="tpu_custom_call" | custom-call | bytes 6000000 | tf_op jit(solution)/shard_map/pallas_call | solution.py:406
  49.5 3.9 %shard_map.73.refs_4_.refs_0_ = f32[1024,128]{1,0:T(8,128)S(1)} custom-call(s32[16384]{0:T(1024)S(1)} %bitcast.17, s32[1024]{0:T(1024)S(1)} %bitcast.23, s32[1024]{0:T(1024)S(1)} %bitcast.29, f32[12296,128]{1,0:T(8,128)S(1)} %shard_map.72.frame_ref.frame_in, bf16[512,128]{1,0:T(8,128)(2,1)S(1)} %shard_map.71.after_ref.refs_0_), custom_call_target="tpu_custom_call" | custom-call | bytes 12000000 | tf_op jit(solution)/shard_map/pallas_call | solution.py:422
  53.5 0.0 collective-permute-done.11.refs_3_
  53.5 0.0 collective-permute-done.10.refs_2_
  53.5 0.0 collective-permute-done.9.refs_1_
  53.5 0.1 collective-permute-start.12
  53.6 4.2 %shard_map.75.after_ref.refs_1_ = f32[1024,128]{1,0:T(8,128)S(1)} custom-call(s32[16384]{0:T(1024)S(1)} %bitcast.18, s32[1024]{0:T(1024)S(1)} %bitcast.24, s32[1024]{0:T(1024)S(1)} %bitcast.30, f32[12296,128]{1,0:T(8,128)S(1)} %shard_map.72.frame_ref.frame_in, bf16[2048,128]{1,0:T(8,128)(2,1)S(1)} %shard_map.74.after_ref.near_ref), custom_call_target="tpu_custom_call" | custom-call | bytes 12000000 | tf_op jit(solution)/shard_map/pallas_call | solution.py:422
  57.9 0.0 copy-start.5
  57.9 0.0 collective-permute-done.12.far_ref
  57.9 0.1 shard_map.76.frame_ref
  58.1 0.5 copy-done.5
  58.5 3.1 %shard_map.77 = (bf16[64,1024]{1,0:T(8,128)(2,1)S(1)}, bf16[128,1024]{1,0:T(8,128)(2,1)S(1)}) custom-call(s32[16384]{0:T(1024)S(1)} %bitcast.19, s32[1024]{0:T(1024)S(1)} %bitcast.31, s32[1024]{0:T(1024)S(1)} %bitcast.32, f32[12296,128]{1,0:T(8,128)S(1)} %shard_map.76.frame_ref, f32[2048,128]{1,0:T(8,128)S(1)} %get-tuple-element.29.refs_4_.scale_ref, ...), custom_call_target="tpu_custom_call" | custom-call | bytes 9000000 | tf_op jit(solution)/shard_map/pallas_call | solution.py:443
  61.7 1.8 %collective-permute-start.13 = (bf16[128,1024]{1,0:T(8,128)(2,1)S(1)}, bf16[128,1024]{1,0:T(8,128)(2,1)S(1)}, u32[]{:S(2)}, u32[]{:S(2)}) collective-permute-start(bf16[128,1024]{1,0:T(8,128)(2,1)S(1)} %get-tuple-element.42), channel_id=1, source_target_pairs={{0,1},{1,0},{2,3},{3,2},{4,5},{5,4},{6,7},{7,6},{8,9},{9,8},{10,11... | collective-permute-start | bytes 786440 | tf_op jit(solution)/shard_map/ppermute | solution.py:459
  63.5 4.5 %shard_map.78 = (bf16[64,512]{1,0:T(8,128)(2,1)S(1)}, bf16[128,512]{1,0:T(8,128)(2,1)S(1)}) custom-call(s32[16384]{0:T(1024)S(1)} %bitcast.15, s32[1024]{0:T(1024)S(1)} %bitcast.25, s32[1024]{0:T(1024)S(1)} %bitcast.27, f32[12296,128]{1,0:T(8,128)S(1)} %shard_map.76.frame_ref, f32[2048,128]{1,0:T(8,128)S(1)} %get-tuple-element.29.refs_4_.scale_ref, ...), custom_call_target="tpu_custom_call" | custom-call | bytes 12000000 | tf_op jit(solution)/shard_map/pallas_call | solution.py:443
  68.0 0.5 collective-permute-start.14
  68.4 4.4 %shard_map.79 = (bf16[64,512]{1,0:T(8,128)(2,1)S(1)}, bf16[64,512]{1,0:T(8,128)(2,1)S(1)}) custom-call(s32[16384]{0:T(1024)S(1)} %bitcast.16, s32[1024]{0:T(1024)S(1)} %bitcast.26, s32[1024]{0:T(1024)S(1)} %bitcast.28, f32[12296,128]{1,0:T(8,128)S(1)} %shard_map.76.frame_ref, f32[2048,128]{1,0:T(8,128)S(1)} %get-tuple-element.29.refs_4_.scale_ref, ...), custom_call_target="tpu_custom_call" | custom-call | bytes 12000000 | tf_op jit(solution)/shard_map/pallas_call | solution.py:443
  72.9 1.8 %collective-permute-start.15 = (bf16[64,512]{1,0:T(8,128)(2,1)S(1)}, bf16[64,512]{1,0:T(8,128)(2,1)S(1)}, u32[]{:S(2)}, u32[]{:S(2)}) collective-permute-start(bf16[64,512]{1,0:T(8,128)(2,1)S(1)} %get-tuple-element.44), channel_id=1, source_target_pairs={{0,1},{1,0},{2,3},{3,2},{4,5},{5,4},{6,7},{7,6},{8,9},{9,8},{10,11... | collective-permute-start | bytes 196616 | tf_op jit(solution)/shard_map/ppermute | solution.py:459
  74.7 2.5 %collective-permute-done.15.refs_5_ = bf16[64,512]{1,0:T(8,128)(2,1)S(1)} collective-permute-done((bf16[64,512]{1,0:T(8,128)(2,1)S(1)}, bf16[64,512]{1,0:T(8,128)(2,1)S(1)}, u32[]{:S(2)}, u32[]{:S(2)}) %collective-permute-start.15) | collective-permute-done | bytes 65568 | tf_op jit(solution)/shard_map/ppermute | solution.py:459
  77.2 0.0 collective-permute-done.14.refs_4_
  77.3 0.0 collective-permute-done.13.refs_3_
  77.3 0.8 %shard_map.80 = bf16[64,4096]{1,0:T(8,128)(2,1)} custom-call(bf16[64,1024]{1,0:T(8,128)(2,1)S(1)} %get-tuple-element.36.after_ref.refs_0_, bf16[64,512]{1,0:T(8,128)(2,1)S(1)} %get-tuple-element.40.after_ref.refs_1_, bf16[64,512]{1,0:T(8,128)(2,1)S(1)} %get-tuple-element.41.refs_2_, bf16[128,1024]{1,0:T(8,128)(2,1)S(1)} %collective-permute-done.13.refs_3_, ...), custom_call_target="tpu_custom_call" | custom-call | bytes 1500000 | tf_op jit(solution)/shard_map/pallas_call | solution.py:461
  (4 shorter events, 0.1 us)
Async XLA Ops:
  0.0 26.8 %collective-permute-start = (bf16[64,4096]{1,0:T(8,128)(2,1)}, bf16[64,4096]{1,0:T(8,128)(2,1)S(1)}, u32[]{:S(2)}, u32[]{:S(2)}) collective-permute-start(bf16[64,4096]{1,0:T(8,128)(2,1)} %x_ref.1), channel_id=1, source_target_pairs={{0,1},{1,0},{2,3},{3,2},{4,5},{5,4},{6,7},{7,6},{8,9},{9,8},{10,11... | collective-permute-start | bytes 1572872 | tf_op jit(solution)/shard_map/ppermute | solution.py:376
  1.3 1.1 %copy-start = (bf16[64,4096]{1,0:T(8,128)(2,1)S(1)}, bf16[64,4096]{1,0:T(8,128)(2,1)}, u32[]{:S(2)}) copy-start(bf16[64,4096]{1,0:T(8,128)(2,1)} %x_ref.1) | copy-start | bytes 1572868
  2.4 0.7 copy-start.4
  3.6 12.6 %collective-permute-start.1 = (bf16[16,128]{1,0:T(8,128)(2,1)S(1)}, bf16[16,128]{1,0:T(8,128)(2,1)S(1)}, u32[]{:S(2)}, u32[]{:S(2)}) collective-permute-start(bf16[16,128]{1,0:T(8,128)(2,1)S(1)} %shard_map.64.after_ref.refs_0_), channel_id=1, source_target_pairs={{0,64},{2,66},{4,68},{6,70},{8,72},{10,74},{12,76},{14,78},{16,80}... | collective-permute-start | bytes 12296 | tf_op jit(solution)/shard_map/ppermute | solution.py:358
  11.9 0.7 copy-start.2
  16.2 6.3 %collective-permute-start.4 = (bf16[32,128]{1,0:T(8,128)(2,1)S(1)}, bf16[32,128]{1,0:T(8,128)(2,1)S(1)}, u32[]{:S(2)}, u32[]{:S(2)}) collective-permute-start(bf16[32,128]{1,0:T(8,128)(2,1)S(1)} %shard_map.66.after_ref.refs_0_), channel_id=1, source_target_pairs={{0,48},{2,50},{4,52},{6,54},{8,56},{10,58},{12,60},{14,62},{16,32}... | collective-permute-start | bytes 24584 | tf_op jit(solution)/shard_map/ppermute | solution.py:358
  18.3 4.5 %collective-permute-start.3 = (bf16[32,128]{1,0:T(8,128)(2,1)S(1)}, bf16[32,128]{1,0:T(8,128)(2,1)S(1)}, u32[]{:S(2)}, u32[]{:S(2)}) collective-permute-start(bf16[32,128]{1,0:T(8,128)(2,1)S(1)} %shard_map.66.after_ref.refs_0_), channel_id=1, source_target_pairs={{0,32},{2,34},{4,36},{6,38},{8,40},{10,42},{12,44},{14,46},{16,48}... | collective-permute-start | bytes 24584 | tf_op jit(solution)/shard_map/ppermute | solution.py:358
  18.8 4.0 %collective-permute-start.2 = (bf16[32,128]{1,0:T(8,128)(2,1)S(1)}, bf16[32,128]{1,0:T(8,128)(2,1)S(1)}, u32[]{:S(2)}, u32[]{:S(2)}) collective-permute-start(bf16[32,128]{1,0:T(8,128)(2,1)S(1)} %shard_map.66.after_ref.refs_0_), channel_id=1, source_target_pairs={{0,16},{2,18},{4,20},{6,22},{8,24},{10,26},{12,28},{14,30},{16,0},... | collective-permute-start | bytes 24584 | tf_op jit(solution)/shard_map/ppermute | solution.py:358
  20.7 0.8 copy-start.3
  21.5 0.7 copy-start.6
  22.8 3.9 %collective-permute-start.5 = (bf16[128,128]{1,0:T(8,128)(2,1)S(1)}, bf16[128,128]{1,0:T(8,128)(2,1)S(1)}, u32[]{:S(2)}, u32[]{:S(2)}) collective-permute-start(bf16[128,128]{1,0:T(8,128)(2,1)S(1)} %shard_map.68.mine_ref), channel_id=1, source_target_pairs={{0,1},{1,0},{2,3},{3,2},{4,5},{5,4},{6,7},{7,6},{8,9},{9,8},{10,11... | collective-permute-start | bytes 98312 | tf_op jit(solution)/shard_map/ppermute | solution.py:388
  26.9 1.0 %copy-start.1 = (bf16[64,4096]{1,0:T(8,128)(2,1)S(1)}, bf16[64,4096]{1,0:T(8,128)(2,1)}, u32[]{:S(2)}) copy-start(bf16[64,4096]{1,0:T(8,128)(2,1)} %x_ref.1) | copy-start | bytes 1572868
  28.0 20.3 %collective-permute-start.7 = (bf16[128,2048]{1,0:T(8,128)(2,1)S(1)}, bf16[128,2048]{1,0:T(8,128)(2,1)S(1)}, u32[]{:S(2)}, u32[]{:S(2)}) collective-permute-start(bf16[128,2048]{1,0:T(8,128)(2,1)S(1)} %get-tuple-element.31.inner_ref), channel_id=1, source_target_pairs={{0,2},{2,0},{4,6},{6,4},{8,10},{10,8},{12,14},{14,12},{16,18},{18,... | collective-permute-start | bytes 1572872 | tf_op jit(solution)/shard_map/ppermute | solution.py:400
  28.1 20.2 %collective-permute-start.6 = (bf16[128,2048]{1,0:T(8,128)(2,1)S(1)}, bf16[128,2048]{1,0:T(8,128)(2,1)S(1)}, u32[]{:S(2)}, u32[]{:S(2)}) collective-permute-start(bf16[128,2048]{1,0:T(8,128)(2,1)S(1)} %get-tuple-element.30.refs_2_.outer_ref), channel_id=1, source_target_pairs={{2,4},{4,2},{6,8},{8,6},{10,12},{12,10},{14,16},{16,14},{18,20},{2... | collective-permute-start | bytes 1572872 | tf_op jit(solution)/shard_map/ppermute | solution.py:401
  33.1 11.0 %collective-permute-start.8 = (bf16[256,128]{1,0:T(8,128)(2,1)S(1)}, bf16[256,128]{1,0:T(8,128)(2,1)S(1)}, u32[]{:S(2)}, u32[]{:S(2)}) collective-permute-start(bf16[256,128]{1,0:T(8,128)(2,1)S(1)} %shard_map.69.after_ref.refs_0_), channel_id=1, source_target_pairs={{0,128},{2,130},{4,132},{6,134},{8,136},{10,138},{12,140},{14,142}... | collective-permute-start | bytes 196616 | tf_op jit(solution)/shard_map/ppermute | solution.py:358
  44.1 9.4 %collective-permute-start.11 = (bf16[512,128]{1,0:T(8,128)(2,1)S(1)}, bf16[512,128]{1,0:T(8,128)(2,1)S(1)}, u32[]{:S(2)}, u32[]{:S(2)}) collective-permute-start(bf16[512,128]{1,0:T(8,128)(2,1)S(1)} %shard_map.71.after_ref.refs_0_), channel_id=1, source_target_pairs={{0,12},{2,14},{4,8},{6,10},{8,4},{10,6},{12,0},{14,2},{16,28},{18,... | collective-permute-start | bytes 393224 | tf_op jit(solution)/shard_map/ppermute | solution.py:358
  44.2 9.3 %collective-permute-start.10 = (bf16[512,128]{1,0:T(8,128)(2,1)S(1)}, bf16[512,128]{1,0:T(8,128)(2,1)S(1)}, u32[]{:S(2)}, u32[]{:S(2)}) collective-permute-start(bf16[512,128]{1,0:T(8,128)(2,1)S(1)} %shard_map.71.after_ref.refs_0_), channel_id=1, source_target_pairs={{0,8},{2,10},{4,12},{6,14},{8,0},{10,2},{12,4},{14,6},{16,24},{18,... | collective-permute-start | bytes 393224 | tf_op jit(solution)/shard_map/ppermute | solution.py:358
  44.3 9.2 %collective-permute-start.9 = (bf16[512,128]{1,0:T(8,128)(2,1)S(1)}, bf16[512,128]{1,0:T(8,128)(2,1)S(1)}, u32[]{:S(2)}, u32[]{:S(2)}) collective-permute-start(bf16[512,128]{1,0:T(8,128)(2,1)S(1)} %shard_map.71.after_ref.refs_0_), channel_id=1, source_target_pairs={{0,4},{2,6},{4,0},{6,2},{8,12},{10,14},{12,8},{14,10},{16,20},{18,... | collective-permute-start | bytes 393224 | tf_op jit(solution)/shard_map/ppermute | solution.py:358
  53.5 4.4 %collective-permute-start.12 = (bf16[2048,128]{1,0:T(8,128)(2,1)S(1)}, bf16[2048,128]{1,0:T(8,128)(2,1)S(1)}, u32[]{:S(2)}, u32[]{:S(2)}) collective-permute-start(bf16[2048,128]{1,0:T(8,128)(2,1)S(1)} %shard_map.74.after_ref.near_ref), channel_id=1, source_target_pairs={{0,2},{2,0},{4,6},{6,4},{8,10},{10,8},{12,14},{14,12},{16,18},{18,... | collective-permute-start | bytes 1572872 | tf_op jit(solution)/shard_map/ppermute | solution.py:358
  57.9 0.7 copy-start.5
  61.7 15.6 %collective-permute-start.13 = (bf16[128,1024]{1,0:T(8,128)(2,1)S(1)}, bf16[128,1024]{1,0:T(8,128)(2,1)S(1)}, u32[]{:S(2)}, u32[]{:S(2)}) collective-permute-start(bf16[128,1024]{1,0:T(8,128)(2,1)S(1)} %get-tuple-element.42), channel_id=1, source_target_pairs={{0,1},{1,0},{2,3},{3,2},{4,5},{5,4},{6,7},{7,6},{8,9},{9,8},{10,11... | collective-permute-start | bytes 786440 | tf_op jit(solution)/shard_map/ppermute | solution.py:459
  68.0 9.3 %collective-permute-start.14 = (bf16[128,512]{1,0:T(8,128)(2,1)S(1)}, bf16[128,512]{1,0:T(8,128)(2,1)S(1)}, u32[]{:S(2)}, u32[]{:S(2)}) collective-permute-start(bf16[128,512]{1,0:T(8,128)(2,1)S(1)} %get-tuple-element.43), channel_id=1, source_target_pairs={{0,1},{1,0},{2,3},{3,2},{4,5},{5,4},{6,7},{7,6},{8,9},{9,8},{10,11... | collective-permute-start | bytes 393224 | tf_op jit(solution)/shard_map/ppermute | solution.py:459
  72.9 4.4 %collective-permute-start.15 = (bf16[64,512]{1,0:T(8,128)(2,1)S(1)}, bf16[64,512]{1,0:T(8,128)(2,1)S(1)}, u32[]{:S(2)}, u32[]{:S(2)}) collective-permute-start(bf16[64,512]{1,0:T(8,128)(2,1)S(1)} %get-tuple-element.44), channel_id=1, source_target_pairs={{0,1},{1,0},{2,3},{3,2},{4,5},{5,4},{6,7},{7,6},{8,9},{9,8},{10,11... | collective-permute-start | bytes 196616 | tf_op jit(solution)/shard_map/ppermute | solution.py:459

commit v4 on v3

--- a/solution.py
+++ b/solution.py
@@ -38,14 +38,14 @@
     out_ref[...] = jnp.concatenate([picked[: hubs // 2], picked[hubs // 2 :]], axis=1)
 
 
-def join_kernel(*refs):
-    blocks, out_ref = refs[:-2], refs[-1]
+def join_kernel(count, *refs):
+    blocks, out_ref = refs[:count], refs[-1]
     rows = blocks[0].shape[0]
     for i, ref in enumerate(blocks):
         out_ref[i * rows : (i + 1) * rows] = ref[...]
 
 
-def join_feat_kernel(mine_ref, other_ref, out_ref):
+def join_feat_kernel(mine_ref, other_ref, after_ref, out_ref):
     first = lax.axis_index("feat") == 0
     lane = lax.broadcasted_iota(jnp.int32, (16, LANES), 1)
     for i in range(mine_ref.shape[0] // 16):
@@ -59,41 +59,59 @@
         out_ref[32 * i + 16 : 32 * i + 32, :] = row.astype(jnp.bfloat16)
 
 
-def halves_kernel(x_ref, other_ref, after_ref, outer_ref, inner_ref, sem):
+def outer_half_kernel(x_ref, after_ref, outer_ref, sem):
+    half = outer_ref.shape[1]
+    part = lax.axis_index("slab") & 1
+    copy = pltpu.make_async_copy(
+        x_ref.at[:, pl.ds(pl.multiple_of(part * half, half), half)], outer_ref, sem
+    )
+    copy.start()
+    copy.wait()
+
+
+def inner_half_kernel(x_ref, other_ref, after_ref, inner_ref, sem):
     feat = lax.axis_index("feat")
-    odd = lax.axis_index("slab") & 1
-    chans, half = x_ref.shape[0], outer_ref.shape[1]
-    copies = []
-    for ref, channels in ((x_ref, feat), (other_ref, 1 - feat)):
-        rows = pl.ds(pl.multiple_of(channels * chans, chans), chans)
-        for out_ref, part in ((outer_ref, odd), (inner_ref, 1 - odd)):
-            cols = pl.ds(pl.multiple_of(part * half, half), half)
-            copies.append(
-                pltpu.make_async_copy(ref.at[:, cols], out_ref.at[rows, :], sem.at[len(copies)])
-            )
+    part = 1 - (lax.axis_index("slab") & 1)
+    chans, half = x_ref.shape[0], inner_ref.shape[1]
+    copies = [
+        pltpu.make_async_copy(
+            ref.at[:, pl.ds(pl.multiple_of(part * half, half), half)],
+            inner_ref.at[pl.ds(pl.multiple_of(channels * chans, chans), chans), :],
+            sem.at[i],
+        )
+        for i, (ref, channels) in enumerate(((x_ref, feat), (other_ref, 1 - feat)))
+    ]
     for copy in copies:
         copy.start()
     for copy in copies:
         copy.wait()
 
 
-def frame_kernel(outer_halo_ref, outer_ref, inner_ref, inner_halo_ref, after_ref, frame_ref):
+def frame_kernel(x_ref, outer_ref, other_x_ref, other_outer_ref, inner_ref, after_ref, frame_ref):
     odd = lax.axis_index("slab") & 1
-    half = outer_ref.shape[1]
+    first = lax.axis_index("feat") == 0
+    half, nodes = outer_ref.shape[1], x_ref.shape[1]
     step = 256
     unit = (
         lax.broadcasted_iota(jnp.int32, (step, step), 0)
         == lax.broadcasted_iota(jnp.int32, (step, step), 1)
     ).astype(jnp.bfloat16)
-    for place, ref in enumerate((outer_halo_ref, outer_ref, inner_ref, inner_halo_ref)):
-        first = (place + odd * (3 - 2 * place)) * half
-        for at in range(0, half, step):
-            frame_ref[pl.ds(pl.multiple_of(first + at, step), step), :] = lax.dot_general(
-                unit,
-                ref[:, at : at + step],
-                (((1,), (1,)), ((), ())),
-                preferred_element_type=jnp.float32,
+
+    def fill(place, *refs):
+        for at in range(0, refs[0].shape[1], step):
+            columns = refs[0][:, at : at + step]
+            if len(refs) == 2:
+                other = refs[1][:, at : at + step]
+                columns = jnp.concatenate(
+                    [jnp.where(first, columns, other), jnp.where(first, other, columns)], axis=0
+                )
+            frame_ref[pl.ds(pl.multiple_of(place + at, step), step), :] = lax.dot_general(
+                unit, columns, (((1,), (1,)), ((), ())), preferred_element_type=jnp.float32
             )
+
+    fill(odd * (half + nodes), outer_ref, other_outer_ref)
+    fill(half, x_ref, other_x_ref)
+    fill((1 - odd) * (half + nodes), inner_ref)
     rows = frame_ref.shape[0]
     frame_ref[rows - 8 :, :] = jnp.zeros((8, LANES), jnp.float32)
 
@@ -324,7 +342,6 @@
 
 IN_VMEM = pl.BlockSpec(memory_space=VMEM)
 ANYWHERE = pl.BlockSpec(memory_space=pl.ANY)
-IN_HBM = pl.BlockSpec(memory_space=pltpu.HBM)
 
 
 def local(node_feats, neighbours, degrees, hub_rows, weight, bias_terms):
@@ -349,7 +366,7 @@
     block = pallas(
         hub_pick_kernel,
         bf16(hubs // 2, 2 * chans),
-        [IN_VMEM, IN_HBM],
+        [IN_VMEM, ANYWHERE],
         [VMEM((chans, nodes), jnp.bfloat16), pltpu.SemaphoreType.DMA((4,))],
     )(hub_rows[None, :], node_feats)
     arrived = None
@@ -357,23 +374,35 @@
     def stage(block, bits):
         return [lax.ppermute(block, "slab", [(i, i ^ bit) for i in range(slabs)]) for bit in bits]
 
-    def join(block, arrived, after):
-        rows = block.shape[0] * (1 + len(arrived))
-        specs = [IN_VMEM] * (1 + len(arrived)) + [ANYWHERE]
-        return pallas(join_kernel, bf16(rows, 2 * chans), specs, us=0.5)(block, *arrived, after)
+    def join(block, arrived, *after):
+        blocks = 1 + len(arrived)
+        return pallas(
+            functools.partial(join_kernel, blocks),
+            bf16(blocks * block.shape[0], 2 * chans),
+            [IN_VMEM] * blocks + [ANYWHERE] * len(after),
+            us=0.1,
+        )(block, *arrived, *after)
 
     arrived = stage(block, STAGES[0])
+    other = lax.ppermute(node_feats, "feat", swap)
+    outer = pallas(
+        outer_half_kernel, bf16(chans, half), [ANYWHERE] * 2, [pltpu.SemaphoreType.DMA], us=0.1
+    )(node_feats, block)
+    pairs = [(i, j) for i in range(slabs) for j in [i + 2 * (i & 1) - 1] if 0 <= j < slabs]
+    outer_halo = lax.ppermute(outer, "slab", pairs)
+    other_outer = lax.ppermute(
+        outer, ("slab", "feat"), [(2 * i + f, 2 * j + 1 - f) for i, j in pairs for f in range(2)]
+    )
     deg_tiles = degrees.reshape(nodes // LANES, LANES)
     table, tile = i32(slots, 8, LANES), i32(8, LANES)
     plan = pallas(
         functools.partial(plan_kernel, frame_rows, frame_rows + hub_count),
         (table, tile, tile) * 3,
         [IN_VMEM, IN_VMEM, ANYWHERE],
-        us=4.0,
-    )(neighbours.reshape(slots, nodes // LANES, LANES), deg_tiles, block)
+        us=0.1,
+    )(neighbours.reshape(slots, nodes // LANES, LANES), deg_tiles, outer)
     plan = [a.reshape(-1) for a in plan]
     near_plan, far_plan, full_plan = plan[:3], plan[3:6], plan[6:]
-    other = lax.ppermute(node_feats, "feat", swap)
 
     block = join(block, arrived, near_plan[1])
     arrived = stage(block, STAGES[1])
@@ -381,34 +410,29 @@
         constants_kernel,
         (f32(half, LANES), bf16(2 * chans, 2 * chans), f32(LANES, LANES)),
         [IN_VMEM] * 3 + [ANYWHERE],
-        us=1.0,
+        us=0.1,
     )(deg_tiles, weight, bias_terms[None, :], block)
 
-    block = join(block, arrived, scale)
+    block = join(block, arrived, scale, outer_halo)
     arrived = lax.ppermute(block, "feat", swap)
     block = pallas(
-        join_feat_kernel, bf16(2 * block.shape[0], 2 * chans), [IN_VMEM] * 2, us=0.5
-    )(block, arrived)
+        join_feat_kernel, bf16(2 * block.shape[0], 2 * chans), [IN_VMEM] * 2 + [ANYWHERE], us=0.1
+    )(block, arrived, other_outer)
     arrived = stage(block, STAGES[2])
-    outer, inner = pallas(
-        halves_kernel,
-        (bf16(2 * chans, half),) * 2,
-        [IN_HBM, ANYWHERE, ANYWHERE],
-        [pltpu.SemaphoreType.DMA((4,))],
-        us=0.5,
+    inner = pallas(
+        inner_half_kernel,
+        bf16(2 * chans, half),
+        [ANYWHERE] * 3,
+        [pltpu.SemaphoreType.DMA((2,))],
+        us=0.1,
     )(node_feats, other, block)
     inner_halo = lax.ppermute(inner, "slab", [(i, i ^ 1) for i in range(slabs)])
-    outer_halo = lax.ppermute(
-        outer, "slab", [(i, j) for i in range(slabs) for j in [i + 2 * (i & 1) - 1] if 0 <= j < slabs]
-    )
-    block = join(block, arrived, outer)
-    arrived = stage(block, STAGES[3])
     frame = pallas(
         frame_kernel,
         f32(frame_rows + hub_count + 8, LANES),
-        [IN_VMEM] * 4 + [ANYWHERE],
+        [IN_VMEM] * 5 + [ANYWHERE],
         us=2.0,
-    )(outer_halo, outer, inner, inner_halo, block)
+    )(node_feats, outer_halo, other, other_outer, inner_halo, block)
 
     def plan_scratch(size):
         return [
@@ -429,8 +453,10 @@
 
     near = [near_sum(0, block)]
     block = join(block, arrived, near[0])
+    arrived = stage(block, STAGES[3])
+    near.append(near_sum(1, block))
+    block = join(block, arrived, near[1])
     arrived = stage(block, STAGES[4])
-    near.append(near_sum(1, block))
     frame = pallas(
         functools.partial(hub_frame_kernel, frame_rows, hubs),
         f32(*frame.shape),

time: 78.9 us -> 81.3 us (1.030)
  starting transfers between devices: 27.3 us -> 28.6 us
    ppermute x1 -> x2, starting transfers between devices: 4.99 us -> 11.1 us  [the longest x1 9.19 us: local(): outer_halo = lax.ppermute(outer, 'slab', pairs)]
    ppermute x9, starting transfers between devices: 16.1 us -> 11.3 us  [stage(): lax.ppermute(block, 'slab', [(i, i ^ bit) for i in range(slabs)])]
    ppermute x9, waiting for transfers between devices: 11.2 us -> 9.6 us  [stage(): lax.ppermute(block, 'slab', [(i, i ^ bit) for i in range(slabs)])]
    ppermute x1, waiting for transfers between devices: 0.01 us -> 1.47 us  [local(): inner_halo = lax.ppermute(inner, 'slab', [(i, i ^ 1) for i in range(slabs)])]
    unnamed x15 -> x17, local copies, waits for them, and re-layouts: 6.38 us -> 6.94 us
  transfers between devices with their start and end apart: 16 -> 17, of which waited for: 4 -> 8; matrix products, arithmetic and copies ran while one was open for 1% -> 1% of each run, Pallas kernels for 29% -> 29%
where the time goes in v4:
time: 81.3 us; the launch traced here: 80 us
  starting transfers between devices  28.6 us (35%)
  Pallas kernels  27.4 us (34%)
  waiting for transfers between devices  16.7 us (21%)
  local copies, waits for them, and re-layouts  6.94 us (9%)
    pallas_call x3, Pallas kernels, layer(): pallas(functools.partial(layer_kernel, slots, first, start, len(near), ha...  12 us
    ppermute x9, starting transfers between devices, stage(): lax.ppermute(block, 'slab', [(i, i ^ bit) for i in range(slabs)])  11.3 us
    ppermute x9, waiting for transfers between devices, stage(): lax.ppermute(block, 'slab', [(i, i ^ bit) for i in range(slabs)])  9.6 us
    ppermute x1, starting transfers between devices, local(): outer_halo = lax.ppermute(outer, 'slab', pairs)  9.19 us
    pallas_call x2, Pallas kernels, near_sum(): pallas(functools.partial(near_kernel, slots, part, 2), f32(CHUNK, LANES),...  8.42 us
    unnamed x17, local copies, waits for them, and re-layouts  6.94 us
    ppermute x3, starting transfers between devices, local(): received.append(lax.ppermute(sent, 'feat', swap))  3.59 us
    pallas_call x1, Pallas kernels, local(): pallas(functools.partial(plan_kernel, frame_rows, frame_rows + hub_count)...  3.58 us
  transfers between devices with their start and end apart: 17, of which 8 were waited for; matrix products, arithmetic and copies ran while one was open for 1% of the time, Pallas kernels for 29%

profile of v4, /device:TPU:16, one launch (start us, length us, event | category | flops | bytes accessed | tf_op | source)
XLA Modules:
  0.0 80.0 jit_solution(14861992613199731985)
XLA Ops:
  0.0 1.3 %collective-permute-start.1 = (bf16[64,4096]{1,0:T(8,128)(2,1)}, bf16[64,4096]{1,0:T(8,128)(2,1)S(1)}, u32[]{:S(2)}, u32[]{:S(2)}) collective-permute-start(bf16[64,4096]{1,0:T(8,128)(2,1)} %x_ref.5), channel_id=1, source_target_pairs={{0,1},{1,0},{2,3},{3,2},{4,5},{5,4},{6,7},{7,6},{8,9},{9,8},{10,11... | collective-permute-start | bytes 1572872 | tf_op jit(solution)/shard_map/ppermute | solution.py:387
  1.3 0.0 copy-start
  1.3 1.1 %copy-done = bf16[64,4096]{1,0:T(8,128)(2,1)S(1)} copy-done((bf16[64,4096]{1,0:T(8,128)(2,1)S(1)}, bf16[64,4096]{1,0:T(8,128)(2,1)}, u32[]{:S(2)}) %copy-start) | copy-done | bytes 524312
  2.4 0.0 copy-start.5
  2.4 0.7 copy-done.5
  3.0 0.6 shard_map.64.after_ref.refs_0_
  3.6 0.0 copy-start.1
  3.6 1.0 %copy-done.1 = bf16[64,4096]{1,0:T(8,128)(2,1)S(1)} copy-done((bf16[64,4096]{1,0:T(8,128)(2,1)S(1)}, bf16[64,4096]{1,0:T(8,128)(2,1)}, u32[]{:S(2)}) %copy-start.1) | copy-done | bytes 524312
  4.7 9.2 %collective-permute-start = (bf16[64,2048]{1,0:T(8,128)(2,1)S(1)}, bf16[64,2048]{1,0:T(8,128)(2,1)S(1)}, u32[]{:S(2)}, u32[]{:S(2)}) collective-permute-start(bf16[64,2048]{1,0:T(8,128)(2,1)S(1)} %shard_map.65.after_ref), channel_id=1, source_target_pairs={{2,4},{4,2},{6,8},{8,6},{10,12},{12,10},{14,16},{16,14},{18,20},{2... | collective-permute-start | bytes 786440 | tf_op jit(solution)/shard_map/ppermute | solution.py:392
  13.9 1.9 %collective-permute-start.2 = (bf16[64,2048]{1,0:T(8,128)(2,1)S(1)}, bf16[64,2048]{1,0:T(8,128)(2,1)S(1)}, u32[]{:S(2)}, u32[]{:S(2)}) collective-permute-start(bf16[64,2048]{1,0:T(8,128)(2,1)S(1)} %shard_map.65.after_ref), channel_id=1, source_target_pairs={{2,5},{3,4},{4,3},{5,2},{6,9},{7,8},{8,7},{9,6},{10,13},{11,12},{1... | collective-permute-start | bytes 786440 | tf_op jit(solution)/shard_map/ppermute | solution.py:393
  15.8 5.2 %collective-permute-start.3 = (bf16[16,128]{1,0:T(8,128)(2,1)S(1)}, bf16[16,128]{1,0:T(8,128)(2,1)S(1)}, u32[]{:S(2)}, u32[]{:S(2)}) collective-permute-start(bf16[16,128]{1,0:T(8,128)(2,1)S(1)} %shard_map.64.after_ref.refs_0_), channel_id=1, source_target_pairs={{0,64},{2,66},{4,68},{6,70},{8,72},{10,74},{12,76},{14,78},{16,80}... | collective-permute-start | bytes 12296 | tf_op jit(solution)/shard_map/ppermute | solution.py:375
  21.1 1.0 %copy.8 = s32[2,8,32,128]{3,2,1,0:T(8,128)S(1)} copy(s32[2,8,32,128]{3,1,2,0:T(8,128)} %bitcast.35) | data formatting | bytes 524288
  22.1 0.0 copy-start.3
  22.1 0.7 copy-done.3
  22.8 3.6 %shard_map.66 = (s32[16,8,128]{2,1,0:T(8,128)S(1)}, s32[8,128]{1,0:T(8,128)S(1)}, s32[8,128]{1,0:T(8,128)S(1)}, s32[16,8,128]{2,1,0:T(8,128)S(1)}, s32[8,128]{1,...) custom-call(s32[16,32,128]{2,1,0:T(8,128)S(1)} %bitcast.14, ...), custom_call_target="tpu_custom_call" | custom-call | bytes 300000 | tf_op jit(solution)/shard_map/pallas_call | solution.py:398
  26.4 0.0 collective-permute-done.3.refs_1_
  26.4 0.8 %collective-permute-start.6 = (bf16[32,128]{1,0:T(8,128)(2,1)S(1)}, bf16[32,128]{1,0:T(8,128)(2,1)S(1)}, u32[]{:S(2)}, u32[]{:S(2)}) collective-permute-start(bf16[32,128]{1,0:T(8,128)(2,1)S(1)} %shard_map.67.after_ref.refs_0_), channel_id=1, source_target_pairs={{0,48},{2,50},{4,52},{6,54},{8,56},{10,58},{12,60},{14,62},{16,32}... | collective-permute-start | bytes 24584 | tf_op jit(solution)/shard_map/ppermute | solution.py:375
  27.2 0.6 collective-permute-start.5
  27.8 4.2 %collective-permute-done.6.refs_3_ = bf16[32,128]{1,0:T(8,128)(2,1)S(1)} collective-permute-done((bf16[32,128]{1,0:T(8,128)(2,1)S(1)}, bf16[32,128]{1,0:T(8,128)(2,1)S(1)}, u32[]{:S(2)}, u32[]{:S(2)}) %collective-permute-start.6) | collective-permute-done | bytes 8224 | tf_op jit(solution)/shard_map/ppermute | solution.py:375
  31.9 0.0 collective-permute-start.4
  31.9 0.0 copy-start.4
  31.9 0.8 copy-done.4
  32.7 0.0 copy-start.7
  32.7 0.7 copy-done.7
  33.4 0.4 shard_map.68
  33.7 0.0 collective-permute-done.5.refs_2_
  33.7 1.8 %collective-permute-done.4.refs_1_ = bf16[32,128]{1,0:T(8,128)(2,1)S(1)} collective-permute-done((bf16[32,128]{1,0:T(8,128)(2,1)S(1)}, bf16[32,128]{1,0:T(8,128)(2,1)S(1)}, u32[]{:S(2)}, u32[]{:S(2)}) %collective-permute-start.4) | collective-permute-done | bytes 8224 | tf_op jit(solution)/shard_map/ppermute | solution.py:375
  35.6 0.0 collective-permute-done.refs_5_.outer_ref
  35.6 1.3 %collective-permute-start.7 = (bf16[128,128]{1,0:T(8,128)(2,1)S(1)}, bf16[128,128]{1,0:T(8,128)(2,1)S(1)}, u32[]{:S(2)}, u32[]{:S(2)}) collective-permute-start(bf16[128,128]{1,0:T(8,128)(2,1)S(1)} %shard_map.69.mine_ref), channel_id=1, source_target_pairs={{0,1},{1,0},{2,3},{3,2},{4,5},{5,4},{6,7},{7,6},{8,9},{9,8},{10,11... | collective-permute-start | bytes 98312 | tf_op jit(solution)/shard_map/ppermute | solution.py:417
  36.9 0.0 collective-permute-done.2.after_ref.other_outer_ref
  36.9 2.6 %collective-permute-done.7.other_ref = bf16[128,128]{1,0:T(8,128)(2,1)S(1)} collective-permute-done((bf16[128,128]{1,0:T(8,128)(2,1)S(1)}, bf16[128,128]{1,0:T(8,128)(2,1)S(1)}, u32[]{:S(2)}, u32[]{:S(2)}) %collective-permute-start.7) | collective-permute-done | bytes 32800 | tf_op jit(solution)/shard_map/ppermute | solution.py:417
  39.5 0.1 shard_map.70.after_ref.refs_0_
  39.6 0.0 collective-permute-done.1.other_ref.other_x_ref
  39.6 0.0 copy-start.2
  39.6 1.0 %copy-done.2 = bf16[64,4096]{1,0:T(8,128)(2,1)S(1)} copy-done((bf16[64,4096]{1,0:T(8,128)(2,1)S(1)}, bf16[64,4096]{1,0:T(8,128)(2,1)}, u32[]{:S(2)}) %copy-start.2) | copy-done | bytes 524312
  40.7 0.1 shard_map.71
  40.7 0.1 collective-permute-start.8
  40.8 0.4 collective-permute-start.9
  41.3 1.5 %collective-permute-done.8.inner_ref = bf16[128,2048]{1,0:T(8,128)(2,1)S(1)} collective-permute-done((bf16[128,2048]{1,0:T(8,128)(2,1)S(1)}, bf16[128,2048]{1,0:T(8,128)(2,1)S(1)}, u32[]{:S(2)}, u32[]{:S(2)}) %collective-permute-start.8) | collective-permute-done | bytes 524320 | tf_op jit(solution)/shard_map/ppermute | solution.py:429
  42.7 1.3 %shard_map.72.frame_ref.frame_in = f32[12296,128]{1,0:T(8,128)S(1)} custom-call(bf16[64,4096]{1,0:T(8,128)(2,1)S(1)} %copy-done.2, bf16[64,2048]{1,0:T(8,128)(2,1)S(1)} %collective-permute-done.refs_5_.outer_ref, bf16[64,4096]{1,0:T(8,128)(2,1)S(1)} %collective-permute-done.1.other_ref.other_x_ref, ...), custom_call_target="tpu_custom_call" | custom-call | bytes 6000000 | tf_op jit(solution)/shard_map/pallas_call | solution.py:430
  44.0 4.1 %shard_map.73.refs_2_.refs_0_ = f32[1024,128]{1,0:T(8,128)S(1)} custom-call(s32[16384]{0:T(1024)S(1)} %bitcast.17, s32[1024]{0:T(1024)S(1)} %bitcast.23, s32[1024]{0:T(1024)S(1)} %bitcast.29, f32[12296,128]{1,0:T(8,128)S(1)} %shard_map.72.frame_ref.frame_in, bf16[256,128]{1,0:T(8,128)(2,1)S(1)} %shard_map.70.after_ref.refs_0_), custom_call_target="tpu_custom_call" | custom-call | bytes 12000000 | tf_op jit(solution)/shard_map/pallas_call | solution.py:446
  48.1 0.0 collective-permute-done.9.refs_1_
  48.1 0.1 collective-permute-start.12
  48.2 0.2 collective-permute-start.11
  48.4 3.9 %collective-permute-start.10 = (bf16[512,128]{1,0:T(8,128)(2,1)S(1)}, bf16[512,128]{1,0:T(8,128)(2,1)S(1)}, u32[]{:S(2)}, u32[]{:S(2)}) collective-permute-start(bf16[512,128]{1,0:T(8,128)(2,1)S(1)} %shard_map.74.after_ref.refs_0_), channel_id=1, source_target_pairs={{0,4},{2,6},{4,0},{6,2},{8,12},{10,14},{12,8},{14,10},{16,20},{18,... | collective-permute-start | bytes 393224 | tf_op jit(solution)/shard_map/ppermute | solution.py:375
  52.3 4.3 %shard_map.75.refs_4_.after_ref.refs_1_ = f32[1024,128]{1,0:T(8,128)S(1)} custom-call(s32[16384]{0:T(1024)S(1)} %bitcast.18, s32[1024]{0:T(1024)S(1)} %bitcast.24, s32[1024]{0:T(1024)S(1)} %bitcast.30, f32[12296,128]{1,0:T(8,128)S(1)} %shard_map.72.frame_ref.frame_in, bf16[512,128]{1,0:T(8,128)(2,1)S(1)} %shard_map.74.after_ref.refs_0_), custom_call_target="tpu_custom_call" | custom-call | bytes 12000000 | tf_op jit(solution)/shard_map/pallas_call | solution.py:446
  56.6 1.1 %collective-permute-done.12.refs_3_ = bf16[512,128]{1,0:T(8,128)(2,1)S(1)} collective-permute-done((bf16[512,128]{1,0:T(8,128)(2,1)S(1)}, bf16[512,128]{1,0:T(8,128)(2,1)S(1)}, u32[]{:S(2)}, u32[]{:S(2)}) %collective-permute-start.12) | collective-permute-done | bytes 131104 | tf_op jit(solution)/shard_map/ppermute | solution.py:375
  57.7 0.0 collective-permute-done.11.refs_2_
  57.7 0.6 collective-permute-done.10.refs_1_
  58.3 0.0 copy-start.6
  58.3 0.1 collective-permute-start.13
  58.4 1.9 %collective-permute-done.13.far_ref = bf16[2048,128]{1,0:T(8,128)(2,1)S(1)} collective-permute-done((bf16[2048,128]{1,0:T(8,128)(2,1)S(1)}, bf16[2048,128]{1,0:T(8,128)(2,1)S(1)}, u32[]{:S(2)}, u32[]{:S(2)}) %collective-permute-start.13) | collective-permute-done | bytes 524320 | tf_op jit(solution)/shard_map/ppermute | solution.py:375
  60.3 0.1 shard_map.77.frame_ref
  60.5 0.0 copy-done.6
  60.5 3.1 %shard_map.78 = (bf16[64,1024]{1,0:T(8,128)(2,1)S(1)}, bf16[128,1024]{1,0:T(8,128)(2,1)S(1)}) custom-call(s32[16384]{0:T(1024)S(1)} %bitcast.19, s32[1024]{0:T(1024)S(1)} %bitcast.31, s32[1024]{0:T(1024)S(1)} %bitcast.32, f32[12296,128]{1,0:T(8,128)S(1)} %shard_map.77.frame_ref, f32[2048,128]{1,0:T(8,128)S(1)} %get-tuple-element.27.refs_4_.scale_ref, ...), custom_call_target="tpu_custom_call" | custom-call | bytes 9000000 | tf_op jit(solution)/shard_map/pallas_call | solution.py:469
  63.6 1.3 %collective-permute-start.14 = (bf16[128,1024]{1,0:T(8,128)(2,1)S(1)}, bf16[128,1024]{1,0:T(8,128)(2,1)S(1)}, u32[]{:S(2)}, u32[]{:S(2)}) collective-permute-start(bf16[128,1024]{1,0:T(8,128)(2,1)S(1)} %get-tuple-element.38), channel_id=1, source_target_pairs={{0,1},{1,0},{2,3},{3,2},{4,5},{5,4},{6,7},{7,6},{8,9},{9,8},{10,11... | collective-permute-start | bytes 786440 | tf_op jit(solution)/shard_map/ppermute | solution.py:485
  64.9 4.4 %shard_map.79 = (bf16[64,512]{1,0:T(8,128)(2,1)S(1)}, bf16[128,512]{1,0:T(8,128)(2,1)S(1)}) custom-call(s32[16384]{0:T(1024)S(1)} %bitcast.15, s32[1024]{0:T(1024)S(1)} %bitcast.25, s32[1024]{0:T(1024)S(1)} %bitcast.27, f32[12296,128]{1,0:T(8,128)S(1)} %shard_map.77.frame_ref, f32[2048,128]{1,0:T(8,128)S(1)} %get-tuple-element.27.refs_4_.scale_ref, ...), custom_call_target="tpu_custom_call" | custom-call | bytes 12000000 | tf_op jit(solution)/shard_map/pallas_call | solution.py:469
  69.4 0.9 %collective-permute-start.15 = (bf16[128,512]{1,0:T(8,128)(2,1)S(1)}, bf16[128,512]{1,0:T(8,128)(2,1)S(1)}, u32[]{:S(2)}, u32[]{:S(2)}) collective-permute-start(bf16[128,512]{1,0:T(8,128)(2,1)S(1)} %get-tuple-element.39), channel_id=1, source_target_pairs={{0,1},{1,0},{2,3},{3,2},{4,5},{5,4},{6,7},{7,6},{8,9},{9,8},{10,11... | collective-permute-start | bytes 393224 | tf_op jit(solution)/shard_map/ppermute | solution.py:485
  70.3 4.5 %shard_map.80 = (bf16[64,512]{1,0:T(8,128)(2,1)S(1)}, bf16[64,512]{1,0:T(8,128)(2,1)S(1)}) custom-call(s32[16384]{0:T(1024)S(1)} %bitcast.16, s32[1024]{0:T(1024)S(1)} %bitcast.26, s32[1024]{0:T(1024)S(1)} %bitcast.28, f32[12296,128]{1,0:T(8,128)S(1)} %shard_map.77.frame_ref, f32[2048,128]{1,0:T(8,128)S(1)} %get-tuple-element.27.refs_4_.scale_ref, ...), custom_call_target="tpu_custom_call" | custom-call | bytes 12000000 | tf_op jit(solution)/shard_map/pallas_call | solution.py:469
  74.8 1.4 %collective-permute-start.16 = (bf16[64,512]{1,0:T(8,128)(2,1)S(1)}, bf16[64,512]{1,0:T(8,128)(2,1)S(1)}, u32[]{:S(2)}, u32[]{:S(2)}) collective-permute-start(bf16[64,512]{1,0:T(8,128)(2,1)S(1)} %get-tuple-element.40), channel_id=1, source_target_pairs={{0,1},{1,0},{2,3},{3,2},{4,5},{5,4},{6,7},{7,6},{8,9},{9,8},{10,11... | collective-permute-start | bytes 196616 | tf_op jit(solution)/shard_map/ppermute | solution.py:485
  76.1 3.0 %collective-permute-done.16.refs_5_ = bf16[64,512]{1,0:T(8,128)(2,1)S(1)} collective-permute-done((bf16[64,512]{1,0:T(8,128)(2,1)S(1)}, bf16[64,512]{1,0:T(8,128)(2,1)S(1)}, u32[]{:S(2)}, u32[]{:S(2)}) %collective-permute-start.16) | collective-permute-done | bytes 65568 | tf_op jit(solution)/shard_map/ppermute | solution.py:485
  79.1 0.0 collective-permute-done.15.refs_4_
  79.1 0.0 collective-permute-done.14.refs_3_
  79.1 0.8 %shard_map.81 = bf16[64,4096]{1,0:T(8,128)(2,1)} custom-call(bf16[64,1024]{1,0:T(8,128)(2,1)S(1)} %get-tuple-element.32.after_ref.refs_0_, bf16[64,512]{1,0:T(8,128)(2,1)S(1)} %get-tuple-element.36.after_ref.refs_1_, bf16[64,512]{1,0:T(8,128)(2,1)S(1)} %get-tuple-element.37.refs_2_, bf16[128,1024]{1,0:T(8,128)(2,1)S(1)} %collective-permute-done.14.refs_3_, ...), custom_call_target="tpu_custom_call" | custom-call | bytes 1500000 | tf_op jit(solution)/shard_map/pallas_call | solution.py:487
  (5 shorter events, 0.1 us)
Async XLA Ops:
  0.0 39.6 %collective-permute-start.1 = (bf16[64,4096]{1,0:T(8,128)(2,1)}, bf16[64,4096]{1,0:T(8,128)(2,1)S(1)}, u32[]{:S(2)}, u32[]{:S(2)}) collective-permute-start(bf16[64,4096]{1,0:T(8,128)(2,1)} %x_ref.5), channel_id=1, source_target_pairs={{0,1},{1,0},{2,3},{3,2},{4,5},{5,4},{6,7},{7,6},{8,9},{9,8},{10,11... | collective-permute-start | bytes 1572872 | tf_op jit(solution)/shard_map/ppermute | solution.py:387
  1.3 1.1 %copy-start = (bf16[64,4096]{1,0:T(8,128)(2,1)S(1)}, bf16[64,4096]{1,0:T(8,128)(2,1)}, u32[]{:S(2)}) copy-start(bf16[64,4096]{1,0:T(8,128)(2,1)} %x_ref.5) | copy-start | bytes 1572868
  2.4 0.7 copy-start.5
  3.6 1.0 %copy-start.1 = (bf16[64,4096]{1,0:T(8,128)(2,1)S(1)}, bf16[64,4096]{1,0:T(8,128)(2,1)}, u32[]{:S(2)}) copy-start(bf16[64,4096]{1,0:T(8,128)(2,1)} %x_ref.5) | copy-start | bytes 1572868
  4.7 30.9 %collective-permute-start = (bf16[64,2048]{1,0:T(8,128)(2,1)S(1)}, bf16[64,2048]{1,0:T(8,128)(2,1)S(1)}, u32[]{:S(2)}, u32[]{:S(2)}) collective-permute-start(bf16[64,2048]{1,0:T(8,128)(2,1)S(1)} %shard_map.65.after_ref), channel_id=1, source_target_pairs={{2,4},{4,2},{6,8},{8,6},{10,12},{12,10},{14,16},{16,14},{18,20},{2... | collective-permute-start | bytes 786440 | tf_op jit(solution)/shard_map/ppermute | solution.py:392
  13.9 23.0 %collective-permute-start.2 = (bf16[64,2048]{1,0:T(8,128)(2,1)S(1)}, bf16[64,2048]{1,0:T(8,128)(2,1)S(1)}, u32[]{:S(2)}, u32[]{:S(2)}) collective-permute-start(bf16[64,2048]{1,0:T(8,128)(2,1)S(1)} %shard_map.65.after_ref), channel_id=1, source_target_pairs={{2,5},{3,4},{4,3},{5,2},{6,9},{7,8},{8,7},{9,6},{10,13},{11,12},{1... | collective-permute-start | bytes 786440 | tf_op jit(solution)/shard_map/ppermute | solution.py:393
  15.8 10.6 %collective-permute-start.3 = (bf16[16,128]{1,0:T(8,128)(2,1)S(1)}, bf16[16,128]{1,0:T(8,128)(2,1)S(1)}, u32[]{:S(2)}, u32[]{:S(2)}) collective-permute-start(bf16[16,128]{1,0:T(8,128)(2,1)S(1)} %shard_map.64.after_ref.refs_0_), channel_id=1, source_target_pairs={{0,64},{2,66},{4,68},{6,70},{8,72},{10,74},{12,76},{14,78},{16,80}... | collective-permute-start | bytes 12296 | tf_op jit(solution)/shard_map/ppermute | solution.py:375
  22.1 0.7 copy-start.3
  26.4 5.5 %collective-permute-start.6 = (bf16[32,128]{1,0:T(8,128)(2,1)S(1)}, bf16[32,128]{1,0:T(8,128)(2,1)S(1)}, u32[]{:S(2)}, u32[]{:S(2)}) collective-permute-start(bf16[32,128]{1,0:T(8,128)(2,1)S(1)} %shard_map.67.after_ref.refs_0_), channel_id=1, source_target_pairs={{0,48},{2,50},{4,52},{6,54},{8,56},{10,58},{12,60},{14,62},{16,32}... | collective-permute-start | bytes 24584 | tf_op jit(solution)/shard_map/ppermute | solution.py:375
  27.2 6.5 %collective-permute-start.5 = (bf16[32,128]{1,0:T(8,128)(2,1)S(1)}, bf16[32,128]{1,0:T(8,128)(2,1)S(1)}, u32[]{:S(2)}, u32[]{:S(2)}) collective-permute-start(bf16[32,128]{1,0:T(8,128)(2,1)S(1)} %shard_map.67.after_ref.refs_0_), channel_id=1, source_target_pairs={{0,32},{2,34},{4,36},{6,38},{8,40},{10,42},{12,44},{14,46},{16,48}... | collective-permute-start | bytes 24584 | tf_op jit(solution)/shard_map/ppermute | solution.py:375
  31.9 3.7 %collective-permute-start.4 = (bf16[32,128]{1,0:T(8,128)(2,1)S(1)}, bf16[32,128]{1,0:T(8,128)(2,1)S(1)}, u32[]{:S(2)}, u32[]{:S(2)}) collective-permute-start(bf16[32,128]{1,0:T(8,128)(2,1)S(1)} %shard_map.67.after_ref.refs_0_), channel_id=1, source_target_pairs={{0,16},{2,18},{4,20},{6,22},{8,24},{10,26},{12,28},{14,30},{16,0},... | collective-permute-start | bytes 24584 | tf_op jit(solution)/shard_map/ppermute | solution.py:375
  31.9 0.8 copy-start.4
  32.7 0.7 copy-start.7
  35.6 3.9 %collective-permute-start.7 = (bf16[128,128]{1,0:T(8,128)(2,1)S(1)}, bf16[128,128]{1,0:T(8,128)(2,1)S(1)}, u32[]{:S(2)}, u32[]{:S(2)}) collective-permute-start(bf16[128,128]{1,0:T(8,128)(2,1)S(1)} %shard_map.69.mine_ref), channel_id=1, source_target_pairs={{0,1},{1,0},{2,3},{3,2},{4,5},{5,4},{6,7},{7,6},{8,9},{9,8},{10,11... | collective-permute-start | bytes 98312 | tf_op jit(solution)/shard_map/ppermute | solution.py:417
  39.6 1.0 %copy-start.2 = (bf16[64,4096]{1,0:T(8,128)(2,1)S(1)}, bf16[64,4096]{1,0:T(8,128)(2,1)}, u32[]{:S(2)}) copy-start(bf16[64,4096]{1,0:T(8,128)(2,1)} %x_ref.5) | copy-start | bytes 1572868
  40.7 2.0 %collective-permute-start.8 = (bf16[128,2048]{1,0:T(8,128)(2,1)S(1)}, bf16[128,2048]{1,0:T(8,128)(2,1)S(1)}, u32[]{:S(2)}, u32[]{:S(2)}) collective-permute-start(bf16[128,2048]{1,0:T(8,128)(2,1)S(1)} %shard_map.71), channel_id=1, source_target_pairs={{0,2},{2,0},{4,6},{6,4},{8,10},{10,8},{12,14},{14,12},{16,18},{18,... | collective-permute-start | bytes 1572872 | tf_op jit(solution)/shard_map/ppermute | solution.py:429
  40.8 7.2 %collective-permute-start.9 = (bf16[256,128]{1,0:T(8,128)(2,1)S(1)}, bf16[256,128]{1,0:T(8,128)(2,1)S(1)}, u32[]{:S(2)}, u32[]{:S(2)}) collective-permute-start(bf16[256,128]{1,0:T(8,128)(2,1)S(1)} %shard_map.70.after_ref.refs_0_), channel_id=1, source_target_pairs={{0,128},{2,130},{4,132},{6,134},{8,136},{10,138},{12,140},{14,142}... | collective-permute-start | bytes 196616 | tf_op jit(solution)/shard_map/ppermute | solution.py:375
  48.1 9.6 %collective-permute-start.12 = (bf16[512,128]{1,0:T(8,128)(2,1)S(1)}, bf16[512,128]{1,0:T(8,128)(2,1)S(1)}, u32[]{:S(2)}, u32[]{:S(2)}) collective-permute-start(bf16[512,128]{1,0:T(8,128)(2,1)S(1)} %shard_map.74.after_ref.refs_0_), channel_id=1, source_target_pairs={{0,12},{2,14},{4,8},{6,10},{8,4},{10,6},{12,0},{14,2},{16,28},{18,... | collective-permute-start | bytes 393224 | tf_op jit(solution)/shard_map/ppermute | solution.py:375
  48.2 9.5 %collective-permute-start.11 = (bf16[512,128]{1,0:T(8,128)(2,1)S(1)}, bf16[512,128]{1,0:T(8,128)(2,1)S(1)}, u32[]{:S(2)}, u32[]{:S(2)}) collective-permute-start(bf16[512,128]{1,0:T(8,128)(2,1)S(1)} %shard_map.74.after_ref.refs_0_), channel_id=1, source_target_pairs={{0,8},{2,10},{4,12},{6,14},{8,0},{10,2},{12,4},{14,6},{16,24},{18,... | collective-permute-start | bytes 393224 | tf_op jit(solution)/shard_map/ppermute | solution.py:375
  48.4 9.9 %collective-permute-start.10 = (bf16[512,128]{1,0:T(8,128)(2,1)S(1)}, bf16[512,128]{1,0:T(8,128)(2,1)S(1)}, u32[]{:S(2)}, u32[]{:S(2)}) collective-permute-start(bf16[512,128]{1,0:T(8,128)(2,1)S(1)} %shard_map.74.after_ref.refs_0_), channel_id=1, source_target_pairs={{0,4},{2,6},{4,0},{6,2},{8,12},{10,14},{12,8},{14,10},{16,20},{18,... | collective-permute-start | bytes 393224 | tf_op jit(solution)/shard_map/ppermute | solution.py:375
  58.3 2.2 %copy-start.6 = (s32[32]{0:T(128)S(1)}, s32[32]{0:T(128)}, u32[]{:S(2)}) copy-start(s32[32]{0:T(128)} %after_ref.1) | copy-start | bytes 388
  58.3 2.0 %collective-permute-start.13 = (bf16[2048,128]{1,0:T(8,128)(2,1)S(1)}, bf16[2048,128]{1,0:T(8,128)(2,1)S(1)}, u32[]{:S(2)}, u32[]{:S(2)}) collective-permute-start(bf16[2048,128]{1,0:T(8,128)(2,1)S(1)} %shard_map.76.near_ref), channel_id=1, source_target_pairs={{0,2},{2,0},{4,6},{6,4},{8,10},{10,8},{12,14},{14,12},{16,18},{18,... | collective-permute-start | bytes 1572872 | tf_op jit(solution)/shard_map/ppermute | solution.py:375
  63.6 15.5 %collective-permute-start.14 = (bf16[128,1024]{1,0:T(8,128)(2,1)S(1)}, bf16[128,1024]{1,0:T(8,128)(2,1)S(1)}, u32[]{:S(2)}, u32[]{:S(2)}) collective-permute-start(bf16[128,1024]{1,0:T(8,128)(2,1)S(1)} %get-tuple-element.38), channel_id=1, source_target_pairs={{0,1},{1,0},{2,3},{3,2},{4,5},{5,4},{6,7},{7,6},{8,9},{9,8},{10,11... | collective-permute-start | bytes 786440 | tf_op jit(solution)/shard_map/ppermute | solution.py:485
  69.4 9.8 %collective-permute-start.15 = (bf16[128,512]{1,0:T(8,128)(2,1)S(1)}, bf16[128,512]{1,0:T(8,128)(2,1)S(1)}, u32[]{:S(2)}, u32[]{:S(2)}) collective-permute-start(bf16[128,512]{1,0:T(8,128)(2,1)S(1)} %get-tuple-element.39), channel_id=1, source_target_pairs={{0,1},{1,0},{2,3},{3,2},{4,5},{5,4},{6,7},{7,6},{8,9},{9,8},{10,11... | collective-permute-start | bytes 393224 | tf_op jit(solution)/shard_map/ppermute | solution.py:485
  74.8 4.4 %collective-permute-start.16 = (bf16[64,512]{1,0:T(8,128)(2,1)S(1)}, bf16[64,512]{1,0:T(8,128)(2,1)S(1)}, u32[]{:S(2)}, u32[]{:S(2)}) collective-permute-start(bf16[64,512]{1,0:T(8,128)(2,1)S(1)} %get-tuple-element.40), channel_id=1, source_target_pairs={{0,1},{1,0},{2,3},{3,2},{4,5},{5,4},{6,7},{7,6},{8,9},{9,8},{10,11... | collective-permute-start | bytes 196616 | tf_op jit(solution)/shard_map/ppermute | solution.py:485

commit v5 on v3

--- a/solution.py
+++ b/solution.py
@@ -12,7 +12,7 @@
 LANES = 128
 CHUNK = 1024
 GROUP = 16
-STAGES = ((32,), (8, 16, 24), (64,), (2, 4, 6), (1,))
+STAGES = ((32,), (64,), (8, 16, 24), (2, 4, 6), (1,))
 
 
 def hub_pick_kernel(rows_ref, x_hbm, out_ref, x_ref, sem):
@@ -161,12 +161,9 @@
     return keys
 
 
-def plan_kernel(frame_rows, all_rows, nbr_ref, deg_ref, after_ref, near_ids, near_order, near_class, far_ids, far_order, far_class, full_ids, full_order, full_class):
+def slots_kernel(frame_rows, all_rows, nbr_ref, deg_ref, after_ref, near_ids, far_ids, full_ids, counts_ref):
     slots = nbr_ref.shape[0]
     first = lax.axis_index("feat") * 16
-    at = lax.broadcasted_iota(jnp.int32, (8, LANES), 0) * LANES + lax.broadcasted_iota(
-        jnp.int32, (8, LANES), 1
-    )
     rows = pl.ds(pl.multiple_of(first, 8), 8)
     degree = deg_ref[rows, :]
     near, far = [], []
@@ -182,17 +179,24 @@
         near_ids[j] = ids
     for j, ids in enumerate(sort_network(far)):
         far_ids[j] = ids
+    counts_ref[0] = near_count
+    counts_ref[1] = degree - near_count
     rows = pl.ds(pl.multiple_of(first + 8, 8), 8)
-    full_degree = deg_ref[rows, :]
+    degree = deg_ref[rows, :]
     for j in range(slots):
-        full_ids[j] = jnp.where(full_degree > j, nbr_ref[j, rows, :], all_rows)
-    counts = (near_count, degree - near_count, full_degree)
-    keys = sorted_tiles(jnp.stack([count * CHUNK + at for count in counts]), 2)
-    for i, order in enumerate((near_order, far_order)):
-        order[...] = keys[i] & (CHUNK - 1)
-    full_order[...] = keys[2] & (CHUNK // 2 - 1)
-    for i, classes in enumerate((near_class, far_class, full_class)):
-        classes[...] = keys[i] >> 10
+        full_ids[j] = jnp.where(degree > j, nbr_ref[j, rows, :], all_rows)
+    counts_ref[2] = degree
+
+
+def order_kernel(counts_ref, after_ref, *refs):
+    orders, classes = refs[:3], refs[3:]
+    at = lax.broadcasted_iota(jnp.int32, (8, LANES), 0) * LANES + lax.broadcasted_iota(
+        jnp.int32, (8, LANES), 1
+    )
+    keys = sorted_tiles(counts_ref[...] * CHUNK + at[None], 2)
+    for i in range(3):
+        orders[i][...] = keys[i] & ((CHUNK if i < 2 else CHUNK // 2) - 1)
+        classes[i][...] = keys[i] >> 10
 
 
 def constants_kernel(deg_ref, weight_ref, bias_ref, after_ref, scale_ref, weight_out, bias_out):
@@ -324,7 +328,6 @@
 
 IN_VMEM = pl.BlockSpec(memory_space=VMEM)
 ANYWHERE = pl.BlockSpec(memory_space=pl.ANY)
-IN_HBM = pl.BlockSpec(memory_space=pltpu.HBM)
 
 
 def local(node_feats, neighbours, degrees, hub_rows, weight, bias_terms):
@@ -349,7 +352,7 @@
     block = pallas(
         hub_pick_kernel,
         bf16(hubs // 2, 2 * chans),
-        [IN_VMEM, IN_HBM],
+        [IN_VMEM, ANYWHERE],
         [VMEM((chans, nodes), jnp.bfloat16), pltpu.SemaphoreType.DMA((4,))],
     )(hub_rows[None, :], node_feats)
     arrived = None
@@ -365,18 +368,23 @@
     arrived = stage(block, STAGES[0])
     deg_tiles = degrees.reshape(nodes // LANES, LANES)
     table, tile = i32(slots, 8, LANES), i32(8, LANES)
-    plan = pallas(
-        functools.partial(plan_kernel, frame_rows, frame_rows + hub_count),
-        (table, tile, tile) * 3,
+    *ids, counts = pallas(
+        functools.partial(slots_kernel, frame_rows, frame_rows + hub_count),
+        (table, table, table, i32(3, 8, LANES)),
         [IN_VMEM, IN_VMEM, ANYWHERE],
-        us=4.0,
+        us=1.0,
     )(neighbours.reshape(slots, nodes // LANES, LANES), deg_tiles, block)
-    plan = [a.reshape(-1) for a in plan]
-    near_plan, far_plan, full_plan = plan[:3], plan[3:6], plan[6:]
     other = lax.ppermute(node_feats, "feat", swap)
 
-    block = join(block, arrived, near_plan[1])
+    block = join(block, arrived, counts)
     arrived = stage(block, STAGES[1])
+    order = pallas(order_kernel, (tile,) * 6, [IN_VMEM, ANYWHERE], us=3.0)(counts, block)
+    near_plan, far_plan, full_plan = (
+        [a.reshape(-1) for a in (ids[i], order[i], order[3 + i])] for i in range(3)
+    )
+
+    block = join(block, arrived, order[0])
+    arrived = stage(block, STAGES[2])
     scale, by_out, bias = pallas(
         constants_kernel,
         (f32(half, LANES), bf16(2 * chans, 2 * chans), f32(LANES, LANES)),
@@ -389,11 +397,11 @@
     block = pallas(
         join_feat_kernel, bf16(2 * block.shape[0], 2 * chans), [IN_VMEM] * 2, us=0.5
     )(block, arrived)
-    arrived = stage(block, STAGES[2])
+    arrived = stage(block, STAGES[3])
     outer, inner = pallas(
         halves_kernel,
         (bf16(2 * chans, half),) * 2,
-        [IN_HBM, ANYWHERE, ANYWHERE],
+        [ANYWHERE] * 3,
         [pltpu.SemaphoreType.DMA((4,))],
         us=0.5,
     )(node_feats, other, block)
@@ -401,8 +409,6 @@
     outer_halo = lax.ppermute(
         outer, "slab", [(i, j) for i in range(slabs) for j in [i + 2 * (i & 1) - 1] if 0 <= j < slabs]
     )
-    block = join(block, arrived, outer)
-    arrived = stage(block, STAGES[3])
     frame = pallas(
         frame_kernel,
         f32(frame_rows + hub_count + 8, LANES),

time: 78.9 us -> 80.1 us (1.015)
  waiting for transfers between devices: 16.9 us -> 18.2 us
  starting transfers between devices: 27.3 us -> 26.3 us
    ppermute x9, waiting for transfers between devices: 11.2 us -> 1.79 us  [stage(): lax.ppermute(block, 'slab', [(i, i ^ bit) for i in range(slabs)])]
    ppermute x1, waiting for transfers between devices: 0.01 us -> 9.18 us  [local(): lax.ppermute(outer, 'slab', [(i, j) for i in range(slabs) for j in [i + 2...]
    ppermute x3, starting transfers between devices: 4.11 us -> 2.67 us  [local(): received.append(lax.ppermute(sent, 'feat', swap))]
    ppermute x3, waiting for transfers between devices: 2.51 us -> 3.71 us  [local(): received.append(lax.ppermute(sent, 'feat', swap))]
    unnamed x15 -> x17, local copies, waits for them, and re-layouts: 6.38 us -> 7.09 us
    pallas_call x3 -> x4, Pallas kernels: 4.3 us -> 4.32 us  [the longest x1 3.5 us: local(): pallas(order_kernel, (tile,) * 6, [IN_VMEM, ANYWHERE], us=3.0)]
  transfers between devices with their start and end apart: 16 -> 16, of which waited for: 4 -> 5; matrix products, arithmetic and copies ran while one was open for 1% -> 1% of each run, Pallas kernels for 29% -> 30%
where the time goes in v5:
time: 80.1 us; the launch traced here: 79.6 us
  Pallas kernels  27.8 us (35%)
  starting transfers between devices  26.3 us (33%)
  waiting for transfers between devices  18.2 us (23%)
  local copies, waits for them, and re-layouts  7.09 us (9%)
    ppermute x9, starting transfers between devices, stage(): lax.ppermute(block, 'slab', [(i, i ^ bit) for i in range(slabs)])  16.7 us
    pallas_call x3, Pallas kernels, layer(): pallas(functools.partial(layer_kernel, slots, first, start, len(near), ha...  12.4 us
    ppermute x1, waiting for transfers between devices, local(): lax.ppermute(outer, 'slab', [(i, j) for i in range(slabs) for j in [i + 2...  9.18 us
    pallas_call x2, Pallas kernels, near_sum(): pallas(functools.partial(near_kernel, slots, part, 2), f32(CHUNK, LANES),...  8.31 us
    unnamed x17, local copies, waits for them, and re-layouts  7.09 us
    ppermute x1, starting transfers between devices, local(): lax.ppermute(outer, 'slab', [(i, j) for i in range(slabs) for j in [i + 2...  4.8 us
    ppermute x3, waiting for transfers between devices, local(): received.append(lax.ppermute(sent, 'feat', swap))  3.71 us
    ppermute x1, waiting for transfers between devices, local(): arrived = lax.ppermute(block, 'feat', swap)  3.52 us
  transfers between devices with their start and end apart: 16, of which 5 were waited for; matrix products, arithmetic and copies ran while one was open for 1% of the time, Pallas kernels for 30%

profile of v5, /device:TPU:16, one launch (start us, length us, event | category | flops | bytes accessed | tf_op | source)
XLA Modules:
  0.0 79.6 jit_solution(9166223070463152429)
XLA Ops:
  0.0 1.3 %collective-permute-start.1 = (bf16[64,4096]{1,0:T(8,128)(2,1)}, bf16[64,4096]{1,0:T(8,128)(2,1)S(1)}, u32[]{:S(2)}, u32[]{:S(2)}) collective-permute-start(bf16[64,4096]{1,0:T(8,128)(2,1)} %x_ref.1), channel_id=1, source_target_pairs={{0,1},{1,0},{2,3},{3,2},{4,5},{5,4},{6,7},{7,6},{8,9},{9,8},{10,11... | collective-permute-start | bytes 1572872 | tf_op jit(solution)/shard_map/ppermute | solution.py:377
  1.3 0.0 copy-start
  1.3 1.1 %copy-done = bf16[64,4096]{1,0:T(8,128)(2,1)S(1)} copy-done((bf16[64,4096]{1,0:T(8,128)(2,1)S(1)}, bf16[64,4096]{1,0:T(8,128)(2,1)}, u32[]{:S(2)}) %copy-start) | copy-done | bytes 524312
  2.4 0.0 copy-start.5
  2.4 0.7 copy-done.5
  3.0 0.6 shard_map.64.after_ref.refs_0_
  3.6 7.3 %collective-permute-start = (bf16[16,128]{1,0:T(8,128)(2,1)S(1)}, bf16[16,128]{1,0:T(8,128)(2,1)S(1)}, u32[]{:S(2)}, u32[]{:S(2)}) collective-permute-start(bf16[16,128]{1,0:T(8,128)(2,1)S(1)} %shard_map.64.after_ref.refs_0_), channel_id=1, source_target_pairs={{0,64},{2,66},{4,68},{6,70},{8,72},{10,74},{12,76},{14,78},{16,80}... | collective-permute-start | bytes 12296 | tf_op jit(solution)/shard_map/ppermute | solution.py:361
  10.9 1.0 %copy.8 = s32[2,8,32,128]{3,2,1,0:T(8,128)S(1)} copy(s32[2,8,32,128]{3,1,2,0:T(8,128)} %bitcast.34) | data formatting | bytes 524288
  11.9 0.0 copy-start.2
  11.9 0.7 copy-done.2
  12.6 0.1 shard_map.65
  12.7 0.0 collective-permute-done.refs_1_
  12.7 0.7 collective-permute-start.2
  13.5 3.5 %shard_map.67 = (s32[8,128]{1,0:T(8,128)S(1)}, s32[8,128]{1,0:T(8,128)S(1)}, s32[8,128]{1,0:T(8,128)S(1)}, s32[8,128]{1,0:T(8,128)S(1)}, s32[8,128]{1,0:T(8,128)S(1)}, /*index=5*/s32[8,128]{1,0:T(8,128)S(1)}) custom-call(s32[3,8,128]{2,1,0:T(8,128)S(1)} %get-tuple-element.27.refs_2_.counts_ref, bf16[32,128]{1,0:T(8,128)(2,1)S(1)} %shard_map.66.after_ref.refs_0_), custom_call_target="tpu_custom_call" | custom-call | bytes 9000000 | tf_op jit(solution)/shard_map/pallas_call | solution.py:381
  17.0 1.0 %collective-permute-done.2.refs_1_ = bf16[32,128]{1,0:T(8,128)(2,1)S(1)} collective-permute-done((bf16[32,128]{1,0:T(8,128)(2,1)S(1)}, bf16[32,128]{1,0:T(8,128)(2,1)S(1)}, u32[]{:S(2)}, u32[]{:S(2)}) %collective-permute-start.2) | collective-permute-done | bytes 8224 | tf_op jit(solution)/shard_map/ppermute | solution.py:361
  18.0 3.0 %collective-permute-start.5 = (bf16[64,128]{1,0:T(8,128)(2,1)S(1)}, bf16[64,128]{1,0:T(8,128)(2,1)S(1)}, u32[]{:S(2)}, u32[]{:S(2)}) collective-permute-start(bf16[64,128]{1,0:T(8,128)(2,1)S(1)} %shard_map.68.after_ref.refs_0_), channel_id=1, source_target_pairs={{0,48},{2,50},{4,52},{6,54},{8,56},{10,58},{12,60},{14,62},{16,32}... | collective-permute-start | bytes 49160 | tf_op jit(solution)/shard_map/ppermute | solution.py:361
  21.0 0.0 collective-permute-start.4
  21.0 1.4 %collective-permute-start.3 = (bf16[64,128]{1,0:T(8,128)(2,1)S(1)}, bf16[64,128]{1,0:T(8,128)(2,1)S(1)}, u32[]{:S(2)}, u32[]{:S(2)}) collective-permute-start(bf16[64,128]{1,0:T(8,128)(2,1)S(1)} %shard_map.68.after_ref.refs_0_), channel_id=1, source_target_pairs={{0,16},{2,18},{4,20},{6,22},{8,24},{10,26},{12,28},{14,30},{16,0},... | collective-permute-start | bytes 49160 | tf_op jit(solution)/shard_map/ppermute | solution.py:361
  22.4 0.0 copy-start.3
  22.4 0.7 copy-done.3
  23.1 0.0 copy-start.4
  23.1 0.8 copy-done.4
  23.9 0.0 copy-start.7
  23.9 0.7 copy-done.7
  24.5 0.4 shard_map.69
  24.9 0.0 collective-permute-done.5.refs_3_
  24.9 0.7 collective-permute-done.4.refs_2_
  25.7 0.0 collective-permute-done.3.refs_1_
  25.7 0.8 %collective-permute-start.6 = (bf16[256,128]{1,0:T(8,128)(2,1)S(1)}, bf16[256,128]{1,0:T(8,128)(2,1)S(1)}, u32[]{:S(2)}, u32[]{:S(2)}) collective-permute-start(bf16[256,128]{1,0:T(8,128)(2,1)S(1)} %shard_map.70.mine_ref), channel_id=1, source_target_pairs={{0,1},{1,0},{2,3},{3,2},{4,5},{5,4},{6,7},{7,6},{8,9},{9,8},{10,11... | collective-permute-start | bytes 196616 | tf_op jit(solution)/shard_map/ppermute | solution.py:396
  26.5 3.5 %collective-permute-done.6.other_ref = bf16[256,128]{1,0:T(8,128)(2,1)S(1)} collective-permute-done((bf16[256,128]{1,0:T(8,128)(2,1)S(1)}, bf16[256,128]{1,0:T(8,128)(2,1)S(1)}, u32[]{:S(2)}, u32[]{:S(2)}) %collective-permute-start.6) | collective-permute-done | bytes 65568 | tf_op jit(solution)/shard_map/ppermute | solution.py:396
  30.0 0.1 shard_map.71.after_ref.refs_0_
  30.1 0.0 collective-permute-done.1.other_ref
  30.1 0.0 copy-start.1
  30.2 1.0 %copy-done.1 = bf16[64,4096]{1,0:T(8,128)(2,1)S(1)} copy-done((bf16[64,4096]{1,0:T(8,128)(2,1)S(1)}, bf16[64,4096]{1,0:T(8,128)(2,1)}, u32[]{:S(2)}) %copy-start.1) | copy-done | bytes 524312
  31.2 0.1 shard_map.72
  31.3 4.8 %collective-permute-start.7 = (bf16[128,2048]{1,0:T(8,128)(2,1)S(1)}, bf16[128,2048]{1,0:T(8,128)(2,1)S(1)}, u32[]{:S(2)}, u32[]{:S(2)}) collective-permute-start(bf16[128,2048]{1,0:T(8,128)(2,1)S(1)} %get-tuple-element.32.outer_ref), channel_id=1, source_target_pairs={{2,4},{4,2},{6,8},{8,6},{10,12},{12,10},{14,16},{16,14},{18,20},{2... | collective-permute-start | bytes 1572872 | tf_op jit(solution)/shard_map/ppermute | solution.py:409
  36.1 0.1 collective-permute-start.8
  36.2 0.3 collective-permute-start.11
  36.5 2.0 %collective-permute-start.10 = (bf16[512,128]{1,0:T(8,128)(2,1)S(1)}, bf16[512,128]{1,0:T(8,128)(2,1)S(1)}, u32[]{:S(2)}, u32[]{:S(2)}) collective-permute-start(bf16[512,128]{1,0:T(8,128)(2,1)S(1)} %shard_map.71.after_ref.refs_0_), channel_id=1, source_target_pairs={{0,8},{2,10},{4,12},{6,14},{8,0},{10,2},{12,4},{14,6},{16,24},{18,... | collective-permute-start | bytes 393224 | tf_op jit(solution)/shard_map/ppermute | solution.py:361
  38.5 1.9 %collective-permute-start.9 = (bf16[512,128]{1,0:T(8,128)(2,1)S(1)}, bf16[512,128]{1,0:T(8,128)(2,1)S(1)}, u32[]{:S(2)}, u32[]{:S(2)}) collective-permute-start(bf16[512,128]{1,0:T(8,128)(2,1)S(1)} %shard_map.71.after_ref.refs_0_), channel_id=1, source_target_pairs={{0,4},{2,6},{4,0},{6,2},{8,12},{10,14},{12,8},{14,10},{16,20},{18,... | collective-permute-start | bytes 393224 | tf_op jit(solution)/shard_map/ppermute | solution.py:361
  40.4 9.2 %collective-permute-done.7.outer_halo_ref = bf16[128,2048]{1,0:T(8,128)(2,1)S(1)} collective-permute-done((bf16[128,2048]{1,0:T(8,128)(2,1)S(1)}, bf16[128,2048]{1,0:T(8,128)(2,1)S(1)}, u32[]{:S(2)}, u32[]{:S(2)}) %collective-permute-start.7) | collective-permute-done | bytes 524320 | tf_op jit(solution)/shard_map/ppermute | solution.py:409
  49.6 0.0 collective-permute-done.8.inner_halo_ref
  49.6 1.2 %shard_map.73.frame_ref.frame_in = f32[12296,128]{1,0:T(8,128)S(1)} custom-call(bf16[128,2048]{1,0:T(8,128)(2,1)S(1)} %collective-permute-done.7.outer_halo_ref, bf16[128,2048]{1,0:T(8,128)(2,1)S(1)} %get-tuple-element.32.outer_ref, bf16[128,2048]{1,0:T(8,128)(2,1)S(1)} %get-tuple-element.33.inner_ref, ...), custom_call_target="tpu_custom_call" | custom-call | bytes 6000000 | tf_op jit(solution)/shard_map/pallas_call | solution.py:412
  50.8 4.0 %shard_map.74.refs_4_.refs_0_ = f32[1024,128]{1,0:T(8,128)S(1)} custom-call(s32[16384]{0:T(1024)S(1)} %bitcast.17, s32[1024]{0:T(1024)S(1)} %bitcast.22, s32[1024]{0:T(1024)S(1)} %bitcast.28, f32[12296,128]{1,0:T(8,128)S(1)} %shard_map.73.frame_ref.frame_in, bf16[512,128]{1,0:T(8,128)(2,1)S(1)} %shard_map.71.after_ref.refs_0_), custom_call_target="tpu_custom_call" | custom-call | bytes 12000000 | tf_op jit(solution)/shard_map/pallas_call | solution.py:428
  54.9 0.0 collective-permute-done.11.refs_3_
  54.9 0.0 collective-permute-done.10.refs_2_
  54.9 0.0 collective-permute-done.9.refs_1_
  54.9 0.1 collective-permute-start.12
  55.0 4.3 %shard_map.76.after_ref.refs_1_ = f32[1024,128]{1,0:T(8,128)S(1)} custom-call(s32[16384]{0:T(1024)S(1)} %bitcast.18, s32[1024]{0:T(1024)S(1)} %bitcast.23, s32[1024]{0:T(1024)S(1)} %bitcast.29, f32[12296,128]{1,0:T(8,128)S(1)} %shard_map.73.frame_ref.frame_in, bf16[2048,128]{1,0:T(8,128)(2,1)S(1)} %shard_map.75.after_ref.near_ref), custom_call_target="tpu_custom_call" | custom-call | bytes 12000000 | tf_op jit(solution)/shard_map/pallas_call | solution.py:428
  59.3 0.0 copy-start.6
  59.3 0.0 collective-permute-done.12.far_ref
  59.4 0.1 shard_map.77.frame_ref
  59.5 0.5 copy-done.6
  60.0 3.1 %shard_map.78 = (bf16[64,1024]{1,0:T(8,128)(2,1)S(1)}, bf16[128,1024]{1,0:T(8,128)(2,1)S(1)}) custom-call(s32[16384]{0:T(1024)S(1)} %bitcast.19, s32[1024]{0:T(1024)S(1)} %bitcast.30, s32[1024]{0:T(1024)S(1)} %bitcast.31, f32[12296,128]{1,0:T(8,128)S(1)} %shard_map.77.frame_ref, f32[2048,128]{1,0:T(8,128)S(1)} %get-tuple-element.31.refs_4_.scale_ref, ...), custom_call_target="tpu_custom_call" | custom-call | bytes 9000000 | tf_op jit(solution)/shard_map/pallas_call | solution.py:449
  63.1 0.8 collective-permute-start.13
  63.9 4.5 %shard_map.79 = (bf16[64,512]{1,0:T(8,128)(2,1)S(1)}, bf16[128,512]{1,0:T(8,128)(2,1)S(1)}) custom-call(s32[16384]{0:T(1024)S(1)} %bitcast.15, s32[1024]{0:T(1024)S(1)} %bitcast.24, s32[1024]{0:T(1024)S(1)} %bitcast.26, f32[12296,128]{1,0:T(8,128)S(1)} %shard_map.77.frame_ref, f32[2048,128]{1,0:T(8,128)S(1)} %get-tuple-element.31.refs_4_.scale_ref, ...), custom_call_target="tpu_custom_call" | custom-call | bytes 12000000 | tf_op jit(solution)/shard_map/pallas_call | solution.py:449
  68.5 1.2 %collective-permute-start.14 = (bf16[128,512]{1,0:T(8,128)(2,1)S(1)}, bf16[128,512]{1,0:T(8,128)(2,1)S(1)}, u32[]{:S(2)}, u32[]{:S(2)}) collective-permute-start(bf16[128,512]{1,0:T(8,128)(2,1)S(1)} %get-tuple-element.45), channel_id=1, source_target_pairs={{0,1},{1,0},{2,3},{3,2},{4,5},{5,4},{6,7},{7,6},{8,9},{9,8},{10,11... | collective-permute-start | bytes 393224 | tf_op jit(solution)/shard_map/ppermute | solution.py:465
  69.7 4.7 %shard_map.80 = (bf16[64,512]{1,0:T(8,128)(2,1)S(1)}, bf16[64,512]{1,0:T(8,128)(2,1)S(1)}) custom-call(s32[16384]{0:T(1024)S(1)} %bitcast.16, s32[1024]{0:T(1024)S(1)} %bitcast.25, s32[1024]{0:T(1024)S(1)} %bitcast.27, f32[12296,128]{1,0:T(8,128)S(1)} %shard_map.77.frame_ref, f32[2048,128]{1,0:T(8,128)S(1)} %get-tuple-element.31.refs_4_.scale_ref, ...), custom_call_target="tpu_custom_call" | custom-call | bytes 12000000 | tf_op jit(solution)/shard_map/pallas_call | solution.py:449
  74.4 0.6 collective-permute-start.15
  75.1 3.7 %collective-permute-done.15.refs_5_ = bf16[64,512]{1,0:T(8,128)(2,1)S(1)} collective-permute-done((bf16[64,512]{1,0:T(8,128)(2,1)S(1)}, bf16[64,512]{1,0:T(8,128)(2,1)S(1)}, u32[]{:S(2)}, u32[]{:S(2)}) %collective-permute-start.15) | collective-permute-done | bytes 65568 | tf_op jit(solution)/shard_map/ppermute | solution.py:465
  78.8 0.0 collective-permute-done.14.refs_4_
  78.8 0.0 collective-permute-done.13.refs_3_
  78.8 0.8 %shard_map.81 = bf16[64,4096]{1,0:T(8,128)(2,1)} custom-call(bf16[64,1024]{1,0:T(8,128)(2,1)S(1)} %get-tuple-element.38.after_ref.refs_0_, bf16[64,512]{1,0:T(8,128)(2,1)S(1)} %get-tuple-element.42.after_ref.refs_1_, bf16[64,512]{1,0:T(8,128)(2,1)S(1)} %get-tuple-element.43.refs_2_, bf16[128,1024]{1,0:T(8,128)(2,1)S(1)} %collective-permute-done.13.refs_3_, ...), custom_call_target="tpu_custom_call" | custom-call | bytes 1500000 | tf_op jit(solution)/shard_map/pallas_call | solution.py:467
  (4 shorter events, 0.0 us)
Async XLA Ops:
  0.0 30.1 %collective-permute-start.1 = (bf16[64,4096]{1,0:T(8,128)(2,1)}, bf16[64,4096]{1,0:T(8,128)(2,1)S(1)}, u32[]{:S(2)}, u32[]{:S(2)}) collective-permute-start(bf16[64,4096]{1,0:T(8,128)(2,1)} %x_ref.1), channel_id=1, source_target_pairs={{0,1},{1,0},{2,3},{3,2},{4,5},{5,4},{6,7},{7,6},{8,9},{9,8},{10,11... | collective-permute-start | bytes 1572872 | tf_op jit(solution)/shard_map/ppermute | solution.py:377
  1.3 1.1 %copy-start = (bf16[64,4096]{1,0:T(8,128)(2,1)S(1)}, bf16[64,4096]{1,0:T(8,128)(2,1)}, u32[]{:S(2)}) copy-start(bf16[64,4096]{1,0:T(8,128)(2,1)} %x_ref.1) | copy-start | bytes 1572868
  2.4 0.7 copy-start.5
  3.6 9.1 %collective-permute-start = (bf16[16,128]{1,0:T(8,128)(2,1)S(1)}, bf16[16,128]{1,0:T(8,128)(2,1)S(1)}, u32[]{:S(2)}, u32[]{:S(2)}) collective-permute-start(bf16[16,128]{1,0:T(8,128)(2,1)S(1)} %shard_map.64.after_ref.refs_0_), channel_id=1, source_target_pairs={{0,64},{2,66},{4,68},{6,70},{8,72},{10,74},{12,76},{14,78},{16,80}... | collective-permute-start | bytes 12296 | tf_op jit(solution)/shard_map/ppermute | solution.py:361
  11.9 0.7 copy-start.2
  12.7 5.2 %collective-permute-start.2 = (bf16[32,128]{1,0:T(8,128)(2,1)S(1)}, bf16[32,128]{1,0:T(8,128)(2,1)S(1)}, u32[]{:S(2)}, u32[]{:S(2)}) collective-permute-start(bf16[32,128]{1,0:T(8,128)(2,1)S(1)} %shard_map.66.after_ref.refs_0_), channel_id=1, source_target_pairs={{0,128},{2,130},{4,132},{6,134},{8,136},{10,138},{12,140},{14,142}... | collective-permute-start | bytes 24584 | tf_op jit(solution)/shard_map/ppermute | solution.py:361
  18.0 6.9 %collective-permute-start.5 = (bf16[64,128]{1,0:T(8,128)(2,1)S(1)}, bf16[64,128]{1,0:T(8,128)(2,1)S(1)}, u32[]{:S(2)}, u32[]{:S(2)}) collective-permute-start(bf16[64,128]{1,0:T(8,128)(2,1)S(1)} %shard_map.68.after_ref.refs_0_), channel_id=1, source_target_pairs={{0,48},{2,50},{4,52},{6,54},{8,56},{10,58},{12,60},{14,62},{16,32}... | collective-permute-start | bytes 49160 | tf_op jit(solution)/shard_map/ppermute | solution.py:361
  21.0 4.6 %collective-permute-start.4 = (bf16[64,128]{1,0:T(8,128)(2,1)S(1)}, bf16[64,128]{1,0:T(8,128)(2,1)S(1)}, u32[]{:S(2)}, u32[]{:S(2)}) collective-permute-start(bf16[64,128]{1,0:T(8,128)(2,1)S(1)} %shard_map.68.after_ref.refs_0_), channel_id=1, source_target_pairs={{0,32},{2,34},{4,36},{6,38},{8,40},{10,42},{12,44},{14,46},{16,48}... | collective-permute-start | bytes 49160 | tf_op jit(solution)/shard_map/ppermute | solution.py:361
  21.0 4.6 %collective-permute-start.3 = (bf16[64,128]{1,0:T(8,128)(2,1)S(1)}, bf16[64,128]{1,0:T(8,128)(2,1)S(1)}, u32[]{:S(2)}, u32[]{:S(2)}) collective-permute-start(bf16[64,128]{1,0:T(8,128)(2,1)S(1)} %shard_map.68.after_ref.refs_0_), channel_id=1, source_target_pairs={{0,16},{2,18},{4,20},{6,22},{8,24},{10,26},{12,28},{14,30},{16,0},... | collective-permute-start | bytes 49160 | tf_op jit(solution)/shard_map/ppermute | solution.py:361
  22.4 0.7 copy-start.3
  23.1 0.8 copy-start.4
  23.9 0.7 copy-start.7
  25.7 4.4 %collective-permute-start.6 = (bf16[256,128]{1,0:T(8,128)(2,1)S(1)}, bf16[256,128]{1,0:T(8,128)(2,1)S(1)}, u32[]{:S(2)}, u32[]{:S(2)}) collective-permute-start(bf16[256,128]{1,0:T(8,128)(2,1)S(1)} %shard_map.70.mine_ref), channel_id=1, source_target_pairs={{0,1},{1,0},{2,3},{3,2},{4,5},{5,4},{6,7},{7,6},{8,9},{9,8},{10,11... | collective-permute-start | bytes 196616 | tf_op jit(solution)/shard_map/ppermute | solution.py:396
  30.1 1.0 %copy-start.1 = (bf16[64,4096]{1,0:T(8,128)(2,1)S(1)}, bf16[64,4096]{1,0:T(8,128)(2,1)}, u32[]{:S(2)}) copy-start(bf16[64,4096]{1,0:T(8,128)(2,1)} %x_ref.1) | copy-start | bytes 1572868
  31.3 18.3 %collective-permute-start.7 = (bf16[128,2048]{1,0:T(8,128)(2,1)S(1)}, bf16[128,2048]{1,0:T(8,128)(2,1)S(1)}, u32[]{:S(2)}, u32[]{:S(2)}) collective-permute-start(bf16[128,2048]{1,0:T(8,128)(2,1)S(1)} %get-tuple-element.32.outer_ref), channel_id=1, source_target_pairs={{2,4},{4,2},{6,8},{8,6},{10,12},{12,10},{14,16},{16,14},{18,20},{2... | collective-permute-start | bytes 1572872 | tf_op jit(solution)/shard_map/ppermute | solution.py:409
  36.1 13.5 %collective-permute-start.8 = (bf16[128,2048]{1,0:T(8,128)(2,1)S(1)}, bf16[128,2048]{1,0:T(8,128)(2,1)S(1)}, u32[]{:S(2)}, u32[]{:S(2)}) collective-permute-start(bf16[128,2048]{1,0:T(8,128)(2,1)S(1)} %get-tuple-element.33.inner_ref), channel_id=1, source_target_pairs={{0,2},{2,0},{4,6},{6,4},{8,10},{10,8},{12,14},{14,12},{16,18},{18,... | collective-permute-start | bytes 1572872 | tf_op jit(solution)/shard_map/ppermute | solution.py:408
  36.2 18.6 %collective-permute-start.11 = (bf16[512,128]{1,0:T(8,128)(2,1)S(1)}, bf16[512,128]{1,0:T(8,128)(2,1)S(1)}, u32[]{:S(2)}, u32[]{:S(2)}) collective-permute-start(bf16[512,128]{1,0:T(8,128)(2,1)S(1)} %shard_map.71.after_ref.refs_0_), channel_id=1, source_target_pairs={{0,12},{2,14},{4,8},{6,10},{8,4},{10,6},{12,0},{14,2},{16,28},{18,... | collective-permute-start | bytes 393224 | tf_op jit(solution)/shard_map/ppermute | solution.py:361
  36.5 18.4 %collective-permute-start.10 = (bf16[512,128]{1,0:T(8,128)(2,1)S(1)}, bf16[512,128]{1,0:T(8,128)(2,1)S(1)}, u32[]{:S(2)}, u32[]{:S(2)}) collective-permute-start(bf16[512,128]{1,0:T(8,128)(2,1)S(1)} %shard_map.71.after_ref.refs_0_), channel_id=1, source_target_pairs={{0,8},{2,10},{4,12},{6,14},{8,0},{10,2},{12,4},{14,6},{16,24},{18,... | collective-permute-start | bytes 393224 | tf_op jit(solution)/shard_map/ppermute | solution.py:361
  38.5 16.4 %collective-permute-start.9 = (bf16[512,128]{1,0:T(8,128)(2,1)S(1)}, bf16[512,128]{1,0:T(8,128)(2,1)S(1)}, u32[]{:S(2)}, u32[]{:S(2)}) collective-permute-start(bf16[512,128]{1,0:T(8,128)(2,1)S(1)} %shard_map.71.after_ref.refs_0_), channel_id=1, source_target_pairs={{0,4},{2,6},{4,0},{6,2},{8,12},{10,14},{12,8},{14,10},{16,20},{18,... | collective-permute-start | bytes 393224 | tf_op jit(solution)/shard_map/ppermute | solution.py:361
  54.9 4.4 %collective-permute-start.12 = (bf16[2048,128]{1,0:T(8,128)(2,1)S(1)}, bf16[2048,128]{1,0:T(8,128)(2,1)S(1)}, u32[]{:S(2)}, u32[]{:S(2)}) collective-permute-start(bf16[2048,128]{1,0:T(8,128)(2,1)S(1)} %shard_map.75.after_ref.near_ref), channel_id=1, source_target_pairs={{0,2},{2,0},{4,6},{6,4},{8,10},{10,8},{12,14},{14,12},{16,18},{18,... | collective-permute-start | bytes 1572872 | tf_op jit(solution)/shard_map/ppermute | solution.py:361
  59.3 0.7 copy-start.6
  63.1 15.7 %collective-permute-start.13 = (bf16[128,1024]{1,0:T(8,128)(2,1)S(1)}, bf16[128,1024]{1,0:T(8,128)(2,1)S(1)}, u32[]{:S(2)}, u32[]{:S(2)}) collective-permute-start(bf16[128,1024]{1,0:T(8,128)(2,1)S(1)} %get-tuple-element.44), channel_id=1, source_target_pairs={{0,1},{1,0},{2,3},{3,2},{4,5},{5,4},{6,7},{7,6},{8,9},{9,8},{10,11... | collective-permute-start | bytes 786440 | tf_op jit(solution)/shard_map/ppermute | solution.py:465
  68.5 10.3 %collective-permute-start.14 = (bf16[128,512]{1,0:T(8,128)(2,1)S(1)}, bf16[128,512]{1,0:T(8,128)(2,1)S(1)}, u32[]{:S(2)}, u32[]{:S(2)}) collective-permute-start(bf16[128,512]{1,0:T(8,128)(2,1)S(1)} %get-tuple-element.45), channel_id=1, source_target_pairs={{0,1},{1,0},{2,3},{3,2},{4,5},{5,4},{6,7},{7,6},{8,9},{9,8},{10,11... | collective-permute-start | bytes 393224 | tf_op jit(solution)/shard_map/ppermute | solution.py:465
  74.4 4.4 %collective-permute-start.15 = (bf16[64,512]{1,0:T(8,128)(2,1)S(1)}, bf16[64,512]{1,0:T(8,128)(2,1)S(1)}, u32[]{:S(2)}, u32[]{:S(2)}) collective-permute-start(bf16[64,512]{1,0:T(8,128)(2,1)S(1)} %get-tuple-element.46), channel_id=1, source_target_pairs={{0,1},{1,0},{2,3},{3,2},{4,5},{5,4},{6,7},{7,6},{8,9},{9,8},{10,11... | collective-permute-start | bytes 196616 | tf_op jit(solution)/shard_map/ppermute | solution.py:465

commit v6 on v5

--- a/solution.py
+++ b/solution.py
@@ -45,7 +45,7 @@
         out_ref[i * rows : (i + 1) * rows] = ref[...]
 
 
-def join_feat_kernel(mine_ref, other_ref, out_ref):
+def join_feat_kernel(mine_ref, other_ref, after_ref, out_ref):
     first = lax.axis_index("feat") == 0
     lane = lax.broadcasted_iota(jnp.int32, (16, LANES), 1)
     for i in range(mine_ref.shape[0] // 16):
@@ -384,20 +384,6 @@
     )
 
     block = join(block, arrived, order[0])
-    arrived = stage(block, STAGES[2])
-    scale, by_out, bias = pallas(
-        constants_kernel,
-        (f32(half, LANES), bf16(2 * chans, 2 * chans), f32(LANES, LANES)),
-        [IN_VMEM] * 3 + [ANYWHERE],
-        us=1.0,
-    )(deg_tiles, weight, bias_terms[None, :], block)
-
-    block = join(block, arrived, scale)
-    arrived = lax.ppermute(block, "feat", swap)
-    block = pallas(
-        join_feat_kernel, bf16(2 * block.shape[0], 2 * chans), [IN_VMEM] * 2, us=0.5
-    )(block, arrived)
-    arrived = stage(block, STAGES[3])
     outer, inner = pallas(
         halves_kernel,
         (bf16(2 * chans, half),) * 2,
@@ -409,6 +395,20 @@
     outer_halo = lax.ppermute(
         outer, "slab", [(i, j) for i in range(slabs) for j in [i + 2 * (i & 1) - 1] if 0 <= j < slabs]
     )
+    arrived = stage(block, STAGES[2])
+
+    block = join(block, arrived, outer)
+    arrived = lax.ppermute(block, "feat", swap)
+    scale, by_out, bias = pallas(
+        constants_kernel,
+        (f32(half, LANES), bf16(2 * chans, 2 * chans), f32(LANES, LANES)),
+        [IN_VMEM] * 3 + [ANYWHERE],
+        us=1.0,
+    )(deg_tiles, weight, bias_terms[None, :], block)
+    block = pallas(
+        join_feat_kernel, bf16(2 * block.shape[0], 2 * chans), [IN_VMEM] * 2 + [ANYWHERE], us=0.5
+    )(block, arrived, scale)
+    arrived = stage(block, STAGES[3])
     frame = pallas(
         frame_kernel,
         f32(frame_rows + hub_count + 8, LANES),

time: 80.1 us -> 74.5 us (0.930)
  waiting for transfers between devices: 18.2 us -> 7.3 us
  starting transfers between devices: 26.3 us -> 31.5 us
    ppermute x1, waiting for transfers between devices: 9.18 us -> 0.01 us  [local(): lax.ppermute(outer, 'slab', [(i, j) for i in range(slabs) for j in [i + 2...]
    ppermute x1, starting transfers between devices: 4.8 us -> 9.79 us  [local(): lax.ppermute(outer, 'slab', [(i, j) for i in range(slabs) for j in [i + 2...]
    ppermute x1, waiting for transfers between devices: 3.52 us -> 1.01 us  [local(): arrived = lax.ppermute(block, 'feat', swap)]
    ppermute x9, waiting for transfers between devices: 1.79 us -> 2.75 us  [stage(): lax.ppermute(block, 'slab', [(i, i ^ bit) for i in range(slabs)])]
  transfers between devices with their start and end apart: 16 -> 16, of which waited for: 5 -> 5; matrix products, arithmetic and copies ran while one was open for 1% -> 1% of each run, Pallas kernels for 30% -> 32%
where the time goes in v6:
time: 74.5 us; the launch traced here: 73.9 us
  starting transfers between devices  31.5 us (42%)
  Pallas kernels  27.8 us (37%)
  waiting for transfers between devices  7.3 us (10%)
  local copies, waits for them, and re-layouts  7.1 us (10%)
    ppermute x9, starting transfers between devices, stage(): lax.ppermute(block, 'slab', [(i, i ^ bit) for i in range(slabs)])  16.7 us
    pallas_call x3, Pallas kernels, layer(): pallas(functools.partial(layer_kernel, slots, first, start, len(near), ha...  12.2 us
    ppermute x1, starting transfers between devices, local(): lax.ppermute(outer, 'slab', [(i, j) for i in range(slabs) for j in [i + 2...  9.79 us
    pallas_call x2, Pallas kernels, near_sum(): pallas(functools.partial(near_kernel, slots, part, 2), f32(CHUNK, LANES),...  8.48 us
    unnamed x17, local copies, waits for them, and re-layouts  7.1 us
    ppermute x3, waiting for transfers between devices, local(): received.append(lax.ppermute(sent, 'feat', swap))  3.53 us
    pallas_call x1, Pallas kernels, local(): pallas(order_kernel, (tile,) * 6, [IN_VMEM, ANYWHERE], us=3.0)  3.5 us
    ppermute x3, starting transfers between devices, local(): received.append(lax.ppermute(sent, 'feat', swap))  2.89 us
  transfers between devices with their start and end apart: 16, of which 5 were waited for; matrix products, arithmetic and copies ran while one was open for 1% of the time, Pallas kernels for 32%

profile of v6, /device:TPU:16, one launch (start us, length us, event | category | flops | bytes accessed | tf_op | source)
XLA Modules:
  0.0 73.9 jit_solution(10965456703959545771)
XLA Ops:
  0.0 1.3 %collective-permute-start.1 = (bf16[64,4096]{1,0:T(8,128)(2,1)}, bf16[64,4096]{1,0:T(8,128)(2,1)S(1)}, u32[]{:S(2)}, u32[]{:S(2)}) collective-permute-start(bf16[64,4096]{1,0:T(8,128)(2,1)} %x_ref.1), channel_id=1, source_target_pairs={{0,1},{1,0},{2,3},{3,2},{4,5},{5,4},{6,7},{7,6},{8,9},{9,8},{10,11... | collective-permute-start | bytes 1572872 | tf_op jit(solution)/shard_map/ppermute | solution.py:377
  1.3 0.0 copy-start
  1.3 1.1 %copy-done = bf16[64,4096]{1,0:T(8,128)(2,1)S(1)} copy-done((bf16[64,4096]{1,0:T(8,128)(2,1)S(1)}, bf16[64,4096]{1,0:T(8,128)(2,1)}, u32[]{:S(2)}) %copy-start) | copy-done | bytes 524312
  2.4 0.0 copy-start.5
  2.4 0.7 copy-done.5
  3.0 0.6 shard_map.64.after_ref.refs_0_
  3.6 7.3 %collective-permute-start = (bf16[16,128]{1,0:T(8,128)(2,1)S(1)}, bf16[16,128]{1,0:T(8,128)(2,1)S(1)}, u32[]{:S(2)}, u32[]{:S(2)}) collective-permute-start(bf16[16,128]{1,0:T(8,128)(2,1)S(1)} %shard_map.64.after_ref.refs_0_), channel_id=1, source_target_pairs={{0,64},{2,66},{4,68},{6,70},{8,72},{10,74},{12,76},{14,78},{16,80}... | collective-permute-start | bytes 12296 | tf_op jit(solution)/shard_map/ppermute | solution.py:361
  10.9 1.0 %copy.8 = s32[2,8,32,128]{3,2,1,0:T(8,128)S(1)} copy(s32[2,8,32,128]{3,1,2,0:T(8,128)} %bitcast.34) | data formatting | bytes 524288
  11.9 0.0 copy-start.2
  11.9 0.7 copy-done.2
  12.6 0.1 shard_map.65
  12.7 0.0 collective-permute-done.refs_1_
  12.7 0.7 collective-permute-start.2
  13.5 3.5 %shard_map.67 = (s32[8,128]{1,0:T(8,128)S(1)}, s32[8,128]{1,0:T(8,128)S(1)}, s32[8,128]{1,0:T(8,128)S(1)}, s32[8,128]{1,0:T(8,128)S(1)}, s32[8,128]{1,0:T(8,128)S(1)}, /*index=5*/s32[8,128]{1,0:T(8,128)S(1)}) custom-call(s32[3,8,128]{2,1,0:T(8,128)S(1)} %get-tuple-element.27.refs_2_.counts_ref, bf16[32,128]{1,0:T(8,128)(2,1)S(1)} %shard_map.66.after_ref.refs_0_), custom_call_target="tpu_custom_call" | custom-call | bytes 9000000 | tf_op jit(solution)/shard_map/pallas_call | solution.py:381
  17.0 1.0 %collective-permute-done.2.refs_1_ = bf16[32,128]{1,0:T(8,128)(2,1)S(1)} collective-permute-done((bf16[32,128]{1,0:T(8,128)(2,1)S(1)}, bf16[32,128]{1,0:T(8,128)(2,1)S(1)}, u32[]{:S(2)}, u32[]{:S(2)}) %collective-permute-start.2) | collective-permute-done | bytes 8224 | tf_op jit(solution)/shard_map/ppermute | solution.py:361
  18.0 0.0 collective-permute-done.1.other_ref
  18.0 0.0 copy-start.1
  18.0 1.0 %copy-done.1 = bf16[64,4096]{1,0:T(8,128)(2,1)S(1)} copy-done((bf16[64,4096]{1,0:T(8,128)(2,1)S(1)}, bf16[64,4096]{1,0:T(8,128)(2,1)}, u32[]{:S(2)}) %copy-start.1) | copy-done | bytes 524312
  19.0 0.1 shard_map.69
  19.2 0.1 collective-permute-start.4
  19.3 9.8 %collective-permute-start.3 = (bf16[128,2048]{1,0:T(8,128)(2,1)S(1)}, bf16[128,2048]{1,0:T(8,128)(2,1)S(1)}, u32[]{:S(2)}, u32[]{:S(2)}) collective-permute-start(bf16[128,2048]{1,0:T(8,128)(2,1)S(1)} %get-tuple-element.31.refs_4_.outer_ref), channel_id=1, source_target_pairs={{2,4},{4,2},{6,8},{8,6},{10,12},{12,10},{14,16},{16,14},{18,20},{2... | collective-permute-start | bytes 1572872 | tf_op jit(solution)/shard_map/ppermute | solution.py:395
  29.1 0.1 collective-permute-start.7
  29.2 0.1 collective-permute-start.6
  29.3 4.3 %collective-permute-start.5 = (bf16[64,128]{1,0:T(8,128)(2,1)S(1)}, bf16[64,128]{1,0:T(8,128)(2,1)S(1)}, u32[]{:S(2)}, u32[]{:S(2)}) collective-permute-start(bf16[64,128]{1,0:T(8,128)(2,1)S(1)} %shard_map.68.after_ref.refs_0_), channel_id=1, source_target_pairs={{0,16},{2,18},{4,20},{6,22},{8,24},{10,26},{12,28},{14,30},{16,0},... | collective-permute-start | bytes 49160 | tf_op jit(solution)/shard_map/ppermute | solution.py:361
  33.5 1.1 %collective-permute-done.7.refs_3_ = bf16[64,128]{1,0:T(8,128)(2,1)S(1)} collective-permute-done((bf16[64,128]{1,0:T(8,128)(2,1)S(1)}, bf16[64,128]{1,0:T(8,128)(2,1)S(1)}, u32[]{:S(2)}, u32[]{:S(2)}) %collective-permute-start.7) | collective-permute-done | bytes 16416 | tf_op jit(solution)/shard_map/ppermute | solution.py:361
  34.7 0.0 collective-permute-done.6.refs_2_
  34.7 0.6 collective-permute-done.5.refs_1_
  35.3 0.7 %collective-permute-start.8 = (bf16[256,128]{1,0:T(8,128)(2,1)S(1)}, bf16[256,128]{1,0:T(8,128)(2,1)S(1)}, u32[]{:S(2)}, u32[]{:S(2)}) collective-permute-start(bf16[256,128]{1,0:T(8,128)(2,1)S(1)} %shard_map.70.after_ref.mine_ref), channel_id=1, source_target_pairs={{0,1},{1,0},{2,3},{3,2},{4,5},{5,4},{6,7},{7,6},{8,9},{9,8},{10,11... | collective-permute-start | bytes 196616 | tf_op jit(solution)/shard_map/ppermute | solution.py:401
  36.0 0.0 copy-start.3
  36.0 0.7 copy-done.3
  36.7 0.0 copy-start.4
  36.7 0.8 %copy-done.4 = bf16[128,128]{1,0:T(8,128)(2,1)S(1)} copy-done((bf16[128,128]{1,0:T(8,128)(2,1)S(1)}, bf16[128,128]{1,0:T(8,128)(2,1)}, u32[]{:S(2)}) %copy-start.4) | copy-done | bytes 32792
  37.5 0.0 copy-start.7
  37.5 0.7 copy-done.7
  38.1 0.4 shard_map.71
  38.5 1.0 %collective-permute-done.8.other_ref = bf16[256,128]{1,0:T(8,128)(2,1)S(1)} collective-permute-done((bf16[256,128]{1,0:T(8,128)(2,1)S(1)}, bf16[256,128]{1,0:T(8,128)(2,1)S(1)}, u32[]{:S(2)}, u32[]{:S(2)}) %collective-permute-start.8) | collective-permute-done | bytes 65568 | tf_op jit(solution)/shard_map/ppermute | solution.py:401
  39.5 0.1 shard_map.72.after_ref.refs_0_
  39.6 0.1 collective-permute-start.11
  39.7 0.1 collective-permute-start.10
  39.8 4.0 %collective-permute-start.9 = (bf16[512,128]{1,0:T(8,128)(2,1)S(1)}, bf16[512,128]{1,0:T(8,128)(2,1)S(1)}, u32[]{:S(2)}, u32[]{:S(2)}) collective-permute-start(bf16[512,128]{1,0:T(8,128)(2,1)S(1)} %shard_map.72.after_ref.refs_0_), channel_id=1, source_target_pairs={{0,4},{2,6},{4,0},{6,2},{8,12},{10,14},{12,8},{14,10},{16,20},{18,... | collective-permute-start | bytes 393224 | tf_op jit(solution)/shard_map/ppermute | solution.py:361
  43.8 0.0 collective-permute-done.4.inner_halo_ref
  43.8 0.0 collective-permute-done.3.outer_halo_ref
  43.8 1.2 %shard_map.73.frame_ref.frame_in = f32[12296,128]{1,0:T(8,128)S(1)} custom-call(bf16[128,2048]{1,0:T(8,128)(2,1)S(1)} %collective-permute-done.3.outer_halo_ref, bf16[128,2048]{1,0:T(8,128)(2,1)S(1)} %get-tuple-element.31.refs_4_.outer_ref, bf16[128,2048]{1,0:T(8,128)(2,1)S(1)} %get-tuple-element.32.inner_ref, ...), custom_call_target="tpu_custom_call" | custom-call | bytes 6000000 | tf_op jit(solution)/shard_map/pallas_call | solution.py:412
  45.1 4.1 %shard_map.74.refs_4_.refs_0_ = f32[1024,128]{1,0:T(8,128)S(1)} custom-call(s32[16384]{0:T(1024)S(1)} %bitcast.17, s32[1024]{0:T(1024)S(1)} %bitcast.22, s32[1024]{0:T(1024)S(1)} %bitcast.28, f32[12296,128]{1,0:T(8,128)S(1)} %shard_map.73.frame_ref.frame_in, bf16[512,128]{1,0:T(8,128)(2,1)S(1)} %shard_map.72.after_ref.refs_0_), custom_call_target="tpu_custom_call" | custom-call | bytes 12000000 | tf_op jit(solution)/shard_map/pallas_call | solution.py:428
  49.2 0.0 collective-permute-done.11.refs_3_
  49.2 0.0 collective-permute-done.10.refs_2_
  49.2 0.0 collective-permute-done.9.refs_1_
  49.3 0.1 collective-permute-start.12
  49.4 4.4 %shard_map.76.after_ref.refs_1_ = f32[1024,128]{1,0:T(8,128)S(1)} custom-call(s32[16384]{0:T(1024)S(1)} %bitcast.18, s32[1024]{0:T(1024)S(1)} %bitcast.23, s32[1024]{0:T(1024)S(1)} %bitcast.29, f32[12296,128]{1,0:T(8,128)S(1)} %shard_map.73.frame_ref.frame_in, bf16[2048,128]{1,0:T(8,128)(2,1)S(1)} %shard_map.75.after_ref.near_ref), custom_call_target="tpu_custom_call" | custom-call | bytes 12000000 | tf_op jit(solution)/shard_map/pallas_call | solution.py:428
  53.8 0.0 copy-start.6
  53.8 0.0 collective-permute-done.12.far_ref
  53.8 0.1 shard_map.77.frame_ref
  53.9 0.5 copy-done.6
  54.4 3.1 %shard_map.78 = (bf16[64,1024]{1,0:T(8,128)(2,1)S(1)}, bf16[128,1024]{1,0:T(8,128)(2,1)S(1)}) custom-call(s32[16384]{0:T(1024)S(1)} %bitcast.19, s32[1024]{0:T(1024)S(1)} %bitcast.30, s32[1024]{0:T(1024)S(1)} %bitcast.31, f32[12296,128]{1,0:T(8,128)S(1)} %shard_map.77.frame_ref, f32[2048,128]{1,0:T(8,128)S(1)} %get-tuple-element.33.after_ref.scale_ref, ...), custom_call_target="tpu_custom_call" | custom-call | bytes 9000000 | tf_op jit(solution)/shard_map/pallas_call | solution.py:449
  57.6 0.6 collective-permute-start.13
  58.2 4.6 %shard_map.79 = (bf16[64,512]{1,0:T(8,128)(2,1)S(1)}, bf16[128,512]{1,0:T(8,128)(2,1)S(1)}) custom-call(s32[16384]{0:T(1024)S(1)} %bitcast.15, s32[1024]{0:T(1024)S(1)} %bitcast.24, s32[1024]{0:T(1024)S(1)} %bitcast.26, f32[12296,128]{1,0:T(8,128)S(1)} %shard_map.77.frame_ref, f32[2048,128]{1,0:T(8,128)S(1)} %get-tuple-element.33.after_ref.scale_ref, ...), custom_call_target="tpu_custom_call" | custom-call | bytes 12000000 | tf_op jit(solution)/shard_map/pallas_call | solution.py:449
  62.8 1.4 %collective-permute-start.14 = (bf16[128,512]{1,0:T(8,128)(2,1)S(1)}, bf16[128,512]{1,0:T(8,128)(2,1)S(1)}, u32[]{:S(2)}, u32[]{:S(2)}) collective-permute-start(bf16[128,512]{1,0:T(8,128)(2,1)S(1)} %get-tuple-element.45), channel_id=1, source_target_pairs={{0,1},{1,0},{2,3},{3,2},{4,5},{5,4},{6,7},{7,6},{8,9},{9,8},{10,11... | collective-permute-start | bytes 393224 | tf_op jit(solution)/shard_map/ppermute | solution.py:465
  64.2 4.5 %shard_map.80 = (bf16[64,512]{1,0:T(8,128)(2,1)S(1)}, bf16[64,512]{1,0:T(8,128)(2,1)S(1)}) custom-call(s32[16384]{0:T(1024)S(1)} %bitcast.16, s32[1024]{0:T(1024)S(1)} %bitcast.25, s32[1024]{0:T(1024)S(1)} %bitcast.27, f32[12296,128]{1,0:T(8,128)S(1)} %shard_map.77.frame_ref, f32[2048,128]{1,0:T(8,128)S(1)} %get-tuple-element.33.after_ref.scale_ref, ...), custom_call_target="tpu_custom_call" | custom-call | bytes 12000000 | tf_op jit(solution)/shard_map/pallas_call | solution.py:449
  68.7 0.8 %collective-permute-start.15 = (bf16[64,512]{1,0:T(8,128)(2,1)S(1)}, bf16[64,512]{1,0:T(8,128)(2,1)S(1)}, u32[]{:S(2)}, u32[]{:S(2)}) collective-permute-start(bf16[64,512]{1,0:T(8,128)(2,1)S(1)} %get-tuple-element.46), channel_id=1, source_target_pairs={{0,1},{1,0},{2,3},{3,2},{4,5},{5,4},{6,7},{7,6},{8,9},{9,8},{10,11... | collective-permute-start | bytes 196616 | tf_op jit(solution)/shard_map/ppermute | solution.py:465
  69.6 3.5 %collective-permute-done.15.refs_5_ = bf16[64,512]{1,0:T(8,128)(2,1)S(1)} collective-permute-done((bf16[64,512]{1,0:T(8,128)(2,1)S(1)}, bf16[64,512]{1,0:T(8,128)(2,1)S(1)}, u32[]{:S(2)}, u32[]{:S(2)}) %collective-permute-start.15) | collective-permute-done | bytes 65568 | tf_op jit(solution)/shard_map/ppermute | solution.py:465
  73.1 0.0 collective-permute-done.14.refs_4_
  73.1 0.0 collective-permute-done.13.refs_3_
  73.1 0.8 %shard_map.81 = bf16[64,4096]{1,0:T(8,128)(2,1)} custom-call(bf16[64,1024]{1,0:T(8,128)(2,1)S(1)} %get-tuple-element.38.after_ref.refs_0_, bf16[64,512]{1,0:T(8,128)(2,1)S(1)} %get-tuple-element.42.after_ref.refs_1_, bf16[64,512]{1,0:T(8,128)(2,1)S(1)} %get-tuple-element.43.refs_2_, bf16[128,1024]{1,0:T(8,128)(2,1)S(1)} %collective-permute-done.13.refs_3_, ...), custom_call_target="tpu_custom_call" | custom-call | bytes 1500000 | tf_op jit(solution)/shard_map/pallas_call | solution.py:467
  (4 shorter events, 0.0 us)
Async XLA Ops:
  0.0 18.0 %collective-permute-start.1 = (bf16[64,4096]{1,0:T(8,128)(2,1)}, bf16[64,4096]{1,0:T(8,128)(2,1)S(1)}, u32[]{:S(2)}, u32[]{:S(2)}) collective-permute-start(bf16[64,4096]{1,0:T(8,128)(2,1)} %x_ref.1), channel_id=1, source_target_pairs={{0,1},{1,0},{2,3},{3,2},{4,5},{5,4},{6,7},{7,6},{8,9},{9,8},{10,11... | collective-permute-start | bytes 1572872 | tf_op jit(solution)/shard_map/ppermute | solution.py:377
  1.3 1.1 %copy-start = (bf16[64,4096]{1,0:T(8,128)(2,1)S(1)}, bf16[64,4096]{1,0:T(8,128)(2,1)}, u32[]{:S(2)}) copy-start(bf16[64,4096]{1,0:T(8,128)(2,1)} %x_ref.1) | copy-start | bytes 1572868
  2.4 0.7 copy-start.5
  3.6 9.1 %collective-permute-start = (bf16[16,128]{1,0:T(8,128)(2,1)S(1)}, bf16[16,128]{1,0:T(8,128)(2,1)S(1)}, u32[]{:S(2)}, u32[]{:S(2)}) collective-permute-start(bf16[16,128]{1,0:T(8,128)(2,1)S(1)} %shard_map.64.after_ref.refs_0_), channel_id=1, source_target_pairs={{0,64},{2,66},{4,68},{6,70},{8,72},{10,74},{12,76},{14,78},{16,80}... | collective-permute-start | bytes 12296 | tf_op jit(solution)/shard_map/ppermute | solution.py:361
  11.9 0.7 copy-start.2
  12.7 5.2 %collective-permute-start.2 = (bf16[32,128]{1,0:T(8,128)(2,1)S(1)}, bf16[32,128]{1,0:T(8,128)(2,1)S(1)}, u32[]{:S(2)}, u32[]{:S(2)}) collective-permute-start(bf16[32,128]{1,0:T(8,128)(2,1)S(1)} %shard_map.66.after_ref.refs_0_), channel_id=1, source_target_pairs={{0,128},{2,130},{4,132},{6,134},{8,136},{10,138},{12,140},{14,142}... | collective-permute-start | bytes 24584 | tf_op jit(solution)/shard_map/ppermute | solution.py:361
  18.0 1.0 %copy-start.1 = (bf16[64,4096]{1,0:T(8,128)(2,1)S(1)}, bf16[64,4096]{1,0:T(8,128)(2,1)}, u32[]{:S(2)}) copy-start(bf16[64,4096]{1,0:T(8,128)(2,1)} %x_ref.1) | copy-start | bytes 1572868
  19.2 24.7 %collective-permute-start.4 = (bf16[128,2048]{1,0:T(8,128)(2,1)S(1)}, bf16[128,2048]{1,0:T(8,128)(2,1)S(1)}, u32[]{:S(2)}, u32[]{:S(2)}) collective-permute-start(bf16[128,2048]{1,0:T(8,128)(2,1)S(1)} %get-tuple-element.32.inner_ref), channel_id=1, source_target_pairs={{0,2},{2,0},{4,6},{6,4},{8,10},{10,8},{12,14},{14,12},{16,18},{18,... | collective-permute-start | bytes 1572872 | tf_op jit(solution)/shard_map/ppermute | solution.py:394
  19.3 24.6 %collective-permute-start.3 = (bf16[128,2048]{1,0:T(8,128)(2,1)S(1)}, bf16[128,2048]{1,0:T(8,128)(2,1)S(1)}, u32[]{:S(2)}, u32[]{:S(2)}) collective-permute-start(bf16[128,2048]{1,0:T(8,128)(2,1)S(1)} %get-tuple-element.31.refs_4_.outer_ref), channel_id=1, source_target_pairs={{2,4},{4,2},{6,8},{8,6},{10,12},{12,10},{14,16},{16,14},{18,20},{2... | collective-permute-start | bytes 1572872 | tf_op jit(solution)/shard_map/ppermute | solution.py:395
  29.1 5.6 %collective-permute-start.7 = (bf16[64,128]{1,0:T(8,128)(2,1)S(1)}, bf16[64,128]{1,0:T(8,128)(2,1)S(1)}, u32[]{:S(2)}, u32[]{:S(2)}) collective-permute-start(bf16[64,128]{1,0:T(8,128)(2,1)S(1)} %shard_map.68.after_ref.refs_0_), channel_id=1, source_target_pairs={{0,48},{2,50},{4,52},{6,54},{8,56},{10,58},{12,60},{14,62},{16,32}... | collective-permute-start | bytes 49160 | tf_op jit(solution)/shard_map/ppermute | solution.py:361
  29.2 5.5 %collective-permute-start.6 = (bf16[64,128]{1,0:T(8,128)(2,1)S(1)}, bf16[64,128]{1,0:T(8,128)(2,1)S(1)}, u32[]{:S(2)}, u32[]{:S(2)}) collective-permute-start(bf16[64,128]{1,0:T(8,128)(2,1)S(1)} %shard_map.68.after_ref.refs_0_), channel_id=1, source_target_pairs={{0,32},{2,34},{4,36},{6,38},{8,40},{10,42},{12,44},{14,46},{16,48}... | collective-permute-start | bytes 49160 | tf_op jit(solution)/shard_map/ppermute | solution.py:361
  29.3 6.0 %collective-permute-start.5 = (bf16[64,128]{1,0:T(8,128)(2,1)S(1)}, bf16[64,128]{1,0:T(8,128)(2,1)S(1)}, u32[]{:S(2)}, u32[]{:S(2)}) collective-permute-start(bf16[64,128]{1,0:T(8,128)(2,1)S(1)} %shard_map.68.after_ref.refs_0_), channel_id=1, source_target_pairs={{0,16},{2,18},{4,20},{6,22},{8,24},{10,26},{12,28},{14,30},{16,0},... | collective-permute-start | bytes 49160 | tf_op jit(solution)/shard_map/ppermute | solution.py:361
  35.3 4.3 %collective-permute-start.8 = (bf16[256,128]{1,0:T(8,128)(2,1)S(1)}, bf16[256,128]{1,0:T(8,128)(2,1)S(1)}, u32[]{:S(2)}, u32[]{:S(2)}) collective-permute-start(bf16[256,128]{1,0:T(8,128)(2,1)S(1)} %shard_map.70.after_ref.mine_ref), channel_id=1, source_target_pairs={{0,1},{1,0},{2,3},{3,2},{4,5},{5,4},{6,7},{7,6},{8,9},{9,8},{10,11... | collective-permute-start | bytes 196616 | tf_op jit(solution)/shard_map/ppermute | solution.py:401
  36.0 0.7 copy-start.3
  36.7 0.8 %copy-start.4 = (bf16[128,128]{1,0:T(8,128)(2,1)S(1)}, bf16[128,128]{1,0:T(8,128)(2,1)}, u32[]{:S(2)}) copy-start(bf16[128,128]{1,0:T(8,128)(2,1)} %weight_ref.1) | copy-start | bytes 98308
  37.5 0.7 copy-start.7
  39.6 9.6 %collective-permute-start.11 = (bf16[512,128]{1,0:T(8,128)(2,1)S(1)}, bf16[512,128]{1,0:T(8,128)(2,1)S(1)}, u32[]{:S(2)}, u32[]{:S(2)}) collective-permute-start(bf16[512,128]{1,0:T(8,128)(2,1)S(1)} %shard_map.72.after_ref.refs_0_), channel_id=1, source_target_pairs={{0,12},{2,14},{4,8},{6,10},{8,4},{10,6},{12,0},{14,2},{16,28},{18,... | collective-permute-start | bytes 393224 | tf_op jit(solution)/shard_map/ppermute | solution.py:361
  39.7 9.5 %collective-permute-start.10 = (bf16[512,128]{1,0:T(8,128)(2,1)S(1)}, bf16[512,128]{1,0:T(8,128)(2,1)S(1)}, u32[]{:S(2)}, u32[]{:S(2)}) collective-permute-start(bf16[512,128]{1,0:T(8,128)(2,1)S(1)} %shard_map.72.after_ref.refs_0_), channel_id=1, source_target_pairs={{0,8},{2,10},{4,12},{6,14},{8,0},{10,2},{12,4},{14,6},{16,24},{18,... | collective-permute-start | bytes 393224 | tf_op jit(solution)/shard_map/ppermute | solution.py:361
  39.8 9.4 %collective-permute-start.9 = (bf16[512,128]{1,0:T(8,128)(2,1)S(1)}, bf16[512,128]{1,0:T(8,128)(2,1)S(1)}, u32[]{:S(2)}, u32[]{:S(2)}) collective-permute-start(bf16[512,128]{1,0:T(8,128)(2,1)S(1)} %shard_map.72.after_ref.refs_0_), channel_id=1, source_target_pairs={{0,4},{2,6},{4,0},{6,2},{8,12},{10,14},{12,8},{14,10},{16,20},{18,... | collective-permute-start | bytes 393224 | tf_op jit(solution)/shard_map/ppermute | solution.py:361
  49.3 4.5 %collective-permute-start.12 = (bf16[2048,128]{1,0:T(8,128)(2,1)S(1)}, bf16[2048,128]{1,0:T(8,128)(2,1)S(1)}, u32[]{:S(2)}, u32[]{:S(2)}) collective-permute-start(bf16[2048,128]{1,0:T(8,128)(2,1)S(1)} %shard_map.75.after_ref.near_ref), channel_id=1, source_target_pairs={{0,2},{2,0},{4,6},{6,4},{8,10},{10,8},{12,14},{14,12},{16,18},{18,... | collective-permute-start | bytes 1572872 | tf_op jit(solution)/shard_map/ppermute | solution.py:361
  53.8 0.7 copy-start.6
  57.6 15.5 %collective-permute-start.13 = (bf16[128,1024]{1,0:T(8,128)(2,1)S(1)}, bf16[128,1024]{1,0:T(8,128)(2,1)S(1)}, u32[]{:S(2)}, u32[]{:S(2)}) collective-permute-start(bf16[128,1024]{1,0:T(8,128)(2,1)S(1)} %get-tuple-element.44), channel_id=1, source_target_pairs={{0,1},{1,0},{2,3},{3,2},{4,5},{5,4},{6,7},{7,6},{8,9},{9,8},{10,11... | collective-permute-start | bytes 786440 | tf_op jit(solution)/shard_map/ppermute | solution.py:465
  62.8 10.3 %collective-permute-start.14 = (bf16[128,512]{1,0:T(8,128)(2,1)S(1)}, bf16[128,512]{1,0:T(8,128)(2,1)S(1)}, u32[]{:S(2)}, u32[]{:S(2)}) collective-permute-start(bf16[128,512]{1,0:T(8,128)(2,1)S(1)} %get-tuple-element.45), channel_id=1, source_target_pairs={{0,1},{1,0},{2,3},{3,2},{4,5},{5,4},{6,7},{7,6},{8,9},{9,8},{10,11... | collective-permute-start | bytes 393224 | tf_op jit(solution)/shard_map/ppermute | solution.py:465
  68.7 4.4 %collective-permute-start.15 = (bf16[64,512]{1,0:T(8,128)(2,1)S(1)}, bf16[64,512]{1,0:T(8,128)(2,1)S(1)}, u32[]{:S(2)}, u32[]{:S(2)}) collective-permute-start(bf16[64,512]{1,0:T(8,128)(2,1)S(1)} %get-tuple-element.46), channel_id=1, source_target_pairs={{0,1},{1,0},{2,3},{3,2},{4,5},{5,4},{6,7},{7,6},{8,9},{9,8},{10,11... | collective-permute-start | bytes 196616 | tf_op jit(solution)/shard_map/ppermute | solution.py:465

commit v7 on v6

--- a/solution.py
+++ b/solution.py
@@ -134,9 +134,8 @@
     return values
 
 
-def sorted_tiles(keys, halved):
+def sorted_tiles(keys):
     shape = keys.shape
-    apart = lax.broadcasted_iota(jnp.int32, shape, 0) == halved
     sub = lax.broadcasted_iota(jnp.int32, shape, 1)
     lane = lax.broadcasted_iota(jnp.int32, shape, 2)
     at = sub * LANES + lane
@@ -150,12 +149,9 @@
                 lower, pltpu.roll(keys, extent - by, axis), pltpu.roll(keys, by, axis)
             )
             ascending = (at & size) == 0
-            if 2 * size == CHUNK:
-                ascending = ascending | apart
-            merged = jnp.where(
+            keys = jnp.where(
                 lower == ascending, jnp.minimum(keys, partner), jnp.maximum(keys, partner)
             )
-            keys = jnp.where(apart, keys, merged) if size == CHUNK else merged
             distance //= 2
         size *= 2
     return keys
@@ -193,9 +189,9 @@
     at = lax.broadcasted_iota(jnp.int32, (8, LANES), 0) * LANES + lax.broadcasted_iota(
         jnp.int32, (8, LANES), 1
     )
-    keys = sorted_tiles(counts_ref[...] * CHUNK + at[None], 2)
+    keys = sorted_tiles(counts_ref[...] * CHUNK + at[None])
     for i in range(3):
-        orders[i][...] = keys[i] & ((CHUNK if i < 2 else CHUNK // 2) - 1)
+        orders[i][...] = keys[i] & (CHUNK - 1)
         classes[i][...] = keys[i] >> 10
 
 
@@ -384,29 +380,30 @@
     )
 
     block = join(block, arrived, order[0])
+    arrived = stage(block, STAGES[2])
+
+    block = join(block, arrived, order[0])
     outer, inner = pallas(
         halves_kernel,
         (bf16(2 * chans, half),) * 2,
         [ANYWHERE] * 3,
         [pltpu.SemaphoreType.DMA((4,))],
-        us=0.5,
+        us=0.1,
     )(node_feats, other, block)
     inner_halo = lax.ppermute(inner, "slab", [(i, i ^ 1) for i in range(slabs)])
     outer_halo = lax.ppermute(
         outer, "slab", [(i, j) for i in range(slabs) for j in [i + 2 * (i & 1) - 1] if 0 <= j < slabs]
     )
-    arrived = stage(block, STAGES[2])
-
-    block = join(block, arrived, outer)
+
     arrived = lax.ppermute(block, "feat", swap)
     scale, by_out, bias = pallas(
         constants_kernel,
         (f32(half, LANES), bf16(2 * chans, 2 * chans), f32(LANES, LANES)),
         [IN_VMEM] * 3 + [ANYWHERE],
-        us=1.0,
-    )(deg_tiles, weight, bias_terms[None, :], block)
+        us=0.1,
+    )(deg_tiles, weight, bias_terms[None, :], outer)
     block = pallas(
-        join_feat_kernel, bf16(2 * block.shape[0], 2 * chans), [IN_VMEM] * 2 + [ANYWHERE], us=0.5
+        join_feat_kernel, bf16(2 * block.shape[0], 2 * chans), [IN_VMEM] * 2 + [ANYWHERE], us=0.1
     )(block, arrived, scale)
     arrived = stage(block, STAGES[3])
     frame = pallas(
@@ -454,11 +451,10 @@
             us=us,
         )(*plan, frame, scale, by_out, bias, after, *near)
 
-    keep, received = [hub_rows], []
+    keep, received = [near[1]], []
     for plan, first, start, size, sent_chans, near, us in (
         (far_plan, 0, 0, CHUNK, 2 * chans, near, 3.0),
-        (full_plan, CHUNK, 0, CHUNK // 2, 2 * chans, [], 4.0),
-        (full_plan, CHUNK + CHUNK // 2, CHUNK // 2, CHUNK // 2, chans, [], 4.0),
+        (full_plan, CHUNK, 0, CHUNK, chans, [], 8.0),
     ):
         kept, sent = layer(plan, first, start, size, sent_chans, near, keep[-1], us)
         keep.append(kept)

time: 74.5 us -> 73.4 us (0.985)
  waiting for transfers between devices: 7.3 us -> 10.6 us
  starting transfers between devices: 31.5 us -> 29.7 us
  Pallas kernels: 27.8 us -> 26.5 us
  local copies, waits for them, and re-layouts: 7.1 us -> 5.89 us
    ppermute x9, waiting for transfers between devices: 2.75 us -> 4.27 us  [stage(): lax.ppermute(block, 'slab', [(i, i ^ bit) for i in range(slabs)])]
    unnamed x17 -> x13, local copies, waits for them, and re-layouts: 7.1 us -> 5.89 us
    pallas_call x3 -> x2, Pallas kernels: 12.2 us -> 11.2 us  [layer(): pallas(functools.partial(layer_kernel, slots, first, start, len(near), ha...]
    ppermute x1, starting transfers between devices: 9.79 us -> 8.81 us  [local(): lax.ppermute(outer, 'slab', [(i, j) for i in range(slabs) for j in [i + 2...]
    ppermute x3 -> x2, starting transfers between devices: 2.89 us -> 2.09 us  [local(): received.append(lax.ppermute(sent, 'feat', swap))]
    ppermute x3 -> x2, waiting for transfers between devices: 3.53 us -> 4.31 us  [local(): received.append(lax.ppermute(sent, 'feat', swap))]
  transfers between devices with their start and end apart: 16 -> 15, of which waited for: 5 -> 6; matrix products, arithmetic and copies ran while one was open for 1% -> 1% of each run, Pallas kernels for 32% -> 30%
where the time goes in v7:
time: 73.4 us; the launch traced here: 72.9 us
  starting transfers between devices  29.7 us (40%)
  Pallas kernels  26.5 us (36%)
  waiting for transfers between devices  10.6 us (14%)
  local copies, waits for them, and re-layouts  5.89 us (8%)
    ppermute x9, starting transfers between devices, stage(): lax.ppermute(block, 'slab', [(i, i ^ bit) for i in range(slabs)])  16.6 us
    pallas_call x2, Pallas kernels, layer(): pallas(functools.partial(layer_kernel, slots, first, start, len(near), ha...  11.2 us
    ppermute x1, starting transfers between devices, local(): lax.ppermute(outer, 'slab', [(i, j) for i in range(slabs) for j in [i + 2...  8.81 us
    pallas_call x2, Pallas kernels, near_sum(): pallas(functools.partial(near_kernel, slots, part, 2), f32(CHUNK, LANES),...  8.18 us
    unnamed x13, local copies, waits for them, and re-layouts  5.89 us
    ppermute x2, waiting for transfers between devices, local(): received.append(lax.ppermute(sent, 'feat', swap))  4.31 us
    ppermute x9, waiting for transfers between devices, stage(): lax.ppermute(block, 'slab', [(i, i ^ bit) for i in range(slabs)])  4.27 us
    pallas_call x1, Pallas kernels, local(): pallas(order_kernel, (tile,) * 6, [IN_VMEM, ANYWHERE], us=3.0)  3.54 us
  transfers between devices with their start and end apart: 15, of which 6 were waited for; matrix products, arithmetic and copies ran while one was open for 1% of the time, Pallas kernels for 30%

profile of v7, /device:TPU:16, one launch (start us, length us, event | category | flops | bytes accessed | tf_op | source)
XLA Modules:
  0.0 72.9 jit_solution(3216435185718621061)
XLA Ops:
  0.0 1.3 %collective-permute-start.1 = (bf16[64,4096]{1,0:T(8,128)(2,1)}, bf16[64,4096]{1,0:T(8,128)(2,1)S(1)}, u32[]{:S(2)}, u32[]{:S(2)}) collective-permute-start(bf16[64,4096]{1,0:T(8,128)(2,1)} %x_ref.1), channel_id=1, source_target_pairs={{0,1},{1,0},{2,3},{3,2},{4,5},{5,4},{6,7},{7,6},{8,9},{9,8},{10,11... | collective-permute-start | bytes 1572872 | tf_op jit(solution)/shard_map/ppermute | solution.py:373
  1.3 0.0 copy-start
  1.3 1.1 %copy-done = bf16[64,4096]{1,0:T(8,128)(2,1)S(1)} copy-done((bf16[64,4096]{1,0:T(8,128)(2,1)S(1)}, bf16[64,4096]{1,0:T(8,128)(2,1)}, u32[]{:S(2)}) %copy-start) | copy-done | bytes 524312
  2.4 0.0 copy-start.4
  2.4 0.7 copy-done.4
  3.0 0.6 shard_map.64.after_ref.refs_0_
  3.6 7.3 %collective-permute-start = (bf16[16,128]{1,0:T(8,128)(2,1)S(1)}, bf16[16,128]{1,0:T(8,128)(2,1)S(1)}, u32[]{:S(2)}, u32[]{:S(2)}) collective-permute-start(bf16[16,128]{1,0:T(8,128)(2,1)S(1)} %shard_map.64.after_ref.refs_0_), channel_id=1, source_target_pairs={{0,64},{2,66},{4,68},{6,70},{8,72},{10,74},{12,76},{14,78},{16,80}... | collective-permute-start | bytes 12296 | tf_op jit(solution)/shard_map/ppermute | solution.py:357
  10.9 1.0 %copy.8 = s32[2,8,32,128]{3,2,1,0:T(8,128)S(1)} copy(s32[2,8,32,128]{3,1,2,0:T(8,128)} %bitcast.31) | data formatting | bytes 524288
  11.9 0.0 copy-start.2
  11.9 0.7 copy-done.2
  12.6 0.1 shard_map.65
  12.7 0.0 collective-permute-done.refs_1_
  12.7 0.7 collective-permute-start.2
  13.5 3.5 %shard_map.67 = (s32[8,128]{1,0:T(8,128)S(1)}, s32[8,128]{1,0:T(8,128)S(1)}, s32[8,128]{1,0:T(8,128)S(1)}, s32[8,128]{1,0:T(8,128)S(1)}, s32[8,128]{1,0:T(8,128)S(1)}, /*index=5*/s32[8,128]{1,0:T(8,128)S(1)}) custom-call(s32[3,8,128]{2,1,0:T(8,128)S(1)} %get-tuple-element.25.refs_2_.counts_ref, bf16[32,128]{1,0:T(8,128)(2,1)S(1)} %shard_map.66.after_ref.refs_0_), custom_call_target="tpu_custom_call" | custom-call | bytes 9000000 | tf_op jit(solution)/shard_map/pallas_call | solution.py:377
  17.0 1.0 %collective-permute-done.2.refs_1_ = bf16[32,128]{1,0:T(8,128)(2,1)S(1)} collective-permute-done((bf16[32,128]{1,0:T(8,128)(2,1)S(1)}, bf16[32,128]{1,0:T(8,128)(2,1)S(1)}, u32[]{:S(2)}, u32[]{:S(2)}) %collective-permute-start.2) | collective-permute-done | bytes 8224 | tf_op jit(solution)/shard_map/ppermute | solution.py:357
  18.0 3.0 %collective-permute-start.5 = (bf16[64,128]{1,0:T(8,128)(2,1)S(1)}, bf16[64,128]{1,0:T(8,128)(2,1)S(1)}, u32[]{:S(2)}, u32[]{:S(2)}) collective-permute-start(bf16[64,128]{1,0:T(8,128)(2,1)S(1)} %shard_map.68.refs_0_), channel_id=1, source_target_pairs={{0,48},{2,50},{4,52},{6,54},{8,56},{10,58},{12,60},{14,62},{16,32}... | collective-permute-start | bytes 49160 | tf_op jit(solution)/shard_map/ppermute | solution.py:357
  21.0 0.0 collective-permute-start.4
  21.0 1.4 %collective-permute-start.3 = (bf16[64,128]{1,0:T(8,128)(2,1)S(1)}, bf16[64,128]{1,0:T(8,128)(2,1)S(1)}, u32[]{:S(2)}, u32[]{:S(2)}) collective-permute-start(bf16[64,128]{1,0:T(8,128)(2,1)S(1)} %shard_map.68.refs_0_), channel_id=1, source_target_pairs={{0,16},{2,18},{4,20},{6,22},{8,24},{10,26},{12,28},{14,30},{16,0},... | collective-permute-start | bytes 49160 | tf_op jit(solution)/shard_map/ppermute | solution.py:357
  22.4 1.1 %collective-permute-done.5.refs_3_ = bf16[64,128]{1,0:T(8,128)(2,1)S(1)} collective-permute-done((bf16[64,128]{1,0:T(8,128)(2,1)S(1)}, bf16[64,128]{1,0:T(8,128)(2,1)S(1)}, u32[]{:S(2)}, u32[]{:S(2)}) %collective-permute-start.5) | collective-permute-done | bytes 16416 | tf_op jit(solution)/shard_map/ppermute | solution.py:357
  23.5 2.1 %collective-permute-done.4.refs_2_ = bf16[64,128]{1,0:T(8,128)(2,1)S(1)} collective-permute-done((bf16[64,128]{1,0:T(8,128)(2,1)S(1)}, bf16[64,128]{1,0:T(8,128)(2,1)S(1)}, u32[]{:S(2)}, u32[]{:S(2)}) %collective-permute-start.4) | collective-permute-done | bytes 16416 | tf_op jit(solution)/shard_map/ppermute | solution.py:357
  25.7 0.0 collective-permute-done.3.refs_1_
  25.7 0.0 collective-permute-done.1.other_ref
  25.7 0.0 copy-start.1
  25.7 1.0 %copy-done.1 = bf16[64,4096]{1,0:T(8,128)(2,1)S(1)} copy-done((bf16[64,4096]{1,0:T(8,128)(2,1)S(1)}, bf16[64,4096]{1,0:T(8,128)(2,1)}, u32[]{:S(2)}) %copy-start.1) | copy-done | bytes 524312
  26.7 0.1 shard_map.70
  26.8 0.1 collective-permute-start.7
  26.9 8.8 %collective-permute-start.6 = (bf16[128,2048]{1,0:T(8,128)(2,1)S(1)}, bf16[128,2048]{1,0:T(8,128)(2,1)S(1)}, u32[]{:S(2)}, u32[]{:S(2)}) collective-permute-start(bf16[128,2048]{1,0:T(8,128)(2,1)S(1)} %get-tuple-element.29.after_ref.outer_ref), channel_id=1, source_target_pairs={{2,4},{4,2},{6,8},{8,6},{10,12},{12,10},{14,16},{16,14},{18,20},{2... | collective-permute-start | bytes 1572872 | tf_op jit(solution)/shard_map/ppermute | solution.py:394
  35.8 0.8 %collective-permute-start.8 = (bf16[256,128]{1,0:T(8,128)(2,1)S(1)}, bf16[256,128]{1,0:T(8,128)(2,1)S(1)}, u32[]{:S(2)}, u32[]{:S(2)}) collective-permute-start(bf16[256,128]{1,0:T(8,128)(2,1)S(1)} %shard_map.69.after_ref.mine_ref), channel_id=1, source_target_pairs={{0,1},{1,0},{2,3},{3,2},{4,5},{5,4},{6,7},{7,6},{8,9},{9,8},{10,11... | collective-permute-start | bytes 196616 | tf_op jit(solution)/shard_map/ppermute | solution.py:398
  36.6 0.0 copy-start.3
  36.6 0.8 %copy-done.3 = bf16[128,128]{1,0:T(8,128)(2,1)S(1)} copy-done((bf16[128,128]{1,0:T(8,128)(2,1)S(1)}, bf16[128,128]{1,0:T(8,128)(2,1)}, u32[]{:S(2)}) %copy-start.3) | copy-done | bytes 32792
  37.3 0.0 copy-start.5
  37.3 0.7 copy-done.5
  38.0 0.4 shard_map.71
  38.4 1.7 %collective-permute-done.8.other_ref = bf16[256,128]{1,0:T(8,128)(2,1)S(1)} collective-permute-done((bf16[256,128]{1,0:T(8,128)(2,1)S(1)}, bf16[256,128]{1,0:T(8,128)(2,1)S(1)}, u32[]{:S(2)}, u32[]{:S(2)}) %collective-permute-start.8) | collective-permute-done | bytes 65568 | tf_op jit(solution)/shard_map/ppermute | solution.py:398
  40.1 0.1 shard_map.72.after_ref.refs_0_
  40.2 0.1 collective-permute-start.11
  40.3 0.1 collective-permute-start.10
  40.4 4.0 %collective-permute-start.9 = (bf16[512,128]{1,0:T(8,128)(2,1)S(1)}, bf16[512,128]{1,0:T(8,128)(2,1)S(1)}, u32[]{:S(2)}, u32[]{:S(2)}) collective-permute-start(bf16[512,128]{1,0:T(8,128)(2,1)S(1)} %shard_map.72.after_ref.refs_0_), channel_id=1, source_target_pairs={{0,4},{2,6},{4,0},{6,2},{8,12},{10,14},{12,8},{14,10},{16,20},{18,... | collective-permute-start | bytes 393224 | tf_op jit(solution)/shard_map/ppermute | solution.py:357
  44.4 0.0 collective-permute-done.7.inner_halo_ref
  44.4 0.3 collective-permute-done.6.outer_halo_ref
  44.7 1.2 %shard_map.73.frame_ref.frame_in = f32[12296,128]{1,0:T(8,128)S(1)} custom-call(bf16[128,2048]{1,0:T(8,128)(2,1)S(1)} %collective-permute-done.6.outer_halo_ref, bf16[128,2048]{1,0:T(8,128)(2,1)S(1)} %get-tuple-element.29.after_ref.outer_ref, bf16[128,2048]{1,0:T(8,128)(2,1)S(1)} %get-tuple-element.30.inner_ref, ...), custom_call_target="tpu_custom_call" | custom-call | bytes 6000000 | tf_op jit(solution)/shard_map/pallas_call | solution.py:409
  45.9 4.0 %shard_map.74.refs_4_.refs_0_ = f32[1024,128]{1,0:T(8,128)S(1)} custom-call(s32[16384]{0:T(1024)S(1)} %bitcast.15, s32[1024]{0:T(1024)S(1)} %bitcast.19, s32[1024]{0:T(1024)S(1)} %bitcast.23, f32[12296,128]{1,0:T(8,128)S(1)} %shard_map.73.frame_ref.frame_in, bf16[512,128]{1,0:T(8,128)(2,1)S(1)} %shard_map.72.after_ref.refs_0_), custom_call_target="tpu_custom_call" | custom-call | bytes 12000000 | tf_op jit(solution)/shard_map/pallas_call | solution.py:425
  49.9 0.0 collective-permute-done.11.refs_3_
  49.9 0.0 collective-permute-done.10.refs_2_
  49.9 0.0 collective-permute-done.9.refs_1_
  50.0 0.1 collective-permute-start.12
  50.1 4.2 %shard_map.76.after_ref.refs_1_ = f32[1024,128]{1,0:T(8,128)S(1)} custom-call(s32[16384]{0:T(1024)S(1)} %bitcast.16, s32[1024]{0:T(1024)S(1)} %bitcast.20, s32[1024]{0:T(1024)S(1)} %bitcast.24, f32[12296,128]{1,0:T(8,128)S(1)} %shard_map.73.frame_ref.frame_in, bf16[2048,128]{1,0:T(8,128)(2,1)S(1)} %shard_map.75.after_ref.near_ref), custom_call_target="tpu_custom_call" | custom-call | bytes 12000000 | tf_op jit(solution)/shard_map/pallas_call | solution.py:425
  54.3 0.0 collective-permute-done.12.far_ref
  54.3 0.1 shard_map.77.frame_ref
  54.5 3.1 %shard_map.78 = (bf16[64,1024]{1,0:T(8,128)(2,1)S(1)}, bf16[128,1024]{1,0:T(8,128)(2,1)S(1)}) custom-call(s32[16384]{0:T(1024)S(1)} %bitcast.18, s32[1024]{0:T(1024)S(1)} %bitcast.25, s32[1024]{0:T(1024)S(1)} %bitcast.26, f32[12296,128]{1,0:T(8,128)S(1)} %shard_map.77.frame_ref, f32[2048,128]{1,0:T(8,128)S(1)} %get-tuple-element.31.after_ref.scale_ref, ...), custom_call_target="tpu_custom_call" | custom-call | bytes 9000000 | tf_op jit(solution)/shard_map/pallas_call | solution.py:446
  57.6 1.1 %collective-permute-start.13 = (bf16[128,1024]{1,0:T(8,128)(2,1)S(1)}, bf16[128,1024]{1,0:T(8,128)(2,1)S(1)}, u32[]{:S(2)}, u32[]{:S(2)}) collective-permute-start(bf16[128,1024]{1,0:T(8,128)(2,1)S(1)} %get-tuple-element.41), channel_id=1, source_target_pairs={{0,1},{1,0},{2,3},{3,2},{4,5},{5,4},{6,7},{7,6},{8,9},{9,8},{10,11... | collective-permute-start | bytes 786440 | tf_op jit(solution)/shard_map/ppermute | solution.py:461
  58.7 8.1 %shard_map.79 = (bf16[64,1024]{1,0:T(8,128)(2,1)S(1)}, bf16[64,1024]{1,0:T(8,128)(2,1)S(1)}) custom-call(s32[16384]{0:T(1024)S(1)} %bitcast.17, s32[1024]{0:T(1024)S(1)} %bitcast.27, s32[1024]{0:T(1024)S(1)} %bitcast.28, f32[12296,128]{1,0:T(8,128)S(1)} %shard_map.77.frame_ref, f32[2048,128]{1,0:T(8,128)S(1)} %get-tuple-element.31.after_ref.scale_ref, ...), custom_call_target="tpu_custom_call" | custom-call | bytes 24000000 | tf_op jit(solution)/shard_map/pallas_call | solution.py:446
  66.7 1.0 %collective-permute-start.14 = (bf16[64,1024]{1,0:T(8,128)(2,1)S(1)}, bf16[64,1024]{1,0:T(8,128)(2,1)S(1)}, u32[]{:S(2)}, u32[]{:S(2)}) collective-permute-start(bf16[64,1024]{1,0:T(8,128)(2,1)S(1)} %get-tuple-element.42), channel_id=1, source_target_pairs={{0,1},{1,0},{2,3},{3,2},{4,5},{5,4},{6,7},{7,6},{8,9},{9,8},{10,11... | collective-permute-start | bytes 393224 | tf_op jit(solution)/shard_map/ppermute | solution.py:461
  67.8 4.3 %collective-permute-done.14.refs_3_ = bf16[64,1024]{1,0:T(8,128)(2,1)S(1)} collective-permute-done((bf16[64,1024]{1,0:T(8,128)(2,1)S(1)}, bf16[64,1024]{1,0:T(8,128)(2,1)S(1)}, u32[]{:S(2)}, u32[]{:S(2)}) %collective-permute-start.14) | collective-permute-done | bytes 131104 | tf_op jit(solution)/shard_map/ppermute | solution.py:461
  72.1 0.0 collective-permute-done.13.refs_2_
  72.1 0.8 %shard_map.80 = bf16[64,4096]{1,0:T(8,128)(2,1)} custom-call(bf16[64,1024]{1,0:T(8,128)(2,1)S(1)} %get-tuple-element.36.after_ref.refs_0_, bf16[64,1024]{1,0:T(8,128)(2,1)S(1)} %get-tuple-element.40.refs_1_, bf16[128,1024]{1,0:T(8,128)(2,1)S(1)} %collective-permute-done.13.refs_2_, bf16[64,1024]{1,0:T(8,128)(2,1)S(1)} %collective-permute-done.14.refs_3_), custom_call_target="tpu_custom_call" | custom-call | bytes 1500000 | tf_op jit(solution)/shard_map/pallas_call | solution.py:463
  (4 shorter events, 0.0 us)
Async XLA Ops:
  0.0 25.7 %collective-permute-start.1 = (bf16[64,4096]{1,0:T(8,128)(2,1)}, bf16[64,4096]{1,0:T(8,128)(2,1)S(1)}, u32[]{:S(2)}, u32[]{:S(2)}) collective-permute-start(bf16[64,4096]{1,0:T(8,128)(2,1)} %x_ref.1), channel_id=1, source_target_pairs={{0,1},{1,0},{2,3},{3,2},{4,5},{5,4},{6,7},{7,6},{8,9},{9,8},{10,11... | collective-permute-start | bytes 1572872 | tf_op jit(solution)/shard_map/ppermute | solution.py:373
  1.3 1.1 %copy-start = (bf16[64,4096]{1,0:T(8,128)(2,1)S(1)}, bf16[64,4096]{1,0:T(8,128)(2,1)}, u32[]{:S(2)}) copy-start(bf16[64,4096]{1,0:T(8,128)(2,1)} %x_ref.1) | copy-start | bytes 1572868
  2.4 0.7 copy-start.4
  3.6 9.1 %collective-permute-start = (bf16[16,128]{1,0:T(8,128)(2,1)S(1)}, bf16[16,128]{1,0:T(8,128)(2,1)S(1)}, u32[]{:S(2)}, u32[]{:S(2)}) collective-permute-start(bf16[16,128]{1,0:T(8,128)(2,1)S(1)} %shard_map.64.after_ref.refs_0_), channel_id=1, source_target_pairs={{0,64},{2,66},{4,68},{6,70},{8,72},{10,74},{12,76},{14,78},{16,80}... | collective-permute-start | bytes 12296 | tf_op jit(solution)/shard_map/ppermute | solution.py:357
  11.9 0.7 copy-start.2
  12.7 5.2 %collective-permute-start.2 = (bf16[32,128]{1,0:T(8,128)(2,1)S(1)}, bf16[32,128]{1,0:T(8,128)(2,1)S(1)}, u32[]{:S(2)}, u32[]{:S(2)}) collective-permute-start(bf16[32,128]{1,0:T(8,128)(2,1)S(1)} %shard_map.66.after_ref.refs_0_), channel_id=1, source_target_pairs={{0,128},{2,130},{4,132},{6,134},{8,136},{10,138},{12,140},{14,142}... | collective-permute-start | bytes 24584 | tf_op jit(solution)/shard_map/ppermute | solution.py:357
  18.0 5.5 %collective-permute-start.5 = (bf16[64,128]{1,0:T(8,128)(2,1)S(1)}, bf16[64,128]{1,0:T(8,128)(2,1)S(1)}, u32[]{:S(2)}, u32[]{:S(2)}) collective-permute-start(bf16[64,128]{1,0:T(8,128)(2,1)S(1)} %shard_map.68.refs_0_), channel_id=1, source_target_pairs={{0,48},{2,50},{4,52},{6,54},{8,56},{10,58},{12,60},{14,62},{16,32}... | collective-permute-start | bytes 49160 | tf_op jit(solution)/shard_map/ppermute | solution.py:357
  21.0 4.6 %collective-permute-start.4 = (bf16[64,128]{1,0:T(8,128)(2,1)S(1)}, bf16[64,128]{1,0:T(8,128)(2,1)S(1)}, u32[]{:S(2)}, u32[]{:S(2)}) collective-permute-start(bf16[64,128]{1,0:T(8,128)(2,1)S(1)} %shard_map.68.refs_0_), channel_id=1, source_target_pairs={{0,32},{2,34},{4,36},{6,38},{8,40},{10,42},{12,44},{14,46},{16,48}... | collective-permute-start | bytes 49160 | tf_op jit(solution)/shard_map/ppermute | solution.py:357
  21.0 4.6 %collective-permute-start.3 = (bf16[64,128]{1,0:T(8,128)(2,1)S(1)}, bf16[64,128]{1,0:T(8,128)(2,1)S(1)}, u32[]{:S(2)}, u32[]{:S(2)}) collective-permute-start(bf16[64,128]{1,0:T(8,128)(2,1)S(1)} %shard_map.68.refs_0_), channel_id=1, source_target_pairs={{0,16},{2,18},{4,20},{6,22},{8,24},{10,26},{12,28},{14,30},{16,0},... | collective-permute-start | bytes 49160 | tf_op jit(solution)/shard_map/ppermute | solution.py:357
  25.7 1.0 %copy-start.1 = (bf16[64,4096]{1,0:T(8,128)(2,1)S(1)}, bf16[64,4096]{1,0:T(8,128)(2,1)}, u32[]{:S(2)}) copy-start(bf16[64,4096]{1,0:T(8,128)(2,1)} %x_ref.1) | copy-start | bytes 1572868
  26.8 17.6 %collective-permute-start.7 = (bf16[128,2048]{1,0:T(8,128)(2,1)S(1)}, bf16[128,2048]{1,0:T(8,128)(2,1)S(1)}, u32[]{:S(2)}, u32[]{:S(2)}) collective-permute-start(bf16[128,2048]{1,0:T(8,128)(2,1)S(1)} %get-tuple-element.30.inner_ref), channel_id=1, source_target_pairs={{0,2},{2,0},{4,6},{6,4},{8,10},{10,8},{12,14},{14,12},{16,18},{18,... | collective-permute-start | bytes 1572872 | tf_op jit(solution)/shard_map/ppermute | solution.py:393
  26.9 17.7 %collective-permute-start.6 = (bf16[128,2048]{1,0:T(8,128)(2,1)S(1)}, bf16[128,2048]{1,0:T(8,128)(2,1)S(1)}, u32[]{:S(2)}, u32[]{:S(2)}) collective-permute-start(bf16[128,2048]{1,0:T(8,128)(2,1)S(1)} %get-tuple-element.29.after_ref.outer_ref), channel_id=1, source_target_pairs={{2,4},{4,2},{6,8},{8,6},{10,12},{12,10},{14,16},{16,14},{18,20},{2... | collective-permute-start | bytes 1572872 | tf_op jit(solution)/shard_map/ppermute | solution.py:394
  35.8 4.4 %collective-permute-start.8 = (bf16[256,128]{1,0:T(8,128)(2,1)S(1)}, bf16[256,128]{1,0:T(8,128)(2,1)S(1)}, u32[]{:S(2)}, u32[]{:S(2)}) collective-permute-start(bf16[256,128]{1,0:T(8,128)(2,1)S(1)} %shard_map.69.after_ref.mine_ref), channel_id=1, source_target_pairs={{0,1},{1,0},{2,3},{3,2},{4,5},{5,4},{6,7},{7,6},{8,9},{9,8},{10,11... | collective-permute-start | bytes 196616 | tf_op jit(solution)/shard_map/ppermute | solution.py:398
  36.6 0.8 %copy-start.3 = (bf16[128,128]{1,0:T(8,128)(2,1)S(1)}, bf16[128,128]{1,0:T(8,128)(2,1)}, u32[]{:S(2)}) copy-start(bf16[128,128]{1,0:T(8,128)(2,1)} %weight_ref.1) | copy-start | bytes 98308
  37.3 0.7 copy-start.5
  40.2 9.7 %collective-permute-start.11 = (bf16[512,128]{1,0:T(8,128)(2,1)S(1)}, bf16[512,128]{1,0:T(8,128)(2,1)S(1)}, u32[]{:S(2)}, u32[]{:S(2)}) collective-permute-start(bf16[512,128]{1,0:T(8,128)(2,1)S(1)} %shard_map.72.after_ref.refs_0_), channel_id=1, source_target_pairs={{0,12},{2,14},{4,8},{6,10},{8,4},{10,6},{12,0},{14,2},{16,28},{18,... | collective-permute-start | bytes 393224 | tf_op jit(solution)/shard_map/ppermute | solution.py:357
  40.3 9.6 %collective-permute-start.10 = (bf16[512,128]{1,0:T(8,128)(2,1)S(1)}, bf16[512,128]{1,0:T(8,128)(2,1)S(1)}, u32[]{:S(2)}, u32[]{:S(2)}) collective-permute-start(bf16[512,128]{1,0:T(8,128)(2,1)S(1)} %shard_map.72.after_ref.refs_0_), channel_id=1, source_target_pairs={{0,8},{2,10},{4,12},{6,14},{8,0},{10,2},{12,4},{14,6},{16,24},{18,... | collective-permute-start | bytes 393224 | tf_op jit(solution)/shard_map/ppermute | solution.py:357
  40.4 9.5 %collective-permute-start.9 = (bf16[512,128]{1,0:T(8,128)(2,1)S(1)}, bf16[512,128]{1,0:T(8,128)(2,1)S(1)}, u32[]{:S(2)}, u32[]{:S(2)}) collective-permute-start(bf16[512,128]{1,0:T(8,128)(2,1)S(1)} %shard_map.72.after_ref.refs_0_), channel_id=1, source_target_pairs={{0,4},{2,6},{4,0},{6,2},{8,12},{10,14},{12,8},{14,10},{16,20},{18,... | collective-permute-start | bytes 393224 | tf_op jit(solution)/shard_map/ppermute | solution.py:357
  50.0 4.3 %collective-permute-start.12 = (bf16[2048,128]{1,0:T(8,128)(2,1)S(1)}, bf16[2048,128]{1,0:T(8,128)(2,1)S(1)}, u32[]{:S(2)}, u32[]{:S(2)}) collective-permute-start(bf16[2048,128]{1,0:T(8,128)(2,1)S(1)} %shard_map.75.after_ref.near_ref), channel_id=1, source_target_pairs={{0,2},{2,0},{4,6},{6,4},{8,10},{10,8},{12,14},{14,12},{16,18},{18,... | collective-permute-start | bytes 1572872 | tf_op jit(solution)/shard_map/ppermute | solution.py:357
  57.6 14.5 %collective-permute-start.13 = (bf16[128,1024]{1,0:T(8,128)(2,1)S(1)}, bf16[128,1024]{1,0:T(8,128)(2,1)S(1)}, u32[]{:S(2)}, u32[]{:S(2)}) collective-permute-start(bf16[128,1024]{1,0:T(8,128)(2,1)S(1)} %get-tuple-element.41), channel_id=1, source_target_pairs={{0,1},{1,0},{2,3},{3,2},{4,5},{5,4},{6,7},{7,6},{8,9},{9,8},{10,11... | collective-permute-start | bytes 786440 | tf_op jit(solution)/shard_map/ppermute | solution.py:461
  66.7 5.3 %collective-permute-start.14 = (bf16[64,1024]{1,0:T(8,128)(2,1)S(1)}, bf16[64,1024]{1,0:T(8,128)(2,1)S(1)}, u32[]{:S(2)}, u32[]{:S(2)}) collective-permute-start(bf16[64,1024]{1,0:T(8,128)(2,1)S(1)} %get-tuple-element.42), channel_id=1, source_target_pairs={{0,1},{1,0},{2,3},{3,2},{4,5},{5,4},{6,7},{7,6},{8,9},{9,8},{10,11... | collective-permute-start | bytes 393224 | tf_op jit(solution)/shard_map/ppermute | solution.py:461

commit v8 on v7

--- a/solution.py
+++ b/solution.py
@@ -15,27 +15,18 @@
 STAGES = ((32,), (64,), (8, 16, 24), (2, 4, 6), (1,))
 
 
-def hub_pick_kernel(rows_ref, x_hbm, out_ref, x_ref, sem):
+def hub_pick_kernel(rows_ref, x_ref, out_ref, x_out_ref):
     hubs, nodes = rows_ref.shape[1], x_ref.shape[1]
-    parts = sem.shape[0]
-    copies = [
-        pltpu.make_async_copy(x_hbm.at[:, part], x_ref.at[:, part], sem.at[i])
-        for i in range(parts)
-        for part in [pl.ds(i * (nodes // parts), nodes // parts)]
-    ]
-    for copy in copies:
-        copy.start()
     diagonal = lax.broadcasted_iota(jnp.int32, (hubs, hubs), 0) == lax.broadcasted_iota(
         jnp.int32, (hubs, hubs), 1
     )
     rows = jnp.sum(jnp.where(diagonal, rows_ref[...], 0), axis=1, keepdims=True)
     onehot = (lax.broadcasted_iota(jnp.int32, (hubs, nodes), 1) == rows).astype(jnp.bfloat16)
-    for copy in copies:
-        copy.wait()
     picked = lax.dot_general(
         onehot, x_ref[...], (((1,), (1,)), ((), ())), preferred_element_type=jnp.float32
     ).astype(jnp.bfloat16)
     out_ref[...] = jnp.concatenate([picked[: hubs // 2], picked[hubs // 2 :]], axis=1)
+    x_out_ref[...] = x_ref[...]
 
 
 def join_kernel(*refs):
@@ -345,11 +336,8 @@
     def i32(*shape):
         return jax.ShapeDtypeStruct(shape, jnp.int32)
 
-    block = pallas(
-        hub_pick_kernel,
-        bf16(hubs // 2, 2 * chans),
-        [IN_VMEM, ANYWHERE],
-        [VMEM((chans, nodes), jnp.bfloat16), pltpu.SemaphoreType.DMA((4,))],
+    block, own_feats = pallas(
+        hub_pick_kernel, (bf16(hubs // 2, 2 * chans), bf16(chans, nodes)), [IN_VMEM] * 2
     )(hub_rows[None, :], node_feats)
     arrived = None
 
@@ -380,31 +368,30 @@
     )
 
     block = join(block, arrived, order[0])
-    arrived = stage(block, STAGES[2])
-
-    block = join(block, arrived, order[0])
+    arrived = lax.ppermute(block, "feat", swap)
+    scale, by_out, bias = pallas(
+        constants_kernel,
+        (f32(half, LANES), bf16(2 * chans, 2 * chans), f32(LANES, LANES)),
+        [IN_VMEM] * 3 + [ANYWHERE],
+        us=0.1,
+    )(deg_tiles, weight, bias_terms[None, :], block)
+    block = pallas(
+        join_feat_kernel, bf16(2 * block.shape[0], 2 * chans), [IN_VMEM] * 2 + [ANYWHERE], us=0.1
+    )(block, arrived, scale)
+
     outer, inner = pallas(
         halves_kernel,
         (bf16(2 * chans, half),) * 2,
         [ANYWHERE] * 3,
         [pltpu.SemaphoreType.DMA((4,))],
         us=0.1,
-    )(node_feats, other, block)
+    )(own_feats, other, block)
     inner_halo = lax.ppermute(inner, "slab", [(i, i ^ 1) for i in range(slabs)])
     outer_halo = lax.ppermute(
         outer, "slab", [(i, j) for i in range(slabs) for j in [i + 2 * (i & 1) - 1] if 0 <= j < slabs]
     )
-
-    arrived = lax.ppermute(block, "feat", swap)
-    scale, by_out, bias = pallas(
-        constants_kernel,
-        (f32(half, LANES), bf16(2 * chans, 2 * chans), f32(LANES, LANES)),
-        [IN_VMEM] * 3 + [ANYWHERE],
-        us=0.1,
-    )(deg_tiles, weight, bias_terms[None, :], outer)
-    block = pallas(
-        join_feat_kernel, bf16(2 * block.shape[0], 2 * chans), [IN_VMEM] * 2 + [ANYWHERE], us=0.1
-    )(block, arrived, scale)
+    arrived = stage(block, STAGES[2])
+    block = join(block, arrived, outer)
     arrived = stage(block, STAGES[3])
     frame = pallas(
         frame_kernel,

time: 73.4 us -> 73.1 us (level)
  the two profiles are of different devices: /device:TPU:16 before, /device:TPU:1 now
where the time goes in v8:
time: 73.1 us
  starting transfers between devices  33.1 us (45%)
  Pallas kernels  26.7 us (37%)
  waiting for transfers between devices  8.26 us (11%)
  local copies, waits for them, and re-layouts  4.85 us (7%)
    ppermute x9, starting transfers between devices, stage(): lax.ppermute(block, 'slab', [(i, i ^ bit) for i in range(slabs)])  23.6 us
    pallas_call x2, Pallas kernels, layer(): pallas(functools.partial(layer_kernel, slots, first, start, len(near), ha...  11.2 us
    pallas_call x2, Pallas kernels, near_sum(): pallas(functools.partial(near_kernel, slots, part, 2), f32(CHUNK, LANES),...  8.52 us
    unnamed x11, local copies, waits for them, and re-layouts  4.85 us
    ppermute x2, waiting for transfers between devices, local(): received.append(lax.ppermute(sent, 'feat', swap))  4.16 us
    pallas_call x1, Pallas kernels, local(): pallas(order_kernel, (tile,) * 6, [IN_VMEM, ANYWHERE], us=3.0)  3.54 us
    ppermute x9, waiting for transfers between devices, stage(): lax.ppermute(block, 'slab', [(i, i ^ bit) for i in range(slabs)])  3.31 us
    ppermute x1, starting transfers between devices, local(): lax.ppermute(outer, 'slab', [(i, j) for i in range(slabs) for j in [i + 2...  3.02 us
  transfers between devices with their start and end apart: 15, of which 4 were waited for; matrix products, arithmetic and copies ran while one was open for 1% of the time, Pallas kernels for 31%

profile of v8, /device:TPU:1, one launch (start us, length us, event | category | flops | bytes accessed | tf_op | source)
XLA Modules:
  0.0 73.1 jit_solution(10996615878966045072)
XLA Ops:
  0.0 2.1 %collective-permute-start.1 = (bf16[64,4096]{1,0:T(8,128)(2,1)}, bf16[64,4096]{1,0:T(8,128)(2,1)S(1)}, u32[]{:S(2)}, u32[]{:S(2)}) collective-permute-start(bf16[64,4096]{1,0:T(8,128)(2,1)} %x_ref.1), channel_id=1, source_target_pairs={{0,1},{1,0},{2,3},{3,2},{4,5},{5,4},{6,7},{7,6},{8,9},{9,8},{10,11... | collective-permute-start | bytes 1572872 | tf_op jit(solution)/shard_map/ppermute | solution.py:361
  2.1 0.0 copy-start
  2.1 1.1 %copy-done = bf16[64,4096]{1,0:T(8,128)(2,1)S(1)} copy-done((bf16[64,4096]{1,0:T(8,128)(2,1)S(1)}, bf16[64,4096]{1,0:T(8,128)(2,1)}, u32[]{:S(2)}) %copy-start) | copy-done | bytes 524312
  3.2 0.0 copy-start.3
  3.2 0.7 copy-done.3
  3.9 0.4 shard_map.64
  4.3 6.9 %collective-permute-start = (bf16[16,128]{1,0:T(8,128)(2,1)S(1)}, bf16[16,128]{1,0:T(8,128)(2,1)S(1)}, u32[]{:S(2)}, u32[]{:S(2)}) collective-permute-start(bf16[16,128]{1,0:T(8,128)(2,1)S(1)} %get-tuple-element.26.after_ref.refs_0_), channel_id=1, source_target_pairs={{0,64},{2,66},{4,68},{6,70},{8,72},{10,74},{12,76},{14,78},{16,80}... | collective-permute-start | bytes 12296 | tf_op jit(solution)/shard_map/ppermute | solution.py:345
  11.2 1.0 %copy.8 = s32[2,8,32,128]{3,2,1,0:T(8,128)S(1)} copy(s32[2,8,32,128]{3,1,2,0:T(8,128)} %bitcast.31) | data formatting | bytes 524288
  12.2 0.0 copy-start.1
  12.3 0.7 copy-done.1
  13.0 0.1 shard_map.65
  13.1 0.0 collective-permute-done.refs_1_
  13.1 2.7 %collective-permute-start.2 = (bf16[32,128]{1,0:T(8,128)(2,1)S(1)}, bf16[32,128]{1,0:T(8,128)(2,1)S(1)}, u32[]{:S(2)}, u32[]{:S(2)}) collective-permute-start(bf16[32,128]{1,0:T(8,128)(2,1)S(1)} %shard_map.66.after_ref.refs_0_), channel_id=1, source_target_pairs={{0,128},{2,130},{4,132},{6,134},{8,136},{10,138},{12,140},{14,142}... | collective-permute-start | bytes 24584 | tf_op jit(solution)/shard_map/ppermute | solution.py:345
  15.8 3.5 %shard_map.67 = (s32[8,128]{1,0:T(8,128)S(1)}, s32[8,128]{1,0:T(8,128)S(1)}, s32[8,128]{1,0:T(8,128)S(1)}, s32[8,128]{1,0:T(8,128)S(1)}, s32[8,128]{1,0:T(8,128)S(1)}, /*index=5*/s32[8,128]{1,0:T(8,128)S(1)}) custom-call(s32[3,8,128]{2,1,0:T(8,128)S(1)} %get-tuple-element.28.refs_2_.counts_ref, bf16[32,128]{1,0:T(8,128)(2,1)S(1)} %shard_map.66.after_ref.refs_0_), custom_call_target="tpu_custom_call" | custom-call | bytes 9000000 | tf_op jit(solution)/shard_map/pallas_call | solution.py:365
  19.3 0.0 collective-permute-done.2.refs_1_
  19.4 0.1 collective-permute-start.3
  19.5 0.0 copy-start.2
  19.5 0.7 %copy-done.2 = bf16[128,128]{1,0:T(8,128)(2,1)S(1)} copy-done((bf16[128,128]{1,0:T(8,128)(2,1)S(1)}, bf16[128,128]{1,0:T(8,128)(2,1)}, u32[]{:S(2)}) %copy-start.2) | copy-done | bytes 32792
  20.2 0.0 copy-start.4
  20.2 0.7 copy-done.4
  20.9 0.4 shard_map.69
  21.3 0.8 %collective-permute-done.3.other_ref = bf16[64,128]{1,0:T(8,128)(2,1)S(1)} collective-permute-done((bf16[64,128]{1,0:T(8,128)(2,1)S(1)}, bf16[64,128]{1,0:T(8,128)(2,1)S(1)}, u32[]{:S(2)}, u32[]{:S(2)}) %collective-permute-start.3) | collective-permute-done | bytes 16416 | tf_op jit(solution)/shard_map/ppermute | solution.py:371
  22.1 0.1 shard_map.70.after_ref.refs_0_
  22.1 0.0 collective-permute-done.1.other_ref
  22.1 0.1 shard_map.71
  22.3 2.8 %collective-permute-start.5 = (bf16[128,2048]{1,0:T(8,128)(2,1)S(1)}, bf16[128,2048]{1,0:T(8,128)(2,1)S(1)}, u32[]{:S(2)}, u32[]{:S(2)}) collective-permute-start(bf16[128,2048]{1,0:T(8,128)(2,1)S(1)} %get-tuple-element.35.inner_ref), channel_id=1, source_target_pairs={{0,2},{2,0},{4,6},{6,4},{8,10},{10,8},{12,14},{14,12},{16,18},{18,... | collective-permute-start | bytes 1572872 | tf_op jit(solution)/shard_map/ppermute | solution.py:389
  25.0 3.0 %collective-permute-start.4 = (bf16[128,2048]{1,0:T(8,128)(2,1)S(1)}, bf16[128,2048]{1,0:T(8,128)(2,1)S(1)}, u32[]{:S(2)}, u32[]{:S(2)}) collective-permute-start(bf16[128,2048]{1,0:T(8,128)(2,1)S(1)} %get-tuple-element.34.refs_4_.outer_ref), channel_id=1, source_target_pairs={{2,4},{4,2},{6,8},{8,6},{10,12},{12,10},{14,16},{16,14},{18,20},{2... | collective-permute-start | bytes 1572872 | tf_op jit(solution)/shard_map/ppermute | solution.py:390
  28.1 2.8 %collective-permute-start.8 = (bf16[128,128]{1,0:T(8,128)(2,1)S(1)}, bf16[128,128]{1,0:T(8,128)(2,1)S(1)}, u32[]{:S(2)}, u32[]{:S(2)}) collective-permute-start(bf16[128,128]{1,0:T(8,128)(2,1)S(1)} %shard_map.70.after_ref.refs_0_), channel_id=1, source_target_pairs={{0,48},{2,50},{4,52},{6,54},{8,56},{10,58},{12,60},{14,62},{16,32}... | collective-permute-start | bytes 98312 | tf_op jit(solution)/shard_map/ppermute | solution.py:345
  30.9 0.0 collective-permute-start.7
  30.9 0.8 %collective-permute-start.6 = (bf16[128,128]{1,0:T(8,128)(2,1)S(1)}, bf16[128,128]{1,0:T(8,128)(2,1)S(1)}, u32[]{:S(2)}, u32[]{:S(2)}) collective-permute-start(bf16[128,128]{1,0:T(8,128)(2,1)S(1)} %shard_map.70.after_ref.refs_0_), channel_id=1, source_target_pairs={{0,16},{2,18},{4,20},{6,22},{8,24},{10,26},{12,28},{14,30},{16,0},... | collective-permute-start | bytes 98312 | tf_op jit(solution)/shard_map/ppermute | solution.py:345
  31.7 1.1 %collective-permute-done.8.refs_3_ = bf16[128,128]{1,0:T(8,128)(2,1)S(1)} collective-permute-done((bf16[128,128]{1,0:T(8,128)(2,1)S(1)}, bf16[128,128]{1,0:T(8,128)(2,1)S(1)}, u32[]{:S(2)}, u32[]{:S(2)}) %collective-permute-start.8) | collective-permute-done | bytes 32800 | tf_op jit(solution)/shard_map/ppermute | solution.py:345
  32.8 2.1 %collective-permute-done.7.refs_2_ = bf16[128,128]{1,0:T(8,128)(2,1)S(1)} collective-permute-done((bf16[128,128]{1,0:T(8,128)(2,1)S(1)}, bf16[128,128]{1,0:T(8,128)(2,1)S(1)}, u32[]{:S(2)}, u32[]{:S(2)}) %collective-permute-start.7) | collective-permute-done | bytes 32800 | tf_op jit(solution)/shard_map/ppermute | solution.py:345
  35.0 0.0 collective-permute-done.6.refs_1_
  35.0 3.7 %collective-permute-start.11 = (bf16[512,128]{1,0:T(8,128)(2,1)S(1)}, bf16[512,128]{1,0:T(8,128)(2,1)S(1)}, u32[]{:S(2)}, u32[]{:S(2)}) collective-permute-start(bf16[512,128]{1,0:T(8,128)(2,1)S(1)} %shard_map.72.after_ref.refs_0_), channel_id=1, source_target_pairs={{0,12},{2,14},{4,8},{6,10},{8,4},{10,6},{12,0},{14,2},{16,28},{18,... | collective-permute-start | bytes 393224 | tf_op jit(solution)/shard_map/ppermute | solution.py:345
  38.7 0.0 collective-permute-start.10
  38.7 0.7 collective-permute-start.9
  39.4 0.0 collective-permute-done.5.inner_halo_ref
  39.4 0.0 collective-permute-done.4.outer_halo_ref
  39.4 1.2 %shard_map.73.frame_ref.frame_in = f32[12296,128]{1,0:T(8,128)S(1)} custom-call(bf16[128,2048]{1,0:T(8,128)(2,1)S(1)} %collective-permute-done.4.outer_halo_ref, bf16[128,2048]{1,0:T(8,128)(2,1)S(1)} %get-tuple-element.34.refs_4_.outer_ref, bf16[128,2048]{1,0:T(8,128)(2,1)S(1)} %get-tuple-element.35.inner_ref, ...), custom_call_target="tpu_custom_call" | custom-call | bytes 6000000 | tf_op jit(solution)/shard_map/pallas_call | solution.py:396
  40.6 4.1 %shard_map.74.refs_4_.refs_0_ = f32[1024,128]{1,0:T(8,128)S(1)} custom-call(s32[16384]{0:T(1024)S(1)} %bitcast.15, s32[1024]{0:T(1024)S(1)} %bitcast.21, s32[1024]{0:T(1024)S(1)} %bitcast.23, f32[12296,128]{1,0:T(8,128)S(1)} %shard_map.73.frame_ref.frame_in, bf16[512,128]{1,0:T(8,128)(2,1)S(1)} %shard_map.72.after_ref.refs_0_), custom_call_target="tpu_custom_call" | custom-call | bytes 12000000 | tf_op jit(solution)/shard_map/pallas_call | solution.py:412
  44.8 0.0 collective-permute-done.11.refs_3_
  44.8 0.0 collective-permute-done.10.refs_2_
  44.8 0.0 collective-permute-done.9.refs_1_
  44.9 5.9 %collective-permute-start.12 = (bf16[2048,128]{1,0:T(8,128)(2,1)S(1)}, bf16[2048,128]{1,0:T(8,128)(2,1)S(1)}, u32[]{:S(2)}, u32[]{:S(2)}) collective-permute-start(bf16[2048,128]{1,0:T(8,128)(2,1)S(1)} %shard_map.75.after_ref.near_ref), channel_id=1, source_target_pairs={{0,2},{2,0},{4,6},{6,4},{8,10},{10,8},{12,14},{14,12},{16,18},{18,... | collective-permute-start | bytes 1572872 | tf_op jit(solution)/shard_map/ppermute | solution.py:345
  50.8 4.4 %shard_map.76.after_ref.refs_1_ = f32[1024,128]{1,0:T(8,128)S(1)} custom-call(s32[16384]{0:T(1024)S(1)} %bitcast.16, s32[1024]{0:T(1024)S(1)} %bitcast.22, s32[1024]{0:T(1024)S(1)} %bitcast.24, f32[12296,128]{1,0:T(8,128)S(1)} %shard_map.73.frame_ref.frame_in, bf16[2048,128]{1,0:T(8,128)(2,1)S(1)} %shard_map.75.after_ref.near_ref), custom_call_target="tpu_custom_call" | custom-call | bytes 12000000 | tf_op jit(solution)/shard_map/pallas_call | solution.py:412
  55.2 0.0 collective-permute-done.12.far_ref
  55.2 0.1 shard_map.77.frame_ref
  55.3 3.2 %shard_map.78 = (bf16[64,1024]{1,0:T(8,128)(2,1)S(1)}, bf16[128,1024]{1,0:T(8,128)(2,1)S(1)}) custom-call(s32[16384]{0:T(1024)S(1)} %bitcast.18, s32[1024]{0:T(1024)S(1)} %bitcast.25, s32[1024]{0:T(1024)S(1)} %bitcast.26, f32[12296,128]{1,0:T(8,128)S(1)} %shard_map.77.frame_ref, f32[2048,128]{1,0:T(8,128)S(1)} %get-tuple-element.33.after_ref.scale_ref, ...), custom_call_target="tpu_custom_call" | custom-call | bytes 9000000 | tf_op jit(solution)/shard_map/pallas_call | solution.py:433
  58.5 0.1 collective-permute-start.13
  58.6 8.1 %shard_map.79 = (bf16[64,1024]{1,0:T(8,128)(2,1)S(1)}, bf16[64,1024]{1,0:T(8,128)(2,1)S(1)}) custom-call(s32[16384]{0:T(1024)S(1)} %bitcast.17, s32[1024]{0:T(1024)S(1)} %bitcast.27, s32[1024]{0:T(1024)S(1)} %bitcast.28, f32[12296,128]{1,0:T(8,128)S(1)} %shard_map.77.frame_ref, f32[2048,128]{1,0:T(8,128)S(1)} %get-tuple-element.33.after_ref.scale_ref, ...), custom_call_target="tpu_custom_call" | custom-call | bytes 24000000 | tf_op jit(solution)/shard_map/pallas_call | solution.py:433
  66.7 1.4 %collective-permute-start.14 = (bf16[64,1024]{1,0:T(8,128)(2,1)S(1)}, bf16[64,1024]{1,0:T(8,128)(2,1)S(1)}, u32[]{:S(2)}, u32[]{:S(2)}) collective-permute-start(bf16[64,1024]{1,0:T(8,128)(2,1)S(1)} %get-tuple-element.46), channel_id=1, source_target_pairs={{0,1},{1,0},{2,3},{3,2},{4,5},{5,4},{6,7},{7,6},{8,9},{9,8},{10,11... | collective-permute-start | bytes 393224 | tf_op jit(solution)/shard_map/ppermute | solution.py:448
  68.0 4.2 %collective-permute-done.14.refs_3_ = bf16[64,1024]{1,0:T(8,128)(2,1)S(1)} collective-permute-done((bf16[64,1024]{1,0:T(8,128)(2,1)S(1)}, bf16[64,1024]{1,0:T(8,128)(2,1)S(1)}, u32[]{:S(2)}, u32[]{:S(2)}) %collective-permute-start.14) | collective-permute-done | bytes 131104 | tf_op jit(solution)/shard_map/ppermute | solution.py:448
  72.2 0.0 collective-permute-done.13.refs_2_
  72.2 0.8 %shard_map.80 = bf16[64,4096]{1,0:T(8,128)(2,1)} custom-call(bf16[64,1024]{1,0:T(8,128)(2,1)S(1)} %get-tuple-element.40.after_ref.refs_0_, bf16[64,1024]{1,0:T(8,128)(2,1)S(1)} %get-tuple-element.44.refs_1_, bf16[128,1024]{1,0:T(8,128)(2,1)S(1)} %collective-permute-done.13.refs_2_, bf16[64,1024]{1,0:T(8,128)(2,1)S(1)} %collective-permute-done.14.refs_3_), custom_call_target="tpu_custom_call" | custom-call | bytes 1500000 | tf_op jit(solution)/shard_map/pallas_call | solution.py:450
  (4 shorter events, 0.1 us)
Async XLA Ops:
  0.0 22.1 %collective-permute-start.1 = (bf16[64,4096]{1,0:T(8,128)(2,1)}, bf16[64,4096]{1,0:T(8,128)(2,1)S(1)}, u32[]{:S(2)}, u32[]{:S(2)}) collective-permute-start(bf16[64,4096]{1,0:T(8,128)(2,1)} %x_ref.1), channel_id=1, source_target_pairs={{0,1},{1,0},{2,3},{3,2},{4,5},{5,4},{6,7},{7,6},{8,9},{9,8},{10,11... | collective-permute-start | bytes 1572872 | tf_op jit(solution)/shard_map/ppermute | solution.py:361
  2.1 1.1 %copy-start = (bf16[64,4096]{1,0:T(8,128)(2,1)S(1)}, bf16[64,4096]{1,0:T(8,128)(2,1)}, u32[]{:S(2)}) copy-start(bf16[64,4096]{1,0:T(8,128)(2,1)} %x_ref.1) | copy-start | bytes 1572868
  3.2 0.7 copy-start.3
  4.3 8.8 %collective-permute-start = (bf16[16,128]{1,0:T(8,128)(2,1)S(1)}, bf16[16,128]{1,0:T(8,128)(2,1)S(1)}, u32[]{:S(2)}, u32[]{:S(2)}) collective-permute-start(bf16[16,128]{1,0:T(8,128)(2,1)S(1)} %get-tuple-element.26.after_ref.refs_0_), channel_id=1, source_target_pairs={{0,64},{2,66},{4,68},{6,70},{8,72},{10,74},{12,76},{14,78},{16,80}... | collective-permute-start | bytes 12296 | tf_op jit(solution)/shard_map/ppermute | solution.py:345
  12.2 0.7 copy-start.1
  13.1 6.3 %collective-permute-start.2 = (bf16[32,128]{1,0:T(8,128)(2,1)S(1)}, bf16[32,128]{1,0:T(8,128)(2,1)S(1)}, u32[]{:S(2)}, u32[]{:S(2)}) collective-permute-start(bf16[32,128]{1,0:T(8,128)(2,1)S(1)} %shard_map.66.after_ref.refs_0_), channel_id=1, source_target_pairs={{0,128},{2,130},{4,132},{6,134},{8,136},{10,138},{12,140},{14,142}... | collective-permute-start | bytes 24584 | tf_op jit(solution)/shard_map/ppermute | solution.py:345
  19.4 2.7 %collective-permute-start.3 = (bf16[64,128]{1,0:T(8,128)(2,1)S(1)}, bf16[64,128]{1,0:T(8,128)(2,1)S(1)}, u32[]{:S(2)}, u32[]{:S(2)}) collective-permute-start(bf16[64,128]{1,0:T(8,128)(2,1)S(1)} %shard_map.68.after_ref.mine_ref), channel_id=1, source_target_pairs={{0,1},{1,0},{2,3},{3,2},{4,5},{5,4},{6,7},{7,6},{8,9},{9,8},{10,11... | collective-permute-start | bytes 49160 | tf_op jit(solution)/shard_map/ppermute | solution.py:371
  19.5 0.8 %copy-start.2 = (bf16[128,128]{1,0:T(8,128)(2,1)S(1)}, bf16[128,128]{1,0:T(8,128)(2,1)}, u32[]{:S(2)}) copy-start(bf16[128,128]{1,0:T(8,128)(2,1)} %weight_ref.1) | copy-start | bytes 98308
  20.2 0.7 copy-start.4
  22.3 17.1 %collective-permute-start.5 = (bf16[128,2048]{1,0:T(8,128)(2,1)S(1)}, bf16[128,2048]{1,0:T(8,128)(2,1)S(1)}, u32[]{:S(2)}, u32[]{:S(2)}) collective-permute-start(bf16[128,2048]{1,0:T(8,128)(2,1)S(1)} %get-tuple-element.35.inner_ref), channel_id=1, source_target_pairs={{0,2},{2,0},{4,6},{6,4},{8,10},{10,8},{12,14},{14,12},{16,18},{18,... | collective-permute-start | bytes 1572872 | tf_op jit(solution)/shard_map/ppermute | solution.py:389
  25.0 14.3 %collective-permute-start.4 = (bf16[128,2048]{1,0:T(8,128)(2,1)S(1)}, bf16[128,2048]{1,0:T(8,128)(2,1)S(1)}, u32[]{:S(2)}, u32[]{:S(2)}) collective-permute-start(bf16[128,2048]{1,0:T(8,128)(2,1)S(1)} %get-tuple-element.34.refs_4_.outer_ref), channel_id=1, source_target_pairs={{2,4},{4,2},{6,8},{8,6},{10,12},{12,10},{14,16},{16,14},{18,20},{2... | collective-permute-start | bytes 1572872 | tf_op jit(solution)/shard_map/ppermute | solution.py:390
  28.1 4.8 %collective-permute-start.8 = (bf16[128,128]{1,0:T(8,128)(2,1)S(1)}, bf16[128,128]{1,0:T(8,128)(2,1)S(1)}, u32[]{:S(2)}, u32[]{:S(2)}) collective-permute-start(bf16[128,128]{1,0:T(8,128)(2,1)S(1)} %shard_map.70.after_ref.refs_0_), channel_id=1, source_target_pairs={{0,48},{2,50},{4,52},{6,54},{8,56},{10,58},{12,60},{14,62},{16,32}... | collective-permute-start | bytes 98312 | tf_op jit(solution)/shard_map/ppermute | solution.py:345
  30.9 4.1 %collective-permute-start.7 = (bf16[128,128]{1,0:T(8,128)(2,1)S(1)}, bf16[128,128]{1,0:T(8,128)(2,1)S(1)}, u32[]{:S(2)}, u32[]{:S(2)}) collective-permute-start(bf16[128,128]{1,0:T(8,128)(2,1)S(1)} %shard_map.70.after_ref.refs_0_), channel_id=1, source_target_pairs={{0,32},{2,34},{4,36},{6,38},{8,40},{10,42},{12,44},{14,46},{16,48}... | collective-permute-start | bytes 98312 | tf_op jit(solution)/shard_map/ppermute | solution.py:345
  30.9 4.1 %collective-permute-start.6 = (bf16[128,128]{1,0:T(8,128)(2,1)S(1)}, bf16[128,128]{1,0:T(8,128)(2,1)S(1)}, u32[]{:S(2)}, u32[]{:S(2)}) collective-permute-start(bf16[128,128]{1,0:T(8,128)(2,1)S(1)} %shard_map.70.after_ref.refs_0_), channel_id=1, source_target_pairs={{0,16},{2,18},{4,20},{6,22},{8,24},{10,26},{12,28},{14,30},{16,0},... | collective-permute-start | bytes 98312 | tf_op jit(solution)/shard_map/ppermute | solution.py:345
  35.0 9.8 %collective-permute-start.11 = (bf16[512,128]{1,0:T(8,128)(2,1)S(1)}, bf16[512,128]{1,0:T(8,128)(2,1)S(1)}, u32[]{:S(2)}, u32[]{:S(2)}) collective-permute-start(bf16[512,128]{1,0:T(8,128)(2,1)S(1)} %shard_map.72.after_ref.refs_0_), channel_id=1, source_target_pairs={{0,12},{2,14},{4,8},{6,10},{8,4},{10,6},{12,0},{14,2},{16,28},{18,... | collective-permute-start | bytes 393224 | tf_op jit(solution)/shard_map/ppermute | solution.py:345
  38.7 6.1 %collective-permute-start.10 = (bf16[512,128]{1,0:T(8,128)(2,1)S(1)}, bf16[512,128]{1,0:T(8,128)(2,1)S(1)}, u32[]{:S(2)}, u32[]{:S(2)}) collective-permute-start(bf16[512,128]{1,0:T(8,128)(2,1)S(1)} %shard_map.72.after_ref.refs_0_), channel_id=1, source_target_pairs={{0,8},{2,10},{4,12},{6,14},{8,0},{10,2},{12,4},{14,6},{16,24},{18,... | collective-permute-start | bytes 393224 | tf_op jit(solution)/shard_map/ppermute | solution.py:345
  38.7 6.1 %collective-permute-start.9 = (bf16[512,128]{1,0:T(8,128)(2,1)S(1)}, bf16[512,128]{1,0:T(8,128)(2,1)S(1)}, u32[]{:S(2)}, u32[]{:S(2)}) collective-permute-start(bf16[512,128]{1,0:T(8,128)(2,1)S(1)} %shard_map.72.after_ref.refs_0_), channel_id=1, source_target_pairs={{0,4},{2,6},{4,0},{6,2},{8,12},{10,14},{12,8},{14,10},{16,20},{18,... | collective-permute-start | bytes 393224 | tf_op jit(solution)/shard_map/ppermute | solution.py:345
  44.9 10.3 %collective-permute-start.12 = (bf16[2048,128]{1,0:T(8,128)(2,1)S(1)}, bf16[2048,128]{1,0:T(8,128)(2,1)S(1)}, u32[]{:S(2)}, u32[]{:S(2)}) collective-permute-start(bf16[2048,128]{1,0:T(8,128)(2,1)S(1)} %shard_map.75.after_ref.near_ref), channel_id=1, source_target_pairs={{0,2},{2,0},{4,6},{6,4},{8,10},{10,8},{12,14},{14,12},{16,18},{18,... | collective-permute-start | bytes 1572872 | tf_op jit(solution)/shard_map/ppermute | solution.py:345
  58.5 13.7 %collective-permute-start.13 = (bf16[128,1024]{1,0:T(8,128)(2,1)S(1)}, bf16[128,1024]{1,0:T(8,128)(2,1)S(1)}, u32[]{:S(2)}, u32[]{:S(2)}) collective-permute-start(bf16[128,1024]{1,0:T(8,128)(2,1)S(1)} %get-tuple-element.45), channel_id=1, source_target_pairs={{0,1},{1,0},{2,3},{3,2},{4,5},{5,4},{6,7},{7,6},{8,9},{9,8},{10,11... | collective-permute-start | bytes 786440 | tf_op jit(solution)/shard_map/ppermute | solution.py:448
  66.7 5.5 %collective-permute-start.14 = (bf16[64,1024]{1,0:T(8,128)(2,1)S(1)}, bf16[64,1024]{1,0:T(8,128)(2,1)S(1)}, u32[]{:S(2)}, u32[]{:S(2)}) collective-permute-start(bf16[64,1024]{1,0:T(8,128)(2,1)S(1)} %get-tuple-element.46), channel_id=1, source_target_pairs={{0,1},{1,0},{2,3},{3,2},{4,5},{5,4},{6,7},{7,6},{8,9},{9,8},{10,11... | collective-permute-start | bytes 393224 | tf_op jit(solution)/shard_map/ppermute | solution.py:448

commit v9 on v7

--- a/solution.py
+++ b/solution.py
@@ -12,30 +12,21 @@
 LANES = 128
 CHUNK = 1024
 GROUP = 16
-STAGES = ((32,), (64,), (8, 16, 24), (2, 4, 6), (1,))
-
-
-def hub_pick_kernel(rows_ref, x_hbm, out_ref, x_ref, sem):
+STAGES = ((32,), (64,), (8, 16, 24), (4,), (2,), (1,))
+
+
+def hub_pick_kernel(rows_ref, x_ref, out_ref, x_out_ref):
     hubs, nodes = rows_ref.shape[1], x_ref.shape[1]
-    parts = sem.shape[0]
-    copies = [
-        pltpu.make_async_copy(x_hbm.at[:, part], x_ref.at[:, part], sem.at[i])
-        for i in range(parts)
-        for part in [pl.ds(i * (nodes // parts), nodes // parts)]
-    ]
-    for copy in copies:
-        copy.start()
     diagonal = lax.broadcasted_iota(jnp.int32, (hubs, hubs), 0) == lax.broadcasted_iota(
         jnp.int32, (hubs, hubs), 1
     )
     rows = jnp.sum(jnp.where(diagonal, rows_ref[...], 0), axis=1, keepdims=True)
     onehot = (lax.broadcasted_iota(jnp.int32, (hubs, nodes), 1) == rows).astype(jnp.bfloat16)
-    for copy in copies:
-        copy.wait()
     picked = lax.dot_general(
         onehot, x_ref[...], (((1,), (1,)), ((), ())), preferred_element_type=jnp.float32
     ).astype(jnp.bfloat16)
     out_ref[...] = jnp.concatenate([picked[: hubs // 2], picked[hubs // 2 :]], axis=1)
+    x_out_ref[...] = x_ref[...]
 
 
 def join_kernel(*refs):
@@ -345,11 +336,8 @@
     def i32(*shape):
         return jax.ShapeDtypeStruct(shape, jnp.int32)
 
-    block = pallas(
-        hub_pick_kernel,
-        bf16(hubs // 2, 2 * chans),
-        [IN_VMEM, ANYWHERE],
-        [VMEM((chans, nodes), jnp.bfloat16), pltpu.SemaphoreType.DMA((4,))],
+    block, own_feats = pallas(
+        hub_pick_kernel, (bf16(hubs // 2, 2 * chans), bf16(chans, nodes)), [IN_VMEM] * 2
     )(hub_rows[None, :], node_feats)
     arrived = None
 
@@ -389,7 +377,7 @@
         [ANYWHERE] * 3,
         [pltpu.SemaphoreType.DMA((4,))],
         us=0.1,
-    )(node_feats, other, block)
+    )(own_feats, other, block)
     inner_halo = lax.ppermute(inner, "slab", [(i, i ^ 1) for i in range(slabs)])
     outer_halo = lax.ppermute(
         outer, "slab", [(i, j) for i in range(slabs) for j in [i + 2 * (i & 1) - 1] if 0 <= j < slabs]
@@ -434,6 +422,8 @@
     block = join(block, arrived, near[0])
     arrived = stage(block, STAGES[4])
     near.append(near_sum(1, block))
+    block = join(block, arrived, near[1])
+    arrived = stage(block, STAGES[5])
     frame = pallas(
         functools.partial(hub_frame_kernel, frame_rows, hubs),
         f32(*frame.shape),

time: 73.4 us -> 76.3 us (1.040)
  waiting for transfers between devices: 10.6 us -> 17.7 us
  starting transfers between devices: 29.7 us -> 25.9 us
    ppermute x1, waiting for transfers between devices: 0.26 us -> 4.43 us  [local(): lax.ppermute(outer, 'slab', [(i, j) for i in range(slabs) for j in [i + 2...]
    ppermute x9 -> x8, waiting for transfers between devices: 4.27 us -> 8.34 us  [stage(): lax.ppermute(block, 'slab', [(i, i ^ bit) for i in range(slabs)])]
    ppermute x9 -> x8, starting transfers between devices: 16.6 us -> 12.8 us  [stage(): lax.ppermute(block, 'slab', [(i, i ^ bit) for i in range(slabs)])]
  transfers between devices with their start and end apart: 15 -> 14, of which waited for: 6 -> 8; matrix products, arithmetic and copies ran while one was open for 1% -> 1% of each run, Pallas kernels for 30% -> 29%
where the time goes in v9:
time: 76.3 us; the launch traced here: 75.9 us
  Pallas kernels  26.5 us (35%)
  starting transfers between devices  25.9 us (34%)
  waiting for transfers between devices  17.7 us (23%)
  local copies, waits for them, and re-layouts  5.57 us (7%)
    ppermute x8, starting transfers between devices, stage(): lax.ppermute(block, 'slab', [(i, i ^ bit) for i in range(slabs)])  12.8 us
    pallas_call x2, Pallas kernels, layer(): pallas(functools.partial(layer_kernel, slots, first, start, len(near), ha...  11.3 us
    ppermute x1, starting transfers between devices, local(): lax.ppermute(outer, 'slab', [(i, j) for i in range(slabs) for j in [i + 2...  8.81 us
    ppermute x8, waiting for transfers between devices, stage(): lax.ppermute(block, 'slab', [(i, i ^ bit) for i in range(slabs)])  8.34 us
    pallas_call x2, Pallas kernels, near_sum(): pallas(functools.partial(near_kernel, slots, part, 2), f32(CHUNK, LANES),...  8.24 us
    unnamed x13, local copies, waits for them, and re-layouts  5.57 us
    ppermute x1, waiting for transfers between devices, local(): lax.ppermute(outer, 'slab', [(i, j) for i in range(slabs) for j in [i + 2...  4.43 us
    ppermute x2, waiting for transfers between devices, local(): received.append(lax.ppermute(sent, 'feat', swap))  3.91 us
  transfers between devices with their start and end apart: 14, of which 8 were waited for; matrix products, arithmetic and copies ran while one was open for 1% of the time, Pallas kernels for 29%

profile of v9, /device:TPU:16, one launch (start us, length us, event | category | flops | bytes accessed | tf_op | source)
XLA Modules:
  0.0 75.9 jit_solution(14332354473059175104)
XLA Ops:
  0.0 1.3 %collective-permute-start.1 = (bf16[64,4096]{1,0:T(8,128)(2,1)}, bf16[64,4096]{1,0:T(8,128)(2,1)S(1)}, u32[]{:S(2)}, u32[]{:S(2)}) collective-permute-start(bf16[64,4096]{1,0:T(8,128)(2,1)} %x_ref.1), channel_id=1, source_target_pairs={{0,1},{1,0},{2,3},{3,2},{4,5},{5,4},{6,7},{7,6},{8,9},{9,8},{10,11... | collective-permute-start | bytes 1572872 | tf_op jit(solution)/shard_map/ppermute | solution.py:361
  1.3 0.0 copy-start
  1.3 1.1 %copy-done = bf16[64,4096]{1,0:T(8,128)(2,1)S(1)} copy-done((bf16[64,4096]{1,0:T(8,128)(2,1)S(1)}, bf16[64,4096]{1,0:T(8,128)(2,1)}, u32[]{:S(2)}) %copy-start) | copy-done | bytes 524312
  2.4 0.0 copy-start.4
  2.4 0.7 copy-done.4
  3.0 0.4 shard_map.64
  3.5 7.2 %collective-permute-start = (bf16[16,128]{1,0:T(8,128)(2,1)S(1)}, bf16[16,128]{1,0:T(8,128)(2,1)S(1)}, u32[]{:S(2)}, u32[]{:S(2)}) collective-permute-start(bf16[16,128]{1,0:T(8,128)(2,1)S(1)} %get-tuple-element.26.after_ref.refs_0_), channel_id=1, source_target_pairs={{0,64},{2,66},{4,68},{6,70},{8,72},{10,74},{12,76},{14,78},{16,80}... | collective-permute-start | bytes 12296 | tf_op jit(solution)/shard_map/ppermute | solution.py:345
  10.7 1.0 %copy.8 = s32[2,8,32,128]{3,2,1,0:T(8,128)S(1)} copy(s32[2,8,32,128]{3,1,2,0:T(8,128)} %bitcast.31) | data formatting | bytes 524288
  11.7 0.0 copy-start.1
  11.7 0.7 copy-done.1
  12.4 0.1 shard_map.65
  12.5 0.0 collective-permute-done.refs_1_
  12.5 0.7 collective-permute-start.2
  13.2 3.5 %shard_map.67 = (s32[8,128]{1,0:T(8,128)S(1)}, s32[8,128]{1,0:T(8,128)S(1)}, s32[8,128]{1,0:T(8,128)S(1)}, s32[8,128]{1,0:T(8,128)S(1)}, s32[8,128]{1,0:T(8,128)S(1)}, /*index=5*/s32[8,128]{1,0:T(8,128)S(1)}) custom-call(s32[3,8,128]{2,1,0:T(8,128)S(1)} %get-tuple-element.28.refs_2_.counts_ref, bf16[32,128]{1,0:T(8,128)(2,1)S(1)} %shard_map.66.after_ref.refs_0_), custom_call_target="tpu_custom_call" | custom-call | bytes 9000000 | tf_op jit(solution)/shard_map/pallas_call | solution.py:365
  16.8 1.0 %collective-permute-done.2.refs_1_ = bf16[32,128]{1,0:T(8,128)(2,1)S(1)} collective-permute-done((bf16[32,128]{1,0:T(8,128)(2,1)S(1)}, bf16[32,128]{1,0:T(8,128)(2,1)S(1)}, u32[]{:S(2)}, u32[]{:S(2)}) %collective-permute-start.2) | collective-permute-done | bytes 8224 | tf_op jit(solution)/shard_map/ppermute | solution.py:345
  17.8 3.0 %collective-permute-start.5 = (bf16[64,128]{1,0:T(8,128)(2,1)S(1)}, bf16[64,128]{1,0:T(8,128)(2,1)S(1)}, u32[]{:S(2)}, u32[]{:S(2)}) collective-permute-start(bf16[64,128]{1,0:T(8,128)(2,1)S(1)} %shard_map.68.refs_0_), channel_id=1, source_target_pairs={{0,48},{2,50},{4,52},{6,54},{8,56},{10,58},{12,60},{14,62},{16,32}... | collective-permute-start | bytes 49160 | tf_op jit(solution)/shard_map/ppermute | solution.py:345
  20.8 0.0 collective-permute-start.4
  20.8 1.4 %collective-permute-start.3 = (bf16[64,128]{1,0:T(8,128)(2,1)S(1)}, bf16[64,128]{1,0:T(8,128)(2,1)S(1)}, u32[]{:S(2)}, u32[]{:S(2)}) collective-permute-start(bf16[64,128]{1,0:T(8,128)(2,1)S(1)} %shard_map.68.refs_0_), channel_id=1, source_target_pairs={{0,16},{2,18},{4,20},{6,22},{8,24},{10,26},{12,28},{14,30},{16,0},... | collective-permute-start | bytes 49160 | tf_op jit(solution)/shard_map/ppermute | solution.py:345
  22.2 1.1 %collective-permute-done.5.refs_3_ = bf16[64,128]{1,0:T(8,128)(2,1)S(1)} collective-permute-done((bf16[64,128]{1,0:T(8,128)(2,1)S(1)}, bf16[64,128]{1,0:T(8,128)(2,1)S(1)}, u32[]{:S(2)}, u32[]{:S(2)}) %collective-permute-start.5) | collective-permute-done | bytes 16416 | tf_op jit(solution)/shard_map/ppermute | solution.py:345
  23.3 2.1 %collective-permute-done.4.refs_2_ = bf16[64,128]{1,0:T(8,128)(2,1)S(1)} collective-permute-done((bf16[64,128]{1,0:T(8,128)(2,1)S(1)}, bf16[64,128]{1,0:T(8,128)(2,1)S(1)}, u32[]{:S(2)}, u32[]{:S(2)}) %collective-permute-start.4) | collective-permute-done | bytes 16416 | tf_op jit(solution)/shard_map/ppermute | solution.py:345
  25.4 0.0 collective-permute-done.3.refs_1_
  25.4 0.0 collective-permute-done.1.other_ref
  25.4 0.1 shard_map.70
  25.6 0.1 collective-permute-start.7
  25.7 8.8 %collective-permute-start.6 = (bf16[128,2048]{1,0:T(8,128)(2,1)S(1)}, bf16[128,2048]{1,0:T(8,128)(2,1)S(1)}, u32[]{:S(2)}, u32[]{:S(2)}) collective-permute-start(bf16[128,2048]{1,0:T(8,128)(2,1)S(1)} %get-tuple-element.33.after_ref.outer_ref), channel_id=1, source_target_pairs={{2,4},{4,2},{6,8},{8,6},{10,12},{12,10},{14,16},{16,14},{18,20},{2... | collective-permute-start | bytes 1572872 | tf_op jit(solution)/shard_map/ppermute | solution.py:382
  34.5 0.8 %collective-permute-start.8 = (bf16[256,128]{1,0:T(8,128)(2,1)S(1)}, bf16[256,128]{1,0:T(8,128)(2,1)S(1)}, u32[]{:S(2)}, u32[]{:S(2)}) collective-permute-start(bf16[256,128]{1,0:T(8,128)(2,1)S(1)} %shard_map.69.after_ref.mine_ref), channel_id=1, source_target_pairs={{0,1},{1,0},{2,3},{3,2},{4,5},{5,4},{6,7},{7,6},{8,9},{9,8},{10,11... | collective-permute-start | bytes 196616 | tf_op jit(solution)/shard_map/ppermute | solution.py:386
  35.3 0.0 copy-start.2
  35.3 0.7 copy-done.2
  36.0 0.0 copy-start.3
  36.1 0.8 copy-done.3
  36.8 0.0 copy-start.5
  36.8 0.7 copy-done.5
  37.5 0.4 shard_map.71
  37.8 1.0 %collective-permute-done.8.other_ref = bf16[256,128]{1,0:T(8,128)(2,1)S(1)} collective-permute-done((bf16[256,128]{1,0:T(8,128)(2,1)S(1)}, bf16[256,128]{1,0:T(8,128)(2,1)S(1)}, u32[]{:S(2)}, u32[]{:S(2)}) %collective-permute-start.8) | collective-permute-done | bytes 65568 | tf_op jit(solution)/shard_map/ppermute | solution.py:386
  38.9 0.1 shard_map.72.after_ref.refs_0_
  39.0 0.1 collective-permute-start.9
  39.1 0.0 collective-permute-done.7.inner_halo_ref
  39.1 4.4 %collective-permute-done.6.outer_halo_ref = bf16[128,2048]{1,0:T(8,128)(2,1)S(1)} collective-permute-done((bf16[128,2048]{1,0:T(8,128)(2,1)S(1)}, bf16[128,2048]{1,0:T(8,128)(2,1)S(1)}, u32[]{:S(2)}, u32[]{:S(2)}) %collective-permute-start.6) | collective-permute-done | bytes 524320 | tf_op jit(solution)/shard_map/ppermute | solution.py:382
  43.5 1.2 %shard_map.73.frame_ref.frame_in = f32[12296,128]{1,0:T(8,128)S(1)} custom-call(bf16[128,2048]{1,0:T(8,128)(2,1)S(1)} %collective-permute-done.6.outer_halo_ref, bf16[128,2048]{1,0:T(8,128)(2,1)S(1)} %get-tuple-element.33.after_ref.outer_ref, bf16[128,2048]{1,0:T(8,128)(2,1)S(1)} %get-tuple-element.34.inner_ref, ...), custom_call_target="tpu_custom_call" | custom-call | bytes 6000000 | tf_op jit(solution)/shard_map/pallas_call | solution.py:397
  44.8 4.1 %shard_map.74.refs_2_.refs_0_ = f32[1024,128]{1,0:T(8,128)S(1)} custom-call(s32[16384]{0:T(1024)S(1)} %bitcast.15, s32[1024]{0:T(1024)S(1)} %bitcast.19, s32[1024]{0:T(1024)S(1)} %bitcast.23, f32[12296,128]{1,0:T(8,128)S(1)} %shard_map.73.frame_ref.frame_in, bf16[512,128]{1,0:T(8,128)(2,1)S(1)} %shard_map.72.after_ref.refs_0_), custom_call_target="tpu_custom_call" | custom-call | bytes 12000000 | tf_op jit(solution)/shard_map/pallas_call | solution.py:413
  48.8 0.0 collective-permute-done.9.refs_1_
  48.9 0.1 collective-permute-start.10
  49.0 4.2 %shard_map.76.refs_2_.after_ref.refs_1_ = f32[1024,128]{1,0:T(8,128)S(1)} custom-call(s32[16384]{0:T(1024)S(1)} %bitcast.16, s32[1024]{0:T(1024)S(1)} %bitcast.20, s32[1024]{0:T(1024)S(1)} %bitcast.24, f32[12296,128]{1,0:T(8,128)S(1)} %shard_map.73.frame_ref.frame_in, bf16[1024,128]{1,0:T(8,128)(2,1)S(1)} %shard_map.75.after_ref.refs_0_), custom_call_target="tpu_custom_call" | custom-call | bytes 12000000 | tf_op jit(solution)/shard_map/pallas_call | solution.py:413
  53.2 2.2 %collective-permute-done.10.refs_1_ = bf16[1024,128]{1,0:T(8,128)(2,1)S(1)} collective-permute-done((bf16[1024,128]{1,0:T(8,128)(2,1)S(1)}, bf16[1024,128]{1,0:T(8,128)(2,1)S(1)}, u32[]{:S(2)}, u32[]{:S(2)}) %collective-permute-start.10) | collective-permute-done | bytes 262176 | tf_op jit(solution)/shard_map/ppermute | solution.py:345
  55.4 0.3 collective-permute-start.11
  55.7 1.9 %collective-permute-done.11.far_ref = bf16[2048,128]{1,0:T(8,128)(2,1)S(1)} collective-permute-done((bf16[2048,128]{1,0:T(8,128)(2,1)S(1)}, bf16[2048,128]{1,0:T(8,128)(2,1)S(1)}, u32[]{:S(2)}, u32[]{:S(2)}) %collective-permute-start.11) | collective-permute-done | bytes 524320 | tf_op jit(solution)/shard_map/ppermute | solution.py:345
  57.6 0.1 shard_map.78.frame_ref
  57.7 3.2 %shard_map.79 = (bf16[64,1024]{1,0:T(8,128)(2,1)S(1)}, bf16[128,1024]{1,0:T(8,128)(2,1)S(1)}) custom-call(s32[16384]{0:T(1024)S(1)} %bitcast.18, s32[1024]{0:T(1024)S(1)} %bitcast.25, s32[1024]{0:T(1024)S(1)} %bitcast.26, f32[12296,128]{1,0:T(8,128)S(1)} %shard_map.78.frame_ref, f32[2048,128]{1,0:T(8,128)S(1)} %get-tuple-element.35.after_ref.scale_ref, ...), custom_call_target="tpu_custom_call" | custom-call | bytes 9000000 | tf_op jit(solution)/shard_map/pallas_call | solution.py:436
  60.9 0.8 %collective-permute-start.12 = (bf16[128,1024]{1,0:T(8,128)(2,1)S(1)}, bf16[128,1024]{1,0:T(8,128)(2,1)S(1)}, u32[]{:S(2)}, u32[]{:S(2)}) collective-permute-start(bf16[128,1024]{1,0:T(8,128)(2,1)S(1)} %get-tuple-element.45), channel_id=1, source_target_pairs={{0,1},{1,0},{2,3},{3,2},{4,5},{5,4},{6,7},{7,6},{8,9},{9,8},{10,11... | collective-permute-start | bytes 786440 | tf_op jit(solution)/shard_map/ppermute | solution.py:451
  61.7 8.1 %shard_map.80 = (bf16[64,1024]{1,0:T(8,128)(2,1)S(1)}, bf16[64,1024]{1,0:T(8,128)(2,1)S(1)}) custom-call(s32[16384]{0:T(1024)S(1)} %bitcast.17, s32[1024]{0:T(1024)S(1)} %bitcast.27, s32[1024]{0:T(1024)S(1)} %bitcast.28, f32[12296,128]{1,0:T(8,128)S(1)} %shard_map.78.frame_ref, f32[2048,128]{1,0:T(8,128)S(1)} %get-tuple-element.35.after_ref.scale_ref, ...), custom_call_target="tpu_custom_call" | custom-call | bytes 24000000 | tf_op jit(solution)/shard_map/pallas_call | solution.py:436
  69.8 1.3 %collective-permute-start.13 = (bf16[64,1024]{1,0:T(8,128)(2,1)S(1)}, bf16[64,1024]{1,0:T(8,128)(2,1)S(1)}, u32[]{:S(2)}, u32[]{:S(2)}) collective-permute-start(bf16[64,1024]{1,0:T(8,128)(2,1)S(1)} %get-tuple-element.46), channel_id=1, source_target_pairs={{0,1},{1,0},{2,3},{3,2},{4,5},{5,4},{6,7},{7,6},{8,9},{9,8},{10,11... | collective-permute-start | bytes 393224 | tf_op jit(solution)/shard_map/ppermute | solution.py:451
  71.1 3.9 %collective-permute-done.13.refs_3_ = bf16[64,1024]{1,0:T(8,128)(2,1)S(1)} collective-permute-done((bf16[64,1024]{1,0:T(8,128)(2,1)S(1)}, bf16[64,1024]{1,0:T(8,128)(2,1)S(1)}, u32[]{:S(2)}, u32[]{:S(2)}) %collective-permute-start.13) | collective-permute-done | bytes 131104 | tf_op jit(solution)/shard_map/ppermute | solution.py:451
  75.0 0.0 collective-permute-done.12.refs_2_
  75.0 0.8 %shard_map.81 = bf16[64,4096]{1,0:T(8,128)(2,1)} custom-call(bf16[64,1024]{1,0:T(8,128)(2,1)S(1)} %get-tuple-element.40.after_ref.refs_0_, bf16[64,1024]{1,0:T(8,128)(2,1)S(1)} %get-tuple-element.44.refs_1_, bf16[128,1024]{1,0:T(8,128)(2,1)S(1)} %collective-permute-done.12.refs_2_, bf16[64,1024]{1,0:T(8,128)(2,1)S(1)} %collective-permute-done.13.refs_3_), custom_call_target="tpu_custom_call" | custom-call | bytes 1500000 | tf_op jit(solution)/shard_map/pallas_call | solution.py:453
  (5 shorter events, 0.1 us)
Async XLA Ops:
  0.0 25.4 %collective-permute-start.1 = (bf16[64,4096]{1,0:T(8,128)(2,1)}, bf16[64,4096]{1,0:T(8,128)(2,1)S(1)}, u32[]{:S(2)}, u32[]{:S(2)}) collective-permute-start(bf16[64,4096]{1,0:T(8,128)(2,1)} %x_ref.1), channel_id=1, source_target_pairs={{0,1},{1,0},{2,3},{3,2},{4,5},{5,4},{6,7},{7,6},{8,9},{9,8},{10,11... | collective-permute-start | bytes 1572872 | tf_op jit(solution)/shard_map/ppermute | solution.py:361
  1.3 1.1 %copy-start = (bf16[64,4096]{1,0:T(8,128)(2,1)S(1)}, bf16[64,4096]{1,0:T(8,128)(2,1)}, u32[]{:S(2)}) copy-start(bf16[64,4096]{1,0:T(8,128)(2,1)} %x_ref.1) | copy-start | bytes 1572868
  2.4 0.7 copy-start.4
  3.5 9.0 %collective-permute-start = (bf16[16,128]{1,0:T(8,128)(2,1)S(1)}, bf16[16,128]{1,0:T(8,128)(2,1)S(1)}, u32[]{:S(2)}, u32[]{:S(2)}) collective-permute-start(bf16[16,128]{1,0:T(8,128)(2,1)S(1)} %get-tuple-element.26.after_ref.refs_0_), channel_id=1, source_target_pairs={{0,64},{2,66},{4,68},{6,70},{8,72},{10,74},{12,76},{14,78},{16,80}... | collective-permute-start | bytes 12296 | tf_op jit(solution)/shard_map/ppermute | solution.py:345
  11.7 0.7 copy-start.1
  12.5 5.2 %collective-permute-start.2 = (bf16[32,128]{1,0:T(8,128)(2,1)S(1)}, bf16[32,128]{1,0:T(8,128)(2,1)S(1)}, u32[]{:S(2)}, u32[]{:S(2)}) collective-permute-start(bf16[32,128]{1,0:T(8,128)(2,1)S(1)} %shard_map.66.after_ref.refs_0_), channel_id=1, source_target_pairs={{0,128},{2,130},{4,132},{6,134},{8,136},{10,138},{12,140},{14,142}... | collective-permute-start | bytes 24584 | tf_op jit(solution)/shard_map/ppermute | solution.py:345
  17.8 5.5 %collective-permute-start.5 = (bf16[64,128]{1,0:T(8,128)(2,1)S(1)}, bf16[64,128]{1,0:T(8,128)(2,1)S(1)}, u32[]{:S(2)}, u32[]{:S(2)}) collective-permute-start(bf16[64,128]{1,0:T(8,128)(2,1)S(1)} %shard_map.68.refs_0_), channel_id=1, source_target_pairs={{0,48},{2,50},{4,52},{6,54},{8,56},{10,58},{12,60},{14,62},{16,32}... | collective-permute-start | bytes 49160 | tf_op jit(solution)/shard_map/ppermute | solution.py:345
  20.8 4.6 %collective-permute-start.4 = (bf16[64,128]{1,0:T(8,128)(2,1)S(1)}, bf16[64,128]{1,0:T(8,128)(2,1)S(1)}, u32[]{:S(2)}, u32[]{:S(2)}) collective-permute-start(bf16[64,128]{1,0:T(8,128)(2,1)S(1)} %shard_map.68.refs_0_), channel_id=1, source_target_pairs={{0,32},{2,34},{4,36},{6,38},{8,40},{10,42},{12,44},{14,46},{16,48}... | collective-permute-start | bytes 49160 | tf_op jit(solution)/shard_map/ppermute | solution.py:345
  20.8 4.6 %collective-permute-start.3 = (bf16[64,128]{1,0:T(8,128)(2,1)S(1)}, bf16[64,128]{1,0:T(8,128)(2,1)S(1)}, u32[]{:S(2)}, u32[]{:S(2)}) collective-permute-start(bf16[64,128]{1,0:T(8,128)(2,1)S(1)} %shard_map.68.refs_0_), channel_id=1, source_target_pairs={{0,16},{2,18},{4,20},{6,22},{8,24},{10,26},{12,28},{14,30},{16,0},... | collective-permute-start | bytes 49160 | tf_op jit(solution)/shard_map/ppermute | solution.py:345
  25.6 13.5 %collective-permute-start.7 = (bf16[128,2048]{1,0:T(8,128)(2,1)S(1)}, bf16[128,2048]{1,0:T(8,128)(2,1)S(1)}, u32[]{:S(2)}, u32[]{:S(2)}) collective-permute-start(bf16[128,2048]{1,0:T(8,128)(2,1)S(1)} %get-tuple-element.34.inner_ref), channel_id=1, source_target_pairs={{0,2},{2,0},{4,6},{6,4},{8,10},{10,8},{12,14},{14,12},{16,18},{18,... | collective-permute-start | bytes 1572872 | tf_op jit(solution)/shard_map/ppermute | solution.py:381
  25.7 17.8 %collective-permute-start.6 = (bf16[128,2048]{1,0:T(8,128)(2,1)S(1)}, bf16[128,2048]{1,0:T(8,128)(2,1)S(1)}, u32[]{:S(2)}, u32[]{:S(2)}) collective-permute-start(bf16[128,2048]{1,0:T(8,128)(2,1)S(1)} %get-tuple-element.33.after_ref.outer_ref), channel_id=1, source_target_pairs={{2,4},{4,2},{6,8},{8,6},{10,12},{12,10},{14,16},{16,14},{18,20},{2... | collective-permute-start | bytes 1572872 | tf_op jit(solution)/shard_map/ppermute | solution.py:382
  34.5 4.4 %collective-permute-start.8 = (bf16[256,128]{1,0:T(8,128)(2,1)S(1)}, bf16[256,128]{1,0:T(8,128)(2,1)S(1)}, u32[]{:S(2)}, u32[]{:S(2)}) collective-permute-start(bf16[256,128]{1,0:T(8,128)(2,1)S(1)} %shard_map.69.after_ref.mine_ref), channel_id=1, source_target_pairs={{0,1},{1,0},{2,3},{3,2},{4,5},{5,4},{6,7},{7,6},{8,9},{9,8},{10,11... | collective-permute-start | bytes 196616 | tf_op jit(solution)/shard_map/ppermute | solution.py:386
  35.3 0.7 copy-start.2
  36.0 0.8 copy-start.3
  36.8 0.7 copy-start.5
  39.0 9.9 %collective-permute-start.9 = (bf16[512,128]{1,0:T(8,128)(2,1)S(1)}, bf16[512,128]{1,0:T(8,128)(2,1)S(1)}, u32[]{:S(2)}, u32[]{:S(2)}) collective-permute-start(bf16[512,128]{1,0:T(8,128)(2,1)S(1)} %shard_map.72.after_ref.refs_0_), channel_id=1, source_target_pairs={{0,8},{2,10},{4,12},{6,14},{8,0},{10,2},{12,4},{14,6},{16,24},{18,... | collective-permute-start | bytes 393224 | tf_op jit(solution)/shard_map/ppermute | solution.py:345
  48.9 6.5 %collective-permute-start.10 = (bf16[1024,128]{1,0:T(8,128)(2,1)S(1)}, bf16[1024,128]{1,0:T(8,128)(2,1)S(1)}, u32[]{:S(2)}, u32[]{:S(2)}) collective-permute-start(bf16[1024,128]{1,0:T(8,128)(2,1)S(1)} %shard_map.75.after_ref.refs_0_), channel_id=1, source_target_pairs={{0,4},{2,6},{4,0},{6,2},{8,12},{10,14},{12,8},{14,10},{16,20},{18,... | collective-permute-start | bytes 786440 | tf_op jit(solution)/shard_map/ppermute | solution.py:345
  55.4 2.2 %collective-permute-start.11 = (bf16[2048,128]{1,0:T(8,128)(2,1)S(1)}, bf16[2048,128]{1,0:T(8,128)(2,1)S(1)}, u32[]{:S(2)}, u32[]{:S(2)}) collective-permute-start(bf16[2048,128]{1,0:T(8,128)(2,1)S(1)} %shard_map.77.near_ref), channel_id=1, source_target_pairs={{0,2},{2,0},{4,6},{6,4},{8,10},{10,8},{12,14},{14,12},{16,18},{18,... | collective-permute-start | bytes 1572872 | tf_op jit(solution)/shard_map/ppermute | solution.py:345
  60.9 14.1 %collective-permute-start.12 = (bf16[128,1024]{1,0:T(8,128)(2,1)S(1)}, bf16[128,1024]{1,0:T(8,128)(2,1)S(1)}, u32[]{:S(2)}, u32[]{:S(2)}) collective-permute-start(bf16[128,1024]{1,0:T(8,128)(2,1)S(1)} %get-tuple-element.45), channel_id=1, source_target_pairs={{0,1},{1,0},{2,3},{3,2},{4,5},{5,4},{6,7},{7,6},{8,9},{9,8},{10,11... | collective-permute-start | bytes 786440 | tf_op jit(solution)/shard_map/ppermute | solution.py:451
  69.8 5.2 %collective-permute-start.13 = (bf16[64,1024]{1,0:T(8,128)(2,1)S(1)}, bf16[64,1024]{1,0:T(8,128)(2,1)S(1)}, u32[]{:S(2)}, u32[]{:S(2)}) collective-permute-start(bf16[64,1024]{1,0:T(8,128)(2,1)S(1)} %get-tuple-element.46), channel_id=1, source_target_pairs={{0,1},{1,0},{2,3},{3,2},{4,5},{5,4},{6,7},{7,6},{8,9},{9,8},{10,11... | collective-permute-start | bytes 393224 | tf_op jit(solution)/shard_map/ppermute | solution.py:451

commit v10 on v8

--- a/solution.py
+++ b/solution.py
@@ -11,7 +11,7 @@
 SMEM = pltpu.SMEM
 LANES = 128
 CHUNK = 1024
-GROUP = 16
+GROUP = 32
 STAGES = ((32,), (64,), (8, 16, 24), (2, 4, 6), (1,))
 
 
@@ -362,19 +362,15 @@
 
     block = join(block, arrived, counts)
     arrived = stage(block, STAGES[1])
-    order = pallas(order_kernel, (tile,) * 6, [IN_VMEM, ANYWHERE], us=3.0)(counts, block)
-    near_plan, far_plan, full_plan = (
-        [a.reshape(-1) for a in (ids[i], order[i], order[3 + i])] for i in range(3)
-    )
-
-    block = join(block, arrived, order[0])
-    arrived = lax.ppermute(block, "feat", swap)
     scale, by_out, bias = pallas(
         constants_kernel,
         (f32(half, LANES), bf16(2 * chans, 2 * chans), f32(LANES, LANES)),
         [IN_VMEM] * 3 + [ANYWHERE],
         us=0.1,
     )(deg_tiles, weight, bias_terms[None, :], block)
+
+    block = join(block, arrived, scale)
+    arrived = lax.ppermute(block, "feat", swap)
     block = pallas(
         join_feat_kernel, bf16(2 * block.shape[0], 2 * chans), [IN_VMEM] * 2 + [ANYWHERE], us=0.1
     )(block, arrived, scale)
@@ -391,7 +387,11 @@
         outer, "slab", [(i, j) for i in range(slabs) for j in [i + 2 * (i & 1) - 1] if 0 <= j < slabs]
     )
     arrived = stage(block, STAGES[2])
-    block = join(block, arrived, outer)
+    order = pallas(order_kernel, (tile,) * 6, [IN_VMEM, ANYWHERE], us=3.0)(counts, outer)
+    near_plan, far_plan, full_plan = (
+        [a.reshape(-1) for a in (ids[i], order[i], order[3 + i])] for i in range(3)
+    )
+    block = join(block, arrived, order[0])
     arrived = stage(block, STAGES[3])
     frame = pallas(
         frame_kernel,

time: 73.1 us -> 71.4 us (0.977)
  the two profiles are of different devices: /device:TPU:1 before, /device:TPU:16 now
where the time goes in v10:
time: 71.4 us; the launch traced here: 71 us
  starting transfers between devices  29.4 us (41%)
  Pallas kernels  25.9 us (36%)
  waiting for transfers between devices  10.5 us (15%)
  local copies, waits for them, and re-layouts  4.86 us (7%)
    ppermute x9, starting transfers between devices, stage(): lax.ppermute(block, 'slab', [(i, i ^ bit) for i in range(slabs)])  16.7 us
    pallas_call x2, Pallas kernels, layer(): pallas(functools.partial(layer_kernel, slots, first, start, len(near), ha...  11 us
    ppermute x1, starting transfers between devices, local(): lax.ppermute(outer, 'slab', [(i, j) for i in range(slabs) for j in [i + 2...  8.56 us
    pallas_call x2, Pallas kernels, near_sum(): pallas(functools.partial(near_kernel, slots, part, 2), f32(CHUNK, LANES),...  8.03 us
    unnamed x11, local copies, waits for them, and re-layouts  4.86 us
    ppermute x2, waiting for transfers between devices, local(): received.append(lax.ppermute(sent, 'feat', swap))  4.76 us
    pallas_call x1, Pallas kernels, local(): pallas(order_kernel, (tile,) * 6, [IN_VMEM, ANYWHERE], us=3.0)  3.54 us
    ppermute x1, waiting for transfers between devices, local(): arrived = lax.ppermute(block, 'feat', swap)  3 us
  transfers between devices with their start and end apart: 15, of which 3 were waited for; matrix products, arithmetic and copies ran while one was open for 1% of the time, Pallas kernels for 31%

profile of v10, /device:TPU:16, one launch (start us, length us, event | category | flops | bytes accessed | tf_op | source)
XLA Modules:
  0.0 71.0 jit_solution(2768079468536952387)
XLA Ops:
  0.0 1.3 %collective-permute-start = (bf16[64,4096]{1,0:T(8,128)(2,1)}, bf16[64,4096]{1,0:T(8,128)(2,1)S(1)}, u32[]{:S(2)}, u32[]{:S(2)}) collective-permute-start(bf16[64,4096]{1,0:T(8,128)(2,1)} %x_ref.1), channel_id=1, source_target_pairs={{0,1},{1,0},{2,3},{3,2},{4,5},{5,4},{6,7},{7,6},{8,9},{9,8},{10,11... | collective-permute-start | bytes 1572872 | tf_op jit(solution)/shard_map/ppermute | solution.py:361
  1.3 0.0 copy-start
  1.3 1.1 %copy-done = bf16[64,4096]{1,0:T(8,128)(2,1)S(1)} copy-done((bf16[64,4096]{1,0:T(8,128)(2,1)S(1)}, bf16[64,4096]{1,0:T(8,128)(2,1)}, u32[]{:S(2)}) %copy-start) | copy-done | bytes 524312
  2.4 0.0 copy-start.3
  2.4 0.7 copy-done.3
  3.0 0.4 shard_map.64
  3.5 7.2 %collective-permute-start.1 = (bf16[16,128]{1,0:T(8,128)(2,1)S(1)}, bf16[16,128]{1,0:T(8,128)(2,1)S(1)}, u32[]{:S(2)}, u32[]{:S(2)}) collective-permute-start(bf16[16,128]{1,0:T(8,128)(2,1)S(1)} %get-tuple-element.26.after_ref.refs_0_), channel_id=1, source_target_pairs={{0,64},{2,66},{4,68},{6,70},{8,72},{10,74},{12,76},{14,78},{16,80}... | collective-permute-start | bytes 12296 | tf_op jit(solution)/shard_map/ppermute | solution.py:345
  10.7 1.0 %copy.8 = s32[2,8,32,128]{3,2,1,0:T(8,128)S(1)} copy(s32[2,8,32,128]{3,1,2,0:T(8,128)} %bitcast.31) | data formatting | bytes 524288
  11.7 0.0 copy-start.1
  11.7 0.7 copy-done.1
  12.4 0.1 shard_map.65
  12.5 0.0 collective-permute-done.1.refs_1_
  12.5 0.7 %collective-permute-start.2 = (bf16[32,128]{1,0:T(8,128)(2,1)S(1)}, bf16[32,128]{1,0:T(8,128)(2,1)S(1)}, u32[]{:S(2)}, u32[]{:S(2)}) collective-permute-start(bf16[32,128]{1,0:T(8,128)(2,1)S(1)} %shard_map.66.after_ref.refs_0_), channel_id=1, source_target_pairs={{0,128},{2,130},{4,132},{6,134},{8,136},{10,138},{12,140},{14,142}... | collective-permute-start | bytes 24584 | tf_op jit(solution)/shard_map/ppermute | solution.py:345
  13.2 0.0 copy-start.2
  13.2 0.8 %copy-done.2 = bf16[128,128]{1,0:T(8,128)(2,1)S(1)} copy-done((bf16[128,128]{1,0:T(8,128)(2,1)S(1)}, bf16[128,128]{1,0:T(8,128)(2,1)}, u32[]{:S(2)}) %copy-start.2) | copy-done | bytes 32792
  14.0 0.0 copy-start.4
  14.0 0.7 copy-done.4
  14.6 0.4 shard_map.67
  15.0 2.7 %collective-permute-done.2.refs_1_ = bf16[32,128]{1,0:T(8,128)(2,1)S(1)} collective-permute-done((bf16[32,128]{1,0:T(8,128)(2,1)S(1)}, bf16[32,128]{1,0:T(8,128)(2,1)S(1)}, u32[]{:S(2)}, u32[]{:S(2)}) %collective-permute-start.2) | collective-permute-done | bytes 8224 | tf_op jit(solution)/shard_map/ppermute | solution.py:345
  17.8 0.7 %collective-permute-start.3 = (bf16[64,128]{1,0:T(8,128)(2,1)S(1)}, bf16[64,128]{1,0:T(8,128)(2,1)S(1)}, u32[]{:S(2)}, u32[]{:S(2)}) collective-permute-start(bf16[64,128]{1,0:T(8,128)(2,1)S(1)} %shard_map.68.mine_ref), channel_id=1, source_target_pairs={{0,1},{1,0},{2,3},{3,2},{4,5},{5,4},{6,7},{7,6},{8,9},{9,8},{10,11... | collective-permute-start | bytes 49160 | tf_op jit(solution)/shard_map/ppermute | solution.py:373
  18.5 3.0 %collective-permute-done.3.other_ref = bf16[64,128]{1,0:T(8,128)(2,1)S(1)} collective-permute-done((bf16[64,128]{1,0:T(8,128)(2,1)S(1)}, bf16[64,128]{1,0:T(8,128)(2,1)S(1)}, u32[]{:S(2)}, u32[]{:S(2)}) %collective-permute-start.3) | collective-permute-done | bytes 16416 | tf_op jit(solution)/shard_map/ppermute | solution.py:373
  21.5 0.1 shard_map.69.after_ref.refs_0_
  21.6 0.0 collective-permute-done.other_ref
  21.6 0.1 shard_map.70
  21.7 0.1 collective-permute-start.5
  21.8 8.6 %collective-permute-start.4 = (bf16[128,2048]{1,0:T(8,128)(2,1)S(1)}, bf16[128,2048]{1,0:T(8,128)(2,1)S(1)}, u32[]{:S(2)}, u32[]{:S(2)}) collective-permute-start(bf16[128,2048]{1,0:T(8,128)(2,1)S(1)} %get-tuple-element.31.after_ref.outer_ref), channel_id=1, source_target_pairs={{2,4},{4,2},{6,8},{8,6},{10,12},{12,10},{14,16},{16,14},{18,20},{2... | collective-permute-start | bytes 1572872 | tf_op jit(solution)/shard_map/ppermute | solution.py:386
  30.4 0.1 collective-permute-start.8
  30.5 0.1 collective-permute-start.7
  30.6 4.3 %collective-permute-start.6 = (bf16[128,128]{1,0:T(8,128)(2,1)S(1)}, bf16[128,128]{1,0:T(8,128)(2,1)S(1)}, u32[]{:S(2)}, u32[]{:S(2)}) collective-permute-start(bf16[128,128]{1,0:T(8,128)(2,1)S(1)} %shard_map.69.after_ref.refs_0_), channel_id=1, source_target_pairs={{0,16},{2,18},{4,20},{6,22},{8,24},{10,26},{12,28},{14,30},{16,0},... | collective-permute-start | bytes 98312 | tf_op jit(solution)/shard_map/ppermute | solution.py:345
  34.9 3.5 %shard_map.71 = (s32[8,128]{1,0:T(8,128)S(1)}, s32[8,128]{1,0:T(8,128)S(1)}, s32[8,128]{1,0:T(8,128)S(1)}, s32[8,128]{1,0:T(8,128)S(1)}, s32[8,128]{1,0:T(8,128)S(1)}, /*index=5*/s32[8,128]{1,0:T(8,128)S(1)}) custom-call(s32[3,8,128]{2,1,0:T(8,128)S(1)} %get-tuple-element.28.refs_2_.counts_ref, bf16[128,2048]{1,0:T(8,128)(2,1)S(1)} %get-tuple-element.31.after_ref.outer_ref), custom_call_target="tpu_custom_call" | custom-call | bytes 9000000 | tf_op jit(solution)/shard_map/pallas_call | solution.py:390
  38.4 0.0 collective-permute-done.8.refs_3_
  38.5 0.0 collective-permute-done.7.refs_2_
  38.5 0.0 collective-permute-done.6.refs_1_
  38.5 0.1 collective-permute-start.11
  38.6 0.1 collective-permute-start.10
  38.7 4.0 %collective-permute-start.9 = (bf16[512,128]{1,0:T(8,128)(2,1)S(1)}, bf16[512,128]{1,0:T(8,128)(2,1)S(1)}, u32[]{:S(2)}, u32[]{:S(2)}) collective-permute-start(bf16[512,128]{1,0:T(8,128)(2,1)S(1)} %shard_map.72.after_ref.refs_0_), channel_id=1, source_target_pairs={{0,4},{2,6},{4,0},{6,2},{8,12},{10,14},{12,8},{14,10},{16,20},{18,... | collective-permute-start | bytes 393224 | tf_op jit(solution)/shard_map/ppermute | solution.py:345
  42.7 0.0 collective-permute-done.5.inner_halo_ref
  42.7 0.0 collective-permute-done.4.outer_halo_ref
  42.7 1.2 %shard_map.73.frame_ref.frame_in = f32[12296,128]{1,0:T(8,128)S(1)} custom-call(bf16[128,2048]{1,0:T(8,128)(2,1)S(1)} %collective-permute-done.4.outer_halo_ref, bf16[128,2048]{1,0:T(8,128)(2,1)S(1)} %get-tuple-element.31.after_ref.outer_ref, bf16[128,2048]{1,0:T(8,128)(2,1)S(1)} %get-tuple-element.34.inner_ref, ...), custom_call_target="tpu_custom_call" | custom-call | bytes 6000000 | tf_op jit(solution)/shard_map/pallas_call | solution.py:396
  43.9 4.0 %shard_map.74.refs_4_.refs_0_ = f32[1024,128]{1,0:T(8,128)S(1)} custom-call(s32[16384]{0:T(1024)S(1)} %bitcast.15, s32[1024]{0:T(1024)S(1)} %bitcast.21, s32[1024]{0:T(1024)S(1)} %bitcast.23, f32[12296,128]{1,0:T(8,128)S(1)} %shard_map.73.frame_ref.frame_in, bf16[512,128]{1,0:T(8,128)(2,1)S(1)} %shard_map.72.after_ref.refs_0_), custom_call_target="tpu_custom_call" | custom-call | bytes 12000000 | tf_op jit(solution)/shard_map/pallas_call | solution.py:412
  48.0 0.0 collective-permute-done.11.refs_3_
  48.0 0.0 collective-permute-done.10.refs_2_
  48.0 0.0 collective-permute-done.9.refs_1_
  48.1 0.1 collective-permute-start.12
  48.2 4.0 %shard_map.76.after_ref.refs_1_ = f32[1024,128]{1,0:T(8,128)S(1)} custom-call(s32[16384]{0:T(1024)S(1)} %bitcast.16, s32[1024]{0:T(1024)S(1)} %bitcast.22, s32[1024]{0:T(1024)S(1)} %bitcast.24, f32[12296,128]{1,0:T(8,128)S(1)} %shard_map.73.frame_ref.frame_in, bf16[2048,128]{1,0:T(8,128)(2,1)S(1)} %shard_map.75.after_ref.near_ref), custom_call_target="tpu_custom_call" | custom-call | bytes 12000000 | tf_op jit(solution)/shard_map/pallas_call | solution.py:412
  52.2 0.0 collective-permute-done.12.far_ref
  52.2 0.1 shard_map.77.frame_ref
  52.3 3.0 %shard_map.78 = (bf16[64,1024]{1,0:T(8,128)(2,1)S(1)}, bf16[128,1024]{1,0:T(8,128)(2,1)S(1)}) custom-call(s32[16384]{0:T(1024)S(1)} %bitcast.18, s32[1024]{0:T(1024)S(1)} %bitcast.25, s32[1024]{0:T(1024)S(1)} %bitcast.26, f32[12296,128]{1,0:T(8,128)S(1)} %shard_map.77.frame_ref, f32[2048,128]{1,0:T(8,128)S(1)} %get-tuple-element.30.refs_2_.after_ref.scale_ref, ...), custom_call_target="tpu_custom_call" | custom-call | bytes 9000000 | tf_op jit(solution)/shard_map/pallas_call | solution.py:433
  55.4 1.3 %collective-permute-start.13 = (bf16[128,1024]{1,0:T(8,128)(2,1)S(1)}, bf16[128,1024]{1,0:T(8,128)(2,1)S(1)}, u32[]{:S(2)}, u32[]{:S(2)}) collective-permute-start(bf16[128,1024]{1,0:T(8,128)(2,1)S(1)} %get-tuple-element.45), channel_id=1, source_target_pairs={{0,1},{1,0},{2,3},{3,2},{4,5},{5,4},{6,7},{7,6},{8,9},{9,8},{10,11... | collective-permute-start | bytes 786440 | tf_op jit(solution)/shard_map/ppermute | solution.py:448
  56.6 7.9 %shard_map.79 = (bf16[64,1024]{1,0:T(8,128)(2,1)S(1)}, bf16[64,1024]{1,0:T(8,128)(2,1)S(1)}) custom-call(s32[16384]{0:T(1024)S(1)} %bitcast.17, s32[1024]{0:T(1024)S(1)} %bitcast.27, s32[1024]{0:T(1024)S(1)} %bitcast.28, f32[12296,128]{1,0:T(8,128)S(1)} %shard_map.77.frame_ref, f32[2048,128]{1,0:T(8,128)S(1)} %get-tuple-element.30.refs_2_.after_ref.scale_ref, ...), custom_call_target="tpu_custom_call" | custom-call | bytes 24000000 | tf_op jit(solution)/shard_map/pallas_call | solution.py:433
  64.6 0.8 %collective-permute-start.14 = (bf16[64,1024]{1,0:T(8,128)(2,1)S(1)}, bf16[64,1024]{1,0:T(8,128)(2,1)S(1)}, u32[]{:S(2)}, u32[]{:S(2)}) collective-permute-start(bf16[64,1024]{1,0:T(8,128)(2,1)S(1)} %get-tuple-element.46), channel_id=1, source_target_pairs={{0,1},{1,0},{2,3},{3,2},{4,5},{5,4},{6,7},{7,6},{8,9},{9,8},{10,11... | collective-permute-start | bytes 393224 | tf_op jit(solution)/shard_map/ppermute | solution.py:448
  65.4 4.8 %collective-permute-done.14.refs_3_ = bf16[64,1024]{1,0:T(8,128)(2,1)S(1)} collective-permute-done((bf16[64,1024]{1,0:T(8,128)(2,1)S(1)}, bf16[64,1024]{1,0:T(8,128)(2,1)S(1)}, u32[]{:S(2)}, u32[]{:S(2)}) %collective-permute-start.14) | collective-permute-done | bytes 131104 | tf_op jit(solution)/shard_map/ppermute | solution.py:448
  70.1 0.0 collective-permute-done.13.refs_2_
  70.1 0.8 %shard_map.80 = bf16[64,4096]{1,0:T(8,128)(2,1)} custom-call(bf16[64,1024]{1,0:T(8,128)(2,1)S(1)} %get-tuple-element.40.after_ref.refs_0_, bf16[64,1024]{1,0:T(8,128)(2,1)S(1)} %get-tuple-element.44.refs_1_, bf16[128,1024]{1,0:T(8,128)(2,1)S(1)} %collective-permute-done.13.refs_2_, bf16[64,1024]{1,0:T(8,128)(2,1)S(1)} %collective-permute-done.14.refs_3_), custom_call_target="tpu_custom_call" | custom-call | bytes 1500000 | tf_op jit(solution)/shard_map/pallas_call | solution.py:450
  (4 shorter events, 0.1 us)
Async XLA Ops:
  0.0 21.6 %collective-permute-start = (bf16[64,4096]{1,0:T(8,128)(2,1)}, bf16[64,4096]{1,0:T(8,128)(2,1)S(1)}, u32[]{:S(2)}, u32[]{:S(2)}) collective-permute-start(bf16[64,4096]{1,0:T(8,128)(2,1)} %x_ref.1), channel_id=1, source_target_pairs={{0,1},{1,0},{2,3},{3,2},{4,5},{5,4},{6,7},{7,6},{8,9},{9,8},{10,11... | collective-permute-start | bytes 1572872 | tf_op jit(solution)/shard_map/ppermute | solution.py:361
  1.3 1.1 %copy-start = (bf16[64,4096]{1,0:T(8,128)(2,1)S(1)}, bf16[64,4096]{1,0:T(8,128)(2,1)}, u32[]{:S(2)}) copy-start(bf16[64,4096]{1,0:T(8,128)(2,1)} %x_ref.1) | copy-start | bytes 1572868
  2.4 0.7 copy-start.3
  3.5 9.0 %collective-permute-start.1 = (bf16[16,128]{1,0:T(8,128)(2,1)S(1)}, bf16[16,128]{1,0:T(8,128)(2,1)S(1)}, u32[]{:S(2)}, u32[]{:S(2)}) collective-permute-start(bf16[16,128]{1,0:T(8,128)(2,1)S(1)} %get-tuple-element.26.after_ref.refs_0_), channel_id=1, source_target_pairs={{0,64},{2,66},{4,68},{6,70},{8,72},{10,74},{12,76},{14,78},{16,80}... | collective-permute-start | bytes 12296 | tf_op jit(solution)/shard_map/ppermute | solution.py:345
  11.7 0.7 %copy-start.1 = (s32[4096]{0:T(1024)S(1)}, s32[4096]{0:T(1024)}, u32[]{:S(2)}) copy-start(s32[4096]{0:T(1024)} %param.8) | copy-start | bytes 49156
  12.5 5.2 %collective-permute-start.2 = (bf16[32,128]{1,0:T(8,128)(2,1)S(1)}, bf16[32,128]{1,0:T(8,128)(2,1)S(1)}, u32[]{:S(2)}, u32[]{:S(2)}) collective-permute-start(bf16[32,128]{1,0:T(8,128)(2,1)S(1)} %shard_map.66.after_ref.refs_0_), channel_id=1, source_target_pairs={{0,128},{2,130},{4,132},{6,134},{8,136},{10,138},{12,140},{14,142}... | collective-permute-start | bytes 24584 | tf_op jit(solution)/shard_map/ppermute | solution.py:345
  13.2 0.8 %copy-start.2 = (bf16[128,128]{1,0:T(8,128)(2,1)S(1)}, bf16[128,128]{1,0:T(8,128)(2,1)}, u32[]{:S(2)}) copy-start(bf16[128,128]{1,0:T(8,128)(2,1)} %weight_ref.1) | copy-start | bytes 98308
  14.0 0.7 copy-start.4
  17.8 3.7 %collective-permute-start.3 = (bf16[64,128]{1,0:T(8,128)(2,1)S(1)}, bf16[64,128]{1,0:T(8,128)(2,1)S(1)}, u32[]{:S(2)}, u32[]{:S(2)}) collective-permute-start(bf16[64,128]{1,0:T(8,128)(2,1)S(1)} %shard_map.68.mine_ref), channel_id=1, source_target_pairs={{0,1},{1,0},{2,3},{3,2},{4,5},{5,4},{6,7},{7,6},{8,9},{9,8},{10,11... | collective-permute-start | bytes 49160 | tf_op jit(solution)/shard_map/ppermute | solution.py:373
  21.7 21.0 %collective-permute-start.5 = (bf16[128,2048]{1,0:T(8,128)(2,1)S(1)}, bf16[128,2048]{1,0:T(8,128)(2,1)S(1)}, u32[]{:S(2)}, u32[]{:S(2)}) collective-permute-start(bf16[128,2048]{1,0:T(8,128)(2,1)S(1)} %get-tuple-element.34.inner_ref), channel_id=1, source_target_pairs={{0,2},{2,0},{4,6},{6,4},{8,10},{10,8},{12,14},{14,12},{16,18},{18,... | collective-permute-start | bytes 1572872 | tf_op jit(solution)/shard_map/ppermute | solution.py:385
  21.8 20.9 %collective-permute-start.4 = (bf16[128,2048]{1,0:T(8,128)(2,1)S(1)}, bf16[128,2048]{1,0:T(8,128)(2,1)S(1)}, u32[]{:S(2)}, u32[]{:S(2)}) collective-permute-start(bf16[128,2048]{1,0:T(8,128)(2,1)S(1)} %get-tuple-element.31.after_ref.outer_ref), channel_id=1, source_target_pairs={{2,4},{4,2},{6,8},{8,6},{10,12},{12,10},{14,16},{16,14},{18,20},{2... | collective-permute-start | bytes 1572872 | tf_op jit(solution)/shard_map/ppermute | solution.py:386
  30.4 8.0 %collective-permute-start.8 = (bf16[128,128]{1,0:T(8,128)(2,1)S(1)}, bf16[128,128]{1,0:T(8,128)(2,1)S(1)}, u32[]{:S(2)}, u32[]{:S(2)}) collective-permute-start(bf16[128,128]{1,0:T(8,128)(2,1)S(1)} %shard_map.69.after_ref.refs_0_), channel_id=1, source_target_pairs={{0,48},{2,50},{4,52},{6,54},{8,56},{10,58},{12,60},{14,62},{16,32}... | collective-permute-start | bytes 98312 | tf_op jit(solution)/shard_map/ppermute | solution.py:345
  30.5 8.0 %collective-permute-start.7 = (bf16[128,128]{1,0:T(8,128)(2,1)S(1)}, bf16[128,128]{1,0:T(8,128)(2,1)S(1)}, u32[]{:S(2)}, u32[]{:S(2)}) collective-permute-start(bf16[128,128]{1,0:T(8,128)(2,1)S(1)} %shard_map.69.after_ref.refs_0_), channel_id=1, source_target_pairs={{0,32},{2,34},{4,36},{6,38},{8,40},{10,42},{12,44},{14,46},{16,48}... | collective-permute-start | bytes 98312 | tf_op jit(solution)/shard_map/ppermute | solution.py:345
  30.6 7.9 %collective-permute-start.6 = (bf16[128,128]{1,0:T(8,128)(2,1)S(1)}, bf16[128,128]{1,0:T(8,128)(2,1)S(1)}, u32[]{:S(2)}, u32[]{:S(2)}) collective-permute-start(bf16[128,128]{1,0:T(8,128)(2,1)S(1)} %shard_map.69.after_ref.refs_0_), channel_id=1, source_target_pairs={{0,16},{2,18},{4,20},{6,22},{8,24},{10,26},{12,28},{14,30},{16,0},... | collective-permute-start | bytes 98312 | tf_op jit(solution)/shard_map/ppermute | solution.py:345
  38.5 9.5 %collective-permute-start.11 = (bf16[512,128]{1,0:T(8,128)(2,1)S(1)}, bf16[512,128]{1,0:T(8,128)(2,1)S(1)}, u32[]{:S(2)}, u32[]{:S(2)}) collective-permute-start(bf16[512,128]{1,0:T(8,128)(2,1)S(1)} %shard_map.72.after_ref.refs_0_), channel_id=1, source_target_pairs={{0,12},{2,14},{4,8},{6,10},{8,4},{10,6},{12,0},{14,2},{16,28},{18,... | collective-permute-start | bytes 393224 | tf_op jit(solution)/shard_map/ppermute | solution.py:345
  38.6 9.4 %collective-permute-start.10 = (bf16[512,128]{1,0:T(8,128)(2,1)S(1)}, bf16[512,128]{1,0:T(8,128)(2,1)S(1)}, u32[]{:S(2)}, u32[]{:S(2)}) collective-permute-start(bf16[512,128]{1,0:T(8,128)(2,1)S(1)} %shard_map.72.after_ref.refs_0_), channel_id=1, source_target_pairs={{0,8},{2,10},{4,12},{6,14},{8,0},{10,2},{12,4},{14,6},{16,24},{18,... | collective-permute-start | bytes 393224 | tf_op jit(solution)/shard_map/ppermute | solution.py:345
  38.7 9.3 %collective-permute-start.9 = (bf16[512,128]{1,0:T(8,128)(2,1)S(1)}, bf16[512,128]{1,0:T(8,128)(2,1)S(1)}, u32[]{:S(2)}, u32[]{:S(2)}) collective-permute-start(bf16[512,128]{1,0:T(8,128)(2,1)S(1)} %shard_map.72.after_ref.refs_0_), channel_id=1, source_target_pairs={{0,4},{2,6},{4,0},{6,2},{8,12},{10,14},{12,8},{14,10},{16,20},{18,... | collective-permute-start | bytes 393224 | tf_op jit(solution)/shard_map/ppermute | solution.py:345
  48.1 4.1 %collective-permute-start.12 = (bf16[2048,128]{1,0:T(8,128)(2,1)S(1)}, bf16[2048,128]{1,0:T(8,128)(2,1)S(1)}, u32[]{:S(2)}, u32[]{:S(2)}) collective-permute-start(bf16[2048,128]{1,0:T(8,128)(2,1)S(1)} %shard_map.75.after_ref.near_ref), channel_id=1, source_target_pairs={{0,2},{2,0},{4,6},{6,4},{8,10},{10,8},{12,14},{14,12},{16,18},{18,... | collective-permute-start | bytes 1572872 | tf_op jit(solution)/shard_map/ppermute | solution.py:345
  55.4 14.8 %collective-permute-start.13 = (bf16[128,1024]{1,0:T(8,128)(2,1)S(1)}, bf16[128,1024]{1,0:T(8,128)(2,1)S(1)}, u32[]{:S(2)}, u32[]{:S(2)}) collective-permute-start(bf16[128,1024]{1,0:T(8,128)(2,1)S(1)} %get-tuple-element.45), channel_id=1, source_target_pairs={{0,1},{1,0},{2,3},{3,2},{4,5},{5,4},{6,7},{7,6},{8,9},{9,8},{10,11... | collective-permute-start | bytes 786440 | tf_op jit(solution)/shard_map/ppermute | solution.py:448
  64.6 5.5 %collective-permute-start.14 = (bf16[64,1024]{1,0:T(8,128)(2,1)S(1)}, bf16[64,1024]{1,0:T(8,128)(2,1)S(1)}, u32[]{:S(2)}, u32[]{:S(2)}) collective-permute-start(bf16[64,1024]{1,0:T(8,128)(2,1)S(1)} %get-tuple-element.46), channel_id=1, source_target_pairs={{0,1},{1,0},{2,3},{3,2},{4,5},{5,4},{6,7},{7,6},{8,9},{9,8},{10,11... | collective-permute-start | bytes 393224 | tf_op jit(solution)/shard_map/ppermute | solution.py:448

commit v11 on v10

--- a/solution.py
+++ b/solution.py
@@ -36,18 +36,23 @@
         out_ref[i * rows : (i + 1) * rows] = ref[...]
 
 
-def join_feat_kernel(mine_ref, other_ref, after_ref, out_ref):
+def join_feat_kernel(*refs):
+    count = len(refs) // 2 - 1
+    out_ref = refs[-1]
+    rows = refs[0].shape[0]
     first = lax.axis_index("feat") == 0
     lane = lax.broadcasted_iota(jnp.int32, (16, LANES), 1)
-    for i in range(mine_ref.shape[0] // 16):
-        mine = mine_ref[16 * i : 16 * i + 16, :].astype(jnp.float32)
-        other = other_ref[16 * i : 16 * i + 16, :].astype(jnp.float32)
-        low = jnp.where(first, mine, other)
-        high = jnp.where(first, other, mine)
-        row = jnp.where(lane < LANES // 2, low, pltpu.roll(high, LANES // 2, 1))
-        out_ref[32 * i : 32 * i + 16, :] = row.astype(jnp.bfloat16)
-        row = jnp.where(lane < LANES // 2, pltpu.roll(low, LANES // 2, 1), high)
-        out_ref[32 * i + 16 : 32 * i + 32, :] = row.astype(jnp.bfloat16)
+    for b, (mine_ref, other_ref) in enumerate(zip(refs[:count], refs[count : 2 * count])):
+        for at in range(0, rows, 16):
+            mine = mine_ref[at : at + 16, :].astype(jnp.float32)
+            other = other_ref[at : at + 16, :].astype(jnp.float32)
+            low = jnp.where(first, mine, other)
+            high = jnp.where(first, other, mine)
+            to = 2 * (b * rows + at)
+            row = jnp.where(lane < LANES // 2, low, pltpu.roll(high, LANES // 2, 1))
+            out_ref[to : to + 16, :] = row.astype(jnp.bfloat16)
+            row = jnp.where(lane < LANES // 2, pltpu.roll(low, LANES // 2, 1), high)
+            out_ref[to + 16 : to + 32, :] = row.astype(jnp.bfloat16)
 
 
 def halves_kernel(x_ref, other_ref, after_ref, outer_ref, inner_ref, sem):
@@ -362,18 +367,18 @@
 
     block = join(block, arrived, counts)
     arrived = stage(block, STAGES[1])
+    arrived.append(lax.ppermute(block, "feat", swap))
+    across = [(2 * i + f, 2 * (i ^ STAGES[1][0]) + 1 - f) for i in range(slabs) for f in range(2)]
+    arrived.append(lax.ppermute(block, ("slab", "feat"), across))
     scale, by_out, bias = pallas(
         constants_kernel,
         (f32(half, LANES), bf16(2 * chans, 2 * chans), f32(LANES, LANES)),
         [IN_VMEM] * 3 + [ANYWHERE],
         us=0.1,
     )(deg_tiles, weight, bias_terms[None, :], block)
-
-    block = join(block, arrived, scale)
-    arrived = lax.ppermute(block, "feat", swap)
     block = pallas(
-        join_feat_kernel, bf16(2 * block.shape[0], 2 * chans), [IN_VMEM] * 2 + [ANYWHERE], us=0.1
-    )(block, arrived, scale)
+        join_feat_kernel, bf16(4 * block.shape[0], 2 * chans), [IN_VMEM] * 4 + [ANYWHERE], us=0.1
+    )(block, *arrived, scale)
 
     outer, inner = pallas(
         halves_kernel,

time: 71.4 us -> 71.4 us (level)
  waiting for transfers between devices: 10.5 us -> 7.31 us
  starting transfers between devices: 29.4 us -> 32.5 us
    ppermute x1 -> x2, waiting for transfers between devices: 3 us -> 0.01 us  [the longest x1 0.01 us: local(): arrived.append(lax.ppermute(block, 'feat', swap))]
    ppermute x1 -> x2, starting transfers between devices: 0.74 us -> 1.88 us  [the longest x1 1.79 us: local(): arrived.append(lax.ppermute(block, 'feat', swap))]
    ppermute x9, waiting for transfers between devices: 2.78 us -> 1.7 us  [stage(): lax.ppermute(block, 'slab', [(i, i ^ bit) for i in range(slabs)])]
    ppermute x1, starting transfers between devices: 8.56 us -> 9.57 us  [local(): lax.ppermute(outer, 'slab', [(i, j) for i in range(slabs) for j in [i + 2...]
    ppermute x9, starting transfers between devices: 16.7 us -> 17.6 us  [stage(): lax.ppermute(block, 'slab', [(i, i ^ bit) for i in range(slabs)])]
    ppermute x2, waiting for transfers between devices: 4.76 us -> 5.6 us  [local(): received.append(lax.ppermute(sent, 'feat', swap))]
  transfers between devices with their start and end apart: 15 -> 16, of which waited for: 3 -> 2; matrix products, arithmetic and copies ran while one was open for 1% -> 1% of each run, Pallas kernels for 31% -> 31%
where the time goes in v11:
time: 71.4 us; the launch traced here: 71 us
  starting transfers between devices  32.5 us (46%)
  Pallas kernels  26.1 us (37%)
  waiting for transfers between devices  7.31 us (10%)
  local copies, waits for them, and re-layouts  4.86 us (7%)
    ppermute x9, starting transfers between devices, stage(): lax.ppermute(block, 'slab', [(i, i ^ bit) for i in range(slabs)])  17.6 us
    pallas_call x2, Pallas kernels, layer(): pallas(functools.partial(layer_kernel, slots, first, start, len(near), ha...  10.9 us
    ppermute x1, starting transfers between devices, local(): lax.ppermute(outer, 'slab', [(i, j) for i in range(slabs) for j in [i + 2...  9.57 us
    pallas_call x2, Pallas kernels, near_sum(): pallas(functools.partial(near_kernel, slots, part, 2), f32(CHUNK, LANES),...  8.18 us
    ppermute x2, waiting for transfers between devices, local(): received.append(lax.ppermute(sent, 'feat', swap))  5.6 us
    unnamed x11, local copies, waits for them, and re-layouts  4.86 us
    pallas_call x1, Pallas kernels, local(): pallas(order_kernel, (tile,) * 6, [IN_VMEM, ANYWHERE], us=3.0)  3.54 us
    ppermute x2, starting transfers between devices, local(): received.append(lax.ppermute(sent, 'feat', swap))  2.07 us
  transfers between devices with their start and end apart: 16, of which 2 were waited for; matrix products, arithmetic and copies ran while one was open for 1% of the time, Pallas kernels for 31%

profile of v11, /device:TPU:16, one launch (start us, length us, event | category | flops | bytes accessed | tf_op | source)
XLA Modules:
  0.0 71.0 jit_solution(12669130116800257327)
XLA Ops:
  0.0 1.3 %collective-permute-start = (bf16[64,4096]{1,0:T(8,128)(2,1)}, bf16[64,4096]{1,0:T(8,128)(2,1)S(1)}, u32[]{:S(2)}, u32[]{:S(2)}) collective-permute-start(bf16[64,4096]{1,0:T(8,128)(2,1)} %x_ref.1), channel_id=1, source_target_pairs={{0,1},{1,0},{2,3},{3,2},{4,5},{5,4},{6,7},{7,6},{8,9},{9,8},{10,11... | collective-permute-start | bytes 1572872 | tf_op jit(solution)/shard_map/ppermute | solution.py:366
  1.3 0.0 copy-start
  1.3 1.1 %copy-done = bf16[64,4096]{1,0:T(8,128)(2,1)S(1)} copy-done((bf16[64,4096]{1,0:T(8,128)(2,1)S(1)}, bf16[64,4096]{1,0:T(8,128)(2,1)}, u32[]{:S(2)}) %copy-start) | copy-done | bytes 524312
  2.4 0.0 copy-start.3
  2.4 0.7 copy-done.3
  3.0 0.4 shard_map.64
  3.5 7.2 %collective-permute-start.1 = (bf16[16,128]{1,0:T(8,128)(2,1)S(1)}, bf16[16,128]{1,0:T(8,128)(2,1)S(1)}, u32[]{:S(2)}, u32[]{:S(2)}) collective-permute-start(bf16[16,128]{1,0:T(8,128)(2,1)S(1)} %get-tuple-element.26.after_ref.refs_0_), channel_id=1, source_target_pairs={{0,64},{2,66},{4,68},{6,70},{8,72},{10,74},{12,76},{14,78},{16,80}... | collective-permute-start | bytes 12296 | tf_op jit(solution)/shard_map/ppermute | solution.py:350
  10.7 1.0 %copy.8 = s32[2,8,32,128]{3,2,1,0:T(8,128)S(1)} copy(s32[2,8,32,128]{3,1,2,0:T(8,128)} %bitcast.31) | data formatting | bytes 524288
  11.7 0.0 copy-start.1
  11.7 0.7 copy-done.1
  12.4 0.1 shard_map.65
  12.5 0.0 collective-permute-done.1.refs_1_
  12.5 0.1 collective-permute-start.4
  12.6 1.8 %collective-permute-start.3 = (bf16[32,128]{1,0:T(8,128)(2,1)S(1)}, bf16[32,128]{1,0:T(8,128)(2,1)S(1)}, u32[]{:S(2)}, u32[]{:S(2)}) collective-permute-start(bf16[32,128]{1,0:T(8,128)(2,1)S(1)} %shard_map.66.after_ref.refs_0_), channel_id=1, source_target_pairs={{0,1},{1,0},{2,3},{3,2},{4,5},{5,4},{6,7},{7,6},{8,9},{9,8},{10,11... | collective-permute-start | bytes 24584 | tf_op jit(solution)/shard_map/ppermute | solution.py:370
  14.4 1.7 %collective-permute-start.2 = (bf16[32,128]{1,0:T(8,128)(2,1)S(1)}, bf16[32,128]{1,0:T(8,128)(2,1)S(1)}, u32[]{:S(2)}, u32[]{:S(2)}) collective-permute-start(bf16[32,128]{1,0:T(8,128)(2,1)S(1)} %shard_map.66.after_ref.refs_0_), channel_id=1, source_target_pairs={{0,128},{2,130},{4,132},{6,134},{8,136},{10,138},{12,140},{14,142}... | collective-permute-start | bytes 24584 | tf_op jit(solution)/shard_map/ppermute | solution.py:350
  16.1 0.0 copy-start.2
  16.1 0.8 %copy-done.2 = bf16[128,128]{1,0:T(8,128)(2,1)S(1)} copy-done((bf16[128,128]{1,0:T(8,128)(2,1)S(1)}, bf16[128,128]{1,0:T(8,128)(2,1)}, u32[]{:S(2)}) %copy-start.2) | copy-done | bytes 32792
  16.9 0.0 copy-start.4
  16.9 0.7 copy-done.4
  17.5 0.4 shard_map.67
  17.9 0.0 collective-permute-done.4.refs_3_
  17.9 0.0 collective-permute-done.3.refs_2_
  17.9 1.7 %collective-permute-done.2.refs_1_ = bf16[32,128]{1,0:T(8,128)(2,1)S(1)} collective-permute-done((bf16[32,128]{1,0:T(8,128)(2,1)S(1)}, bf16[32,128]{1,0:T(8,128)(2,1)S(1)}, u32[]{:S(2)}, u32[]{:S(2)}) %collective-permute-start.2) | collective-permute-done | bytes 8224 | tf_op jit(solution)/shard_map/ppermute | solution.py:350
  19.6 0.1 shard_map.68.after_ref.refs_0_
  19.6 0.0 collective-permute-done.other_ref
  19.7 0.1 shard_map.69
  19.8 0.1 collective-permute-start.6
  19.9 9.6 %collective-permute-start.5 = (bf16[128,2048]{1,0:T(8,128)(2,1)S(1)}, bf16[128,2048]{1,0:T(8,128)(2,1)S(1)}, u32[]{:S(2)}, u32[]{:S(2)}) collective-permute-start(bf16[128,2048]{1,0:T(8,128)(2,1)S(1)} %get-tuple-element.31.after_ref.outer_ref), channel_id=1, source_target_pairs={{2,4},{4,2},{6,8},{8,6},{10,12},{12,10},{14,16},{16,14},{18,20},{2... | collective-permute-start | bytes 1572872 | tf_op jit(solution)/shard_map/ppermute | solution.py:391
  29.5 0.1 collective-permute-start.9
  29.6 0.1 collective-permute-start.8
  29.7 4.3 %collective-permute-start.7 = (bf16[128,128]{1,0:T(8,128)(2,1)S(1)}, bf16[128,128]{1,0:T(8,128)(2,1)S(1)}, u32[]{:S(2)}, u32[]{:S(2)}) collective-permute-start(bf16[128,128]{1,0:T(8,128)(2,1)S(1)} %shard_map.68.after_ref.refs_0_), channel_id=1, source_target_pairs={{0,16},{2,18},{4,20},{6,22},{8,24},{10,26},{12,28},{14,30},{16,0},... | collective-permute-start | bytes 98312 | tf_op jit(solution)/shard_map/ppermute | solution.py:350
  33.9 3.5 %shard_map.70 = (s32[8,128]{1,0:T(8,128)S(1)}, s32[8,128]{1,0:T(8,128)S(1)}, s32[8,128]{1,0:T(8,128)S(1)}, s32[8,128]{1,0:T(8,128)S(1)}, s32[8,128]{1,0:T(8,128)S(1)}, /*index=5*/s32[8,128]{1,0:T(8,128)S(1)}) custom-call(s32[3,8,128]{2,1,0:T(8,128)S(1)} %get-tuple-element.28.refs_2_.counts_ref, bf16[128,2048]{1,0:T(8,128)(2,1)S(1)} %get-tuple-element.31.after_ref.outer_ref), custom_call_target="tpu_custom_call" | custom-call | bytes 9000000 | tf_op jit(solution)/shard_map/pallas_call | solution.py:395
  37.5 0.0 collective-permute-done.9.refs_3_
  37.5 0.0 collective-permute-done.8.refs_2_
  37.5 0.0 collective-permute-done.7.refs_1_
  37.6 0.1 collective-permute-start.12
  37.7 0.1 collective-permute-start.11
  37.8 4.0 %collective-permute-start.10 = (bf16[512,128]{1,0:T(8,128)(2,1)S(1)}, bf16[512,128]{1,0:T(8,128)(2,1)S(1)}, u32[]{:S(2)}, u32[]{:S(2)}) collective-permute-start(bf16[512,128]{1,0:T(8,128)(2,1)S(1)} %shard_map.71.after_ref.refs_0_), channel_id=1, source_target_pairs={{0,4},{2,6},{4,0},{6,2},{8,12},{10,14},{12,8},{14,10},{16,20},{18,... | collective-permute-start | bytes 393224 | tf_op jit(solution)/shard_map/ppermute | solution.py:350
  41.7 0.0 collective-permute-done.6.inner_halo_ref
  41.8 0.0 collective-permute-done.5.outer_halo_ref
  41.8 1.2 %shard_map.72.frame_ref.frame_in = f32[12296,128]{1,0:T(8,128)S(1)} custom-call(bf16[128,2048]{1,0:T(8,128)(2,1)S(1)} %collective-permute-done.5.outer_halo_ref, bf16[128,2048]{1,0:T(8,128)(2,1)S(1)} %get-tuple-element.31.after_ref.outer_ref, bf16[128,2048]{1,0:T(8,128)(2,1)S(1)} %get-tuple-element.34.inner_ref, ...), custom_call_target="tpu_custom_call" | custom-call | bytes 6000000 | tf_op jit(solution)/shard_map/pallas_call | solution.py:401
  43.0 4.1 %shard_map.73.refs_4_.refs_0_ = f32[1024,128]{1,0:T(8,128)S(1)} custom-call(s32[16384]{0:T(1024)S(1)} %bitcast.15, s32[1024]{0:T(1024)S(1)} %bitcast.21, s32[1024]{0:T(1024)S(1)} %bitcast.23, f32[12296,128]{1,0:T(8,128)S(1)} %shard_map.72.frame_ref.frame_in, bf16[512,128]{1,0:T(8,128)(2,1)S(1)} %shard_map.71.after_ref.refs_0_), custom_call_target="tpu_custom_call" | custom-call | bytes 12000000 | tf_op jit(solution)/shard_map/pallas_call | solution.py:417
  47.1 0.0 collective-permute-done.12.refs_3_
  47.1 0.0 collective-permute-done.11.refs_2_
  47.2 0.0 collective-permute-done.10.refs_1_
  47.2 0.1 collective-permute-start.13
  47.3 4.1 %shard_map.75.after_ref.refs_1_ = f32[1024,128]{1,0:T(8,128)S(1)} custom-call(s32[16384]{0:T(1024)S(1)} %bitcast.16, s32[1024]{0:T(1024)S(1)} %bitcast.22, s32[1024]{0:T(1024)S(1)} %bitcast.24, f32[12296,128]{1,0:T(8,128)S(1)} %shard_map.72.frame_ref.frame_in, bf16[2048,128]{1,0:T(8,128)(2,1)S(1)} %shard_map.74.after_ref.near_ref), custom_call_target="tpu_custom_call" | custom-call | bytes 12000000 | tf_op jit(solution)/shard_map/pallas_call | solution.py:417
  51.4 0.0 collective-permute-done.13.far_ref
  51.4 0.1 shard_map.76.frame_ref
  51.6 3.0 %shard_map.77 = (bf16[64,1024]{1,0:T(8,128)(2,1)S(1)}, bf16[128,1024]{1,0:T(8,128)(2,1)S(1)}) custom-call(s32[16384]{0:T(1024)S(1)} %bitcast.18, s32[1024]{0:T(1024)S(1)} %bitcast.25, s32[1024]{0:T(1024)S(1)} %bitcast.26, f32[12296,128]{1,0:T(8,128)S(1)} %shard_map.76.frame_ref, f32[2048,128]{1,0:T(8,128)S(1)} %get-tuple-element.30.refs_4_.scale_ref, ...), custom_call_target="tpu_custom_call" | custom-call | bytes 9000000 | tf_op jit(solution)/shard_map/pallas_call | solution.py:438
  54.5 2.0 %collective-permute-start.14 = (bf16[128,1024]{1,0:T(8,128)(2,1)S(1)}, bf16[128,1024]{1,0:T(8,128)(2,1)S(1)}, u32[]{:S(2)}, u32[]{:S(2)}) collective-permute-start(bf16[128,1024]{1,0:T(8,128)(2,1)S(1)} %get-tuple-element.45), channel_id=1, source_target_pairs={{0,1},{1,0},{2,3},{3,2},{4,5},{5,4},{6,7},{7,6},{8,9},{9,8},{10,11... | collective-permute-start | bytes 786440 | tf_op jit(solution)/shard_map/ppermute | solution.py:453
  56.5 7.9 %shard_map.78 = (bf16[64,1024]{1,0:T(8,128)(2,1)S(1)}, bf16[64,1024]{1,0:T(8,128)(2,1)S(1)}) custom-call(s32[16384]{0:T(1024)S(1)} %bitcast.17, s32[1024]{0:T(1024)S(1)} %bitcast.27, s32[1024]{0:T(1024)S(1)} %bitcast.28, f32[12296,128]{1,0:T(8,128)S(1)} %shard_map.76.frame_ref, f32[2048,128]{1,0:T(8,128)S(1)} %get-tuple-element.30.refs_4_.scale_ref, ...), custom_call_target="tpu_custom_call" | custom-call | bytes 24000000 | tf_op jit(solution)/shard_map/pallas_call | solution.py:438
  64.5 0.1 collective-permute-start.15
  64.6 5.6 %collective-permute-done.15.refs_3_ = bf16[64,1024]{1,0:T(8,128)(2,1)S(1)} collective-permute-done((bf16[64,1024]{1,0:T(8,128)(2,1)S(1)}, bf16[64,1024]{1,0:T(8,128)(2,1)S(1)}, u32[]{:S(2)}, u32[]{:S(2)}) %collective-permute-start.15) | collective-permute-done | bytes 131104 | tf_op jit(solution)/shard_map/ppermute | solution.py:453
  70.2 0.0 collective-permute-done.14.refs_2_
  70.2 0.8 %shard_map.79 = bf16[64,4096]{1,0:T(8,128)(2,1)} custom-call(bf16[64,1024]{1,0:T(8,128)(2,1)S(1)} %get-tuple-element.40.after_ref.refs_0_, bf16[64,1024]{1,0:T(8,128)(2,1)S(1)} %get-tuple-element.44.refs_1_, bf16[128,1024]{1,0:T(8,128)(2,1)S(1)} %collective-permute-done.14.refs_2_, bf16[64,1024]{1,0:T(8,128)(2,1)S(1)} %collective-permute-done.15.refs_3_), custom_call_target="tpu_custom_call" | custom-call | bytes 1500000 | tf_op jit(solution)/shard_map/pallas_call | solution.py:455
  (3 shorter events, 0.1 us)
Async XLA Ops:
  0.0 19.6 %collective-permute-start = (bf16[64,4096]{1,0:T(8,128)(2,1)}, bf16[64,4096]{1,0:T(8,128)(2,1)S(1)}, u32[]{:S(2)}, u32[]{:S(2)}) collective-permute-start(bf16[64,4096]{1,0:T(8,128)(2,1)} %x_ref.1), channel_id=1, source_target_pairs={{0,1},{1,0},{2,3},{3,2},{4,5},{5,4},{6,7},{7,6},{8,9},{9,8},{10,11... | collective-permute-start | bytes 1572872 | tf_op jit(solution)/shard_map/ppermute | solution.py:366
  1.3 1.1 %copy-start = (bf16[64,4096]{1,0:T(8,128)(2,1)S(1)}, bf16[64,4096]{1,0:T(8,128)(2,1)}, u32[]{:S(2)}) copy-start(bf16[64,4096]{1,0:T(8,128)(2,1)} %x_ref.1) | copy-start | bytes 1572868
  2.4 0.7 copy-start.3
  3.5 9.0 %collective-permute-start.1 = (bf16[16,128]{1,0:T(8,128)(2,1)S(1)}, bf16[16,128]{1,0:T(8,128)(2,1)S(1)}, u32[]{:S(2)}, u32[]{:S(2)}) collective-permute-start(bf16[16,128]{1,0:T(8,128)(2,1)S(1)} %get-tuple-element.26.after_ref.refs_0_), channel_id=1, source_target_pairs={{0,64},{2,66},{4,68},{6,70},{8,72},{10,74},{12,76},{14,78},{16,80}... | collective-permute-start | bytes 12296 | tf_op jit(solution)/shard_map/ppermute | solution.py:350
  11.7 0.7 %copy-start.1 = (s32[4096]{0:T(1024)S(1)}, s32[4096]{0:T(1024)}, u32[]{:S(2)}) copy-start(s32[4096]{0:T(1024)} %param.8) | copy-start | bytes 49156
  12.5 5.4 %collective-permute-start.4 = (bf16[32,128]{1,0:T(8,128)(2,1)S(1)}, bf16[32,128]{1,0:T(8,128)(2,1)S(1)}, u32[]{:S(2)}, u32[]{:S(2)}) collective-permute-start(bf16[32,128]{1,0:T(8,128)(2,1)S(1)} %shard_map.66.after_ref.refs_0_), channel_id=1, source_target_pairs={{0,129},{1,128},{2,131},{3,130},{4,133},{5,132},{6,135},{7,134},{8... | collective-permute-start | bytes 24584 | tf_op jit(solution)/shard_map/ppermute | solution.py:372
  12.6 5.3 %collective-permute-start.3 = (bf16[32,128]{1,0:T(8,128)(2,1)S(1)}, bf16[32,128]{1,0:T(8,128)(2,1)S(1)}, u32[]{:S(2)}, u32[]{:S(2)}) collective-permute-start(bf16[32,128]{1,0:T(8,128)(2,1)S(1)} %shard_map.66.after_ref.refs_0_), channel_id=1, source_target_pairs={{0,1},{1,0},{2,3},{3,2},{4,5},{5,4},{6,7},{7,6},{8,9},{9,8},{10,11... | collective-permute-start | bytes 24584 | tf_op jit(solution)/shard_map/ppermute | solution.py:370
  14.4 5.2 %collective-permute-start.2 = (bf16[32,128]{1,0:T(8,128)(2,1)S(1)}, bf16[32,128]{1,0:T(8,128)(2,1)S(1)}, u32[]{:S(2)}, u32[]{:S(2)}) collective-permute-start(bf16[32,128]{1,0:T(8,128)(2,1)S(1)} %shard_map.66.after_ref.refs_0_), channel_id=1, source_target_pairs={{0,128},{2,130},{4,132},{6,134},{8,136},{10,138},{12,140},{14,142}... | collective-permute-start | bytes 24584 | tf_op jit(solution)/shard_map/ppermute | solution.py:350
  16.1 0.8 %copy-start.2 = (bf16[128,128]{1,0:T(8,128)(2,1)S(1)}, bf16[128,128]{1,0:T(8,128)(2,1)}, u32[]{:S(2)}) copy-start(bf16[128,128]{1,0:T(8,128)(2,1)} %weight_ref.1) | copy-start | bytes 98308
  16.9 0.7 copy-start.4
  19.8 22.0 %collective-permute-start.6 = (bf16[128,2048]{1,0:T(8,128)(2,1)S(1)}, bf16[128,2048]{1,0:T(8,128)(2,1)S(1)}, u32[]{:S(2)}, u32[]{:S(2)}) collective-permute-start(bf16[128,2048]{1,0:T(8,128)(2,1)S(1)} %get-tuple-element.34.inner_ref), channel_id=1, source_target_pairs={{0,2},{2,0},{4,6},{6,4},{8,10},{10,8},{12,14},{14,12},{16,18},{18,... | collective-permute-start | bytes 1572872 | tf_op jit(solution)/shard_map/ppermute | solution.py:390
  19.9 21.9 %collective-permute-start.5 = (bf16[128,2048]{1,0:T(8,128)(2,1)S(1)}, bf16[128,2048]{1,0:T(8,128)(2,1)S(1)}, u32[]{:S(2)}, u32[]{:S(2)}) collective-permute-start(bf16[128,2048]{1,0:T(8,128)(2,1)S(1)} %get-tuple-element.31.after_ref.outer_ref), channel_id=1, source_target_pairs={{2,4},{4,2},{6,8},{8,6},{10,12},{12,10},{14,16},{16,14},{18,20},{2... | collective-permute-start | bytes 1572872 | tf_op jit(solution)/shard_map/ppermute | solution.py:391
  29.5 8.0 %collective-permute-start.9 = (bf16[128,128]{1,0:T(8,128)(2,1)S(1)}, bf16[128,128]{1,0:T(8,128)(2,1)S(1)}, u32[]{:S(2)}, u32[]{:S(2)}) collective-permute-start(bf16[128,128]{1,0:T(8,128)(2,1)S(1)} %shard_map.68.after_ref.refs_0_), channel_id=1, source_target_pairs={{0,48},{2,50},{4,52},{6,54},{8,56},{10,58},{12,60},{14,62},{16,32}... | collective-permute-start | bytes 98312 | tf_op jit(solution)/shard_map/ppermute | solution.py:350
  29.6 8.0 %collective-permute-start.8 = (bf16[128,128]{1,0:T(8,128)(2,1)S(1)}, bf16[128,128]{1,0:T(8,128)(2,1)S(1)}, u32[]{:S(2)}, u32[]{:S(2)}) collective-permute-start(bf16[128,128]{1,0:T(8,128)(2,1)S(1)} %shard_map.68.after_ref.refs_0_), channel_id=1, source_target_pairs={{0,32},{2,34},{4,36},{6,38},{8,40},{10,42},{12,44},{14,46},{16,48}... | collective-permute-start | bytes 98312 | tf_op jit(solution)/shard_map/ppermute | solution.py:350
  29.7 7.9 %collective-permute-start.7 = (bf16[128,128]{1,0:T(8,128)(2,1)S(1)}, bf16[128,128]{1,0:T(8,128)(2,1)S(1)}, u32[]{:S(2)}, u32[]{:S(2)}) collective-permute-start(bf16[128,128]{1,0:T(8,128)(2,1)S(1)} %shard_map.68.after_ref.refs_0_), channel_id=1, source_target_pairs={{0,16},{2,18},{4,20},{6,22},{8,24},{10,26},{12,28},{14,30},{16,0},... | collective-permute-start | bytes 98312 | tf_op jit(solution)/shard_map/ppermute | solution.py:350
  37.6 9.6 %collective-permute-start.12 = (bf16[512,128]{1,0:T(8,128)(2,1)S(1)}, bf16[512,128]{1,0:T(8,128)(2,1)S(1)}, u32[]{:S(2)}, u32[]{:S(2)}) collective-permute-start(bf16[512,128]{1,0:T(8,128)(2,1)S(1)} %shard_map.71.after_ref.refs_0_), channel_id=1, source_target_pairs={{0,12},{2,14},{4,8},{6,10},{8,4},{10,6},{12,0},{14,2},{16,28},{18,... | collective-permute-start | bytes 393224 | tf_op jit(solution)/shard_map/ppermute | solution.py:350
  37.7 9.5 %collective-permute-start.11 = (bf16[512,128]{1,0:T(8,128)(2,1)S(1)}, bf16[512,128]{1,0:T(8,128)(2,1)S(1)}, u32[]{:S(2)}, u32[]{:S(2)}) collective-permute-start(bf16[512,128]{1,0:T(8,128)(2,1)S(1)} %shard_map.71.after_ref.refs_0_), channel_id=1, source_target_pairs={{0,8},{2,10},{4,12},{6,14},{8,0},{10,2},{12,4},{14,6},{16,24},{18,... | collective-permute-start | bytes 393224 | tf_op jit(solution)/shard_map/ppermute | solution.py:350
  37.8 9.4 %collective-permute-start.10 = (bf16[512,128]{1,0:T(8,128)(2,1)S(1)}, bf16[512,128]{1,0:T(8,128)(2,1)S(1)}, u32[]{:S(2)}, u32[]{:S(2)}) collective-permute-start(bf16[512,128]{1,0:T(8,128)(2,1)S(1)} %shard_map.71.after_ref.refs_0_), channel_id=1, source_target_pairs={{0,4},{2,6},{4,0},{6,2},{8,12},{10,14},{12,8},{14,10},{16,20},{18,... | collective-permute-start | bytes 393224 | tf_op jit(solution)/shard_map/ppermute | solution.py:350
  47.2 4.2 %collective-permute-start.13 = (bf16[2048,128]{1,0:T(8,128)(2,1)S(1)}, bf16[2048,128]{1,0:T(8,128)(2,1)S(1)}, u32[]{:S(2)}, u32[]{:S(2)}) collective-permute-start(bf16[2048,128]{1,0:T(8,128)(2,1)S(1)} %shard_map.74.after_ref.near_ref), channel_id=1, source_target_pairs={{0,2},{2,0},{4,6},{6,4},{8,10},{10,8},{12,14},{14,12},{16,18},{18,... | collective-permute-start | bytes 1572872 | tf_op jit(solution)/shard_map/ppermute | solution.py:350
  54.5 15.6 %collective-permute-start.14 = (bf16[128,1024]{1,0:T(8,128)(2,1)S(1)}, bf16[128,1024]{1,0:T(8,128)(2,1)S(1)}, u32[]{:S(2)}, u32[]{:S(2)}) collective-permute-start(bf16[128,1024]{1,0:T(8,128)(2,1)S(1)} %get-tuple-element.45), channel_id=1, source_target_pairs={{0,1},{1,0},{2,3},{3,2},{4,5},{5,4},{6,7},{7,6},{8,9},{9,8},{10,11... | collective-permute-start | bytes 786440 | tf_op jit(solution)/shard_map/ppermute | solution.py:453
  64.5 5.7 %collective-permute-start.15 = (bf16[64,1024]{1,0:T(8,128)(2,1)S(1)}, bf16[64,1024]{1,0:T(8,128)(2,1)S(1)}, u32[]{:S(2)}, u32[]{:S(2)}) collective-permute-start(bf16[64,1024]{1,0:T(8,128)(2,1)S(1)} %get-tuple-element.46), channel_id=1, source_target_pairs={{0,1},{1,0},{2,3},{3,2},{4,5},{5,4},{6,7},{7,6},{8,9},{9,8},{10,11... | collective-permute-start | bytes 393224 | tf_op jit(solution)/shard_map/ppermute | solution.py:453

commit v12 on v11

--- a/solution.py
+++ b/solution.py
@@ -363,7 +363,7 @@
         [IN_VMEM, IN_VMEM, ANYWHERE],
         us=1.0,
     )(neighbours.reshape(slots, nodes // LANES, LANES), deg_tiles, block)
-    other = lax.ppermute(node_feats, "feat", swap)
+    other = lax.ppermute(own_feats, "feat", swap)
 
     block = join(block, arrived, counts)
     arrived = stage(block, STAGES[1])

time: 71.4 us -> 71.4 us (level)
  transfers between devices with their start and end apart: 16 -> 16, of which waited for: 2 -> 2; matrix products, arithmetic and copies ran while one was open for 1% -> 1% of each run, Pallas kernels for 31% -> 30%
where the time goes in v12:
time: 71.4 us; the launch traced here: 71 us
  starting transfers between devices  32.7 us (46%)
  Pallas kernels  25.9 us (36%)
  waiting for transfers between devices  7.28 us (10%)
  local copies, waits for them, and re-layouts  4.82 us (7%)
    ppermute x9, starting transfers between devices, stage(): lax.ppermute(block, 'slab', [(i, i ^ bit) for i in range(slabs)])  17.6 us
    pallas_call x2, Pallas kernels, layer(): pallas(functools.partial(layer_kernel, slots, first, start, len(near), ha...  10.8 us
    ppermute x1, starting transfers between devices, local(): lax.ppermute(outer, 'slab', [(i, j) for i in range(slabs) for j in [i + 2...  9.57 us
    pallas_call x2, Pallas kernels, near_sum(): pallas(functools.partial(near_kernel, slots, part, 2), f32(CHUNK, LANES),...  8.18 us
    ppermute x2, waiting for transfers between devices, local(): received.append(lax.ppermute(sent, 'feat', swap))  5.57 us
    unnamed x11, local copies, waits for them, and re-layouts  4.82 us
    pallas_call x1, Pallas kernels, local(): pallas(order_kernel, (tile,) * 6, [IN_VMEM, ANYWHERE], us=3.0)  3.54 us
    ppermute x2, starting transfers between devices, local(): received.append(lax.ppermute(sent, 'feat', swap))  2.21 us
  transfers between devices with their start and end apart: 16, of which 2 were waited for; matrix products, arithmetic and copies ran while one was open for 1% of the time, Pallas kernels for 30%

profile of v12, /device:TPU:16, one launch (start us, length us, event | category | flops | bytes accessed | tf_op | source)
XLA Modules:
  0.0 71.0 jit_solution(6600466753201378159)
XLA Ops:
  0.0 0.0 copy-start
  0.0 1.0 %copy-done = bf16[64,4096]{1,0:T(8,128)(2,1)S(1)} copy-done((bf16[64,4096]{1,0:T(8,128)(2,1)S(1)}, bf16[64,4096]{1,0:T(8,128)(2,1)}, u32[]{:S(2)}) %copy-start) | copy-done | bytes 524312
  1.0 0.0 copy-start.3
  1.0 0.7 copy-done.3
  1.7 0.4 shard_map.64
  2.1 1.3 %collective-permute-start = (bf16[64,4096]{1,0:T(8,128)(2,1)S(1)}, bf16[64,4096]{1,0:T(8,128)(2,1)S(1)}, u32[]{:S(2)}, u32[]{:S(2)}) collective-permute-start(bf16[64,4096]{1,0:T(8,128)(2,1)S(1)} %get-tuple-element.29.x_ref), channel_id=1, source_target_pairs={{0,1},{1,0},{2,3},{3,2},{4,5},{5,4},{6,7},{7,6},{8,9},{9,8},{10,11... | collective-permute-start | bytes 1572872 | tf_op jit(solution)/shard_map/ppermute | solution.py:366
  3.5 7.2 %collective-permute-start.1 = (bf16[16,128]{1,0:T(8,128)(2,1)S(1)}, bf16[16,128]{1,0:T(8,128)(2,1)S(1)}, u32[]{:S(2)}, u32[]{:S(2)}) collective-permute-start(bf16[16,128]{1,0:T(8,128)(2,1)S(1)} %get-tuple-element.26.after_ref.refs_0_), channel_id=1, source_target_pairs={{0,64},{2,66},{4,68},{6,70},{8,72},{10,74},{12,76},{14,78},{16,80}... | collective-permute-start | bytes 12296 | tf_op jit(solution)/shard_map/ppermute | solution.py:350
  10.6 1.0 %copy.8 = s32[2,8,32,128]{3,2,1,0:T(8,128)S(1)} copy(s32[2,8,32,128]{3,1,2,0:T(8,128)} %bitcast.31) | data formatting | bytes 524288
  11.6 0.0 copy-start.1
  11.7 0.7 copy-done.1
  12.4 0.1 shard_map.65
  12.5 0.0 collective-permute-done.1.refs_1_
  12.5 0.1 collective-permute-start.4
  12.6 1.8 %collective-permute-start.3 = (bf16[32,128]{1,0:T(8,128)(2,1)S(1)}, bf16[32,128]{1,0:T(8,128)(2,1)S(1)}, u32[]{:S(2)}, u32[]{:S(2)}) collective-permute-start(bf16[32,128]{1,0:T(8,128)(2,1)S(1)} %shard_map.66.after_ref.refs_0_), channel_id=1, source_target_pairs={{0,1},{1,0},{2,3},{3,2},{4,5},{5,4},{6,7},{7,6},{8,9},{9,8},{10,11... | collective-permute-start | bytes 24584 | tf_op jit(solution)/shard_map/ppermute | solution.py:370
  14.4 1.7 %collective-permute-start.2 = (bf16[32,128]{1,0:T(8,128)(2,1)S(1)}, bf16[32,128]{1,0:T(8,128)(2,1)S(1)}, u32[]{:S(2)}, u32[]{:S(2)}) collective-permute-start(bf16[32,128]{1,0:T(8,128)(2,1)S(1)} %shard_map.66.after_ref.refs_0_), channel_id=1, source_target_pairs={{0,128},{2,130},{4,132},{6,134},{8,136},{10,138},{12,140},{14,142}... | collective-permute-start | bytes 24584 | tf_op jit(solution)/shard_map/ppermute | solution.py:350
  16.1 0.0 copy-start.2
  16.1 0.8 %copy-done.2 = bf16[128,128]{1,0:T(8,128)(2,1)S(1)} copy-done((bf16[128,128]{1,0:T(8,128)(2,1)S(1)}, bf16[128,128]{1,0:T(8,128)(2,1)}, u32[]{:S(2)}) %copy-start.2) | copy-done | bytes 32792
  16.8 0.0 copy-start.4
  16.8 0.7 copy-done.4
  17.5 0.4 shard_map.67
  17.9 0.0 collective-permute-done.4.refs_3_
  17.9 0.0 collective-permute-done.3.refs_2_
  17.9 1.7 %collective-permute-done.2.refs_1_ = bf16[32,128]{1,0:T(8,128)(2,1)S(1)} collective-permute-done((bf16[32,128]{1,0:T(8,128)(2,1)S(1)}, bf16[32,128]{1,0:T(8,128)(2,1)S(1)}, u32[]{:S(2)}, u32[]{:S(2)}) %collective-permute-start.2) | collective-permute-done | bytes 8224 | tf_op jit(solution)/shard_map/ppermute | solution.py:350
  19.5 0.1 shard_map.68.after_ref.refs_0_
  19.6 0.0 collective-permute-done.other_ref
  19.6 0.1 shard_map.69
  19.8 0.1 collective-permute-start.6
  19.9 9.6 %collective-permute-start.5 = (bf16[128,2048]{1,0:T(8,128)(2,1)S(1)}, bf16[128,2048]{1,0:T(8,128)(2,1)S(1)}, u32[]{:S(2)}, u32[]{:S(2)}) collective-permute-start(bf16[128,2048]{1,0:T(8,128)(2,1)S(1)} %get-tuple-element.31.after_ref.outer_ref), channel_id=1, source_target_pairs={{2,4},{4,2},{6,8},{8,6},{10,12},{12,10},{14,16},{16,14},{18,20},{2... | collective-permute-start | bytes 1572872 | tf_op jit(solution)/shard_map/ppermute | solution.py:391
  29.4 0.1 collective-permute-start.9
  29.5 0.1 collective-permute-start.8
  29.6 4.3 %collective-permute-start.7 = (bf16[128,128]{1,0:T(8,128)(2,1)S(1)}, bf16[128,128]{1,0:T(8,128)(2,1)S(1)}, u32[]{:S(2)}, u32[]{:S(2)}) collective-permute-start(bf16[128,128]{1,0:T(8,128)(2,1)S(1)} %shard_map.68.after_ref.refs_0_), channel_id=1, source_target_pairs={{0,16},{2,18},{4,20},{6,22},{8,24},{10,26},{12,28},{14,30},{16,0},... | collective-permute-start | bytes 98312 | tf_op jit(solution)/shard_map/ppermute | solution.py:350
  33.9 3.5 %shard_map.70 = (s32[8,128]{1,0:T(8,128)S(1)}, s32[8,128]{1,0:T(8,128)S(1)}, s32[8,128]{1,0:T(8,128)S(1)}, s32[8,128]{1,0:T(8,128)S(1)}, s32[8,128]{1,0:T(8,128)S(1)}, /*index=5*/s32[8,128]{1,0:T(8,128)S(1)}) custom-call(s32[3,8,128]{2,1,0:T(8,128)S(1)} %get-tuple-element.28.refs_2_.counts_ref, bf16[128,2048]{1,0:T(8,128)(2,1)S(1)} %get-tuple-element.31.after_ref.outer_ref), custom_call_target="tpu_custom_call" | custom-call | bytes 9000000 | tf_op jit(solution)/shard_map/pallas_call | solution.py:395
  37.5 0.0 collective-permute-done.9.refs_3_
  37.5 0.0 collective-permute-done.8.refs_2_
  37.5 0.0 collective-permute-done.7.refs_1_
  37.5 0.1 collective-permute-start.12
  37.6 0.1 collective-permute-start.11
  37.7 4.0 %collective-permute-start.10 = (bf16[512,128]{1,0:T(8,128)(2,1)S(1)}, bf16[512,128]{1,0:T(8,128)(2,1)S(1)}, u32[]{:S(2)}, u32[]{:S(2)}) collective-permute-start(bf16[512,128]{1,0:T(8,128)(2,1)S(1)} %shard_map.71.after_ref.refs_0_), channel_id=1, source_target_pairs={{0,4},{2,6},{4,0},{6,2},{8,12},{10,14},{12,8},{14,10},{16,20},{18,... | collective-permute-start | bytes 393224 | tf_op jit(solution)/shard_map/ppermute | solution.py:350
  41.7 0.0 collective-permute-done.6.inner_halo_ref
  41.7 0.0 collective-permute-done.5.outer_halo_ref
  41.7 1.2 %shard_map.72.frame_ref.frame_in = f32[12296,128]{1,0:T(8,128)S(1)} custom-call(bf16[128,2048]{1,0:T(8,128)(2,1)S(1)} %collective-permute-done.5.outer_halo_ref, bf16[128,2048]{1,0:T(8,128)(2,1)S(1)} %get-tuple-element.31.after_ref.outer_ref, bf16[128,2048]{1,0:T(8,128)(2,1)S(1)} %get-tuple-element.34.inner_ref, ...), custom_call_target="tpu_custom_call" | custom-call | bytes 6000000 | tf_op jit(solution)/shard_map/pallas_call | solution.py:401
  43.0 4.1 %shard_map.73.refs_4_.refs_0_ = f32[1024,128]{1,0:T(8,128)S(1)} custom-call(s32[16384]{0:T(1024)S(1)} %bitcast.15, s32[1024]{0:T(1024)S(1)} %bitcast.21, s32[1024]{0:T(1024)S(1)} %bitcast.23, f32[12296,128]{1,0:T(8,128)S(1)} %shard_map.72.frame_ref.frame_in, bf16[512,128]{1,0:T(8,128)(2,1)S(1)} %shard_map.71.after_ref.refs_0_), custom_call_target="tpu_custom_call" | custom-call | bytes 12000000 | tf_op jit(solution)/shard_map/pallas_call | solution.py:417
  47.1 0.0 collective-permute-done.12.refs_3_
  47.1 0.0 collective-permute-done.11.refs_2_
  47.1 0.0 collective-permute-done.10.refs_1_
  47.2 0.1 collective-permute-start.13
  47.3 4.1 %shard_map.75.after_ref.refs_1_ = f32[1024,128]{1,0:T(8,128)S(1)} custom-call(s32[16384]{0:T(1024)S(1)} %bitcast.16, s32[1024]{0:T(1024)S(1)} %bitcast.22, s32[1024]{0:T(1024)S(1)} %bitcast.24, f32[12296,128]{1,0:T(8,128)S(1)} %shard_map.72.frame_ref.frame_in, bf16[2048,128]{1,0:T(8,128)(2,1)S(1)} %shard_map.74.after_ref.near_ref), custom_call_target="tpu_custom_call" | custom-call | bytes 12000000 | tf_op jit(solution)/shard_map/pallas_call | solution.py:417
  51.4 0.0 collective-permute-done.13.far_ref
  51.4 0.1 shard_map.76.frame_ref
  51.5 3.0 %shard_map.77 = (bf16[64,1024]{1,0:T(8,128)(2,1)S(1)}, bf16[128,1024]{1,0:T(8,128)(2,1)S(1)}) custom-call(s32[16384]{0:T(1024)S(1)} %bitcast.18, s32[1024]{0:T(1024)S(1)} %bitcast.25, s32[1024]{0:T(1024)S(1)} %bitcast.26, f32[12296,128]{1,0:T(8,128)S(1)} %shard_map.76.frame_ref, f32[2048,128]{1,0:T(8,128)S(1)} %get-tuple-element.30.refs_4_.scale_ref, ...), custom_call_target="tpu_custom_call" | custom-call | bytes 9000000 | tf_op jit(solution)/shard_map/pallas_call | solution.py:438
  54.5 2.1 %collective-permute-start.14 = (bf16[128,1024]{1,0:T(8,128)(2,1)S(1)}, bf16[128,1024]{1,0:T(8,128)(2,1)S(1)}, u32[]{:S(2)}, u32[]{:S(2)}) collective-permute-start(bf16[128,1024]{1,0:T(8,128)(2,1)S(1)} %get-tuple-element.45), channel_id=1, source_target_pairs={{0,1},{1,0},{2,3},{3,2},{4,5},{5,4},{6,7},{7,6},{8,9},{9,8},{10,11... | collective-permute-start | bytes 786440 | tf_op jit(solution)/shard_map/ppermute | solution.py:453
  56.6 7.8 %shard_map.78 = (bf16[64,1024]{1,0:T(8,128)(2,1)S(1)}, bf16[64,1024]{1,0:T(8,128)(2,1)S(1)}) custom-call(s32[16384]{0:T(1024)S(1)} %bitcast.17, s32[1024]{0:T(1024)S(1)} %bitcast.27, s32[1024]{0:T(1024)S(1)} %bitcast.28, f32[12296,128]{1,0:T(8,128)S(1)} %shard_map.76.frame_ref, f32[2048,128]{1,0:T(8,128)S(1)} %get-tuple-element.30.refs_4_.scale_ref, ...), custom_call_target="tpu_custom_call" | custom-call | bytes 24000000 | tf_op jit(solution)/shard_map/pallas_call | solution.py:438
  64.5 0.1 collective-permute-start.15
  64.6 5.6 %collective-permute-done.15.refs_3_ = bf16[64,1024]{1,0:T(8,128)(2,1)S(1)} collective-permute-done((bf16[64,1024]{1,0:T(8,128)(2,1)S(1)}, bf16[64,1024]{1,0:T(8,128)(2,1)S(1)}, u32[]{:S(2)}, u32[]{:S(2)}) %collective-permute-start.15) | collective-permute-done | bytes 131104 | tf_op jit(solution)/shard_map/ppermute | solution.py:453
  70.1 0.0 collective-permute-done.14.refs_2_
  70.1 0.8 %shard_map.79 = bf16[64,4096]{1,0:T(8,128)(2,1)} custom-call(bf16[64,1024]{1,0:T(8,128)(2,1)S(1)} %get-tuple-element.40.after_ref.refs_0_, bf16[64,1024]{1,0:T(8,128)(2,1)S(1)} %get-tuple-element.44.refs_1_, bf16[128,1024]{1,0:T(8,128)(2,1)S(1)} %collective-permute-done.14.refs_2_, bf16[64,1024]{1,0:T(8,128)(2,1)S(1)} %collective-permute-done.15.refs_3_), custom_call_target="tpu_custom_call" | custom-call | bytes 1500000 | tf_op jit(solution)/shard_map/pallas_call | solution.py:455
  (3 shorter events, 0.1 us)
Async XLA Ops:
  0.0 1.0 %copy-start = (bf16[64,4096]{1,0:T(8,128)(2,1)S(1)}, bf16[64,4096]{1,0:T(8,128)(2,1)}, u32[]{:S(2)}) copy-start(bf16[64,4096]{1,0:T(8,128)(2,1)} %x_ref.1) | copy-start | bytes 1572868
  1.0 0.7 copy-start.3
  2.1 17.5 %collective-permute-start = (bf16[64,4096]{1,0:T(8,128)(2,1)S(1)}, bf16[64,4096]{1,0:T(8,128)(2,1)S(1)}, u32[]{:S(2)}, u32[]{:S(2)}) collective-permute-start(bf16[64,4096]{1,0:T(8,128)(2,1)S(1)} %get-tuple-element.29.x_ref), channel_id=1, source_target_pairs={{0,1},{1,0},{2,3},{3,2},{4,5},{5,4},{6,7},{7,6},{8,9},{9,8},{10,11... | collective-permute-start | bytes 1572872 | tf_op jit(solution)/shard_map/ppermute | solution.py:366
  3.5 9.0 %collective-permute-start.1 = (bf16[16,128]{1,0:T(8,128)(2,1)S(1)}, bf16[16,128]{1,0:T(8,128)(2,1)S(1)}, u32[]{:S(2)}, u32[]{:S(2)}) collective-permute-start(bf16[16,128]{1,0:T(8,128)(2,1)S(1)} %get-tuple-element.26.after_ref.refs_0_), channel_id=1, source_target_pairs={{0,64},{2,66},{4,68},{6,70},{8,72},{10,74},{12,76},{14,78},{16,80}... | collective-permute-start | bytes 12296 | tf_op jit(solution)/shard_map/ppermute | solution.py:350
  11.6 0.7 %copy-start.1 = (s32[4096]{0:T(1024)S(1)}, s32[4096]{0:T(1024)}, u32[]{:S(2)}) copy-start(s32[4096]{0:T(1024)} %param.8) | copy-start | bytes 49156
  12.5 5.4 %collective-permute-start.4 = (bf16[32,128]{1,0:T(8,128)(2,1)S(1)}, bf16[32,128]{1,0:T(8,128)(2,1)S(1)}, u32[]{:S(2)}, u32[]{:S(2)}) collective-permute-start(bf16[32,128]{1,0:T(8,128)(2,1)S(1)} %shard_map.66.after_ref.refs_0_), channel_id=1, source_target_pairs={{0,129},{1,128},{2,131},{3,130},{4,133},{5,132},{6,135},{7,134},{8... | collective-permute-start | bytes 24584 | tf_op jit(solution)/shard_map/ppermute | solution.py:372
  12.6 5.3 %collective-permute-start.3 = (bf16[32,128]{1,0:T(8,128)(2,1)S(1)}, bf16[32,128]{1,0:T(8,128)(2,1)S(1)}, u32[]{:S(2)}, u32[]{:S(2)}) collective-permute-start(bf16[32,128]{1,0:T(8,128)(2,1)S(1)} %shard_map.66.after_ref.refs_0_), channel_id=1, source_target_pairs={{0,1},{1,0},{2,3},{3,2},{4,5},{5,4},{6,7},{7,6},{8,9},{9,8},{10,11... | collective-permute-start | bytes 24584 | tf_op jit(solution)/shard_map/ppermute | solution.py:370
  14.4 5.2 %collective-permute-start.2 = (bf16[32,128]{1,0:T(8,128)(2,1)S(1)}, bf16[32,128]{1,0:T(8,128)(2,1)S(1)}, u32[]{:S(2)}, u32[]{:S(2)}) collective-permute-start(bf16[32,128]{1,0:T(8,128)(2,1)S(1)} %shard_map.66.after_ref.refs_0_), channel_id=1, source_target_pairs={{0,128},{2,130},{4,132},{6,134},{8,136},{10,138},{12,140},{14,142}... | collective-permute-start | bytes 24584 | tf_op jit(solution)/shard_map/ppermute | solution.py:350
  16.1 0.8 %copy-start.2 = (bf16[128,128]{1,0:T(8,128)(2,1)S(1)}, bf16[128,128]{1,0:T(8,128)(2,1)}, u32[]{:S(2)}) copy-start(bf16[128,128]{1,0:T(8,128)(2,1)} %weight_ref.1) | copy-start | bytes 98308
  16.8 0.7 copy-start.4
  19.8 22.0 %collective-permute-start.6 = (bf16[128,2048]{1,0:T(8,128)(2,1)S(1)}, bf16[128,2048]{1,0:T(8,128)(2,1)S(1)}, u32[]{:S(2)}, u32[]{:S(2)}) collective-permute-start(bf16[128,2048]{1,0:T(8,128)(2,1)S(1)} %get-tuple-element.34.inner_ref), channel_id=1, source_target_pairs={{0,2},{2,0},{4,6},{6,4},{8,10},{10,8},{12,14},{14,12},{16,18},{18,... | collective-permute-start | bytes 1572872 | tf_op jit(solution)/shard_map/ppermute | solution.py:390
  19.9 21.9 %collective-permute-start.5 = (bf16[128,2048]{1,0:T(8,128)(2,1)S(1)}, bf16[128,2048]{1,0:T(8,128)(2,1)S(1)}, u32[]{:S(2)}, u32[]{:S(2)}) collective-permute-start(bf16[128,2048]{1,0:T(8,128)(2,1)S(1)} %get-tuple-element.31.after_ref.outer_ref), channel_id=1, source_target_pairs={{2,4},{4,2},{6,8},{8,6},{10,12},{12,10},{14,16},{16,14},{18,20},{2... | collective-permute-start | bytes 1572872 | tf_op jit(solution)/shard_map/ppermute | solution.py:391
  29.4 8.0 %collective-permute-start.9 = (bf16[128,128]{1,0:T(8,128)(2,1)S(1)}, bf16[128,128]{1,0:T(8,128)(2,1)S(1)}, u32[]{:S(2)}, u32[]{:S(2)}) collective-permute-start(bf16[128,128]{1,0:T(8,128)(2,1)S(1)} %shard_map.68.after_ref.refs_0_), channel_id=1, source_target_pairs={{0,48},{2,50},{4,52},{6,54},{8,56},{10,58},{12,60},{14,62},{16,32}... | collective-permute-start | bytes 98312 | tf_op jit(solution)/shard_map/ppermute | solution.py:350
  29.5 8.0 %collective-permute-start.8 = (bf16[128,128]{1,0:T(8,128)(2,1)S(1)}, bf16[128,128]{1,0:T(8,128)(2,1)S(1)}, u32[]{:S(2)}, u32[]{:S(2)}) collective-permute-start(bf16[128,128]{1,0:T(8,128)(2,1)S(1)} %shard_map.68.after_ref.refs_0_), channel_id=1, source_target_pairs={{0,32},{2,34},{4,36},{6,38},{8,40},{10,42},{12,44},{14,46},{16,48}... | collective-permute-start | bytes 98312 | tf_op jit(solution)/shard_map/ppermute | solution.py:350
  29.6 7.9 %collective-permute-start.7 = (bf16[128,128]{1,0:T(8,128)(2,1)S(1)}, bf16[128,128]{1,0:T(8,128)(2,1)S(1)}, u32[]{:S(2)}, u32[]{:S(2)}) collective-permute-start(bf16[128,128]{1,0:T(8,128)(2,1)S(1)} %shard_map.68.after_ref.refs_0_), channel_id=1, source_target_pairs={{0,16},{2,18},{4,20},{6,22},{8,24},{10,26},{12,28},{14,30},{16,0},... | collective-permute-start | bytes 98312 | tf_op jit(solution)/shard_map/ppermute | solution.py:350
  37.5 9.6 %collective-permute-start.12 = (bf16[512,128]{1,0:T(8,128)(2,1)S(1)}, bf16[512,128]{1,0:T(8,128)(2,1)S(1)}, u32[]{:S(2)}, u32[]{:S(2)}) collective-permute-start(bf16[512,128]{1,0:T(8,128)(2,1)S(1)} %shard_map.71.after_ref.refs_0_), channel_id=1, source_target_pairs={{0,12},{2,14},{4,8},{6,10},{8,4},{10,6},{12,0},{14,2},{16,28},{18,... | collective-permute-start | bytes 393224 | tf_op jit(solution)/shard_map/ppermute | solution.py:350
  37.6 9.5 %collective-permute-start.11 = (bf16[512,128]{1,0:T(8,128)(2,1)S(1)}, bf16[512,128]{1,0:T(8,128)(2,1)S(1)}, u32[]{:S(2)}, u32[]{:S(2)}) collective-permute-start(bf16[512,128]{1,0:T(8,128)(2,1)S(1)} %shard_map.71.after_ref.refs_0_), channel_id=1, source_target_pairs={{0,8},{2,10},{4,12},{6,14},{8,0},{10,2},{12,4},{14,6},{16,24},{18,... | collective-permute-start | bytes 393224 | tf_op jit(solution)/shard_map/ppermute | solution.py:350
  37.7 9.4 %collective-permute-start.10 = (bf16[512,128]{1,0:T(8,128)(2,1)S(1)}, bf16[512,128]{1,0:T(8,128)(2,1)S(1)}, u32[]{:S(2)}, u32[]{:S(2)}) collective-permute-start(bf16[512,128]{1,0:T(8,128)(2,1)S(1)} %shard_map.71.after_ref.refs_0_), channel_id=1, source_target_pairs={{0,4},{2,6},{4,0},{6,2},{8,12},{10,14},{12,8},{14,10},{16,20},{18,... | collective-permute-start | bytes 393224 | tf_op jit(solution)/shard_map/ppermute | solution.py:350
  47.2 4.2 %collective-permute-start.13 = (bf16[2048,128]{1,0:T(8,128)(2,1)S(1)}, bf16[2048,128]{1,0:T(8,128)(2,1)S(1)}, u32[]{:S(2)}, u32[]{:S(2)}) collective-permute-start(bf16[2048,128]{1,0:T(8,128)(2,1)S(1)} %shard_map.74.after_ref.near_ref), channel_id=1, source_target_pairs={{0,2},{2,0},{4,6},{6,4},{8,10},{10,8},{12,14},{14,12},{16,18},{18,... | collective-permute-start | bytes 1572872 | tf_op jit(solution)/shard_map/ppermute | solution.py:350
  54.5 15.6 %collective-permute-start.14 = (bf16[128,1024]{1,0:T(8,128)(2,1)S(1)}, bf16[128,1024]{1,0:T(8,128)(2,1)S(1)}, u32[]{:S(2)}, u32[]{:S(2)}) collective-permute-start(bf16[128,1024]{1,0:T(8,128)(2,1)S(1)} %get-tuple-element.45), channel_id=1, source_target_pairs={{0,1},{1,0},{2,3},{3,2},{4,5},{5,4},{6,7},{7,6},{8,9},{9,8},{10,11... | collective-permute-start | bytes 786440 | tf_op jit(solution)/shard_map/ppermute | solution.py:453
  64.5 5.7 %collective-permute-start.15 = (bf16[64,1024]{1,0:T(8,128)(2,1)S(1)}, bf16[64,1024]{1,0:T(8,128)(2,1)S(1)}, u32[]{:S(2)}, u32[]{:S(2)}) collective-permute-start(bf16[64,1024]{1,0:T(8,128)(2,1)S(1)} %get-tuple-element.46), channel_id=1, source_target_pairs={{0,1},{1,0},{2,3},{3,2},{4,5},{5,4},{6,7},{7,6},{8,9},{9,8},{10,11... | collective-permute-start | bytes 393224 | tf_op jit(solution)/shard_map/ppermute | solution.py:453
